TPU v7x, 32 devices: a whole 2x2x4 slice. The times are simulated.
32 devices in a mesh: aux: 2 (over core), occ: 16 (over z, y, x).
Axes of the slice: x: 2, y: 2, z: 4, core: 2. Of those that a mesh axis runs over, the one named last changes fastest.
Arguments:
- factors: float32 [2048, 16, 512], P('aux', 'occ'), may hold values from -0.3 to 0.3
- eps_occ: float32 [16], P('occ'), may hold values from -2 to -0.3
- eps_virt: float32 [512], replicated, may hold values from 0.2 to 3
- pair_mask: int32 [16, 4], P('occ'), may hold values 0 or 1
Outputs:
- gradient: float32 [2048, 16, 512], P('aux', 'occ')
Inputs may be any that keep to these rules, and one draw needn't show every extreme that they name: `pair_mask`: 1 marks a surviving pair.
All inputs are finite; a program needn't handle non-finite values. No bound on the sum of `pair_mask` on one device may be relied on, other than what follows from the above.
Results may differ from a plain program's by a relative error of at most 0.0003.
Values sent between devices are 32-bit elements; how exact they have to be, the bound alone decides.
No kernel may reach another device: no remote copies, remote signals or barrier semaphores. Data moves between devices by JAX's collectives and lax.ppermute only.
A program may use at most 128 MiB of HBM per device.

v0:
```python
import dataclasses
import functools

import jax
import jax.numpy as jnp
from jax import lax
from jax.experimental import pallas as pl
from jax.experimental.pallas import tpu as pltpu
from jax.sharding import PartitionSpec as P

LANES = 128
SUBLANES = 8
PLANE = 4
CHUNKS = 4
VMEM_LIMIT = 60 * 1024 * 1024


def split(value):
    high = value.astype(jnp.bfloat16)
    low = (value - high.astype(jnp.float32)).astype(jnp.bfloat16)
    return high, low


def deep_left(value):
    high, low = split(value)
    return jnp.concatenate([high, low, high], axis=1)


def deep_right(value):
    high, low = split(value)
    return jnp.concatenate([high, high, low], axis=0)


def dot(left, right):
    numbers = (((1,), (0,)), ((), ()))
    return lax.dot_general(left, right, numbers, preferred_element_type=jnp.float32)


def rows_of(ref, start, count, width):
    lines = width // LANES
    columns = [ref[pl.ds(start * lines + at, count, stride=lines), :] for at in range(lines)]
    return jnp.concatenate(columns, axis=1)


def distinct(arrays):
    return list({id(array): array for array in arrays}.values())


class Copies:
    def __init__(self, semaphores):
        self.semaphores = semaphores
        self.used = 0

    def start(self, source, target):
        copy = pltpu.make_async_copy(source, target, self.semaphores.at[self.used])
        self.used += 1
        copy.start()
        return copy

    def start_piece(self, piece, ref_of, choices, count, target):
        made = []
        for array, base in piece.places:
            source = ref_of[id(array)].at[pl.ds(base, count)]
            made.append(pltpu.make_async_copy(source, target, self.semaphores.at[self.used]))
        self.used += 1
        if len(made) == 1:
            made[0].start()
        else:
            for at, copy in enumerate(made):
                pl.when(choices[piece.choice] == at)(copy.start)
        return made[0]


@dataclasses.dataclass(frozen=True)
class Piece:
    places: tuple
    choice: int = 0


def call(kernel, smem, vmem, anywhere, outputs, out_space, scratch):
    spaces = [pltpu.SMEM] * len(smem) + [pltpu.VMEM] * len(vmem) + [pl.ANY] * len(anywhere)
    return pl.pallas_call(
        kernel,
        out_shape=outputs,
        in_specs=[pl.BlockSpec(memory_space=space) for space in spaces],
        out_specs=[pl.BlockSpec(memory_space=out_space)] * len(outputs),
        scratch_shapes=scratch,
        compiler_params=pltpu.CompilerParams(vmem_limit_bytes=VMEM_LIMIT),
        cost_estimate=pl.CostEstimate(flops=0, bytes_accessed=0, transcendentals=0),
    )(*smem, *vmem, *anywhere)


def prepare(own, rows, width):
    size = rows // CHUNKS
    cut = size * width // LANES

    def kernel(own_ref, high_ref, low_ref, integrals_ref, block_ref, semaphores):
        copies = Copies(semaphores)
        coming = [copies.start(own_ref.at[pl.ds(at * cut, cut)], block_ref.at[at]) for at in range(CHUNKS)]
        for at in range(CHUNKS):
            coming[at].wait()
            block = rows_of(block_ref.at[at], 0, size, width)
            high, low = split(block.T)
            high_ref[at] = high
            low_ref[at] = low
            value = dot(jnp.concatenate([high, low, high], axis=1), deep_right(block))
            integrals_ref[...] = integrals_ref[...] + value if at else value

    half = jax.ShapeDtypeStruct((CHUNKS, width, size), jnp.bfloat16)
    square = jax.ShapeDtypeStruct((width, width), jnp.float32)
    scratch = [pltpu.VMEM((CHUNKS, cut, LANES), jnp.float32), pltpu.SemaphoreType.DMA((CHUNKS,))]
    return call(kernel, [], [], [own], [half, half, square], pltpu.VMEM, scratch)


def arrays_of(pieces):
    return distinct([array for piece in pieces for array, _ in piece.places])


def integrate(turned, slots, first, flags, size, width, before=()):
    cut = size * width // LANES
    count = len(slots)
    pieces = [piece for slot in slots for piece in slot]
    arrays = arrays_of(pieces)
    numbers = [list(range(start, start + len(slot))) for slot, start in zip(slots, first)]
    needed = sorted({number for some in numbers for number in some})
    before = list(before)

    def kernel(flag_ref, *refs):
        given = iter(refs)
        high_ref, low_ref = next(given), next(given)
        before_refs = [next(given) for _ in before]
        ref_of = {id(array): next(given) for array in arrays}
        outs = [next(given) for _ in range(count)]
        turned_ref, block_ref, before_ref, semaphores = given
        copies = Copies(semaphores)
        coming, turning = [], {}

        def turn(number):
            if number not in turning:
                at = needed.index(number)
                turning[number] = [
                    copies.start(high_ref.at[number], turned_ref.at[at, 0]),
                    copies.start(low_ref.at[number], turned_ref.at[at, 1]),
                ]

        at = 0
        for slot in range(count):
            for number, piece in zip(numbers[slot], slots[slot]):
                turn(number)
                coming.append(copies.start_piece(piece, ref_of, flag_ref, cut, block_ref.at[at]))
                at += 1
        adding = [copies.start(ref, before_ref.at[slot]) for slot, ref in enumerate(before_refs)]
        at = 0
        for slot in range(count):
            for place, number in enumerate(numbers[slot]):
                for copy in turning.pop(number, []):
                    copy.wait()
                coming[at].wait()
                there = needed.index(number)
                high, low = turned_ref[there, 0], turned_ref[there, 1]
                left = jnp.concatenate([high, low, high], axis=1)
                value = dot(left, deep_right(rows_of(block_ref.at[at], 0, size, width)))
                outs[slot][...] = outs[slot][...] + value if place else value
                at += 1
            if before:
                adding[slot].wait()
                outs[slot][...] += before_ref[slot]

    out = [jax.ShapeDtypeStruct((width, width), jnp.float32)] * count
    scratch = [
        pltpu.VMEM((len(needed), 2, width, size), jnp.bfloat16),
        pltpu.VMEM((len(pieces), cut, LANES), jnp.float32),
        pltpu.VMEM((max(len(before), 1), width, width), jnp.float32),
        pltpu.SemaphoreType.DMA((2 * len(needed) + len(pieces) + len(before),)),
    ]
    return call(kernel, [flags], [], [*turned, *before, *arrays], out, pltpu.VMEM, scratch)


def contract(partials, slots, signs, energies, flags, eps_virt, size, before=None):
    count = len(slots)
    chunks = len(slots[0])
    virt = eps_virt.shape[1]
    width = partials[0][0].shape[0]
    occ_rows = width // virt
    lines = width // LANES
    cut = size * lines
    sums = [array for slot in partials for array in slot]
    pieces = [piece for slot in slots for piece in slot]
    arrays = arrays_of([*pieces, *energies])
    last = [before] if before is not None else []

    def kernel(*refs):
        given = iter(refs)
        sign_ref, flag_ref, virt_ref = next(given), next(given), next(given)
        sum_refs = [next(given) for _ in sums]
        before_refs = [next(given) for _ in last]
        ref_of = {id(array): next(given) for array in arrays}
        out_ref, energy_ref, sum_ref, block_ref, result_ref, right_ref, semaphores = given
        copies = Copies(semaphores)
        arriving = [
            copies.start_piece(piece, ref_of, flag_ref, SUBLANES, energy_ref.at[at])
            for at, piece in enumerate(energies)
        ]
        arriving += [copies.start(ref, sum_ref.at[at]) for at, ref in enumerate(sum_refs)]
        coming = [
            [
                copies.start_piece(slots[slot][at], ref_of, flag_ref, cut, block_ref.at[slot, at])
                for slot in range(count)
            ]
            for at in range(chunks)
        ]
        adding = [
            [copies.start(ref.at[pl.ds(at * cut, cut)], result_ref.at[at]) for ref in before_refs]
            for at in range(chunks)
        ]
        for copy in arriving:
            copy.wait()

        def line(at):
            virtual = virt_ref[...]
            energy = energy_ref[at]
            return jnp.concatenate([virtual - energy[:1, i : i + 1] for i in range(occ_rows)], axis=1)

        row = jnp.broadcast_to(line(0), (SUBLANES, width)).T[:, :1]
        at = 0
        for slot in range(count):
            total = sum_ref[at]
            for extra in range(1, len(partials[slot])):
                total = total + sum_ref[at + extra]
            at += len(partials[slot])
            amplitude = (sign_ref[slot] * total) / (row + line(slot + 1))
            right_ref[pl.ds(slot * 3 * width, 3 * width), :] = deep_right(amplitude.T)
        leaving = []
        for at in range(chunks):
            for copy in coming[at] + adding[at]:
                copy.wait()
            left = [deep_left(rows_of(block_ref.at[slot, at], 0, size, width)) for slot in range(count)]
            value = dot(jnp.concatenate(left, axis=1), right_ref[...])
            for column in range(lines):
                lanes = value[:, column * LANES : (column + 1) * LANES]
                where = pl.ds(column, size, stride=lines)
                if last:
                    lanes = lanes + result_ref[at, where, :]
                result_ref[at, where, :] = lanes
            leaving.append(copies.start(result_ref.at[at], out_ref.at[pl.ds(at * cut, cut)]))
        for copy in leaving:
            copy.wait()

    rows = chunks * size
    out = jax.ShapeDtypeStruct((rows * lines, LANES), jnp.float32)
    scratch = [
        pltpu.VMEM((len(energies), SUBLANES, LANES), jnp.float32),
        pltpu.VMEM((len(sums), width, width), jnp.float32),
        pltpu.VMEM((count, chunks, cut, LANES), jnp.float32),
        pltpu.VMEM((chunks, cut, LANES), jnp.float32),
        pltpu.VMEM((count * 3 * width, width), jnp.bfloat16),
        pltpu.SemaphoreType.DMA((len(energies) + len(sums) + len(pieces) + 2 * chunks,)),
    ]
    return call(kernel, [signs, flags], [eps_virt], [*sums, *last, *arrays], [out], pl.ANY, scratch)[0]


def after(block, *others):
    return lax.optimization_barrier((block, *others))[0]


def on_device(factors, eps_occ, eps_virt, pair_mask):
    rows, occ_rows, virt = factors.shape
    width = occ_rows * virt
    lines = width // LANES
    groups = lax.axis_size("occ")
    shares = lax.axis_size("aux")
    size = rows // CHUNKS
    cut = size * lines
    last = CHUNKS - 1
    group = lax.axis_index("occ")
    place = group % PLANE
    odd_x = place % 2 == 1
    odd_y = place // 2 == 1

    own = factors.reshape(rows * lines, LANES)
    energies = jnp.zeros((SUBLANES * LANES,), jnp.float32).at[:occ_rows].set(eps_occ)
    energies = energies.reshape(SUBLANES, LANES)

    def part(whole, at):
        return whole[at * cut : (at + 1) * cut]

    def within(block, moves):
        planes = range(0, groups, PLANE)
        return lax.ppermute(block, "occ", [(g + a, g + b) for g in planes for a, b in moves])

    def up(block):
        return lax.ppermute(block, "occ", [(g, g + PLANE) for g in range(groups - PLANE)])

    def totals(partial):
        if shares == 2:
            return [partial, lax.ppermute(partial, "aux", [(0, 1), (1, 0)])]
        return [lax.psum(partial, "aux")]

    def sign(offset):
        flag = lax.dynamic_index_in_dim(pair_mask[0], offset - 1, 0, keepdims=False)
        return jnp.where((group >= offset) & (flag > 0), -1.0, 0.0).astype(jnp.float32)

    sign_own = jnp.float32(-1.0)
    sign_z = sign(jnp.int32(PLANE))
    sign_x = sign(jnp.where(odd_x, 1, PLANE - 1))
    sign_y = sign(jnp.int32(PLANE // 2))
    sign_d = sign(jnp.where(odd_x, PLANE - 1, 1))

    first_sent = jnp.concatenate([part(own, 0), energies])
    down_x, down_y = 1 - place % 2, 1 - place // 2
    flags = jnp.stack(
        [down_x, down_y, jnp.where(odd_y, 0, 1 + place), jnp.where(odd_y, place - 1, 0)]
    ).astype(jnp.int32)

    def add(partials, slots, signs, carriers, before=None):
        return contract(partials, slots, jnp.stack(signs), carriers, flags, eps_virt[None, :], size, before)

    from_z = [up(first_sent)]
    up_x = within(first_sent, [(0, 1), (2, 3), (1, 0)])
    up_y = within(first_sent, [(0, 2), (1, 3)])
    high, low, partial_own = prepare(own, rows, width)
    turned = (high, low)
    sums_own = totals(partial_own)
    swap_x, swap_y = [], []
    passed = [partial_own, up_x, up_y]
    for at in range(CHUNKS):
        came, mine, *_ = lax.optimization_barrier((from_z[at], own, *passed))
        if at < last:
            from_z.append(up(part(mine, at + 1)))
            up_part = part(mine, at + 1)
            if at == 0:
                up_part = jnp.concatenate([up_part, energies])
            swap_x.append(within(jnp.where(odd_x, came, up_part), [(0, 1), (1, 0), (2, 3), (3, 2)]))
            swap_y.append(within(jnp.where(odd_y, came, up_part), [(0, 2), (2, 0), (1, 3), (3, 1)]))
        else:
            came_x = jnp.concatenate([came, energies])
            swap_x.append(within(jnp.where(odd_x, came_x, swap_y[0]), [(0, 1), (1, 0), (2, 3), (3, 2)]))
            swap_y.append(within(jnp.where(odd_y, came_x, up_x), [(0, 2), (2, 0), (1, 3), (3, 1)]))
        passed = [swap_x[at], swap_y[at]]

    middle = (place == 1) | (place == 2)
    cross = within(jnp.where(place == 2, swap_x[0], swap_y[0]), [(2, 0), (3, 2)])
    cycle = within(jnp.where(middle, swap_x[1], swap_y[1]), [(0, 1), (1, 3), (3, 2), (2, 0)])
    swap_d = within(swap_y[2], [(0, 1), (1, 0), (2, 3), (3, 2)])
    last_d = within(swap_y[3], [(0, 1), (1, 0)])

    def pieces_of(first, swaps, choice, base):
        arrays = [first, *swaps]
        return [Piece(((arrays[at], base), (arrays[at + 1], base)), choice) for at in range(CHUNKS)]

    def whole(array, base):
        return Piece(((array, base),))

    slot_own = [whole(own, at * cut) for at in range(CHUNKS)]
    slot_z = [whole(block, 0) for block in from_z]
    slot_x = pieces_of(up_x, swap_x, 0, 0)
    slot_y = pieces_of(up_y, swap_y, 1, 0)
    slot_d = [
        Piece(((swap_y[last], 0), (cross, 0), (swap_x[last], 0)), 2),
        Piece(((cycle, 0), (cross, 0), (swap_x[last], 0)), 3),
        Piece(((cycle, 0), (swap_d, 0)), 1),
        Piece(((swap_d, 0), (last_d, 0)), 1),
    ]
    eps_x = pieces_of(up_x, swap_x, 0, cut)[0]
    eps_y = pieces_of(up_y, swap_y, 1, cut)[0]
    eps_d = Piece(((swap_y[last], cut), (cross, cut), (swap_x[last], cut)), 2)

    partial_z, *early = integrate(
        turned, [slot_z, slot_x[:last], slot_y[:last]], [0, 0, 0], flags, size, width
    )
    gradient = add(
        [after(sums_own, cross), totals(partial_z)], [slot_own, slot_z], [sign_own, sign_z],
        [whole(first_sent, cut), whole(first_sent, cut), whole(from_z[0], cut)],
    )
    partial_x, partial_y = integrate(
        turned, [slot_x[last:], slot_y[last:]], [last, last], flags, size, width, early
    )
    gradient = add(
        [after(totals(partial_x), cycle), totals(partial_y)], [slot_x, slot_y], [sign_x, sign_y],
        [whole(first_sent, cut), eps_x, eps_y], gradient,
    )
    turned = after(turned, gradient)
    half = CHUNKS // 2
    partial_d = integrate(turned, [slot_d[:half]], [0], flags, size, width)
    (partial_d,) = integrate(turned, [slot_d[half:]], [half], flags, size, width, partial_d)
    gradient = add([totals(partial_d)], [slot_d], [sign_d], [whole(first_sent, cut), eps_d], gradient)
    return gradient.reshape(rows, occ_rows, virt)


def solution(mesh):
    if mesh.shape["occ"] % PLANE:
        raise ValueError("incomplete plane")
    in_specs = (P("aux", "occ", None), P("occ"), P(), P("occ", None))
    out_specs = P("aux", "occ", None)
    return jax.shard_map(
        on_device, mesh=mesh, in_specs=in_specs, out_specs=out_specs, check_vma=False
    )
```

profile of v0, /device:TPU:0, one launch (start us, length us, event | category | flops | bytes accessed | tf_op | source)
XLA Modules:
  0.0 147.9 jit_solution(1649999648054086471)
XLA Ops:
  2.3 4.8 %collective-permute-start.1 = (f32[1032,128]{1,0:T(8,128)S(1)}, f32[1032,128]{1,0:T(8,128)S(1)}, u32[]{:S(2)}, u32[]{:S(2)}) collective-permute-start(f32[1032,128]{1,0:T(8,128)S(1)} %pad_maximum_fusion.2.refs_12_.refs_18_), channel_id=1, source_target_pairs={{0,1},{2,3},{1,0},{4,5},{6,7},{5,4},{8,9},{10,11},{9,8},{12,13},{1... | collective-permute-start | bytes 1585160 | tf_op jit(solution)/shard_map/ppermute | solution.py:289
  7.1 4.3 %collective-permute-start = (f32[1032,128]{1,0:T(8,128)S(1)}, f32[1032,128]{1,0:T(8,128)}, u32[]{:S(2)}, u32[]{:S(2)}) collective-permute-start(f32[1032,128]{1,0:T(8,128)S(1)} %pad_maximum_fusion.2.refs_12_.refs_18_), channel_id=1, source_target_pairs={{0,4},{1,5},{2,6},{3,7},{4,8},{5,9},{6,10},{7,11},{8,12},{9,13},{1... | collective-permute-start | bytes 1585160 | tf_op jit(solution)/shard_map/ppermute | solution.py:292
  11.4 4.2 %collective-permute-start.2 = (f32[1032,128]{1,0:T(8,128)S(1)}, f32[1032,128]{1,0:T(8,128)}, u32[]{:S(2)}, u32[]{:S(2)}) collective-permute-start(f32[1032,128]{1,0:T(8,128)S(1)} %pad_maximum_fusion.2.refs_12_.refs_18_), channel_id=1, source_target_pairs={{0,2},{1,3},{4,6},{5,7},{8,10},{9,11},{12,14},{13,15},{16,18},{17,... | collective-permute-start | bytes 1585160 | tf_op jit(solution)/shard_map/ppermute | solution.py:289
  15.7 4.6 %shard_map.46 = (bf16[4,512,256]{2,1,0:T(8,128)(2,1)}, bf16[4,512,256]{2,1,0:T(8,128)(2,1)}, f32[512,512]{1,0:T(8,128)}) custom-call(f32[4096,128]{1,0:T(8,128)} %bitcast.18), custom_call_target="tpu_custom_call" | custom-call | tf_op jit(solution)/shard_map/pallas_call | solution.py:82
  21.6 4.0 %collective-permute-done.2.refs_10_.refs_13_ = f32[1032,128]{1,0:T(8,128)} collective-permute-done((f32[1032,128]{1,0:T(8,128)S(1)}, f32[1032,128]{1,0:T(8,128)}, u32[]{:S(2)}, u32[]{:S(2)}) %collective-permute-start.2) | collective-permute-done | bytes 528416 | tf_op jit(solution)/shard_map/ppermute | solution.py:289
  26.8 2.7 %collective-permute-start.5 = (f32[1032,128]{1,0:T(8,128)S(1)}, f32[1032,128]{1,0:T(8,128)}, u32[]{:S(2)}, u32[]{:S(2)}) collective-permute-start(f32[1032,128]{1,0:T(8,128)S(1)} %get-tuple-element.65), channel_id=1, source_target_pairs={{0,2},{2,0},{1,3},{3,1},{4,6},{6,4},{5,7},{7,5},{8,10},{10,8},{9,1... | collective-permute-start | bytes 1585160 | tf_op jit(solution)/shard_map/ppermute | solution.py:289
  29.5 2.7 %collective-permute-start.3 = (f32[1024,128]{1,0:T(8,128)S(1)}, f32[1024,128]{1,0:T(8,128)S(1)}, u32[]{:S(2)}, u32[]{:S(2)}) collective-permute-start(f32[1024,128]{1,0:T(8,128)S(1)} %slice.33), channel_id=1, source_target_pairs={{0,4},{1,5},{2,6},{3,7},{4,8},{5,9},{6,10},{7,11},{8,12},{9,13},{1... | collective-permute-start | bytes 1572872 | tf_op jit(solution)/shard_map/ppermute | solution.py:292
  32.2 9.4 %collective-permute-done.3.refs_3_.refs_9_ = f32[1024,128]{1,0:T(8,128)S(1)} collective-permute-done((f32[1024,128]{1,0:T(8,128)S(1)}, f32[1024,128]{1,0:T(8,128)S(1)}, u32[]{:S(2)}, u32[]{:S(2)}) %collective-permute-start.3) | collective-permute-done | bytes 524320 | tf_op jit(solution)/shard_map/ppermute | solution.py:292
  41.7 4.4 %collective-permute-start.6 = (f32[1024,128]{1,0:T(8,128)S(1)}, f32[1024,128]{1,0:T(8,128)S(1)}, u32[]{:S(2)}, u32[]{:S(2)}) collective-permute-start(f32[1024,128]{1,0:T(8,128)S(1)} %get-tuple-element.64), channel_id=1, source_target_pairs={{0,4},{1,5},{2,6},{3,7},{4,8},{5,9},{6,10},{7,11},{8,12},{9,13},{1... | collective-permute-start | bytes 1572872 | tf_op jit(solution)/shard_map/ppermute | solution.py:292
  48.1 6.4 %collective-permute-done.6.refs_4_.refs_10_ = f32[1024,128]{1,0:T(8,128)S(1)} collective-permute-done((f32[1024,128]{1,0:T(8,128)S(1)}, f32[1024,128]{1,0:T(8,128)S(1)}, u32[]{:S(2)}, u32[]{:S(2)}) %collective-permute-start.6) | collective-permute-done | bytes 524320 | tf_op jit(solution)/shard_map/ppermute | solution.py:292
  54.6 2.4 %collective-permute-done.7.refs_8_.refs_10_ = f32[1024,128]{1,0:T(8,128)} collective-permute-done((f32[1024,128]{1,0:T(8,128)S(1)}, f32[1024,128]{1,0:T(8,128)}, u32[]{:S(2)}, u32[]{:S(2)}) %collective-permute-start.7) | collective-permute-done | bytes 524320 | tf_op jit(solution)/shard_map/ppermute | solution.py:289
  60.7 3.5 %collective-permute-start.9 = (f32[1024,128]{1,0:T(8,128)}, f32[1024,128]{1,0:T(8,128)S(1)}, u32[]{:S(2)}, u32[]{:S(2)}) collective-permute-start(f32[1024,128]{1,0:T(8,128)} %get-tuple-element.63), channel_id=1, source_target_pairs={{0,4},{1,5},{2,6},{3,7},{4,8},{5,9},{6,10},{7,11},{8,12},{9,13},{1... | collective-permute-start | bytes 1572872 | tf_op jit(solution)/shard_map/ppermute | solution.py:292
  64.2 4.7 %collective-permute-done.10.refs_9_.refs_4_.refs_11_ = f32[1024,128]{1,0:T(8,128)S(1)} collective-permute-done((f32[1024,128]{1,0:T(8,128)}, f32[1024,128]{1,0:T(8,128)S(1)}, u32[]{:S(2)}, u32[]{:S(2)}) %collective-permute-start.10) | collective-permute-done | bytes 524320 | tf_op jit(solution)/shard_map/ppermute | solution.py:289
  71.3 2.6 %broadcast_select_fusion = (f32[1032,128]{1,0:T(8,128)}, f32[1032,128]{1,0:T(8,128)}, f32[1032,128]{1,0:T(8,128)}) fusion(f32[1032,128]{1,0:T(8,128)S(1)} %collective-permute-done.4.refs_7_.refs_9_, f32[1032,128]{1,0:T(8,128)} %collective-permute-done.5.refs_11_.refs_14_, pred[]{:T(512)S(6)} %eq.20, f32[8,128]{1,0:T(8,128)S(1)} %pad_bitcast_fusion, ...), kind=kLoop, calls=%fused_computation.7 | loop fusion | flops 528384 | bytes 3698691 | tf_op jit(solution)/shard_map/jit(_where)/select_n | solution.py:342
  77.1 8.2 %shard_map.47 = (f32[512,512]{1,0:T(8,128)}, f32[512,512]{1,0:T(8,128)}, f32[512,512]{1,0:T(8,128)}) custom-call(s32[4]{0:T(128)} %pad_add_fusion.flag_ref.refs_1_, bf16[4,512,256]{2,1,0:T(8,128)(2,1)} %get-tuple-element.57.refs_0_, bf16[4,512,256]{2,1,0:T(8,128)(2,1)} %get-tuple-element.58.refs_1_, f32[1032,128]{1,0:T(8,128)} %collective-permute-done.refs_2_.refs_8_, ...), custom_call_target="tpu_custom_call" | custom-call | tf_op jit(solution)/shard_map/pallas_call | solution.py:82
  87.7 4.7 %shard_map.48 = (f32[512,512]{1,0:T(8,128)}, f32[512,512]{1,0:T(8,128)}) custom-call(s32[4]{0:T(128)} %pad_add_fusion.flag_ref.refs_1_, bf16[4,512,256]{2,1,0:T(8,128)(2,1)} %get-tuple-element.57.refs_0_, bf16[4,512,256]{2,1,0:T(8,128)(2,1)} %get-tuple-element.58.refs_1_, f32[512,512]{1,0:T(8,128)} %get-tuple-element.47.refs_2_, ...), custom_call_target="tpu_custom_call" | custom-call | tf_op jit(solution)/shard_map/pallas_call | solution.py:82
  96.0 5.7 %collective-permute-done.18.refs_3_.refs_7_ = f32[1032,128]{1,0:T(8,128)S(1)} collective-permute-done((f32[1032,128]{1,0:T(8,128)S(1)}, f32[1032,128]{1,0:T(8,128)S(1)}, u32[]{:S(2)}, u32[]{:S(2)}) %collective-permute-start.18) | collective-permute-done | bytes 528416 | tf_op jit(solution)/shard_map/ppermute | solution.py:289
  105.6 8.7 %shard_map.49.refs_7_ = f32[4096,128]{1,0:T(8,128)} custom-call(f32[2]{0:T(128)} %pad_maximum_fusion.4.refs_0_, s32[4]{0:T(128)} %pad_add_fusion.flag_ref.refs_1_, f32[1,512]{1,0:T(1,128)} %bitcast.24, f32[512,512]{1,0:T(8,128)} %get-tuple-element.54.refs_3_, f32[512,512]{1,0:T(8,128)} %collective-permute-done.17.refs_4_, ...), custom_call_target="tpu_custom_call" | custom-call | tf_op jit(solution)/shard_map/pallas_call | solution.py:82
  114.3 4.5 %collective-permute-done.15.refs_5_.refs_3_.refs_9_ = f32[1024,128]{1,0:T(8,128)S(1)} collective-permute-done((f32[1024,128]{1,0:T(8,128)S(1)}, f32[1024,128]{1,0:T(8,128)S(1)}, u32[]{:S(2)}, u32[]{:S(2)}) %collective-permute-start.15) | collective-permute-done | bytes 524320 | tf_op jit(solution)/shard_map/ppermute | solution.py:289
  118.8 9.2 %shard_map.50.refs_5_ = f32[4096,128]{1,0:T(8,128)} custom-call(f32[2]{0:T(128)} %pad_maximum_fusion.3.refs_0_, s32[4]{0:T(128)} %pad_add_fusion.flag_ref.refs_1_, f32[1,512]{1,0:T(1,128)} %bitcast.25, f32[512,512]{1,0:T(8,128)} %get-tuple-element.51.refs_3_, f32[512,512]{1,0:T(8,128)} %collective-permute-done.14.refs_4_, ...), custom_call_target="tpu_custom_call" | custom-call | tf_op jit(solution)/shard_map/pallas_call | solution.py:82
  128.0 3.9 %shard_map.51.refs_2_ = f32[512,512]{1,0:T(8,128)} custom-call(s32[4]{0:T(128)} %pad_add_fusion.flag_ref.refs_1_, bf16[4,512,256]{2,1,0:T(8,128)(2,1)} %get-tuple-element.57.refs_0_, bf16[4,512,256]{2,1,0:T(8,128)(2,1)} %get-tuple-element.58.refs_1_, f32[1032,128]{1,0:T(8,128)} %copy-done.2, f32[1032,128]{1,0:T(8,128)} %copy-done.13, f32[1032,128]{1,0:T(8,128)} %copy-done.1, ...), custom_call_target="tpu_custom_call" | custom-call | tf_op jit(solution)/shard_map/pallas_call | solution.py:82
  133.5 4.1 %shard_map.52.refs_3_ = f32[512,512]{1,0:T(8,128)} custom-call(s32[4]{0:T(128)} %pad_add_fusion.flag_ref.refs_1_, bf16[4,512,256]{2,1,0:T(8,128)(2,1)} %get-tuple-element.57.refs_0_, bf16[4,512,256]{2,1,0:T(8,128)(2,1)} %get-tuple-element.58.refs_1_, f32[512,512]{1,0:T(8,128)} %shard_map.51.refs_2_, f32[1024,128]{1,0:T(8,128)} %copy-done.12, ...), custom_call_target="tpu_custom_call" | custom-call | tf_op jit(solution)/shard_map/pallas_call | solution.py:82
  138.3 2.2 %collective-permute-done.22.refs_4_ = f32[512,512]{1,0:T(8,128)S(1)} collective-permute-done((f32[512,512]{1,0:T(8,128)}, f32[512,512]{1,0:T(8,128)S(1)}, u32[]{:S(2)}, u32[]{:S(2)}) %collective-permute-start.22) | collective-permute-done | bytes 1048608 | tf_op jit(solution)/shard_map/ppermute | solution.py:296
  141.5 6.2 %shard_map.53 = f32[4096,128]{1,0:T(8,128)} custom-call(f32[1]{0:T(128)} %bitcast.1.refs_0_, s32[4]{0:T(128)} %pad_add_fusion.flag_ref.refs_1_, f32[1,512]{1,0:T(1,128)} %bitcast.26, f32[512,512]{1,0:T(8,128)} %shard_map.52.refs_3_, f32[512,512]{1,0:T(8,128)} %copy-done.16, f32[4096,128]{1,0:T(8,128)} %shard_map.50.refs_5_, f32[1032,128]{1,0:T(8,128)} %copy-done.2, ...), custom_call_target="tpu_custom_call" | custom-call | tf_op jit(solution)/shard_map/pallas_call | solution.py:82
  (81 shorter events, 26.2 us)
Async XLA Ops:
  2.3 18.0 %collective-permute-start.1 = (f32[1032,128]{1,0:T(8,128)S(1)}, f32[1032,128]{1,0:T(8,128)S(1)}, u32[]{:S(2)}, u32[]{:S(2)}) collective-permute-start(f32[1032,128]{1,0:T(8,128)S(1)} %pad_maximum_fusion.2.refs_12_.refs_18_), channel_id=1, source_target_pairs={{0,1},{2,3},{1,0},{4,5},{6,7},{5,4},{8,9},{10,11},{9,8},{12,13},{1... | collective-permute-start | bytes 1585160 | tf_op jit(solution)/shard_map/ppermute | solution.py:289
  7.1 14.5 %collective-permute-start = (f32[1032,128]{1,0:T(8,128)S(1)}, f32[1032,128]{1,0:T(8,128)}, u32[]{:S(2)}, u32[]{:S(2)}) collective-permute-start(f32[1032,128]{1,0:T(8,128)S(1)} %pad_maximum_fusion.2.refs_12_.refs_18_), channel_id=1, source_target_pairs={{0,4},{1,5},{2,6},{3,7},{4,8},{5,9},{6,10},{7,11},{8,12},{9,13},{1... | collective-permute-start | bytes 1585160 | tf_op jit(solution)/shard_map/ppermute | solution.py:292
  11.4 14.1 %collective-permute-start.2 = (f32[1032,128]{1,0:T(8,128)S(1)}, f32[1032,128]{1,0:T(8,128)}, u32[]{:S(2)}, u32[]{:S(2)}) collective-permute-start(f32[1032,128]{1,0:T(8,128)S(1)} %pad_maximum_fusion.2.refs_12_.refs_18_), channel_id=1, source_target_pairs={{0,2},{1,3},{4,6},{5,7},{8,10},{9,11},{12,14},{13,15},{16,18},{17,... | collective-permute-start | bytes 1585160 | tf_op jit(solution)/shard_map/ppermute | solution.py:289
  20.2 51.0 %copy-start.4 = (f32[1032,128]{1,0:T(8,128)}, f32[1032,128]{1,0:T(8,128)S(1)}, u32[]{:S(2)}) copy-start(f32[1032,128]{1,0:T(8,128)S(1)} %collective-permute-done.1.refs_6_.refs_8_) | copy-start | bytes 1585156
  26.7 14.8 %collective-permute-start.4 = (f32[1032,128]{1,0:T(8,128)S(1)}, f32[1032,128]{1,0:T(8,128)S(1)}, u32[]{:S(2)}, u32[]{:S(2)}) collective-permute-start(f32[1032,128]{1,0:T(8,128)S(1)} %get-tuple-element.66), channel_id=1, source_target_pairs={{0,1},{1,0},{2,3},{3,2},{4,5},{5,4},{6,7},{7,6},{8,9},{9,8},{10,11... | collective-permute-start | bytes 1585160 | tf_op jit(solution)/shard_map/ppermute | solution.py:289
  26.8 14.8 %collective-permute-start.5 = (f32[1032,128]{1,0:T(8,128)S(1)}, f32[1032,128]{1,0:T(8,128)}, u32[]{:S(2)}, u32[]{:S(2)}) collective-permute-start(f32[1032,128]{1,0:T(8,128)S(1)} %get-tuple-element.65), channel_id=1, source_target_pairs={{0,2},{2,0},{1,3},{3,1},{4,6},{6,4},{5,7},{7,5},{8,10},{10,8},{9,1... | collective-permute-start | bytes 1585160 | tf_op jit(solution)/shard_map/ppermute | solution.py:289
  29.5 12.1 %collective-permute-start.3 = (f32[1024,128]{1,0:T(8,128)S(1)}, f32[1024,128]{1,0:T(8,128)S(1)}, u32[]{:S(2)}, u32[]{:S(2)}) collective-permute-start(f32[1024,128]{1,0:T(8,128)S(1)} %slice.33), channel_id=1, source_target_pairs={{0,4},{1,5},{2,6},{3,7},{4,8},{5,9},{6,10},{7,11},{8,12},{9,13},{1... | collective-permute-start | bytes 1572872 | tf_op jit(solution)/shard_map/ppermute | solution.py:292
  41.7 12.9 %collective-permute-start.6 = (f32[1024,128]{1,0:T(8,128)S(1)}, f32[1024,128]{1,0:T(8,128)S(1)}, u32[]{:S(2)}, u32[]{:S(2)}) collective-permute-start(f32[1024,128]{1,0:T(8,128)S(1)} %get-tuple-element.64), channel_id=1, source_target_pairs={{0,4},{1,5},{2,6},{3,7},{4,8},{5,9},{6,10},{7,11},{8,12},{9,13},{1... | collective-permute-start | bytes 1572872 | tf_op jit(solution)/shard_map/ppermute | solution.py:292
  46.1 10.9 %collective-permute-start.7 = (f32[1024,128]{1,0:T(8,128)S(1)}, f32[1024,128]{1,0:T(8,128)}, u32[]{:S(2)}, u32[]{:S(2)}) collective-permute-start(f32[1024,128]{1,0:T(8,128)S(1)} %get-tuple-element.62), channel_id=1, source_target_pairs={{0,1},{1,0},{2,3},{3,2},{4,5},{5,4},{6,7},{7,6},{8,9},{9,8},{10,11... | collective-permute-start | bytes 1572872 | tf_op jit(solution)/shard_map/ppermute | solution.py:289
  47.9 10.3 %collective-permute-start.8 = (f32[1024,128]{1,0:T(8,128)S(1)}, f32[1024,128]{1,0:T(8,128)}, u32[]{:S(2)}, u32[]{:S(2)}) collective-permute-start(f32[1024,128]{1,0:T(8,128)S(1)} %get-tuple-element.61), channel_id=1, source_target_pairs={{0,2},{2,0},{1,3},{3,1},{4,6},{6,4},{5,7},{7,5},{8,10},{10,8},{9,1... | collective-permute-start | bytes 1572872 | tf_op jit(solution)/shard_map/ppermute | solution.py:289
  59.4 9.5 %collective-permute-start.10 = (f32[1024,128]{1,0:T(8,128)}, f32[1024,128]{1,0:T(8,128)S(1)}, u32[]{:S(2)}, u32[]{:S(2)}) collective-permute-start(f32[1024,128]{1,0:T(8,128)} %get-tuple-element.60), channel_id=1, source_target_pairs={{0,1},{1,0},{2,3},{3,2},{4,5},{5,4},{6,7},{7,6},{8,9},{9,8},{10,11... | collective-permute-start | bytes 1572872 | tf_op jit(solution)/shard_map/ppermute | solution.py:289
  60.0 9.4 %collective-permute-start.11 = (f32[1024,128]{1,0:T(8,128)}, f32[1024,128]{1,0:T(8,128)S(1)}, u32[]{:S(2)}, u32[]{:S(2)}) collective-permute-start(f32[1024,128]{1,0:T(8,128)} %get-tuple-element.59), channel_id=1, source_target_pairs={{0,2},{2,0},{1,3},{3,1},{4,6},{6,4},{5,7},{7,5},{8,10},{10,8},{9,1... | collective-permute-start | bytes 1572872 | tf_op jit(solution)/shard_map/ppermute | solution.py:289
  60.7 10.6 %collective-permute-start.9 = (f32[1024,128]{1,0:T(8,128)}, f32[1024,128]{1,0:T(8,128)S(1)}, u32[]{:S(2)}, u32[]{:S(2)}) collective-permute-start(f32[1024,128]{1,0:T(8,128)} %get-tuple-element.63), channel_id=1, source_target_pairs={{0,4},{1,5},{2,6},{3,7},{4,8},{5,9},{6,10},{7,11},{8,12},{9,13},{1... | collective-permute-start | bytes 1572872 | tf_op jit(solution)/shard_map/ppermute | solution.py:292
  64.2 28.9 %collective-permute-start.17 = (f32[512,512]{1,0:T(8,128)}, f32[512,512]{1,0:T(8,128)}, u32[]{:S(2)}, u32[]{:S(2)}) collective-permute-start(f32[512,512]{1,0:T(8,128)} %get-tuple-element.54.refs_3_), channel_id=1, source_target_pairs={{0,16},{16,0},{1,17},{17,1},{2,18},{18,2},{3,19},{19,3},{4,20},{20... | collective-permute-start | bytes 3145736 | tf_op jit(solution)/shard_map/ppermute | solution.py:296
  73.8 12.9 %collective-permute-start.12 = (f32[1032,128]{1,0:T(8,128)}, f32[1032,128]{1,0:T(8,128)S(1)}, u32[]{:S(2)}, u32[]{:S(2)}) collective-permute-start(f32[1032,128]{1,0:T(8,128)} %get-tuple-element.68), channel_id=1, source_target_pairs={{0,1},{1,0},{2,3},{3,2},{4,5},{5,4},{6,7},{7,6},{8,9},{9,8},{10,11... | collective-permute-start | bytes 1585160 | tf_op jit(solution)/shard_map/ppermute | solution.py:289
  75.1 11.7 %collective-permute-start.13 = (f32[1032,128]{1,0:T(8,128)}, f32[1032,128]{1,0:T(8,128)S(1)}, u32[]{:S(2)}, u32[]{:S(2)}) collective-permute-start(f32[1032,128]{1,0:T(8,128)} %get-tuple-element.69), channel_id=1, source_target_pairs={{0,2},{2,0},{1,3},{3,1},{4,6},{6,4},{5,7},{7,5},{8,10},{10,8},{9,1... | collective-permute-start | bytes 1585160 | tf_op jit(solution)/shard_map/ppermute | solution.py:289
  85.3 16.4 %collective-permute-start.19 = (f32[512,512]{1,0:T(8,128)}, f32[512,512]{1,0:T(8,128)}, u32[]{:S(2)}, u32[]{:S(2)}) collective-permute-start(f32[512,512]{1,0:T(8,128)} %get-tuple-element.56.refs_5_), channel_id=1, source_target_pairs={{0,16},{16,0},{1,17},{17,1},{2,18},{18,2},{3,19},{19,3},{4,20},{20... | collective-permute-start | bytes 3145736 | tf_op jit(solution)/shard_map/ppermute | solution.py:296
  85.4 16.3 %collective-permute-start.18 = (f32[1032,128]{1,0:T(8,128)S(1)}, f32[1032,128]{1,0:T(8,128)S(1)}, u32[]{:S(2)}, u32[]{:S(2)}) collective-permute-start(f32[1032,128]{1,0:T(8,128)S(1)} %copy-done.17), channel_id=1, source_target_pairs={{2,0},{3,2},{6,4},{7,6},{10,8},{11,10},{14,12},{15,14},{18,16},{19... | collective-permute-start | bytes 1585160 | tf_op jit(solution)/shard_map/ppermute | solution.py:289
  92.4 26.4 %collective-permute-start.14 = (f32[512,512]{1,0:T(8,128)}, f32[512,512]{1,0:T(8,128)}, u32[]{:S(2)}, u32[]{:S(2)}) collective-permute-start(f32[512,512]{1,0:T(8,128)} %get-tuple-element.51.refs_3_), channel_id=1, source_target_pairs={{0,16},{16,0},{1,17},{17,1},{2,18},{18,2},{3,19},{19,3},{4,20},{20... | collective-permute-start | bytes 3145736 | tf_op jit(solution)/shard_map/ppermute | solution.py:296
  92.9 25.8 %collective-permute-start.16 = (f32[512,512]{1,0:T(8,128)}, f32[512,512]{1,0:T(8,128)}, u32[]{:S(2)}, u32[]{:S(2)}) collective-permute-start(f32[512,512]{1,0:T(8,128)} %get-tuple-element.53.refs_5_), channel_id=1, source_target_pairs={{0,16},{16,0},{1,17},{17,1},{2,18},{18,2},{3,19},{19,3},{4,20},{20... | collective-permute-start | bytes 3145736 | tf_op jit(solution)/shard_map/ppermute | solution.py:296
  93.0 38.9 %collective-permute-start.21 = (f32[1032,128]{1,0:T(8,128)}, f32[1032,128]{1,0:T(8,128)S(1)}, u32[]{:S(2)}, u32[]{:S(2)}) collective-permute-start(f32[1032,128]{1,0:T(8,128)} %copy-done.2), channel_id=1, source_target_pairs={{0,1},{1,0},{4,5},{5,4},{8,9},{9,8},{12,13},{13,12},{16,17},{17,16... | collective-permute-start | bytes 1585160 | tf_op jit(solution)/shard_map/ppermute | solution.py:289
  101.7 17.0 %collective-permute-start.15 = (f32[1024,128]{1,0:T(8,128)S(1)}, f32[1024,128]{1,0:T(8,128)S(1)}, u32[]{:S(2)}, u32[]{:S(2)}) collective-permute-start(f32[1024,128]{1,0:T(8,128)S(1)} %broadcast_select_fusion.1), channel_id=1, source_target_pairs={{0,1},{1,3},{3,2},{2,0},{4,5},{5,7},{7,6},{6,4},{8,9},{9,11},{11,1... | collective-permute-start | bytes 1572872 | tf_op jit(solution)/shard_map/ppermute | solution.py:289
  101.7 30.2 %collective-permute-start.20 = (f32[1024,128]{1,0:T(8,128)S(1)}, f32[1024,128]{1,0:T(8,128)S(1)}, u32[]{:S(2)}, u32[]{:S(2)}) collective-permute-start(f32[1024,128]{1,0:T(8,128)S(1)} %copy-done.9), channel_id=1, source_target_pairs={{0,1},{1,0},{2,3},{3,2},{4,5},{5,4},{6,7},{7,6},{8,9},{9,8},{10,11... | collective-permute-start | bytes 1572872 | tf_op jit(solution)/shard_map/ppermute | solution.py:289
  137.6 2.9 %collective-permute-start.22 = (f32[512,512]{1,0:T(8,128)}, f32[512,512]{1,0:T(8,128)S(1)}, u32[]{:S(2)}, u32[]{:S(2)}) collective-permute-start(f32[512,512]{1,0:T(8,128)} %shard_map.52.refs_3_), channel_id=1, source_target_pairs={{0,16},{16,0},{1,17},{17,1},{2,18},{18,2},{3,19},{19,3},{4,20},{20... | collective-permute-start | bytes 3145736 | tf_op jit(solution)/shard_map/ppermute | solution.py:296
  (18 other events, 179.5 us)
where the time goes:
time: 149 us; the launch traced here: 148 us
  Pallas kernels  49.6 us (33%)
  waiting for transfers between devices  44.1 us (30%)
  starting transfers between devices  36.8 us (25%)
  other arithmetic  7.98 us (5%)
  local copies, waits for them, and re-layouts  5.78 us (4%)
  between operations  3.67 us (2%)
    pallas_call x8, Pallas kernels, call(): pl.pallas_call(kernel, out_shape=outputs, in_specs=[pl.BlockSpec(memory_s...  49.6 us
    ppermute x14, waiting for transfers between devices, within(): lax.ppermute(block, 'occ', [(g + a, g + b) for g in planes for a, b in mo...  22.9 us
    ppermute x14, starting transfers between devices, within(): lax.ppermute(block, 'occ', [(g + a, g + b) for g in planes for a, b in mo...  21.1 us
    ppermute x4, waiting for transfers between devices, up(): lax.ppermute(block, 'occ', [(g, g + PLANE) for g in range(groups - PLANE)])  19 us
    ppermute x4, starting transfers between devices, up(): lax.ppermute(block, 'occ', [(g, g + PLANE) for g in range(groups - PLANE)])  14.9 us
    unnamed x38, local copies, waits for them, and re-layouts  3.55 us
  transfers between devices with their start and end apart: 23, of which 12 were waited for; matrix products, arithmetic and copies ran while one was open for 4% of the time, Pallas kernels for 27%

commit v1 on v0

--- a/solution.py
+++ b/solution.py
@@ -176,7 +176,7 @@
     return call(kernel, [flags], [], [*turned, *before, *arrays], out, pltpu.VMEM, scratch)
 
 
-def contract(partials, slots, signs, energies, flags, eps_virt, size, before=None):
+def contract(partials, slots, signs, first_sign, energies, flags, eps_virt, size, before=None):
     count = len(slots)
     chunks = len(slots[0])
     virt = eps_virt.shape[1]
@@ -228,7 +228,7 @@
             for extra in range(1, len(partials[slot])):
                 total = total + sum_ref[at + extra]
             at += len(partials[slot])
-            amplitude = (sign_ref[slot] * total) / (row + line(slot + 1))
+            amplitude = (sign_ref[first_sign + slot] * total) / (row + line(slot + 1))
             right_ref[pl.ds(slot * 3 * width, 3 * width), :] = deep_right(amplitude.T)
         leaving = []
         for at in range(chunks):
@@ -297,14 +297,11 @@
         return [lax.psum(partial, "aux")]
 
     def sign(offset):
-        flag = lax.dynamic_index_in_dim(pair_mask[0], offset - 1, 0, keepdims=False)
+        flag = jnp.sum(jnp.where(jnp.arange(1, PLANE + 1) == offset, pair_mask[0], 0))
         return jnp.where((group >= offset) & (flag > 0), -1.0, 0.0).astype(jnp.float32)
 
-    sign_own = jnp.float32(-1.0)
-    sign_z = sign(jnp.int32(PLANE))
-    sign_x = sign(jnp.where(odd_x, 1, PLANE - 1))
-    sign_y = sign(jnp.int32(PLANE // 2))
-    sign_d = sign(jnp.where(odd_x, PLANE - 1, 1))
+    near, far = jnp.where(odd_x, 1, PLANE - 1), jnp.where(odd_x, PLANE - 1, 1)
+    signs = jnp.stack([jnp.float32(-1.0), sign(PLANE), sign(near), sign(PLANE // 2), sign(far)])
 
     first_sent = jnp.concatenate([part(own, 0), energies])
     down_x, down_y = 1 - place % 2, 1 - place // 2
@@ -312,17 +309,18 @@
         [down_x, down_y, jnp.where(odd_y, 0, 1 + place), jnp.where(odd_y, place - 1, 0)]
     ).astype(jnp.int32)
 
-    def add(partials, slots, signs, carriers, before=None):
-        return contract(partials, slots, jnp.stack(signs), carriers, flags, eps_virt[None, :], size, before)
+    def add(first_sign, partials, slots, carriers, before=None):
+        return contract(partials, slots, signs, first_sign, carriers, flags, eps_virt[None, :], size, before)
 
     from_z = [up(first_sent)]
+    first_sent, signs, flags = lax.optimization_barrier((first_sent, signs, flags))
     up_x = within(first_sent, [(0, 1), (2, 3), (1, 0)])
     up_y = within(first_sent, [(0, 2), (1, 3)])
     high, low, partial_own = prepare(own, rows, width)
     turned = (high, low)
     sums_own = totals(partial_own)
     swap_x, swap_y = [], []
-    passed = [partial_own, up_x, up_y]
+    passed = [partial_own]
     for at in range(CHUNKS):
         came, mine, *_ = lax.optimization_barrier((from_z[at], own, *passed))
         if at < last:
@@ -330,8 +328,11 @@
             up_part = part(mine, at + 1)
             if at == 0:
                 up_part = jnp.concatenate([up_part, energies])
-            swap_x.append(within(jnp.where(odd_x, came, up_part), [(0, 1), (1, 0), (2, 3), (3, 2)]))
-            swap_y.append(within(jnp.where(odd_y, came, up_part), [(0, 2), (2, 0), (1, 3), (3, 1)]))
+            send_x, send_y = jnp.where(odd_x, came, up_part), jnp.where(odd_y, came, up_part)
+            if at == 0:
+                send_x, send_y = after(send_x, up_x), after(send_y, up_y)
+            swap_x.append(within(send_x, [(0, 1), (1, 0), (2, 3), (3, 2)]))
+            swap_y.append(within(send_y, [(0, 2), (2, 0), (1, 3), (3, 1)]))
         else:
             came_x = jnp.concatenate([came, energies])
             swap_x.append(within(jnp.where(odd_x, came_x, swap_y[0]), [(0, 1), (1, 0), (2, 3), (3, 2)]))
@@ -368,22 +369,21 @@
     partial_z, *early = integrate(
         turned, [slot_z, slot_x[:last], slot_y[:last]], [0, 0, 0], flags, size, width
     )
+    own_eps = whole(first_sent, cut)
     gradient = add(
-        [after(sums_own, cross), totals(partial_z)], [slot_own, slot_z], [sign_own, sign_z],
-        [whole(first_sent, cut), whole(first_sent, cut), whole(from_z[0], cut)],
+        0, [after(sums_own, cross), totals(partial_z)], [slot_own, slot_z], [own_eps, own_eps, whole(from_z[0], cut)]
     )
     partial_x, partial_y = integrate(
         turned, [slot_x[last:], slot_y[last:]], [last, last], flags, size, width, early
     )
     gradient = add(
-        [after(totals(partial_x), cycle), totals(partial_y)], [slot_x, slot_y], [sign_x, sign_y],
-        [whole(first_sent, cut), eps_x, eps_y], gradient,
+        2, [totals(partial_x), totals(partial_y)], [slot_x, slot_y], [own_eps, eps_x, eps_y], gradient
     )
     turned = after(turned, gradient)
     half = CHUNKS // 2
     partial_d = integrate(turned, [slot_d[:half]], [0], flags, size, width)
     (partial_d,) = integrate(turned, [slot_d[half:]], [half], flags, size, width, partial_d)
-    gradient = add([totals(partial_d)], [slot_d], [sign_d], [whole(first_sent, cut), eps_d], gradient)
+    gradient = add(4, [totals(partial_d)], [slot_d], [own_eps, eps_d], gradient)
     return gradient.reshape(rows, occ_rows, virt)
 
 

time: 149 us -> 149 us (level)
  waiting for transfers between devices: 44.1 us -> 41.9 us
  local copies, waits for them, and re-layouts: 5.78 us -> 7.66 us
    ppermute x14, waiting for transfers between devices: 22.9 us -> 20.5 us  [within(): lax.ppermute(block, 'occ', [(g + a, g + b) for g in planes for a, b in mo...]
    unnamed x38 -> x40, local copies, waits for them, and re-layouts: 3.55 us -> 5.49 us
    ppermute x4, starting transfers between devices: 14.9 us -> 16.4 us  [up(): lax.ppermute(block, 'occ', [(g, g + PLANE) for g in range(groups - PLANE)])]
  transfers between devices with their start and end apart: 23 -> 23, of which waited for: 12 -> 12; matrix products, arithmetic and copies ran while one was open for 4% -> 5% of each run, Pallas kernels for 27% -> 26%
where the time goes in v1:
time: 149 us; the launch traced here: 148 us
  Pallas kernels  49.5 us (33%)
  waiting for transfers between devices  41.9 us (28%)
  starting transfers between devices  36.9 us (25%)
  other arithmetic  8.24 us (6%)
  local copies, waits for them, and re-layouts  7.66 us (5%)
  between operations  3.74 us (3%)
    pallas_call x8, Pallas kernels, call(): pl.pallas_call(kernel, out_shape=outputs, in_specs=[pl.BlockSpec(memory_s...  49.5 us
    ppermute x14, waiting for transfers between devices, within(): lax.ppermute(block, 'occ', [(g + a, g + b) for g in planes for a, b in mo...  20.5 us
    ppermute x14, starting transfers between devices, within(): lax.ppermute(block, 'occ', [(g + a, g + b) for g in planes for a, b in mo...  19.7 us
    ppermute x4, waiting for transfers between devices, up(): lax.ppermute(block, 'occ', [(g, g + PLANE) for g in range(groups - PLANE)])  18.5 us
    ppermute x4, starting transfers between devices, up(): lax.ppermute(block, 'occ', [(g, g + PLANE) for g in range(groups - PLANE)])  16.4 us
    unnamed x40, local copies, waits for them, and re-layouts  5.49 us
  transfers between devices with their start and end apart: 23, of which 12 were waited for; matrix products, arithmetic and copies ran while one was open for 5% of the time, Pallas kernels for 26%

profile of v1, /device:TPU:0, one launch (start us, length us, event | category | flops | bytes accessed | tf_op | source)
XLA Modules:
  0.0 147.9 jit_solution(12600694491887957633)
XLA Ops:
  2.3 5.8 %collective-permute-start = (f32[1032,128]{1,0:T(8,128)S(1)}, f32[1032,128]{1,0:T(8,128)}, u32[]{:S(2)}, u32[]{:S(2)}) collective-permute-start(f32[1032,128]{1,0:T(8,128)S(1)} %pad_maximum_fusion.2.refs_12_.refs_18_), channel_id=1, source_target_pairs={{0,4},{1,5},{2,6},{3,7},{4,8},{5,9},{6,10},{7,11},{8,12},{9,13},{1... | collective-permute-start | bytes 1585160 | tf_op jit(solution)/shard_map/ppermute | solution.py:292
  12.5 3.4 %collective-permute-start.4 = (f32[1032,128]{1,0:T(8,128)S(1)}, f32[1032,128]{1,0:T(8,128)S(1)}, u32[]{:S(2)}, u32[]{:S(2)}) collective-permute-start(f32[1032,128]{1,0:T(8,128)S(1)} %pad_maximum_fusion.2.refs_12_.refs_18_), channel_id=1, source_target_pairs={{0,2},{1,3},{4,6},{5,7},{8,10},{9,11},{12,14},{13,15},{16,18},{17,... | collective-permute-start | bytes 1585160 | tf_op jit(solution)/shard_map/ppermute | solution.py:289
  15.9 3.4 %collective-permute-start.2 = (f32[1032,128]{1,0:T(8,128)S(1)}, f32[1032,128]{1,0:T(8,128)S(1)}, u32[]{:S(2)}, u32[]{:S(2)}) collective-permute-start(f32[1032,128]{1,0:T(8,128)S(1)} %pad_maximum_fusion.2.refs_12_.refs_18_), channel_id=1, source_target_pairs={{0,1},{2,3},{1,0},{4,5},{6,7},{5,4},{8,9},{10,11},{9,8},{12,13},{1... | collective-permute-start | bytes 1585160 | tf_op jit(solution)/shard_map/ppermute | solution.py:289
  19.4 4.5 %shard_map.46 = (bf16[4,512,256]{2,1,0:T(8,128)(2,1)}, bf16[4,512,256]{2,1,0:T(8,128)(2,1)}, f32[512,512]{1,0:T(8,128)}) custom-call(f32[4096,128]{1,0:T(8,128)} %bitcast.19), custom_call_target="tpu_custom_call" | custom-call | tf_op jit(solution)/shard_map/pallas_call | solution.py:82
  26.9 2.5 %collective-permute-start.5 = (f32[1032,128]{1,0:T(8,128)S(1)}, f32[1032,128]{1,0:T(8,128)}, u32[]{:S(2)}, u32[]{:S(2)}) collective-permute-start(f32[1032,128]{1,0:T(8,128)S(1)} %get-tuple-element.50), channel_id=1, source_target_pairs={{0,2},{2,0},{1,3},{3,1},{4,6},{6,4},{5,7},{7,5},{8,10},{10,8},{9,1... | collective-permute-start | bytes 1585160 | tf_op jit(solution)/shard_map/ppermute | solution.py:289
  32.5 2.8 %collective-permute-start.1 = (f32[1024,128]{1,0:T(8,128)S(1)}, f32[1024,128]{1,0:T(8,128)S(1)}, u32[]{:S(2)}, u32[]{:S(2)}) collective-permute-start(f32[1024,128]{1,0:T(8,128)S(1)} %slice.31), channel_id=1, source_target_pairs={{0,4},{1,5},{2,6},{3,7},{4,8},{5,9},{6,10},{7,11},{8,12},{9,13},{1... | collective-permute-start | bytes 1572872 | tf_op jit(solution)/shard_map/ppermute | solution.py:292
  35.3 9.4 %collective-permute-done.1.refs_3_.refs_9_ = f32[1024,128]{1,0:T(8,128)S(1)} collective-permute-done((f32[1024,128]{1,0:T(8,128)S(1)}, f32[1024,128]{1,0:T(8,128)S(1)}, u32[]{:S(2)}, u32[]{:S(2)}) %collective-permute-start.1) | collective-permute-done | bytes 524320 | tf_op jit(solution)/shard_map/ppermute | solution.py:292
  44.8 4.4 %collective-permute-start.6 = (f32[1024,128]{1,0:T(8,128)S(1)}, f32[1024,128]{1,0:T(8,128)S(1)}, u32[]{:S(2)}, u32[]{:S(2)}) collective-permute-start(f32[1024,128]{1,0:T(8,128)S(1)} %get-tuple-element.74), channel_id=1, source_target_pairs={{0,4},{1,5},{2,6},{3,7},{4,8},{5,9},{6,10},{7,11},{8,12},{9,13},{1... | collective-permute-start | bytes 1572872 | tf_op jit(solution)/shard_map/ppermute | solution.py:292
  49.8 7.8 %collective-permute-done.6.refs_4_.refs_10_ = f32[1024,128]{1,0:T(8,128)S(1)} collective-permute-done((f32[1024,128]{1,0:T(8,128)S(1)}, f32[1024,128]{1,0:T(8,128)S(1)}, u32[]{:S(2)}, u32[]{:S(2)}) %collective-permute-start.6) | collective-permute-done | bytes 524320 | tf_op jit(solution)/shard_map/ppermute | solution.py:292
  57.7 2.4 %collective-permute-done.7.refs_8_.refs_10_ = f32[1024,128]{1,0:T(8,128)} collective-permute-done((f32[1024,128]{1,0:T(8,128)S(1)}, f32[1024,128]{1,0:T(8,128)}, u32[]{:S(2)}, u32[]{:S(2)}) %collective-permute-start.7) | collective-permute-done | bytes 524320 | tf_op jit(solution)/shard_map/ppermute | solution.py:289
  63.5 3.5 %collective-permute-start.9 = (f32[1024,128]{1,0:T(8,128)}, f32[1024,128]{1,0:T(8,128)S(1)}, u32[]{:S(2)}, u32[]{:S(2)}) collective-permute-start(f32[1024,128]{1,0:T(8,128)} %get-tuple-element.73), channel_id=1, source_target_pairs={{0,4},{1,5},{2,6},{3,7},{4,8},{5,9},{6,10},{7,11},{8,12},{9,13},{1... | collective-permute-start | bytes 1572872 | tf_op jit(solution)/shard_map/ppermute | solution.py:292
  67.0 4.4 %collective-permute-done.10.refs_9_.refs_4_.refs_11_ = f32[1024,128]{1,0:T(8,128)S(1)} collective-permute-done((f32[1024,128]{1,0:T(8,128)}, f32[1024,128]{1,0:T(8,128)S(1)}, u32[]{:S(2)}, u32[]{:S(2)}) %collective-permute-start.10) | collective-permute-done | bytes 524320 | tf_op jit(solution)/shard_map/ppermute | solution.py:289
  73.9 2.5 %broadcast_select_fusion = (f32[1032,128]{1,0:T(8,128)}, f32[1032,128]{1,0:T(8,128)}, f32[1032,128]{1,0:T(8,128)}) fusion(f32[1032,128]{1,0:T(8,128)S(1)} %collective-permute-done.3.refs_7_.refs_9_, f32[1032,128]{1,0:T(8,128)} %collective-permute-done.5.refs_11_.refs_14_, pred[]{:T(512)S(6)} %eq.43, f32[8,128]{1,0:T(8,128)S(1)} %pad_bitcast_fusion, ...), kind=kLoop, calls=%fused_computation.7 | loop fusion | flops 528384 | bytes 3698691 | tf_op jit(solution)/shard_map/jit(_where)/select_n | solution.py:343
  78.7 8.1 %shard_map.47 = (f32[512,512]{1,0:T(8,128)}, f32[512,512]{1,0:T(8,128)}, f32[512,512]{1,0:T(8,128)}) custom-call(s32[4]{0:T(128)} %pad_add_fusion.flag_ref.refs_1_, bf16[4,512,256]{2,1,0:T(8,128)(2,1)} %get-tuple-element.63.refs_0_, bf16[4,512,256]{2,1,0:T(8,128)(2,1)} %get-tuple-element.64.refs_1_, f32[1032,128]{1,0:T(8,128)} %collective-permute-done.refs_2_.refs_8_, ...), custom_call_target="tpu_custom_call" | custom-call | tf_op jit(solution)/shard_map/pallas_call | solution.py:82
  89.2 4.7 %shard_map.48 = (f32[512,512]{1,0:T(8,128)}, f32[512,512]{1,0:T(8,128)}) custom-call(s32[4]{0:T(128)} %pad_add_fusion.flag_ref.refs_1_, bf16[4,512,256]{2,1,0:T(8,128)(2,1)} %get-tuple-element.63.refs_0_, bf16[4,512,256]{2,1,0:T(8,128)(2,1)} %get-tuple-element.64.refs_1_, f32[512,512]{1,0:T(8,128)} %get-tuple-element.55.refs_2_, ...), custom_call_target="tpu_custom_call" | custom-call | tf_op jit(solution)/shard_map/pallas_call | solution.py:82
  94.5 2.8 %collective-permute-start.21 = (f32[1032,128]{1,0:T(8,128)}, f32[1032,128]{1,0:T(8,128)S(1)}, u32[]{:S(2)}, u32[]{:S(2)}) collective-permute-start(f32[1032,128]{1,0:T(8,128)} %copy-done.2), channel_id=1, source_target_pairs={{0,1},{1,0},{4,5},{5,4},{8,9},{9,8},{12,13},{13,12},{16,17},{17,16... | collective-permute-start | bytes 1585160 | tf_op jit(solution)/shard_map/ppermute | solution.py:289
  99.3 4.1 %collective-permute-done.17.refs_3_.refs_7_ = f32[1032,128]{1,0:T(8,128)S(1)} collective-permute-done((f32[1032,128]{1,0:T(8,128)}, f32[1032,128]{1,0:T(8,128)S(1)}, u32[]{:S(2)}, u32[]{:S(2)}) %collective-permute-start.17) | collective-permute-done | bytes 528416 | tf_op jit(solution)/shard_map/ppermute | solution.py:289
  103.5 8.7 %shard_map.49.refs_7_ = f32[4096,128]{1,0:T(8,128)} custom-call(f32[5]{0:T(128)} %stack.34.refs_0_, s32[4]{0:T(128)} %pad_add_fusion.flag_ref.refs_1_, f32[1,512]{1,0:T(1,128)} %bitcast.25, f32[512,512]{1,0:T(8,128)} %get-tuple-element.60.refs_3_, f32[512,512]{1,0:T(8,128)} %collective-permute-done.16.refs_4_, f32[512,512]{1,0:T(8,128)} %get-tuple-element.62.refs_5_, ...), custom_call_target="tpu_custom_call" | custom-call | tf_op jit(solution)/shard_map/pallas_call | solution.py:82
  113.3 9.1 %shard_map.50.refs_5_ = f32[4096,128]{1,0:T(8,128)} custom-call(f32[5]{0:T(128)} %stack.34.refs_0_, s32[4]{0:T(128)} %pad_add_fusion.flag_ref.refs_1_, f32[1,512]{1,0:T(1,128)} %bitcast.26, f32[512,512]{1,0:T(8,128)} %get-tuple-element.58.refs_3_, f32[512,512]{1,0:T(8,128)} %copy-done.17, f32[512,512]{1,0:T(8,128)} %get-tuple-element.59.refs_5_, ...), custom_call_target="tpu_custom_call" | custom-call | tf_op jit(solution)/shard_map/pallas_call | solution.py:82
  123.3 3.9 %shard_map.51.refs_2_ = f32[512,512]{1,0:T(8,128)} custom-call(s32[4]{0:T(128)} %pad_add_fusion.flag_ref.refs_1_, bf16[4,512,256]{2,1,0:T(8,128)(2,1)} %get-tuple-element.63.refs_0_, bf16[4,512,256]{2,1,0:T(8,128)(2,1)} %get-tuple-element.64.refs_1_, f32[1032,128]{1,0:T(8,128)} %copy-done.2, f32[1032,128]{1,0:T(8,128)} %copy-done.14, f32[1032,128]{1,0:T(8,128)} %copy-done.1, ...), custom_call_target="tpu_custom_call" | custom-call | tf_op jit(solution)/shard_map/pallas_call | solution.py:82
  127.2 4.6 %collective-permute-done.20.refs_4_.refs_10_ = f32[1024,128]{1,0:T(8,128)S(1)} collective-permute-done((f32[1024,128]{1,0:T(8,128)S(1)}, f32[1024,128]{1,0:T(8,128)S(1)}, u32[]{:S(2)}, u32[]{:S(2)}) %collective-permute-start.20) | collective-permute-done | bytes 524320 | tf_op jit(solution)/shard_map/ppermute | solution.py:289
  133.5 4.1 %shard_map.52.refs_3_ = f32[512,512]{1,0:T(8,128)} custom-call(s32[4]{0:T(128)} %pad_add_fusion.flag_ref.refs_1_, bf16[4,512,256]{2,1,0:T(8,128)(2,1)} %get-tuple-element.63.refs_0_, bf16[4,512,256]{2,1,0:T(8,128)(2,1)} %get-tuple-element.64.refs_1_, f32[512,512]{1,0:T(8,128)} %shard_map.51.refs_2_, f32[1024,128]{1,0:T(8,128)} %copy-done.12, ...), custom_call_target="tpu_custom_call" | custom-call | tf_op jit(solution)/shard_map/pallas_call | solution.py:82
  137.6 2.9 %collective-permute-done.22.refs_4_ = f32[512,512]{1,0:T(8,128)S(1)} collective-permute-done((f32[512,512]{1,0:T(8,128)}, f32[512,512]{1,0:T(8,128)S(1)}, u32[]{:S(2)}, u32[]{:S(2)}) %collective-permute-start.22) | collective-permute-done | bytes 1048608 | tf_op jit(solution)/shard_map/ppermute | solution.py:296
  141.5 6.2 %shard_map.53 = f32[4096,128]{1,0:T(8,128)} custom-call(f32[5]{0:T(128)} %stack.34.refs_0_, s32[4]{0:T(128)} %pad_add_fusion.flag_ref.refs_1_, f32[1,512]{1,0:T(1,128)} %bitcast.27, f32[512,512]{1,0:T(8,128)} %shard_map.52.refs_3_, f32[512,512]{1,0:T(8,128)} %copy-done.18, f32[4096,128]{1,0:T(8,128)} %shard_map.50.refs_5_, f32[1032,128]{1,0:T(8,128)} %copy-done.2, ...), custom_call_target="tpu_custom_call" | custom-call | tf_op jit(solution)/shard_map/pallas_call | solution.py:82
  (82 shorter events, 28.1 us)
Async XLA Ops:
  2.3 21.6 %collective-permute-start = (f32[1032,128]{1,0:T(8,128)S(1)}, f32[1032,128]{1,0:T(8,128)}, u32[]{:S(2)}, u32[]{:S(2)}) collective-permute-start(f32[1032,128]{1,0:T(8,128)S(1)} %pad_maximum_fusion.2.refs_12_.refs_18_), channel_id=1, source_target_pairs={{0,4},{1,5},{2,6},{3,7},{4,8},{5,9},{6,10},{7,11},{8,12},{9,13},{1... | collective-permute-start | bytes 1585160 | tf_op jit(solution)/shard_map/ppermute | solution.py:292
  12.5 14.4 %collective-permute-start.4 = (f32[1032,128]{1,0:T(8,128)S(1)}, f32[1032,128]{1,0:T(8,128)S(1)}, u32[]{:S(2)}, u32[]{:S(2)}) collective-permute-start(f32[1032,128]{1,0:T(8,128)S(1)} %pad_maximum_fusion.2.refs_12_.refs_18_), channel_id=1, source_target_pairs={{0,2},{1,3},{4,6},{5,7},{8,10},{9,11},{12,14},{13,15},{16,18},{17,... | collective-permute-start | bytes 1585160 | tf_op jit(solution)/shard_map/ppermute | solution.py:289
  15.9 15.1 %collective-permute-start.2 = (f32[1032,128]{1,0:T(8,128)S(1)}, f32[1032,128]{1,0:T(8,128)S(1)}, u32[]{:S(2)}, u32[]{:S(2)}) collective-permute-start(f32[1032,128]{1,0:T(8,128)S(1)} %pad_maximum_fusion.2.refs_12_.refs_18_), channel_id=1, source_target_pairs={{0,1},{2,3},{1,0},{4,5},{6,7},{5,4},{8,9},{10,11},{9,8},{12,13},{1... | collective-permute-start | bytes 1585160 | tf_op jit(solution)/shard_map/ppermute | solution.py:289
  26.9 17.8 %collective-permute-start.5 = (f32[1032,128]{1,0:T(8,128)S(1)}, f32[1032,128]{1,0:T(8,128)}, u32[]{:S(2)}, u32[]{:S(2)}) collective-permute-start(f32[1032,128]{1,0:T(8,128)S(1)} %get-tuple-element.50), channel_id=1, source_target_pairs={{0,2},{2,0},{1,3},{3,1},{4,6},{6,4},{5,7},{7,5},{8,10},{10,8},{9,1... | collective-permute-start | bytes 1585160 | tf_op jit(solution)/shard_map/ppermute | solution.py:289
  31.0 42.9 %copy-start.4 = (f32[1032,128]{1,0:T(8,128)}, f32[1032,128]{1,0:T(8,128)S(1)}, u32[]{:S(2)}) copy-start(f32[1032,128]{1,0:T(8,128)S(1)} %collective-permute-done.2.refs_6_.refs_8_) | copy-start | bytes 1585156
  31.0 13.6 %collective-permute-start.3 = (f32[1032,128]{1,0:T(8,128)S(1)}, f32[1032,128]{1,0:T(8,128)S(1)}, u32[]{:S(2)}, u32[]{:S(2)}) collective-permute-start(f32[1032,128]{1,0:T(8,128)S(1)} %get-tuple-element.49), channel_id=1, source_target_pairs={{0,1},{1,0},{2,3},{3,2},{4,5},{5,4},{6,7},{7,6},{8,9},{9,8},{10,11... | collective-permute-start | bytes 1585160 | tf_op jit(solution)/shard_map/ppermute | solution.py:289
  32.5 12.1 %collective-permute-start.1 = (f32[1024,128]{1,0:T(8,128)S(1)}, f32[1024,128]{1,0:T(8,128)S(1)}, u32[]{:S(2)}, u32[]{:S(2)}) collective-permute-start(f32[1024,128]{1,0:T(8,128)S(1)} %slice.31), channel_id=1, source_target_pairs={{0,4},{1,5},{2,6},{3,7},{4,8},{5,9},{6,10},{7,11},{8,12},{9,13},{1... | collective-permute-start | bytes 1572872 | tf_op jit(solution)/shard_map/ppermute | solution.py:292
  44.8 12.9 %collective-permute-start.6 = (f32[1024,128]{1,0:T(8,128)S(1)}, f32[1024,128]{1,0:T(8,128)S(1)}, u32[]{:S(2)}, u32[]{:S(2)}) collective-permute-start(f32[1024,128]{1,0:T(8,128)S(1)} %get-tuple-element.74), channel_id=1, source_target_pairs={{0,4},{1,5},{2,6},{3,7},{4,8},{5,9},{6,10},{7,11},{8,12},{9,13},{1... | collective-permute-start | bytes 1572872 | tf_op jit(solution)/shard_map/ppermute | solution.py:292
  49.2 10.9 %collective-permute-start.7 = (f32[1024,128]{1,0:T(8,128)S(1)}, f32[1024,128]{1,0:T(8,128)}, u32[]{:S(2)}, u32[]{:S(2)}) collective-permute-start(f32[1024,128]{1,0:T(8,128)S(1)} %get-tuple-element.72), channel_id=1, source_target_pairs={{0,1},{1,0},{2,3},{3,2},{4,5},{5,4},{6,7},{7,6},{8,9},{9,8},{10,11... | collective-permute-start | bytes 1572872 | tf_op jit(solution)/shard_map/ppermute | solution.py:289
  49.8 10.5 %collective-permute-start.8 = (f32[1024,128]{1,0:T(8,128)S(1)}, f32[1024,128]{1,0:T(8,128)}, u32[]{:S(2)}, u32[]{:S(2)}) collective-permute-start(f32[1024,128]{1,0:T(8,128)S(1)} %get-tuple-element.71), channel_id=1, source_target_pairs={{0,2},{2,0},{1,3},{3,1},{4,6},{6,4},{5,7},{7,5},{8,10},{10,8},{9,1... | collective-permute-start | bytes 1572872 | tf_op jit(solution)/shard_map/ppermute | solution.py:289
  61.6 9.8 %collective-permute-start.10 = (f32[1024,128]{1,0:T(8,128)}, f32[1024,128]{1,0:T(8,128)S(1)}, u32[]{:S(2)}, u32[]{:S(2)}) collective-permute-start(f32[1024,128]{1,0:T(8,128)} %get-tuple-element.70), channel_id=1, source_target_pairs={{0,1},{1,0},{2,3},{3,2},{4,5},{5,4},{6,7},{7,6},{8,9},{9,8},{10,11... | collective-permute-start | bytes 1572872 | tf_op jit(solution)/shard_map/ppermute | solution.py:289
  63.2 9.4 %collective-permute-start.11 = (f32[1024,128]{1,0:T(8,128)}, f32[1024,128]{1,0:T(8,128)S(1)}, u32[]{:S(2)}, u32[]{:S(2)}) collective-permute-start(f32[1024,128]{1,0:T(8,128)} %get-tuple-element.69), channel_id=1, source_target_pairs={{0,2},{2,0},{1,3},{3,1},{4,6},{6,4},{5,7},{7,5},{8,10},{10,8},{9,1... | collective-permute-start | bytes 1572872 | tf_op jit(solution)/shard_map/ppermute | solution.py:289
  63.5 10.5 %collective-permute-start.9 = (f32[1024,128]{1,0:T(8,128)}, f32[1024,128]{1,0:T(8,128)S(1)}, u32[]{:S(2)}, u32[]{:S(2)}) collective-permute-start(f32[1024,128]{1,0:T(8,128)} %get-tuple-element.73), channel_id=1, source_target_pairs={{0,4},{1,5},{2,6},{3,7},{4,8},{5,9},{6,10},{7,11},{8,12},{9,13},{1... | collective-permute-start | bytes 1572872 | tf_op jit(solution)/shard_map/ppermute | solution.py:292
  66.9 27.6 %collective-permute-start.16 = (f32[512,512]{1,0:T(8,128)}, f32[512,512]{1,0:T(8,128)}, u32[]{:S(2)}, u32[]{:S(2)}) collective-permute-start(f32[512,512]{1,0:T(8,128)} %get-tuple-element.60.refs_3_), channel_id=1, source_target_pairs={{0,16},{16,0},{1,17},{17,1},{2,18},{18,2},{3,19},{19,3},{4,20},{20... | collective-permute-start | bytes 3145736 | tf_op jit(solution)/shard_map/ppermute | solution.py:296
  76.4 11.7 %collective-permute-start.12 = (f32[1032,128]{1,0:T(8,128)}, f32[1032,128]{1,0:T(8,128)S(1)}, u32[]{:S(2)}, u32[]{:S(2)}) collective-permute-start(f32[1032,128]{1,0:T(8,128)} %get-tuple-element.78), channel_id=1, source_target_pairs={{0,1},{1,0},{2,3},{3,2},{4,5},{5,4},{6,7},{7,6},{8,9},{9,8},{10,11... | collective-permute-start | bytes 1585160 | tf_op jit(solution)/shard_map/ppermute | solution.py:289
  77.0 11.2 %collective-permute-start.13 = (f32[1032,128]{1,0:T(8,128)}, f32[1032,128]{1,0:T(8,128)S(1)}, u32[]{:S(2)}, u32[]{:S(2)}) collective-permute-start(f32[1032,128]{1,0:T(8,128)} %get-tuple-element.79), channel_id=1, source_target_pairs={{0,2},{2,0},{1,3},{3,1},{4,6},{6,4},{5,7},{7,5},{8,10},{10,8},{9,1... | collective-permute-start | bytes 1585160 | tf_op jit(solution)/shard_map/ppermute | solution.py:289
  86.8 16.6 %collective-permute-start.18 = (f32[512,512]{1,0:T(8,128)}, f32[512,512]{1,0:T(8,128)}, u32[]{:S(2)}, u32[]{:S(2)}) collective-permute-start(f32[512,512]{1,0:T(8,128)} %get-tuple-element.62.refs_5_), channel_id=1, source_target_pairs={{0,16},{16,0},{1,17},{17,1},{2,18},{18,2},{3,19},{19,3},{4,20},{20... | collective-permute-start | bytes 3145736 | tf_op jit(solution)/shard_map/ppermute | solution.py:296
  86.9 16.5 %collective-permute-start.17 = (f32[1032,128]{1,0:T(8,128)}, f32[1032,128]{1,0:T(8,128)S(1)}, u32[]{:S(2)}, u32[]{:S(2)}) collective-permute-start(f32[1032,128]{1,0:T(8,128)} %get-tuple-element.77), channel_id=1, source_target_pairs={{2,0},{3,2},{6,4},{7,6},{10,8},{11,10},{14,12},{15,14},{18,16},{19... | collective-permute-start | bytes 1585160 | tf_op jit(solution)/shard_map/ppermute | solution.py:289
  93.9 18.3 %collective-permute-start.14 = (f32[512,512]{1,0:T(8,128)}, f32[512,512]{1,0:T(8,128)S(1)}, u32[]{:S(2)}, u32[]{:S(2)}) collective-permute-start(f32[512,512]{1,0:T(8,128)} %get-tuple-element.58.refs_3_), channel_id=1, source_target_pairs={{0,16},{16,0},{1,17},{17,1},{2,18},{18,2},{3,19},{19,3},{4,20},{20... | collective-permute-start | bytes 3145736 | tf_op jit(solution)/shard_map/ppermute | solution.py:296
  94.4 17.8 %collective-permute-start.15 = (f32[512,512]{1,0:T(8,128)}, f32[512,512]{1,0:T(8,128)}, u32[]{:S(2)}, u32[]{:S(2)}) collective-permute-start(f32[512,512]{1,0:T(8,128)} %get-tuple-element.59.refs_5_), channel_id=1, source_target_pairs={{0,16},{16,0},{1,17},{17,1},{2,18},{18,2},{3,19},{19,3},{4,20},{20... | collective-permute-start | bytes 3145736 | tf_op jit(solution)/shard_map/ppermute | solution.py:296
  94.5 37.3 %collective-permute-start.21 = (f32[1032,128]{1,0:T(8,128)}, f32[1032,128]{1,0:T(8,128)S(1)}, u32[]{:S(2)}, u32[]{:S(2)}) collective-permute-start(f32[1032,128]{1,0:T(8,128)} %copy-done.2), channel_id=1, source_target_pairs={{0,1},{1,0},{4,5},{5,4},{8,9},{9,8},{12,13},{13,12},{16,17},{17,16... | collective-permute-start | bytes 1585160 | tf_op jit(solution)/shard_map/ppermute | solution.py:289
  103.4 19.1 %collective-permute-start.19 = (f32[1024,128]{1,0:T(8,128)}, f32[1024,128]{1,0:T(8,128)S(1)}, u32[]{:S(2)}, u32[]{:S(2)}) collective-permute-start(f32[1024,128]{1,0:T(8,128)} %broadcast_select_fusion.1), channel_id=1, source_target_pairs={{0,1},{1,3},{3,2},{2,0},{4,5},{5,7},{7,6},{6,4},{8,9},{9,11},{11,1... | collective-permute-start | bytes 1572872 | tf_op jit(solution)/shard_map/ppermute | solution.py:289
  103.4 28.5 %collective-permute-start.20 = (f32[1024,128]{1,0:T(8,128)S(1)}, f32[1024,128]{1,0:T(8,128)S(1)}, u32[]{:S(2)}, u32[]{:S(2)}) collective-permute-start(f32[1024,128]{1,0:T(8,128)S(1)} %copy-done.9), channel_id=1, source_target_pairs={{0,1},{1,0},{2,3},{3,2},{4,5},{5,4},{6,7},{7,6},{8,9},{9,8},{10,11... | collective-permute-start | bytes 1572872 | tf_op jit(solution)/shard_map/ppermute | solution.py:289
  137.6 2.9 %collective-permute-start.22 = (f32[512,512]{1,0:T(8,128)}, f32[512,512]{1,0:T(8,128)S(1)}, u32[]{:S(2)}, u32[]{:S(2)}) collective-permute-start(f32[512,512]{1,0:T(8,128)} %shard_map.52.refs_3_), channel_id=1, source_target_pairs={{0,16},{16,0},{1,17},{17,1},{2,18},{18,2},{3,19},{19,3},{4,20},{20... | collective-permute-start | bytes 3145736 | tf_op jit(solution)/shard_map/ppermute | solution.py:296
  (19 other events, 181.9 us)

commit v2 on v1

--- a/solution.py
+++ b/solution.py
@@ -313,7 +313,6 @@
         return contract(partials, slots, signs, first_sign, carriers, flags, eps_virt[None, :], size, before)
 
     from_z = [up(first_sent)]
-    first_sent, signs, flags = lax.optimization_barrier((first_sent, signs, flags))
     up_x = within(first_sent, [(0, 1), (2, 3), (1, 0)])
     up_y = within(first_sent, [(0, 2), (1, 3)])
     high, low, partial_own = prepare(own, rows, width)
@@ -334,14 +333,20 @@
             swap_x.append(within(send_x, [(0, 1), (1, 0), (2, 3), (3, 2)]))
             swap_y.append(within(send_y, [(0, 2), (2, 0), (1, 3), (3, 1)]))
         else:
+            cycle = within(after(turning, came), [(0, 1), (1, 3), (3, 2), (2, 0)])
             came_x = jnp.concatenate([came, energies])
             swap_x.append(within(jnp.where(odd_x, came_x, swap_y[0]), [(0, 1), (1, 0), (2, 3), (3, 2)]))
             swap_y.append(within(jnp.where(odd_y, came_x, up_x), [(0, 2), (2, 0), (1, 3), (3, 1)]))
         passed = [swap_x[at], swap_y[at]]
-
-    middle = (place == 1) | (place == 2)
+        if at == 0:
+            passed += [signs, flags]
+        if at == 1:
+            middle = (place == 1) | (place == 2)
+            turning = jnp.where(middle, swap_x[1], swap_y[1])
+        if at == 2:
+            passed.append(turning)
+
     cross = within(jnp.where(place == 2, swap_x[0], swap_y[0]), [(2, 0), (3, 2)])
-    cycle = within(jnp.where(middle, swap_x[1], swap_y[1]), [(0, 1), (1, 3), (3, 2), (2, 0)])
     swap_d = within(swap_y[2], [(0, 1), (1, 0), (2, 3), (3, 2)])
     last_d = within(swap_y[3], [(0, 1), (1, 0)])
 
@@ -371,7 +376,7 @@
     )
     own_eps = whole(first_sent, cut)
     gradient = add(
-        0, [after(sums_own, cross), totals(partial_z)], [slot_own, slot_z], [own_eps, own_eps, whole(from_z[0], cut)]
+        0, [after(sums_own, cycle), totals(partial_z)], [slot_own, slot_z], [own_eps, own_eps, whole(from_z[0], cut)]
     )
     partial_x, partial_y = integrate(
         turned, [slot_x[last:], slot_y[last:]], [last, last], flags, size, width, early

time: 149 us -> 142 us (0.953)
  waiting for transfers between devices: 41.9 us -> 27.3 us
  starting transfers between devices: 36.9 us -> 41.6 us
  other arithmetic: 8.24 us -> 10.7 us
    ppermute x4, waiting for transfers between devices: 18.5 us -> 8.52 us  [up(): lax.ppermute(block, 'occ', [(g, g + PLANE) for g in range(groups - PLANE)])]
    ppermute x14, waiting for transfers between devices: 20.5 us -> 15.9 us  [within(): lax.ppermute(block, 'occ', [(g + a, g + b) for g in planes for a, b in mo...]
    ppermute x14, starting transfers between devices: 19.7 us -> 22.4 us  [within(): lax.ppermute(block, 'occ', [(g + a, g + b) for g in planes for a, b in mo...]
    select_n x3, other arithmetic: 2.49 us -> 4.91 us  [on_device(): jnp.where(odd_y, came, up_part)]
    ppermute x4, starting transfers between devices: 16.4 us -> 18.1 us  [up(): lax.ppermute(block, 'occ', [(g, g + PLANE) for g in range(groups - PLANE)])]
  transfers between devices with their start and end apart: 23 -> 23, of which waited for: 12 -> 9; matrix products, arithmetic and copies ran while one was open for 5% -> 5% of each run, Pallas kernels for 26% -> 28%
where the time goes in v2:
time: 142 us
  Pallas kernels  49.4 us (35%)
  starting transfers between devices  41.6 us (29%)
  waiting for transfers between devices  27.3 us (19%)
  other arithmetic  10.7 us (8%)
  local copies, waits for them, and re-layouts  9.02 us (6%)
  between operations  3.55 us (2%)
    pallas_call x8, Pallas kernels, call(): pl.pallas_call(kernel, out_shape=outputs, in_specs=[pl.BlockSpec(memory_s...  49.4 us
    ppermute x14, starting transfers between devices, within(): lax.ppermute(block, 'occ', [(g + a, g + b) for g in planes for a, b in mo...  22.4 us
    ppermute x4, starting transfers between devices, up(): lax.ppermute(block, 'occ', [(g, g + PLANE) for g in range(groups - PLANE)])  18.1 us
    ppermute x14, waiting for transfers between devices, within(): lax.ppermute(block, 'occ', [(g + a, g + b) for g in planes for a, b in mo...  15.9 us
    ppermute x4, waiting for transfers between devices, up(): lax.ppermute(block, 'occ', [(g, g + PLANE) for g in range(groups - PLANE)])  8.52 us
    unnamed x40, local copies, waits for them, and re-layouts  6.02 us
    select_n x3, other arithmetic, on_device(): jnp.where(odd_y, came, up_part)  4.91 us
    ppermute x5, waiting for transfers between devices, totals(): return [partial, lax.ppermute(partial, 'aux', [(0, 1), (1, 0)])]  2.87 us
  transfers between devices with their start and end apart: 23, of which 9 were waited for; matrix products, arithmetic and copies ran while one was open for 5% of the time, Pallas kernels for 28%

profile of v2, /device:TPU:0, one launch (start us, length us, event | category | flops | bytes accessed | tf_op | source)
XLA Modules:
  0.0 141.6 jit_solution(10607091226040927467)
XLA Ops:
  2.3 5.7 %collective-permute-start = (f32[1032,128]{1,0:T(8,128)S(1)}, f32[1032,128]{1,0:T(8,128)}, u32[]{:S(2)}, u32[]{:S(2)}) collective-permute-start(f32[1032,128]{1,0:T(8,128)S(1)} %pad_maximum_fusion.2.refs_12_.refs_18_), channel_id=1, source_target_pairs={{0,4},{1,5},{2,6},{3,7},{4,8},{5,9},{6,10},{7,11},{8,12},{9,13},{1... | collective-permute-start | bytes 1585160 | tf_op jit(solution)/shard_map/ppermute | solution.py:292
  8.0 4.2 %collective-permute-start.4 = (f32[1032,128]{1,0:T(8,128)S(1)}, f32[1032,128]{1,0:T(8,128)}, u32[]{:S(2)}, u32[]{:S(2)}) collective-permute-start(f32[1032,128]{1,0:T(8,128)S(1)} %pad_maximum_fusion.2.refs_12_.refs_18_), channel_id=1, source_target_pairs={{0,2},{1,3},{4,6},{5,7},{8,10},{9,11},{12,14},{13,15},{16,18},{17,... | collective-permute-start | bytes 1585160 | tf_op jit(solution)/shard_map/ppermute | solution.py:289
  12.3 3.4 %collective-permute-start.2 = (f32[1032,128]{1,0:T(8,128)S(1)}, f32[1032,128]{1,0:T(8,128)S(1)}, u32[]{:S(2)}, u32[]{:S(2)}) collective-permute-start(f32[1032,128]{1,0:T(8,128)S(1)} %pad_maximum_fusion.2.refs_12_.refs_18_), channel_id=1, source_target_pairs={{0,1},{2,3},{1,0},{4,5},{6,7},{5,4},{8,9},{10,11},{9,8},{12,13},{1... | collective-permute-start | bytes 1585160 | tf_op jit(solution)/shard_map/ppermute | solution.py:289
  15.7 4.5 %shard_map.46 = (bf16[4,512,256]{2,1,0:T(8,128)(2,1)}, bf16[4,512,256]{2,1,0:T(8,128)(2,1)}, f32[512,512]{1,0:T(8,128)}) custom-call(f32[4096,128]{1,0:T(8,128)} %bitcast.19), custom_call_target="tpu_custom_call" | custom-call | tf_op jit(solution)/shard_map/pallas_call | solution.py:82
  21.1 2.2 %fusion = (f32[1032,128]{1,0:T(8,128)}, f32[1032,128]{1,0:T(8,128)}) fusion(f32[1032,128]{1,0:T(8,128)} %collective-permute-done.refs_2_.refs_8_, f32[8,128]{1,0:T(8,128)S(1)} %pad_bitcast_fusion, f32[1024,128]{1,0:T(8,128)} %slice.31, pred[]{:T(512)S(6)} %eq.42, pred[]{:T(512)S(6)} %eq.36), kind=kLoop, calls=%fused_computation.3 | loop fusion | flops 396288 | bytes 2113538 | tf_op jit(solution)/shard_map/jit(_where)/select_n | solution.py:330
  25.0 2.3 %collective-permute-done.2.refs_6_.refs_8_ = f32[1032,128]{1,0:T(8,128)S(1)} collective-permute-done((f32[1032,128]{1,0:T(8,128)S(1)}, f32[1032,128]{1,0:T(8,128)S(1)}, u32[]{:S(2)}, u32[]{:S(2)}) %collective-permute-start.2) | collective-permute-done | bytes 528416 | tf_op jit(solution)/shard_map/ppermute | solution.py:289
  28.8 3.5 %collective-permute-start.1 = (f32[1024,128]{1,0:T(8,128)}, f32[1024,128]{1,0:T(8,128)}, u32[]{:S(2)}, u32[]{:S(2)}) collective-permute-start(f32[1024,128]{1,0:T(8,128)} %slice.31), channel_id=1, source_target_pairs={{0,4},{1,5},{2,6},{3,7},{4,8},{5,9},{6,10},{7,11},{8,12},{9,13},{1... | collective-permute-start | bytes 1572872 | tf_op jit(solution)/shard_map/ppermute | solution.py:292
  36.6 4.6 %collective-permute-done.1.refs_3_.refs_9_ = f32[1024,128]{1,0:T(8,128)} collective-permute-done((f32[1024,128]{1,0:T(8,128)}, f32[1024,128]{1,0:T(8,128)}, u32[]{:S(2)}, u32[]{:S(2)}) %collective-permute-start.1) | collective-permute-done | bytes 524320 | tf_op jit(solution)/shard_map/ppermute | solution.py:292
  43.2 4.4 %collective-permute-start.6 = (f32[1024,128]{1,0:T(8,128)S(1)}, f32[1024,128]{1,0:T(8,128)S(1)}, u32[]{:S(2)}, u32[]{:S(2)}) collective-permute-start(f32[1024,128]{1,0:T(8,128)S(1)} %get-tuple-element.70), channel_id=1, source_target_pairs={{0,4},{1,5},{2,6},{3,7},{4,8},{5,9},{6,10},{7,11},{8,12},{9,13},{1... | collective-permute-start | bytes 1572872 | tf_op jit(solution)/shard_map/ppermute | solution.py:292
  47.6 6.0 %collective-permute-done.7.refs_8_.refs_10_ = f32[1024,128]{1,0:T(8,128)S(1)} collective-permute-done((f32[1024,128]{1,0:T(8,128)S(1)}, f32[1024,128]{1,0:T(8,128)S(1)}, u32[]{:S(2)}, u32[]{:S(2)}) %collective-permute-start.7) | collective-permute-done | bytes 524320 | tf_op jit(solution)/shard_map/ppermute | solution.py:289
  60.3 4.4 %collective-permute-start.9 = (f32[1024,128]{1,0:T(8,128)}, f32[1024,128]{1,0:T(8,128)S(1)}, u32[]{:S(2)}, u32[]{:S(2)}) collective-permute-start(f32[1024,128]{1,0:T(8,128)} %get-tuple-element.69), channel_id=1, source_target_pairs={{0,4},{1,5},{2,6},{3,7},{4,8},{5,9},{6,10},{7,11},{8,12},{9,13},{1... | collective-permute-start | bytes 1572872 | tf_op jit(solution)/shard_map/ppermute | solution.py:292
  64.7 1.9 %broadcast_select_fusion.1 = f32[1024,128]{1,0:T(8,128)} fusion(f32[1024,128]{1,0:T(8,128)} %copy-done.10, f32[1024,128]{1,0:T(8,128)} %copy-done.11, pred[]{:T(512)S(6)} %or.3), kind=kLoop, calls=%fused_computation.8 | loop fusion | flops 131072 | bytes 1572865 | tf_op jit(solution)/shard_map/jit(_where)/select_n | solution.py:345
  68.3 3.4 %collective-permute-done.9.refs_5_.refs_11_ = f32[1024,128]{1,0:T(8,128)S(1)} collective-permute-done((f32[1024,128]{1,0:T(8,128)}, f32[1024,128]{1,0:T(8,128)S(1)}, u32[]{:S(2)}, u32[]{:S(2)}) %collective-permute-start.9) | collective-permute-done | bytes 524320 | tf_op jit(solution)/shard_map/ppermute | solution.py:292
  71.7 2.5 %broadcast_select_fusion = (f32[1032,128]{1,0:T(8,128)}, f32[1032,128]{1,0:T(8,128)}, f32[1032,128]{1,0:T(8,128)}) fusion(f32[1032,128]{1,0:T(8,128)S(1)} %collective-permute-done.3.refs_7_.refs_9_, f32[1032,128]{1,0:T(8,128)} %collective-permute-done.5.refs_11_.refs_14_, pred[]{:T(512)S(6)} %eq.44, f32[8,128]{1,0:T(8,128)S(1)} %pad_bitcast_fusion, ...), kind=kLoop, calls=%fused_computation.7 | loop fusion | flops 528384 | bytes 3698691 | tf_op jit(solution)/shard_map/jit(_where)/select_n | solution.py:349
  75.1 8.1 %shard_map.47 = (f32[512,512]{1,0:T(8,128)}, f32[512,512]{1,0:T(8,128)}, f32[512,512]{1,0:T(8,128)}) custom-call(s32[4]{0:T(128)} %pad_add_fusion.flag_ref.refs_1_, bf16[4,512,256]{2,1,0:T(8,128)(2,1)} %get-tuple-element.59.refs_0_, bf16[4,512,256]{2,1,0:T(8,128)(2,1)} %get-tuple-element.60.refs_1_, f32[1032,128]{1,0:T(8,128)} %collective-permute-done.refs_2_.refs_8_, ...), custom_call_target="tpu_custom_call" | custom-call | tf_op jit(solution)/shard_map/pallas_call | solution.py:82
  86.2 4.7 %shard_map.48 = (f32[512,512]{1,0:T(8,128)}, f32[512,512]{1,0:T(8,128)}) custom-call(s32[4]{0:T(128)} %pad_add_fusion.flag_ref.refs_1_, bf16[4,512,256]{2,1,0:T(8,128)(2,1)} %get-tuple-element.59.refs_0_, bf16[4,512,256]{2,1,0:T(8,128)(2,1)} %get-tuple-element.60.refs_1_, f32[512,512]{1,0:T(8,128)} %get-tuple-element.50.refs_2_, ...), custom_call_target="tpu_custom_call" | custom-call | tf_op jit(solution)/shard_map/pallas_call | solution.py:82
  92.8 5.9 %collective-permute-done.17.refs_5_.refs_3_.refs_9_ = f32[1024,128]{1,0:T(8,128)S(1)} collective-permute-done((f32[1024,128]{1,0:T(8,128)}, f32[1024,128]{1,0:T(8,128)S(1)}, u32[]{:S(2)}, u32[]{:S(2)}) %collective-permute-start.17) | collective-permute-done | bytes 524320 | tf_op jit(solution)/shard_map/ppermute | solution.py:289
  98.7 2.7 %collective-permute-start.21 = (f32[1032,128]{1,0:T(8,128)}, f32[1032,128]{1,0:T(8,128)S(1)}, u32[]{:S(2)}, u32[]{:S(2)}) collective-permute-start(f32[1032,128]{1,0:T(8,128)} %copy-done.2), channel_id=1, source_target_pairs={{0,1},{1,0},{4,5},{5,4},{8,9},{9,8},{12,13},{13,12},{16,17},{17,16... | collective-permute-start | bytes 1585160 | tf_op jit(solution)/shard_map/ppermute | solution.py:289
  102.9 8.7 %shard_map.49.refs_7_ = f32[4096,128]{1,0:T(8,128)} custom-call(f32[5]{0:T(128)} %stack.34.refs_0_, s32[4]{0:T(128)} %pad_add_fusion.flag_ref.refs_1_, f32[1,512]{1,0:T(1,128)} %bitcast.25, f32[512,512]{1,0:T(8,128)} %get-tuple-element.56.refs_3_, f32[512,512]{1,0:T(8,128)} %collective-permute-done.16.refs_4_, f32[512,512]{1,0:T(8,128)} %get-tuple-element.58.refs_5_, ...), custom_call_target="tpu_custom_call" | custom-call | tf_op jit(solution)/shard_map/pallas_call | solution.py:82
  111.6 9.2 %shard_map.50.refs_5_ = f32[4096,128]{1,0:T(8,128)} custom-call(f32[5]{0:T(128)} %stack.34.refs_0_, s32[4]{0:T(128)} %pad_add_fusion.flag_ref.refs_1_, f32[1,512]{1,0:T(1,128)} %bitcast.26, f32[512,512]{1,0:T(8,128)} %get-tuple-element.53.refs_3_, f32[512,512]{1,0:T(8,128)} %collective-permute-done.14.refs_4_, f32[512,512]{1,0:T(8,128)} %get-tuple-element.54.refs_5_, ...), custom_call_target="tpu_custom_call" | custom-call | tf_op jit(solution)/shard_map/pallas_call | solution.py:82
  121.6 3.9 %shard_map.51.refs_2_ = f32[512,512]{1,0:T(8,128)} custom-call(s32[4]{0:T(128)} %pad_add_fusion.flag_ref.refs_1_, bf16[4,512,256]{2,1,0:T(8,128)(2,1)} %get-tuple-element.59.refs_0_, bf16[4,512,256]{2,1,0:T(8,128)(2,1)} %get-tuple-element.60.refs_1_, f32[1032,128]{1,0:T(8,128)} %copy-done.2, f32[1032,128]{1,0:T(8,128)} %copy-done.14, f32[1032,128]{1,0:T(8,128)} %copy-done.1, ...), custom_call_target="tpu_custom_call" | custom-call | tf_op jit(solution)/shard_map/pallas_call | solution.py:82
  127.2 4.1 %shard_map.52.refs_3_ = f32[512,512]{1,0:T(8,128)} custom-call(s32[4]{0:T(128)} %pad_add_fusion.flag_ref.refs_1_, bf16[4,512,256]{2,1,0:T(8,128)(2,1)} %get-tuple-element.59.refs_0_, bf16[4,512,256]{2,1,0:T(8,128)(2,1)} %get-tuple-element.60.refs_1_, f32[512,512]{1,0:T(8,128)} %shard_map.51.refs_2_, f32[1024,128]{1,0:T(8,128)} %copy-done.13, ...), custom_call_target="tpu_custom_call" | custom-call | tf_op jit(solution)/shard_map/pallas_call | solution.py:82
  131.4 2.9 %collective-permute-done.22.refs_4_ = f32[512,512]{1,0:T(8,128)S(1)} collective-permute-done((f32[512,512]{1,0:T(8,128)}, f32[512,512]{1,0:T(8,128)S(1)}, u32[]{:S(2)}, u32[]{:S(2)}) %collective-permute-start.22) | collective-permute-done | bytes 1048608 | tf_op jit(solution)/shard_map/ppermute | solution.py:296
  135.2 6.2 %shard_map.53 = f32[4096,128]{1,0:T(8,128)} custom-call(f32[5]{0:T(128)} %stack.34.refs_0_, s32[4]{0:T(128)} %pad_add_fusion.flag_ref.refs_1_, f32[1,512]{1,0:T(1,128)} %bitcast.27, f32[512,512]{1,0:T(8,128)} %shard_map.52.refs_3_, f32[512,512]{1,0:T(8,128)} %copy-done.17, f32[4096,128]{1,0:T(8,128)} %shard_map.50.refs_5_, f32[1032,128]{1,0:T(8,128)} %copy-done.2, ...), custom_call_target="tpu_custom_call" | custom-call | tf_op jit(solution)/shard_map/pallas_call | solution.py:82
  (82 shorter events, 28.5 us)
Async XLA Ops:
  2.3 18.0 %collective-permute-start = (f32[1032,128]{1,0:T(8,128)S(1)}, f32[1032,128]{1,0:T(8,128)}, u32[]{:S(2)}, u32[]{:S(2)}) collective-permute-start(f32[1032,128]{1,0:T(8,128)S(1)} %pad_maximum_fusion.2.refs_12_.refs_18_), channel_id=1, source_target_pairs={{0,4},{1,5},{2,6},{3,7},{4,8},{5,9},{6,10},{7,11},{8,12},{9,13},{1... | collective-permute-start | bytes 1585160 | tf_op jit(solution)/shard_map/ppermute | solution.py:292
  8.0 15.3 %collective-permute-start.4 = (f32[1032,128]{1,0:T(8,128)S(1)}, f32[1032,128]{1,0:T(8,128)}, u32[]{:S(2)}, u32[]{:S(2)}) collective-permute-start(f32[1032,128]{1,0:T(8,128)S(1)} %pad_maximum_fusion.2.refs_12_.refs_18_), channel_id=1, source_target_pairs={{0,2},{1,3},{4,6},{5,7},{8,10},{9,11},{12,14},{13,15},{16,18},{17,... | collective-permute-start | bytes 1585160 | tf_op jit(solution)/shard_map/ppermute | solution.py:289
  12.3 15.1 %collective-permute-start.2 = (f32[1032,128]{1,0:T(8,128)S(1)}, f32[1032,128]{1,0:T(8,128)S(1)}, u32[]{:S(2)}, u32[]{:S(2)}) collective-permute-start(f32[1032,128]{1,0:T(8,128)S(1)} %pad_maximum_fusion.2.refs_12_.refs_18_), channel_id=1, source_target_pairs={{0,1},{2,3},{1,0},{4,5},{6,7},{5,4},{8,9},{10,11},{9,8},{12,13},{1... | collective-permute-start | bytes 1585160 | tf_op jit(solution)/shard_map/ppermute | solution.py:289
  23.4 17.9 %collective-permute-start.5 = (f32[1032,128]{1,0:T(8,128)}, f32[1032,128]{1,0:T(8,128)}, u32[]{:S(2)}, u32[]{:S(2)}) collective-permute-start(f32[1032,128]{1,0:T(8,128)} %get-tuple-element.45), channel_id=1, source_target_pairs={{0,2},{2,0},{1,3},{3,1},{4,6},{6,4},{5,7},{7,5},{8,10},{10,8},{9,1... | collective-permute-start | bytes 1585160 | tf_op jit(solution)/shard_map/ppermute | solution.py:289
  27.3 44.4 %copy-start.4 = (f32[1032,128]{1,0:T(8,128)}, f32[1032,128]{1,0:T(8,128)S(1)}, u32[]{:S(2)}) copy-start(f32[1032,128]{1,0:T(8,128)S(1)} %collective-permute-done.2.refs_6_.refs_8_) | copy-start | bytes 1585156
  27.3 13.9 %collective-permute-start.3 = (f32[1032,128]{1,0:T(8,128)}, f32[1032,128]{1,0:T(8,128)S(1)}, u32[]{:S(2)}, u32[]{:S(2)}) collective-permute-start(f32[1032,128]{1,0:T(8,128)} %get-tuple-element.44), channel_id=1, source_target_pairs={{0,1},{1,0},{2,3},{3,2},{4,5},{5,4},{6,7},{7,6},{8,9},{9,8},{10,11... | collective-permute-start | bytes 1585160 | tf_op jit(solution)/shard_map/ppermute | solution.py:289
  28.8 12.4 %collective-permute-start.1 = (f32[1024,128]{1,0:T(8,128)}, f32[1024,128]{1,0:T(8,128)}, u32[]{:S(2)}, u32[]{:S(2)}) collective-permute-start(f32[1024,128]{1,0:T(8,128)} %slice.31), channel_id=1, source_target_pairs={{0,4},{1,5},{2,6},{3,7},{4,8},{5,9},{6,10},{7,11},{8,12},{9,13},{1... | collective-permute-start | bytes 1572872 | tf_op jit(solution)/shard_map/ppermute | solution.py:292
  42.6 11.0 %collective-permute-start.7 = (f32[1024,128]{1,0:T(8,128)S(1)}, f32[1024,128]{1,0:T(8,128)S(1)}, u32[]{:S(2)}, u32[]{:S(2)}) collective-permute-start(f32[1024,128]{1,0:T(8,128)S(1)} %get-tuple-element.68), channel_id=1, source_target_pairs={{0,1},{1,0},{2,3},{3,2},{4,5},{5,4},{6,7},{7,6},{8,9},{9,8},{10,11... | collective-permute-start | bytes 1572872 | tf_op jit(solution)/shard_map/ppermute | solution.py:289
  43.2 11.3 %collective-permute-start.8 = (f32[1024,128]{1,0:T(8,128)S(1)}, f32[1024,128]{1,0:T(8,128)S(1)}, u32[]{:S(2)}, u32[]{:S(2)}) collective-permute-start(f32[1024,128]{1,0:T(8,128)S(1)} %get-tuple-element.67), channel_id=1, source_target_pairs={{0,2},{2,0},{1,3},{3,1},{4,6},{6,4},{5,7},{7,5},{8,10},{10,8},{9,1... | collective-permute-start | bytes 1572872 | tf_op jit(solution)/shard_map/ppermute | solution.py:289
  43.2 12.6 %collective-permute-start.6 = (f32[1024,128]{1,0:T(8,128)S(1)}, f32[1024,128]{1,0:T(8,128)S(1)}, u32[]{:S(2)}, u32[]{:S(2)}) collective-permute-start(f32[1024,128]{1,0:T(8,128)S(1)} %get-tuple-element.70), channel_id=1, source_target_pairs={{0,4},{1,5},{2,6},{3,7},{4,8},{5,9},{6,10},{7,11},{8,12},{9,13},{1... | collective-permute-start | bytes 1572872 | tf_op jit(solution)/shard_map/ppermute | solution.py:292
  57.1 10.0 %collective-permute-start.10 = (f32[1024,128]{1,0:T(8,128)}, f32[1024,128]{1,0:T(8,128)S(1)}, u32[]{:S(2)}, u32[]{:S(2)}) collective-permute-start(f32[1024,128]{1,0:T(8,128)} %get-tuple-element.66), channel_id=1, source_target_pairs={{0,1},{1,0},{2,3},{3,2},{4,5},{5,4},{6,7},{7,6},{8,9},{9,8},{10,11... | collective-permute-start | bytes 1572872 | tf_op jit(solution)/shard_map/ppermute | solution.py:289
  58.6 9.7 %collective-permute-start.11 = (f32[1024,128]{1,0:T(8,128)}, f32[1024,128]{1,0:T(8,128)S(1)}, u32[]{:S(2)}, u32[]{:S(2)}) collective-permute-start(f32[1024,128]{1,0:T(8,128)} %get-tuple-element.65), channel_id=1, source_target_pairs={{0,2},{2,0},{1,3},{3,1},{4,6},{6,4},{5,7},{7,5},{8,10},{10,8},{9,1... | collective-permute-start | bytes 1572872 | tf_op jit(solution)/shard_map/ppermute | solution.py:289
  60.3 11.4 %collective-permute-start.9 = (f32[1024,128]{1,0:T(8,128)}, f32[1024,128]{1,0:T(8,128)S(1)}, u32[]{:S(2)}, u32[]{:S(2)}) collective-permute-start(f32[1024,128]{1,0:T(8,128)} %get-tuple-element.69), channel_id=1, source_target_pairs={{0,4},{1,5},{2,6},{3,7},{4,8},{5,9},{6,10},{7,11},{8,12},{9,13},{1... | collective-permute-start | bytes 1572872 | tf_op jit(solution)/shard_map/ppermute | solution.py:292
  74.2 11.0 %collective-permute-start.12 = (f32[1032,128]{1,0:T(8,128)}, f32[1032,128]{1,0:T(8,128)S(1)}, u32[]{:S(2)}, u32[]{:S(2)}) collective-permute-start(f32[1032,128]{1,0:T(8,128)} %get-tuple-element.74), channel_id=1, source_target_pairs={{0,1},{1,0},{2,3},{3,2},{4,5},{5,4},{6,7},{7,6},{8,9},{9,8},{10,11... | collective-permute-start | bytes 1585160 | tf_op jit(solution)/shard_map/ppermute | solution.py:289
  74.7 10.5 %collective-permute-start.13 = (f32[1032,128]{1,0:T(8,128)}, f32[1032,128]{1,0:T(8,128)S(1)}, u32[]{:S(2)}, u32[]{:S(2)}) collective-permute-start(f32[1032,128]{1,0:T(8,128)} %get-tuple-element.75), channel_id=1, source_target_pairs={{0,2},{2,0},{1,3},{3,1},{4,6},{6,4},{5,7},{7,5},{8,10},{10,8},{9,1... | collective-permute-start | bytes 1585160 | tf_op jit(solution)/shard_map/ppermute | solution.py:289
  75.1 16.4 %collective-permute-start.16 = (f32[512,512]{1,0:T(8,128)}, f32[512,512]{1,0:T(8,128)}, u32[]{:S(2)}, u32[]{:S(2)}) collective-permute-start(f32[512,512]{1,0:T(8,128)} %get-tuple-element.56.refs_3_), channel_id=1, source_target_pairs={{0,16},{16,0},{1,17},{17,1},{2,18},{18,2},{3,19},{19,3},{4,20},{20... | collective-permute-start | bytes 3145736 | tf_op jit(solution)/shard_map/ppermute | solution.py:296
  83.2 18.3 %collective-permute-start.18 = (f32[512,512]{1,0:T(8,128)}, f32[512,512]{1,0:T(8,128)}, u32[]{:S(2)}, u32[]{:S(2)}) collective-permute-start(f32[512,512]{1,0:T(8,128)} %get-tuple-element.58.refs_5_), channel_id=1, source_target_pairs={{0,16},{16,0},{1,17},{17,1},{2,18},{18,2},{3,19},{19,3},{4,20},{20... | collective-permute-start | bytes 3145736 | tf_op jit(solution)/shard_map/ppermute | solution.py:296
  83.7 15.0 %collective-permute-start.17 = (f32[1024,128]{1,0:T(8,128)}, f32[1024,128]{1,0:T(8,128)S(1)}, u32[]{:S(2)}, u32[]{:S(2)}) collective-permute-start(f32[1024,128]{1,0:T(8,128)} %broadcast_select_fusion.1), channel_id=1, source_target_pairs={{0,1},{1,3},{3,2},{2,0},{4,5},{5,7},{7,6},{6,4},{8,9},{9,11},{11,1... | collective-permute-start | bytes 1572872 | tf_op jit(solution)/shard_map/ppermute | solution.py:289
  90.9 20.7 %collective-permute-start.14 = (f32[512,512]{1,0:T(8,128)}, f32[512,512]{1,0:T(8,128)}, u32[]{:S(2)}, u32[]{:S(2)}) collective-permute-start(f32[512,512]{1,0:T(8,128)} %get-tuple-element.53.refs_3_), channel_id=1, source_target_pairs={{0,16},{16,0},{1,17},{17,1},{2,18},{18,2},{3,19},{19,3},{4,20},{20... | collective-permute-start | bytes 3145736 | tf_op jit(solution)/shard_map/ppermute | solution.py:296
  91.0 20.6 %collective-permute-start.15 = (f32[512,512]{1,0:T(8,128)}, f32[512,512]{1,0:T(8,128)}, u32[]{:S(2)}, u32[]{:S(2)}) collective-permute-start(f32[512,512]{1,0:T(8,128)} %get-tuple-element.54.refs_5_), channel_id=1, source_target_pairs={{0,16},{16,0},{1,17},{17,1},{2,18},{18,2},{3,19},{19,3},{4,20},{20... | collective-permute-start | bytes 3145736 | tf_op jit(solution)/shard_map/ppermute | solution.py:296
  91.5 29.3 %collective-permute-start.19 = (f32[1032,128]{1,0:T(8,128)S(1)}, f32[1032,128]{1,0:T(8,128)S(1)}, u32[]{:S(2)}, u32[]{:S(2)}) collective-permute-start(f32[1032,128]{1,0:T(8,128)S(1)} %copy-done.18), channel_id=1, source_target_pairs={{2,0},{3,2},{6,4},{7,6},{10,8},{11,10},{14,12},{15,14},{18,16},{19... | collective-permute-start | bytes 1585160 | tf_op jit(solution)/shard_map/ppermute | solution.py:289
  98.7 26.9 %collective-permute-start.21 = (f32[1032,128]{1,0:T(8,128)}, f32[1032,128]{1,0:T(8,128)S(1)}, u32[]{:S(2)}, u32[]{:S(2)}) collective-permute-start(f32[1032,128]{1,0:T(8,128)} %copy-done.2), channel_id=1, source_target_pairs={{0,1},{1,0},{4,5},{5,4},{8,9},{9,8},{12,13},{13,12},{16,17},{17,16... | collective-permute-start | bytes 1585160 | tf_op jit(solution)/shard_map/ppermute | solution.py:289
  101.5 24.1 %collective-permute-start.20 = (f32[1024,128]{1,0:T(8,128)S(1)}, f32[1024,128]{1,0:T(8,128)S(1)}, u32[]{:S(2)}, u32[]{:S(2)}) collective-permute-start(f32[1024,128]{1,0:T(8,128)S(1)} %copy-done.7), channel_id=1, source_target_pairs={{0,1},{1,0},{2,3},{3,2},{4,5},{5,4},{6,7},{7,6},{8,9},{9,8},{10,11... | collective-permute-start | bytes 1572872 | tf_op jit(solution)/shard_map/ppermute | solution.py:289
  131.3 2.9 %collective-permute-start.22 = (f32[512,512]{1,0:T(8,128)}, f32[512,512]{1,0:T(8,128)S(1)}, u32[]{:S(2)}, u32[]{:S(2)}) collective-permute-start(f32[512,512]{1,0:T(8,128)} %shard_map.52.refs_3_), channel_id=1, source_target_pairs={{0,16},{16,0},{1,17},{17,1},{2,18},{18,2},{3,19},{19,3},{4,20},{20... | collective-permute-start | bytes 3145736 | tf_op jit(solution)/shard_map/ppermute | solution.py:296
  (19 other events, 143.6 us)

commit v3 on v2

--- a/solution.py
+++ b/solution.py
@@ -26,13 +26,13 @@
     return jnp.concatenate([high, low, high], axis=1)
 
 
-def deep_right(value):
+def deep_right(value, axis=0):
     high, low = split(value)
-    return jnp.concatenate([high, high, low], axis=0)
-
-
-def dot(left, right):
-    numbers = (((1,), (0,)), ((), ()))
+    return jnp.concatenate([high, high, low], axis=axis)
+
+
+def dot(left, right, axis=0):
+    numbers = (((1,), (axis,)), ((), ()))
     return lax.dot_general(left, right, numbers, preferred_element_type=jnp.float32)
 
 
@@ -90,26 +90,43 @@
     )(*smem, *vmem, *anywhere)
 
 
-def prepare(own, rows, width):
+def prepare(own, energies, rows, width):
     size = rows // CHUNKS
     cut = size * width // LANES
 
-    def kernel(own_ref, high_ref, low_ref, integrals_ref, block_ref, semaphores):
+    def kernel(energy_ref, own_ref, high_out, low_out, integrals_out, *refs):
+        sent_refs = refs[: CHUNKS - 1]
+        block_ref, turned_ref, integrals_ref, semaphores = refs[CHUNKS - 1 :]
         copies = Copies(semaphores)
         coming = [copies.start(own_ref.at[pl.ds(at * cut, cut)], block_ref.at[at]) for at in range(CHUNKS)]
+        leaving = [copies.start(energy_ref, ref.at[pl.ds(cut, SUBLANES)]) for ref in sent_refs]
         for at in range(CHUNKS):
             coming[at].wait()
+            if at:
+                leaving.append(copies.start(block_ref.at[at], sent_refs[at - 1].at[pl.ds(0, cut)]))
             block = rows_of(block_ref.at[at], 0, size, width)
             high, low = split(block.T)
-            high_ref[at] = high
-            low_ref[at] = low
+            turned_ref[0, at] = high
+            turned_ref[1, at] = low
+            leaving.append(copies.start(turned_ref.at[0, at], high_out.at[at]))
+            leaving.append(copies.start(turned_ref.at[1, at], low_out.at[at]))
             value = dot(jnp.concatenate([high, low, high], axis=1), deep_right(block))
             integrals_ref[...] = integrals_ref[...] + value if at else value
-
-    half = jax.ShapeDtypeStruct((CHUNKS, width, size), jnp.bfloat16)
+        leaving.append(copies.start(integrals_ref, integrals_out))
+        for copy in leaving:
+            copy.wait()
+
+    turned = jax.ShapeDtypeStruct((CHUNKS, width, size), jnp.bfloat16)
     square = jax.ShapeDtypeStruct((width, width), jnp.float32)
-    scratch = [pltpu.VMEM((CHUNKS, cut, LANES), jnp.float32), pltpu.SemaphoreType.DMA((CHUNKS,))]
-    return call(kernel, [], [], [own], [half, half, square], pltpu.VMEM, scratch)
+    sent = jax.ShapeDtypeStruct((cut + SUBLANES, LANES), jnp.float32)
+    scratch = [
+        pltpu.VMEM((CHUNKS, cut, LANES), jnp.float32),
+        pltpu.VMEM((2, CHUNKS, width, size), jnp.bfloat16),
+        pltpu.VMEM((width, width), jnp.float32),
+        pltpu.SemaphoreType.DMA((5 * CHUNKS,)),
+    ]
+    outs = [turned, turned, square] + [sent] * (CHUNKS - 1)
+    return call(kernel, [], [energies], [own], outs, pl.ANY, scratch)
 
 
 def arrays_of(pieces):
@@ -229,13 +246,13 @@
                 total = total + sum_ref[at + extra]
             at += len(partials[slot])
             amplitude = (sign_ref[first_sign + slot] * total) / (row + line(slot + 1))
-            right_ref[pl.ds(slot * 3 * width, 3 * width), :] = deep_right(amplitude.T)
+            right_ref[:, pl.ds(slot * 3 * width, 3 * width)] = deep_right(amplitude, 1)
         leaving = []
         for at in range(chunks):
             for copy in coming[at] + adding[at]:
                 copy.wait()
             left = [deep_left(rows_of(block_ref.at[slot, at], 0, size, width)) for slot in range(count)]
-            value = dot(jnp.concatenate(left, axis=1), right_ref[...])
+            value = dot(jnp.concatenate(left, axis=1), right_ref[...], 1)
             for column in range(lines):
                 lanes = value[:, column * LANES : (column + 1) * LANES]
                 where = pl.ds(column, size, stride=lines)
@@ -253,7 +270,7 @@
         pltpu.VMEM((len(sums), width, width), jnp.float32),
         pltpu.VMEM((count, chunks, cut, LANES), jnp.float32),
         pltpu.VMEM((chunks, cut, LANES), jnp.float32),
-        pltpu.VMEM((count * 3 * width, width), jnp.bfloat16),
+        pltpu.VMEM((width, count * 3 * width), jnp.bfloat16),
         pltpu.SemaphoreType.DMA((len(energies) + len(sums) + len(pieces) + 2 * chunks,)),
     ]
     return call(kernel, [signs, flags], [eps_virt], [*sums, *last, *arrays], [out], pl.ANY, scratch)[0]
@@ -312,21 +329,21 @@
     def add(first_sign, partials, slots, carriers, before=None):
         return contract(partials, slots, signs, first_sign, carriers, flags, eps_virt[None, :], size, before)
 
+    from_own = [first_sent]
     from_z = [up(first_sent)]
     up_x = within(first_sent, [(0, 1), (2, 3), (1, 0)])
     up_y = within(first_sent, [(0, 2), (1, 3)])
-    high, low, partial_own = prepare(own, rows, width)
+    high, low, partial_own, *own_sent = prepare(own, energies, rows, width)
+    from_own += own_sent
     turned = (high, low)
     sums_own = totals(partial_own)
     swap_x, swap_y = [], []
     passed = [partial_own]
     for at in range(CHUNKS):
-        came, mine, *_ = lax.optimization_barrier((from_z[at], own, *passed))
+        came, *_ = lax.optimization_barrier((from_z[at], *passed))
         if at < last:
-            from_z.append(up(part(mine, at + 1)))
-            up_part = part(mine, at + 1)
-            if at == 0:
-                up_part = jnp.concatenate([up_part, energies])
+            from_z.append(up(after(from_own[at + 1], came)))
+            up_part = after(from_own[at + 1], came)
             send_x, send_y = jnp.where(odd_x, came, up_part), jnp.where(odd_y, came, up_part)
             if at == 0:
                 send_x, send_y = after(send_x, up_x), after(send_y, up_y)
@@ -334,9 +351,8 @@
             swap_y.append(within(send_y, [(0, 2), (2, 0), (1, 3), (3, 1)]))
         else:
             cycle = within(after(turning, came), [(0, 1), (1, 3), (3, 2), (2, 0)])
-            came_x = jnp.concatenate([came, energies])
-            swap_x.append(within(jnp.where(odd_x, came_x, swap_y[0]), [(0, 1), (1, 0), (2, 3), (3, 2)]))
-            swap_y.append(within(jnp.where(odd_y, came_x, up_x), [(0, 2), (2, 0), (1, 3), (3, 1)]))
+            swap_x.append(within(jnp.where(odd_x, came, swap_y[0]), [(0, 1), (1, 0), (2, 3), (3, 2)]))
+            swap_y.append(within(jnp.where(odd_y, came, up_x), [(0, 2), (2, 0), (1, 3), (3, 1)]))
         passed = [swap_x[at], swap_y[at]]
         if at == 0:
             passed += [signs, flags]
@@ -375,14 +391,14 @@
         turned, [slot_z, slot_x[:last], slot_y[:last]], [0, 0, 0], flags, size, width
     )
     own_eps = whole(first_sent, cut)
-    gradient = add(
-        0, [after(sums_own, cycle), totals(partial_z)], [slot_own, slot_z], [own_eps, own_eps, whole(from_z[0], cut)]
-    )
     partial_x, partial_y = integrate(
         turned, [slot_x[last:], slot_y[last:]], [last, last], flags, size, width, early
     )
     gradient = add(
-        2, [totals(partial_x), totals(partial_y)], [slot_x, slot_y], [own_eps, eps_x, eps_y], gradient
+        0,
+        [after(sums_own, cycle), totals(partial_z), totals(partial_x), totals(partial_y)],
+        [slot_own, slot_z, slot_x, slot_y],
+        [own_eps, own_eps, whole(from_z[0], cut), eps_x, eps_y],
     )
     turned = after(turned, gradient)
     half = CHUNKS // 2

time: 142 us -> 137 us (0.965)
  Pallas kernels: 49.4 us -> 46.1 us
  local copies, waits for them, and re-layouts: 9.02 us -> 6.61 us
  waiting for transfers between devices: 27.3 us -> 29.2 us
    pallas_call x8 -> x7, Pallas kernels: 49.4 us -> 46.1 us  [call(): pl.pallas_call(kernel, out_shape=outputs, in_specs=[pl.BlockSpec(memory_s...]
    ppermute x14, waiting for transfers between devices: 15.9 us -> 19 us  [within(): lax.ppermute(block, 'occ', [(g + a, g + b) for g in planes for a, b in mo...]
    unnamed x40 -> x48, local copies, waits for them, and re-layouts: 6.02 us -> 4.54 us
  transfers between devices with their start and end apart: 23 -> 23, of which waited for: 9 -> 13; matrix products, arithmetic and copies ran while one was open for 5% -> 4% of each run, Pallas kernels for 28% -> 26%
where the time goes in v3:
time: 137 us
  Pallas kernels  46.1 us (34%)
  starting transfers between devices  41.8 us (31%)
  waiting for transfers between devices  29.2 us (21%)
  other arithmetic  9.37 us (7%)
  local copies, waits for them, and re-layouts  6.61 us (5%)
  between operations  3.68 us (3%)
    pallas_call x7, Pallas kernels, call(): pl.pallas_call(kernel, out_shape=outputs, in_specs=[pl.BlockSpec(memory_s...  46.1 us
    ppermute x14, starting transfers between devices, within(): lax.ppermute(block, 'occ', [(g + a, g + b) for g in planes for a, b in mo...  22.6 us
    ppermute x14, waiting for transfers between devices, within(): lax.ppermute(block, 'occ', [(g + a, g + b) for g in planes for a, b in mo...  19 us
    ppermute x4, starting transfers between devices, up(): lax.ppermute(block, 'occ', [(g, g + PLANE) for g in range(groups - PLANE)])  17.9 us
    ppermute x4, waiting for transfers between devices, up(): lax.ppermute(block, 'occ', [(g, g + PLANE) for g in range(groups - PLANE)])  7.41 us
    select_n x3, other arithmetic, on_device(): jnp.where(odd_y, came, up_part)  4.72 us
    unnamed x48, local copies, waits for them, and re-layouts  4.54 us
    ppermute x5, waiting for transfers between devices, totals(): return [partial, lax.ppermute(partial, 'aux', [(0, 1), (1, 0)])]  2.87 us
  transfers between devices with their start and end apart: 23, of which 13 were waited for; matrix products, arithmetic and copies ran while one was open for 4% of the time, Pallas kernels for 26%

profile of v3, /device:TPU:0, one launch (start us, length us, event | category | flops | bytes accessed | tf_op | source)
XLA Modules:
  0.0 136.7 jit_solution(4486815185742398429)
XLA Ops:
  2.1 5.0 %collective-permute-start.1 = (f32[1032,128]{1,0:T(8,128)S(1)}, f32[1032,128]{1,0:T(8,128)S(1)}, u32[]{:S(2)}, u32[]{:S(2)}) collective-permute-start(f32[1032,128]{1,0:T(8,128)S(1)} %pad_maximum_fusion.refs_26_.refs_12_), channel_id=1, source_target_pairs={{0,4},{1,5},{2,6},{3,7},{4,8},{5,9},{6,10},{7,11},{8,12},{9,13},{1... | collective-permute-start | bytes 1585160 | tf_op jit(solution)/shard_map/ppermute | solution.py:309
  7.1 3.5 %collective-permute-start.5 = (f32[1032,128]{1,0:T(8,128)S(1)}, f32[1032,128]{1,0:T(8,128)S(1)}, u32[]{:S(2)}, u32[]{:S(2)}) collective-permute-start(f32[1032,128]{1,0:T(8,128)S(1)} %pad_maximum_fusion.refs_26_.refs_12_), channel_id=1, source_target_pairs={{0,2},{1,3},{4,6},{5,7},{8,10},{9,11},{12,14},{13,15},{16,18},{17,... | collective-permute-start | bytes 1585160 | tf_op jit(solution)/shard_map/ppermute | solution.py:306
  10.6 3.4 %collective-permute-start.3 = (f32[1032,128]{1,0:T(8,128)S(1)}, f32[1032,128]{1,0:T(8,128)S(1)}, u32[]{:S(2)}, u32[]{:S(2)}) collective-permute-start(f32[1032,128]{1,0:T(8,128)S(1)} %pad_maximum_fusion.refs_26_.refs_12_), channel_id=1, source_target_pairs={{0,1},{2,3},{1,0},{4,5},{6,7},{5,4},{8,9},{10,11},{9,8},{12,13},{1... | collective-permute-start | bytes 1585160 | tf_op jit(solution)/shard_map/ppermute | solution.py:306
  14.0 5.1 %shard_map.46 = (bf16[4,512,256]{2,1,0:T(8,128)(2,1)}, bf16[4,512,256]{2,1,0:T(8,128)(2,1)}, f32[512,512]{1,0:T(8,128)}, f32[1032,128]{1,0:T(8,128)}, f32[1032,128]{1,0:T(8,128)}, /*index=5*/f32[1032,128]{1,0:T(8,128)}) custom-call(f32[8,128]{1,0:T(8,128)} %copy-done.22, f32[4096,128]{1,0:T(8,128)} %bitcast.19), custom_call_target="tpu_custom_call" | custom-call | tf_op jit(solution)/shard_map/pallas_call | solution.py:82
  19.1 2.4 %broadcast_select_fusion.4 = (f32[1032,128]{1,0:T(8,128)}, f32[1032,128]{1,0:T(8,128)}) fusion(f32[1032,128]{1,0:T(8,128)S(1)} %collective-permute-done.1.refs_2_.refs_12_, f32[1032,128]{1,0:T(8,128)} %get-tuple-element.47, pred[]{:T(512)S(6)} %eq.42, pred[]{:T(512)S(6)} %eq.36), kind=kLoop, calls=%fused_computation.5 | loop fusion | flops 264192 | bytes 2113538 | tf_op jit(solution)/shard_map/jit(_where)/select_n | solution.py:347
  22.3 2.5 %collective-permute-start.6 = (f32[1032,128]{1,0:T(8,128)}, f32[1032,128]{1,0:T(8,128)S(1)}, u32[]{:S(2)}, u32[]{:S(2)}) collective-permute-start(f32[1032,128]{1,0:T(8,128)} %get-tuple-element.49), channel_id=1, source_target_pairs={{0,2},{2,0},{1,3},{3,1},{4,6},{6,4},{5,7},{7,5},{8,10},{10,8},{9,1... | collective-permute-start | bytes 1585160 | tf_op jit(solution)/shard_map/ppermute | solution.py:306
  27.1 3.5 %collective-permute-start.2 = (f32[1032,128]{1,0:T(8,128)}, f32[1032,128]{1,0:T(8,128)S(1)}, u32[]{:S(2)}, u32[]{:S(2)}) collective-permute-start(f32[1032,128]{1,0:T(8,128)} %get-tuple-element.47), channel_id=1, source_target_pairs={{0,4},{1,5},{2,6},{3,7},{4,8},{5,9},{6,10},{7,11},{8,12},{9,13},{1... | collective-permute-start | bytes 1585160 | tf_op jit(solution)/shard_map/ppermute | solution.py:309
  35.8 2.3 %collective-permute-done.4.refs_7_.refs_17_ = f32[1032,128]{1,0:T(8,128)S(1)} collective-permute-done((f32[1032,128]{1,0:T(8,128)}, f32[1032,128]{1,0:T(8,128)S(1)}, u32[]{:S(2)}, u32[]{:S(2)}) %collective-permute-start.4) | collective-permute-done | bytes 528416 | tf_op jit(solution)/shard_map/ppermute | solution.py:306
  38.1 2.3 %collective-permute-done.2.refs_3_.refs_13_ = f32[1032,128]{1,0:T(8,128)S(1)} collective-permute-done((f32[1032,128]{1,0:T(8,128)}, f32[1032,128]{1,0:T(8,128)S(1)}, u32[]{:S(2)}, u32[]{:S(2)}) %collective-permute-start.2) | collective-permute-done | bytes 528416 | tf_op jit(solution)/shard_map/ppermute | solution.py:309
  41.1 4.3 %collective-permute-start.9 = (f32[1032,128]{1,0:T(8,128)S(1)}, f32[1032,128]{1,0:T(8,128)S(1)}, u32[]{:S(2)}, u32[]{:S(2)}) collective-permute-start(f32[1032,128]{1,0:T(8,128)S(1)} %copy-done.21), channel_id=1, source_target_pairs={{0,4},{1,5},{2,6},{3,7},{4,8},{5,9},{6,10},{7,11},{8,12},{9,13},{1... | collective-permute-start | bytes 1585160 | tf_op jit(solution)/shard_map/ppermute | solution.py:309
  45.4 6.2 %collective-permute-done.7.refs_8_.refs_18_ = f32[1032,128]{1,0:T(8,128)S(1)} collective-permute-done((f32[1032,128]{1,0:T(8,128)S(1)}, f32[1032,128]{1,0:T(8,128)S(1)}, u32[]{:S(2)}, u32[]{:S(2)}) %collective-permute-start.7) | collective-permute-done | bytes 528416 | tf_op jit(solution)/shard_map/ppermute | solution.py:306
  53.7 2.3 %broadcast_select_fusion.2 = (f32[1032,128]{1,0:T(8,128)}, f32[1032,128]{1,0:T(8,128)}) fusion(f32[1032,128]{1,0:T(8,128)S(1)} %collective-permute-done.9.refs_4_.refs_14_, f32[1032,128]{1,0:T(8,128)} %get-tuple-element.55, pred[]{:T(512)S(6)} %eq.42, pred[]{:T(512)S(6)} %eq.36), kind=kLoop, calls=%fused_computation.3 | loop fusion | flops 264192 | bytes 2113538 | tf_op jit(solution)/shard_map/jit(_where)/select_n | solution.py:347
  59.2 5.2 %collective-permute-start.10 = (f32[1032,128]{1,0:T(8,128)}, f32[1032,128]{1,0:T(8,128)}, u32[]{:S(2)}, u32[]{:S(2)}) collective-permute-start(f32[1032,128]{1,0:T(8,128)} %get-tuple-element.55), channel_id=1, source_target_pairs={{0,4},{1,5},{2,6},{3,7},{4,8},{5,9},{6,10},{7,11},{8,12},{9,13},{1... | collective-permute-start | bytes 1585160 | tf_op jit(solution)/shard_map/ppermute | solution.py:309
  67.2 3.4 %collective-permute-done.10.refs_5_.refs_15_ = f32[1032,128]{1,0:T(8,128)} collective-permute-done((f32[1032,128]{1,0:T(8,128)}, f32[1032,128]{1,0:T(8,128)}, u32[]{:S(2)}, u32[]{:S(2)}) %collective-permute-start.10) | collective-permute-done | bytes 528416 | tf_op jit(solution)/shard_map/ppermute | solution.py:309
  70.6 2.4 %broadcast_select_fusion = (f32[1032,128]{1,0:T(8,128)}, f32[1032,128]{1,0:T(8,128)}, f32[1032,128]{1,0:T(8,128)}) fusion(f32[1032,128]{1,0:T(8,128)} %copy-done.14, f32[1032,128]{1,0:T(8,128)} %copy-done.13, pred[]{:T(512)S(6)} %eq.44, f32[1032,128]{1,0:T(8,128)} %collective-permute-done.10.refs_5_.refs_15_, pred[]{:T(512)S(6)} %eq.36, ...), kind=kLoop, calls=%fused_computation.1 | loop fusion | flops 396288 | bytes 3698691 | tf_op jit(solution)/shard_map/jit(_where)/select_n | solution.py:365
  74.0 8.1 %shard_map.47 = (f32[512,512]{1,0:T(8,128)}, f32[512,512]{1,0:T(8,128)}, f32[512,512]{1,0:T(8,128)}) custom-call(s32[4]{0:T(128)} %pad_add_fusion.flag_ref.refs_1_, bf16[4,512,256]{2,1,0:T(8,128)(2,1)} %get-tuple-element.65.refs_0_, bf16[4,512,256]{2,1,0:T(8,128)(2,1)} %get-tuple-element.66.refs_1_, f32[1032,128]{1,0:T(8,128)} %copy-done.9, ...), custom_call_target="tpu_custom_call" | custom-call | tf_op jit(solution)/shard_map/pallas_call | solution.py:82
  85.3 4.7 %shard_map.48 = (f32[512,512]{1,0:T(8,128)}, f32[512,512]{1,0:T(8,128)}) custom-call(s32[4]{0:T(128)} %pad_add_fusion.flag_ref.refs_1_, bf16[4,512,256]{2,1,0:T(8,128)(2,1)} %get-tuple-element.65.refs_0_, bf16[4,512,256]{2,1,0:T(8,128)(2,1)} %get-tuple-element.66.refs_1_, f32[512,512]{1,0:T(8,128)} %get-tuple-element.61.refs_2_, ...), custom_call_target="tpu_custom_call" | custom-call | tf_op jit(solution)/shard_map/pallas_call | solution.py:82
  91.9 5.8 %collective-permute-done.13.refs_5_.refs_3_.refs_9_ = f32[1032,128]{1,0:T(8,128)S(1)} collective-permute-done((f32[1032,128]{1,0:T(8,128)}, f32[1032,128]{1,0:T(8,128)S(1)}, u32[]{:S(2)}, u32[]{:S(2)}) %collective-permute-start.13) | collective-permute-done | bytes 528416 | tf_op jit(solution)/shard_map/ppermute | solution.py:306
  98.5 3.3 %collective-permute-start.21 = (f32[1032,128]{1,0:T(8,128)}, f32[1032,128]{1,0:T(8,128)S(1)}, u32[]{:S(2)}, u32[]{:S(2)}) collective-permute-start(f32[1032,128]{1,0:T(8,128)} %copy-done.1), channel_id=1, source_target_pairs={{0,1},{1,0},{4,5},{5,4},{8,9},{9,8},{12,13},{13,12},{16,17},{17,16... | collective-permute-start | bytes 1585160 | tf_op jit(solution)/shard_map/ppermute | solution.py:306
  101.9 13.9 %shard_map.49.refs_5_ = f32[4096,128]{1,0:T(8,128)} custom-call(f32[5]{0:T(128)} %stack.34.refs_0_, s32[4]{0:T(128)} %pad_add_fusion.flag_ref.refs_1_, f32[1,512]{1,0:T(1,128)} %bitcast.22, f32[512,512]{1,0:T(8,128)} %get-tuple-element.58.refs_3_, f32[512,512]{1,0:T(8,128)} %collective-permute-done.refs_4_, f32[512,512]{1,0:T(8,128)} %get-tuple-element.60.refs_5_, ...), custom_call_target="tpu_custom_call" | custom-call | tf_op jit(solution)/shard_map/pallas_call | solution.py:82
  116.6 4.0 %shard_map.50.refs_2_ = f32[512,512]{1,0:T(8,128)} custom-call(s32[4]{0:T(128)} %pad_add_fusion.flag_ref.refs_1_, bf16[4,512,256]{2,1,0:T(8,128)(2,1)} %get-tuple-element.65.refs_0_, bf16[4,512,256]{2,1,0:T(8,128)(2,1)} %get-tuple-element.66.refs_1_, f32[1032,128]{1,0:T(8,128)} %copy-done.1, f32[1032,128]{1,0:T(8,128)} %copy-done.16, f32[1032,128]{1,0:T(8,128)} %copy-done, ...), custom_call_target="tpu_custom_call" | custom-call | tf_op jit(solution)/shard_map/pallas_call | solution.py:82
  122.2 4.1 %shard_map.51.refs_3_ = f32[512,512]{1,0:T(8,128)} custom-call(s32[4]{0:T(128)} %pad_add_fusion.flag_ref.refs_1_, bf16[4,512,256]{2,1,0:T(8,128)(2,1)} %get-tuple-element.65.refs_0_, bf16[4,512,256]{2,1,0:T(8,128)(2,1)} %get-tuple-element.66.refs_1_, f32[512,512]{1,0:T(8,128)} %shard_map.50.refs_2_, f32[1032,128]{1,0:T(8,128)} %copy-done.5, ...), custom_call_target="tpu_custom_call" | custom-call | tf_op jit(solution)/shard_map/pallas_call | solution.py:82
  126.3 2.9 %collective-permute-done.22.refs_4_ = f32[512,512]{1,0:T(8,128)S(1)} collective-permute-done((f32[512,512]{1,0:T(8,128)}, f32[512,512]{1,0:T(8,128)S(1)}, u32[]{:S(2)}, u32[]{:S(2)}) %collective-permute-start.22) | collective-permute-done | bytes 1048608 | tf_op jit(solution)/shard_map/ppermute | solution.py:313
  130.2 6.4 %shard_map.52 = f32[4096,128]{1,0:T(8,128)} custom-call(f32[5]{0:T(128)} %stack.34.refs_0_, s32[4]{0:T(128)} %pad_add_fusion.flag_ref.refs_1_, f32[1,512]{1,0:T(1,128)} %bitcast.23, f32[512,512]{1,0:T(8,128)} %shard_map.51.refs_3_, f32[512,512]{1,0:T(8,128)} %copy-done.20, f32[4096,128]{1,0:T(8,128)} %shard_map.49.refs_5_, f32[1032,128]{1,0:T(8,128)} %copy-done.1, ...), custom_call_target="tpu_custom_call" | custom-call | tf_op jit(solution)/shard_map/pallas_call | solution.py:82
  (88 shorter events, 26.5 us)
Async XLA Ops:
  2.1 17.0 %collective-permute-start.1 = (f32[1032,128]{1,0:T(8,128)S(1)}, f32[1032,128]{1,0:T(8,128)S(1)}, u32[]{:S(2)}, u32[]{:S(2)}) collective-permute-start(f32[1032,128]{1,0:T(8,128)S(1)} %pad_maximum_fusion.refs_26_.refs_12_), channel_id=1, source_target_pairs={{0,4},{1,5},{2,6},{3,7},{4,8},{5,9},{6,10},{7,11},{8,12},{9,13},{1... | collective-permute-start | bytes 1585160 | tf_op jit(solution)/shard_map/ppermute | solution.py:309
  7.1 14.4 %collective-permute-start.5 = (f32[1032,128]{1,0:T(8,128)S(1)}, f32[1032,128]{1,0:T(8,128)S(1)}, u32[]{:S(2)}, u32[]{:S(2)}) collective-permute-start(f32[1032,128]{1,0:T(8,128)S(1)} %pad_maximum_fusion.refs_26_.refs_12_), channel_id=1, source_target_pairs={{0,2},{1,3},{4,6},{5,7},{8,10},{9,11},{12,14},{13,15},{16,18},{17,... | collective-permute-start | bytes 1585160 | tf_op jit(solution)/shard_map/ppermute | solution.py:306
  10.6 15.1 %collective-permute-start.3 = (f32[1032,128]{1,0:T(8,128)S(1)}, f32[1032,128]{1,0:T(8,128)S(1)}, u32[]{:S(2)}, u32[]{:S(2)}) collective-permute-start(f32[1032,128]{1,0:T(8,128)S(1)} %pad_maximum_fusion.refs_26_.refs_12_), channel_id=1, source_target_pairs={{0,1},{2,3},{1,0},{4,5},{6,7},{5,4},{8,9},{10,11},{9,8},{12,13},{1... | collective-permute-start | bytes 1585160 | tf_op jit(solution)/shard_map/ppermute | solution.py:306
  22.3 13.5 %collective-permute-start.6 = (f32[1032,128]{1,0:T(8,128)}, f32[1032,128]{1,0:T(8,128)S(1)}, u32[]{:S(2)}, u32[]{:S(2)}) collective-permute-start(f32[1032,128]{1,0:T(8,128)} %get-tuple-element.49), channel_id=1, source_target_pairs={{0,2},{2,0},{1,3},{3,1},{4,6},{6,4},{5,7},{7,5},{8,10},{10,8},{9,1... | collective-permute-start | bytes 1585160 | tf_op jit(solution)/shard_map/ppermute | solution.py:306
  25.7 44.9 %copy-start.12 = (f32[1032,128]{1,0:T(8,128)}, f32[1032,128]{1,0:T(8,128)S(1)}, u32[]{:S(2)}) copy-start(f32[1032,128]{1,0:T(8,128)S(1)} %collective-permute-done.3.refs_6_.refs_16_) | copy-start | bytes 1585156
  25.7 12.5 %collective-permute-start.4 = (f32[1032,128]{1,0:T(8,128)}, f32[1032,128]{1,0:T(8,128)S(1)}, u32[]{:S(2)}, u32[]{:S(2)}) collective-permute-start(f32[1032,128]{1,0:T(8,128)} %get-tuple-element.48), channel_id=1, source_target_pairs={{0,1},{1,0},{2,3},{3,2},{4,5},{5,4},{6,7},{7,6},{8,9},{9,8},{10,11... | collective-permute-start | bytes 1585160 | tf_op jit(solution)/shard_map/ppermute | solution.py:306
  27.1 13.2 %collective-permute-start.2 = (f32[1032,128]{1,0:T(8,128)}, f32[1032,128]{1,0:T(8,128)S(1)}, u32[]{:S(2)}, u32[]{:S(2)}) collective-permute-start(f32[1032,128]{1,0:T(8,128)} %get-tuple-element.47), channel_id=1, source_target_pairs={{0,4},{1,5},{2,6},{3,7},{4,8},{5,9},{6,10},{7,11},{8,12},{9,13},{1... | collective-permute-start | bytes 1585160 | tf_op jit(solution)/shard_map/ppermute | solution.py:309
  40.5 11.1 %collective-permute-start.7 = (f32[1032,128]{1,0:T(8,128)S(1)}, f32[1032,128]{1,0:T(8,128)S(1)}, u32[]{:S(2)}, u32[]{:S(2)}) collective-permute-start(f32[1032,128]{1,0:T(8,128)S(1)} %get-tuple-element.74), channel_id=1, source_target_pairs={{0,1},{1,0},{2,3},{3,2},{4,5},{5,4},{6,7},{7,6},{8,9},{9,8},{10,11... | collective-permute-start | bytes 1585160 | tf_op jit(solution)/shard_map/ppermute | solution.py:306
  41.1 10.8 %collective-permute-start.8 = (f32[1032,128]{1,0:T(8,128)S(1)}, f32[1032,128]{1,0:T(8,128)S(1)}, u32[]{:S(2)}, u32[]{:S(2)}) collective-permute-start(f32[1032,128]{1,0:T(8,128)S(1)} %get-tuple-element.73), channel_id=1, source_target_pairs={{0,2},{2,0},{1,3},{3,1},{4,6},{6,4},{5,7},{7,5},{8,10},{10,8},{9,1... | collective-permute-start | bytes 1585160 | tf_op jit(solution)/shard_map/ppermute | solution.py:306
  41.1 12.6 %collective-permute-start.9 = (f32[1032,128]{1,0:T(8,128)S(1)}, f32[1032,128]{1,0:T(8,128)S(1)}, u32[]{:S(2)}, u32[]{:S(2)}) collective-permute-start(f32[1032,128]{1,0:T(8,128)S(1)} %copy-done.21), channel_id=1, source_target_pairs={{0,4},{1,5},{2,6},{3,7},{4,8},{5,9},{6,10},{7,11},{8,12},{9,13},{1... | collective-permute-start | bytes 1585160 | tf_op jit(solution)/shard_map/ppermute | solution.py:309
  55.9 10.1 %collective-permute-start.11 = (f32[1032,128]{1,0:T(8,128)}, f32[1032,128]{1,0:T(8,128)S(1)}, u32[]{:S(2)}, u32[]{:S(2)}) collective-permute-start(f32[1032,128]{1,0:T(8,128)} %get-tuple-element.72), channel_id=1, source_target_pairs={{0,1},{1,0},{2,3},{3,2},{4,5},{5,4},{6,7},{7,6},{8,9},{9,8},{10,11... | collective-permute-start | bytes 1585160 | tf_op jit(solution)/shard_map/ppermute | solution.py:306
  57.4 9.8 %collective-permute-start.12 = (f32[1032,128]{1,0:T(8,128)}, f32[1032,128]{1,0:T(8,128)S(1)}, u32[]{:S(2)}, u32[]{:S(2)}) collective-permute-start(f32[1032,128]{1,0:T(8,128)} %get-tuple-element.71), channel_id=1, source_target_pairs={{0,2},{2,0},{1,3},{3,1},{4,6},{6,4},{5,7},{7,5},{8,10},{10,8},{9,1... | collective-permute-start | bytes 1585160 | tf_op jit(solution)/shard_map/ppermute | solution.py:306
  59.2 11.4 %collective-permute-start.10 = (f32[1032,128]{1,0:T(8,128)}, f32[1032,128]{1,0:T(8,128)}, u32[]{:S(2)}, u32[]{:S(2)}) collective-permute-start(f32[1032,128]{1,0:T(8,128)} %get-tuple-element.55), channel_id=1, source_target_pairs={{0,4},{1,5},{2,6},{3,7},{4,8},{5,9},{6,10},{7,11},{8,12},{9,13},{1... | collective-permute-start | bytes 1585160 | tf_op jit(solution)/shard_map/ppermute | solution.py:309
  73.0 11.3 %collective-permute-start.15 = (f32[1032,128]{1,0:T(8,128)}, f32[1032,128]{1,0:T(8,128)S(1)}, u32[]{:S(2)}, u32[]{:S(2)}) collective-permute-start(f32[1032,128]{1,0:T(8,128)} %get-tuple-element.78), channel_id=1, source_target_pairs={{0,1},{1,0},{2,3},{3,2},{4,5},{5,4},{6,7},{7,6},{8,9},{9,8},{10,11... | collective-permute-start | bytes 1585160 | tf_op jit(solution)/shard_map/ppermute | solution.py:306
  73.6 10.7 %collective-permute-start.16 = (f32[1032,128]{1,0:T(8,128)}, f32[1032,128]{1,0:T(8,128)S(1)}, u32[]{:S(2)}, u32[]{:S(2)}) collective-permute-start(f32[1032,128]{1,0:T(8,128)} %get-tuple-element.79), channel_id=1, source_target_pairs={{0,2},{2,0},{1,3},{3,1},{4,6},{6,4},{5,7},{7,5},{8,10},{10,8},{9,1... | collective-permute-start | bytes 1585160 | tf_op jit(solution)/shard_map/ppermute | solution.py:306
  74.0 16.6 %collective-permute-start = (f32[512,512]{1,0:T(8,128)}, f32[512,512]{1,0:T(8,128)}, u32[]{:S(2)}, u32[]{:S(2)}) collective-permute-start(f32[512,512]{1,0:T(8,128)} %get-tuple-element.58.refs_3_), channel_id=1, source_target_pairs={{0,16},{16,0},{1,17},{17,1},{2,18},{18,2},{3,19},{19,3},{4,20},{20... | collective-permute-start | bytes 3145736 | tf_op jit(solution)/shard_map/ppermute | solution.py:313
  82.1 16.4 %collective-permute-start.14 = (f32[512,512]{1,0:T(8,128)}, f32[512,512]{1,0:T(8,128)S(1)}, u32[]{:S(2)}, u32[]{:S(2)}) collective-permute-start(f32[512,512]{1,0:T(8,128)} %get-tuple-element.60.refs_5_), channel_id=1, source_target_pairs={{0,16},{16,0},{1,17},{17,1},{2,18},{18,2},{3,19},{19,3},{4,20},{20... | collective-permute-start | bytes 3145736 | tf_op jit(solution)/shard_map/ppermute | solution.py:313
  82.7 15.1 %collective-permute-start.13 = (f32[1032,128]{1,0:T(8,128)}, f32[1032,128]{1,0:T(8,128)S(1)}, u32[]{:S(2)}, u32[]{:S(2)}) collective-permute-start(f32[1032,128]{1,0:T(8,128)} %broadcast_select_fusion.9), channel_id=1, source_target_pairs={{0,1},{1,3},{3,2},{2,0},{4,5},{5,7},{7,6},{6,4},{8,9},{9,11},{11,1... | collective-permute-start | bytes 1585160 | tf_op jit(solution)/shard_map/ppermute | solution.py:306
  90.0 11.8 %collective-permute-start.17 = (f32[512,512]{1,0:T(8,128)}, f32[512,512]{1,0:T(8,128)}, u32[]{:S(2)}, u32[]{:S(2)}) collective-permute-start(f32[512,512]{1,0:T(8,128)} %get-tuple-element.63.refs_7_), channel_id=1, source_target_pairs={{0,16},{16,0},{1,17},{17,1},{2,18},{18,2},{3,19},{19,3},{4,20},{20... | collective-permute-start | bytes 3145736 | tf_op jit(solution)/shard_map/ppermute | solution.py:313
  90.1 11.8 %collective-permute-start.18 = (f32[512,512]{1,0:T(8,128)}, f32[512,512]{1,0:T(8,128)}, u32[]{:S(2)}, u32[]{:S(2)}) collective-permute-start(f32[512,512]{1,0:T(8,128)} %get-tuple-element.64.refs_9_), channel_id=1, source_target_pairs={{0,16},{16,0},{1,17},{17,1},{2,18},{18,2},{3,19},{19,3},{4,20},{20... | collective-permute-start | bytes 3145736 | tf_op jit(solution)/shard_map/ppermute | solution.py:313
  90.6 25.2 %collective-permute-start.19 = (f32[1032,128]{1,0:T(8,128)}, f32[1032,128]{1,0:T(8,128)S(1)}, u32[]{:S(2)}, u32[]{:S(2)}) collective-permute-start(f32[1032,128]{1,0:T(8,128)} %get-tuple-element.77), channel_id=1, source_target_pairs={{2,0},{3,2},{6,4},{7,6},{10,8},{11,10},{14,12},{15,14},{18,16},{19... | collective-permute-start | bytes 1585160 | tf_op jit(solution)/shard_map/ppermute | solution.py:306
  97.7 22.8 %collective-permute-start.20 = (f32[1032,128]{1,0:T(8,128)S(1)}, f32[1032,128]{1,0:T(8,128)S(1)}, u32[]{:S(2)}, u32[]{:S(2)}) collective-permute-start(f32[1032,128]{1,0:T(8,128)S(1)} %copy-done.3), channel_id=1, source_target_pairs={{0,1},{1,0},{2,3},{3,2},{4,5},{5,4},{6,7},{7,6},{8,9},{9,8},{10,11... | collective-permute-start | bytes 1585160 | tf_op jit(solution)/shard_map/ppermute | solution.py:306
  98.5 22.8 %collective-permute-start.21 = (f32[1032,128]{1,0:T(8,128)}, f32[1032,128]{1,0:T(8,128)S(1)}, u32[]{:S(2)}, u32[]{:S(2)}) collective-permute-start(f32[1032,128]{1,0:T(8,128)} %copy-done.1), channel_id=1, source_target_pairs={{0,1},{1,0},{4,5},{5,4},{8,9},{9,8},{12,13},{13,12},{16,17},{17,16... | collective-permute-start | bytes 1585160 | tf_op jit(solution)/shard_map/ppermute | solution.py:306
  126.3 2.9 %collective-permute-start.22 = (f32[512,512]{1,0:T(8,128)}, f32[512,512]{1,0:T(8,128)S(1)}, u32[]{:S(2)}, u32[]{:S(2)}) collective-permute-start(f32[512,512]{1,0:T(8,128)} %shard_map.51.refs_3_), channel_id=1, source_target_pairs={{0,16},{16,0},{1,17},{17,1},{2,18},{18,2},{3,19},{19,3},{4,20},{20... | collective-permute-start | bytes 3145736 | tf_op jit(solution)/shard_map/ppermute | solution.py:313
  (23 other events, 232.4 us)

commit v4 on v3

--- a/solution.py
+++ b/solution.py
@@ -13,6 +13,7 @@
 PLANE = 4
 CHUNKS = 4
 VMEM_LIMIT = 60 * 1024 * 1024
+LAST_LIMIT = 24 * 1024 * 1024
 
 
 def split(value):
@@ -77,7 +78,7 @@
     choice: int = 0
 
 
-def call(kernel, smem, vmem, anywhere, outputs, out_space, scratch):
+def call(kernel, smem, vmem, anywhere, outputs, out_space, scratch, limit=VMEM_LIMIT):
     spaces = [pltpu.SMEM] * len(smem) + [pltpu.VMEM] * len(vmem) + [pl.ANY] * len(anywhere)
     return pl.pallas_call(
         kernel,
@@ -85,7 +86,7 @@
         in_specs=[pl.BlockSpec(memory_space=space) for space in spaces],
         out_specs=[pl.BlockSpec(memory_space=out_space)] * len(outputs),
         scratch_shapes=scratch,
-        compiler_params=pltpu.CompilerParams(vmem_limit_bytes=VMEM_LIMIT),
+        compiler_params=pltpu.CompilerParams(vmem_limit_bytes=limit),
         cost_estimate=pl.CostEstimate(flops=0, bytes_accessed=0, transcendentals=0),
     )(*smem, *vmem, *anywhere)
 
@@ -133,7 +134,7 @@
     return distinct([array for piece in pieces for array, _ in piece.places])
 
 
-def integrate(turned, slots, first, flags, size, width, before=()):
+def integrate(turned, slots, first, flags, size, width, before=(), limit=VMEM_LIMIT):
     cut = size * width // LANES
     count = len(slots)
     pieces = [piece for slot in slots for piece in slot]
@@ -190,10 +191,10 @@
         pltpu.VMEM((max(len(before), 1), width, width), jnp.float32),
         pltpu.SemaphoreType.DMA((2 * len(needed) + len(pieces) + len(before),)),
     ]
-    return call(kernel, [flags], [], [*turned, *before, *arrays], out, pltpu.VMEM, scratch)
-
-
-def contract(partials, slots, signs, first_sign, energies, flags, eps_virt, size, before=None):
+    return call(kernel, [flags], [], [*turned, *before, *arrays], out, pltpu.VMEM, scratch, limit)
+
+
+def contract(partials, slots, signs, first_sign, energies, flags, eps_virt, size, before=None, limit=VMEM_LIMIT):
     count = len(slots)
     chunks = len(slots[0])
     virt = eps_virt.shape[1]
@@ -273,7 +274,7 @@
         pltpu.VMEM((width, count * 3 * width), jnp.bfloat16),
         pltpu.SemaphoreType.DMA((len(energies) + len(sums) + len(pieces) + 2 * chunks,)),
     ]
-    return call(kernel, [signs, flags], [eps_virt], [*sums, *last, *arrays], [out], pl.ANY, scratch)[0]
+    return call(kernel, [signs, flags], [eps_virt], [*sums, *last, *arrays], [out], pl.ANY, scratch, limit)[0]
 
 
 def after(block, *others):
@@ -313,21 +314,30 @@
             return [partial, lax.ppermute(partial, "aux", [(0, 1), (1, 0)])]
         return [lax.psum(partial, "aux")]
 
-    def sign(offset):
-        flag = jnp.sum(jnp.where(jnp.arange(1, PLANE + 1) == offset, pair_mask[0], 0))
-        return jnp.where((group >= offset) & (flag > 0), -1.0, 0.0).astype(jnp.float32)
-
-    near, far = jnp.where(odd_x, 1, PLANE - 1), jnp.where(odd_x, PLANE - 1, 1)
-    signs = jnp.stack([jnp.float32(-1.0), sign(PLANE), sign(near), sign(PLANE // 2), sign(far)])
-
     first_sent = jnp.concatenate([part(own, 0), energies])
-    down_x, down_y = 1 - place % 2, 1 - place // 2
-    flags = jnp.stack(
-        [down_x, down_y, jnp.where(odd_y, 0, 1 + place), jnp.where(odd_y, place - 1, 0)]
-    ).astype(jnp.int32)
-
-    def add(first_sign, partials, slots, carriers, before=None):
-        return contract(partials, slots, signs, first_sign, carriers, flags, eps_virt[None, :], size, before)
+    def choices(sent):
+        group_then, mask_row, _ = lax.optimization_barrier((group, pair_mask[0], sent))
+        place_then = group_then % PLANE
+
+        def sign(offset):
+            flag = jnp.sum(jnp.where(jnp.arange(1, PLANE + 1) == offset, mask_row, 0))
+            return jnp.where((group_then >= offset) & (flag > 0), -1.0, 0.0).astype(jnp.float32)
+
+        near = jnp.where(place_then % 2 == 1, 1, PLANE - 1)
+        signs = [jnp.float32(-1.0), sign(PLANE), sign(near), sign(PLANE // 2), sign(PLANE - near)]
+        up_then = place_then // 2 == 1
+        flags = [
+            1 - place_then % 2,
+            1 - place_then // 2,
+            jnp.where(up_then, 0, 1 + place_then),
+            jnp.where(up_then, place_then - 1, 0),
+        ]
+        return jnp.stack(signs), jnp.stack(flags).astype(jnp.int32)
+
+    def add(first_sign, partials, slots, carriers, before=None, limit=VMEM_LIMIT):
+        return contract(
+            partials, slots, signs, first_sign, carriers, flags, eps_virt[None, :], size, before, limit
+        )
 
     from_own = [first_sent]
     from_z = [up(first_sent)]
@@ -340,23 +350,26 @@
     swap_x, swap_y = [], []
     passed = [partial_own]
     for at in range(CHUNKS):
-        came, *_ = lax.optimization_barrier((from_z[at], *passed))
+        came = after(from_z[at], *passed)
         if at < last:
             from_z.append(up(after(from_own[at + 1], came)))
             up_part = after(from_own[at + 1], came)
             send_x, send_y = jnp.where(odd_x, came, up_part), jnp.where(odd_y, came, up_part)
+            send_x = after(send_x, swap_x[at - 1] if at else up_x)
+            send_y = after(send_y, swap_y[at - 1] if at else up_y)
             if at == 0:
-                send_x, send_y = after(send_x, up_x), after(send_y, up_y)
+                signs, flags = choices((send_x, send_y))
             swap_x.append(within(send_x, [(0, 1), (1, 0), (2, 3), (3, 2)]))
             swap_y.append(within(send_y, [(0, 2), (2, 0), (1, 3), (3, 1)]))
         else:
-            cycle = within(after(turning, came), [(0, 1), (1, 3), (3, 2), (2, 0)])
-            swap_x.append(within(jnp.where(odd_x, came, swap_y[0]), [(0, 1), (1, 0), (2, 3), (3, 2)]))
-            swap_y.append(within(jnp.where(odd_y, came, up_x), [(0, 2), (2, 0), (1, 3), (3, 1)]))
-        passed = [swap_x[at], swap_y[at]]
-        if at == 0:
-            passed += [signs, flags]
+            cycle = within(after(turning, came, swap_x[last - 1]), [(0, 1), (1, 3), (3, 2), (2, 0)])
+            send_x = after(jnp.where(odd_x, came, swap_y[0]), swap_x[last - 1])
+            send_y = after(jnp.where(odd_y, came, up_x), swap_y[last - 1])
+            swap_x.append(within(send_x, [(0, 1), (1, 0), (2, 3), (3, 2)]))
+            swap_y.append(within(send_y, [(0, 2), (2, 0), (1, 3), (3, 1)]))
+        passed = []
         if at == 1:
+            passed = [signs, flags]
             middle = (place == 1) | (place == 2)
             turning = jnp.where(middle, swap_x[1], swap_y[1])
         if at == 2:
@@ -403,8 +416,8 @@
     turned = after(turned, gradient)
     half = CHUNKS // 2
     partial_d = integrate(turned, [slot_d[:half]], [0], flags, size, width)
-    (partial_d,) = integrate(turned, [slot_d[half:]], [half], flags, size, width, partial_d)
-    gradient = add(4, [totals(partial_d)], [slot_d], [own_eps, eps_d], gradient)
+    (partial_d,) = integrate(turned, [slot_d[half:]], [half], flags, size, width, partial_d, LAST_LIMIT)
+    gradient = add(4, [totals(partial_d)], [slot_d], [own_eps, eps_d], gradient, LAST_LIMIT)
     return gradient.reshape(rows, occ_rows, virt)
 
 

time: 137 us -> 129 us (0.942)
  waiting for transfers between devices: 29.2 us -> 23 us
  Pallas kernels: 46.1 us -> 43.3 us
    ppermute x14, waiting for transfers between devices: 19 us -> 10.9 us  [within(): lax.ppermute(block, 'occ', [(g + a, g + b) for g in planes for a, b in mo...]
    pallas_call x7, Pallas kernels: 46.1 us -> 43.3 us  [call(): pl.pallas_call(kernel, out_shape=outputs, in_specs=[pl.BlockSpec(memory_s...]
    ppermute x4, waiting for transfers between devices: 7.41 us -> 9.46 us  [up(): lax.ppermute(block, 'occ', [(g, g + PLANE) for g in range(groups - PLANE)])]
    ppermute x14, starting transfers between devices: 22.6 us -> 24.3 us  [within(): lax.ppermute(block, 'occ', [(g + a, g + b) for g in planes for a, b in mo...]
    unnamed x48 -> x64, local copies, waits for them, and re-layouts: 4.54 us -> 4.95 us
  transfers between devices with their start and end apart: 23 -> 23, of which waited for: 13 -> 7; matrix products, arithmetic and copies ran while one was open for 4% -> 7% of each run, Pallas kernels for 26% -> 28%
where the time goes in v4:
time: 129 us; the launch traced here: 128 us
  Pallas kernels  43.3 us (34%)
  starting transfers between devices  42.7 us (33%)
  waiting for transfers between devices  23 us (18%)
  other arithmetic  8.04 us (6%)
  local copies, waits for them, and re-layouts  6.98 us (5%)
  between operations  3.94 us (3%)
    pallas_call x7, Pallas kernels, call(): pl.pallas_call(kernel, out_shape=outputs, in_specs=[pl.BlockSpec(memory_s...  43.3 us
    ppermute x14, starting transfers between devices, within(): lax.ppermute(block, 'occ', [(g + a, g + b) for g in planes for a, b in mo...  24.3 us
    ppermute x4, starting transfers between devices, up(): lax.ppermute(block, 'occ', [(g, g + PLANE) for g in range(groups - PLANE)])  17.2 us
    ppermute x14, waiting for transfers between devices, within(): lax.ppermute(block, 'occ', [(g + a, g + b) for g in planes for a, b in mo...  10.9 us
    ppermute x4, waiting for transfers between devices, up(): lax.ppermute(block, 'occ', [(g, g + PLANE) for g in range(groups - PLANE)])  9.46 us
    unnamed x64, local copies, waits for them, and re-layouts  4.95 us
    select_n x3, other arithmetic, on_device(): jnp.where(odd_y, came, up_part)  4.41 us
    ppermute x5, waiting for transfers between devices, totals(): return [partial, lax.ppermute(partial, 'aux', [(0, 1), (1, 0)])]  2.66 us
  transfers between devices with their start and end apart: 23, of which 7 were waited for; matrix products, arithmetic and copies ran while one was open for 7% of the time, Pallas kernels for 28%

profile of v4, /device:TPU:0, one launch (start us, length us, event | category | flops | bytes accessed | tf_op | source)
XLA Modules:
  0.0 128.0 jit_solution(18200683025145739453)
XLA Ops:
  2.1 5.0 %collective-permute-start = (f32[1032,128]{1,0:T(8,128)S(1)}, f32[1032,128]{1,0:T(8,128)S(1)}, u32[]{:S(2)}, u32[]{:S(2)}) collective-permute-start(f32[1032,128]{1,0:T(8,128)S(1)} %pad_maximum_fusion.refs_26_.refs_12_), channel_id=1, source_target_pairs={{0,4},{1,5},{2,6},{3,7},{4,8},{5,9},{6,10},{7,11},{8,12},{9,13},{1... | collective-permute-start | bytes 1585160 | tf_op jit(solution)/shard_map/ppermute | solution.py:310
  7.1 3.5 %collective-permute-start.2 = (f32[1032,128]{1,0:T(8,128)S(1)}, f32[1032,128]{1,0:T(8,128)S(1)}, u32[]{:S(2)}, u32[]{:S(2)}) collective-permute-start(f32[1032,128]{1,0:T(8,128)S(1)} %pad_maximum_fusion.refs_26_.refs_12_), channel_id=1, source_target_pairs={{0,2},{1,3},{4,6},{5,7},{8,10},{9,11},{12,14},{13,15},{16,18},{17,... | collective-permute-start | bytes 1585160 | tf_op jit(solution)/shard_map/ppermute | solution.py:307
  10.6 3.4 %collective-permute-start.1 = (f32[1032,128]{1,0:T(8,128)S(1)}, f32[1032,128]{1,0:T(8,128)S(1)}, u32[]{:S(2)}, u32[]{:S(2)}) collective-permute-start(f32[1032,128]{1,0:T(8,128)S(1)} %pad_maximum_fusion.refs_26_.refs_12_), channel_id=1, source_target_pairs={{0,1},{2,3},{1,0},{4,5},{6,7},{5,4},{8,9},{10,11},{9,8},{12,13},{1... | collective-permute-start | bytes 1585160 | tf_op jit(solution)/shard_map/ppermute | solution.py:307
  14.0 5.0 %shard_map.46 = (bf16[4,512,256]{2,1,0:T(8,128)(2,1)}, bf16[4,512,256]{2,1,0:T(8,128)(2,1)}, f32[512,512]{1,0:T(8,128)}, f32[1032,128]{1,0:T(8,128)}, f32[1032,128]{1,0:T(8,128)}, /*index=5*/f32[1032,128]{1,0:T(8,128)}) custom-call(f32[8,128]{1,0:T(8,128)} %copy-done.30, f32[4096,128]{1,0:T(8,128)} %bitcast.17), custom_call_target="tpu_custom_call" | custom-call | tf_op jit(solution)/shard_map/pallas_call | solution.py:83
  19.1 3.6 %collective-permute-start.4 = (f32[1032,128]{1,0:T(8,128)}, f32[1032,128]{1,0:T(8,128)S(1)}, u32[]{:S(2)}, u32[]{:S(2)}) collective-permute-start(f32[1032,128]{1,0:T(8,128)} %get-tuple-element.52), channel_id=1, source_target_pairs={{0,4},{1,5},{2,6},{3,7},{4,8},{5,9},{6,10},{7,11},{8,12},{9,13},{1... | collective-permute-start | bytes 1585160 | tf_op jit(solution)/shard_map/ppermute | solution.py:310
  22.7 2.1 %broadcast_select_fusion.5 = (f32[1032,128]{1,0:T(8,128)}, f32[1032,128]{1,0:T(8,128)}) fusion(f32[1032,128]{1,0:T(8,128)S(1)} %collective-permute-done.refs_2_.refs_12_, f32[1032,128]{1,0:T(8,128)} %get-tuple-element.52, pred[]{:T(512)S(6)} %eq.44, pred[]{:T(512)S(6)} %eq.43), kind=kLoop, calls=%fused_computation.6 | loop fusion | flops 264192 | bytes 2113538 | tf_op jit(solution)/shard_map/jit(_where)/select_n | solution.py:357
  33.4 4.3 %collective-permute-start.9 = (f32[1032,128]{1,0:T(8,128)}, f32[1032,128]{1,0:T(8,128)S(1)}, u32[]{:S(2)}, u32[]{:S(2)}) collective-permute-start(f32[1032,128]{1,0:T(8,128)} %get-tuple-element.60), channel_id=1, source_target_pairs={{0,4},{1,5},{2,6},{3,7},{4,8},{5,9},{6,10},{7,11},{8,12},{9,13},{1... | collective-permute-start | bytes 1585160 | tf_op jit(solution)/shard_map/ppermute | solution.py:310
  39.7 1.5 %collective-permute-start.8 = (f32[1032,128]{1,0:T(8,128)S(1)}, f32[1032,128]{1,0:T(8,128)S(1)}, u32[]{:S(2)}, u32[]{:S(2)}) collective-permute-start(f32[1032,128]{1,0:T(8,128)S(1)} %get-tuple-element.62), channel_id=1, source_target_pairs={{0,2},{2,0},{1,3},{3,1},{4,6},{6,4},{5,7},{7,5},{8,10},{10,8},{9,1... | collective-permute-start | bytes 1585160 | tf_op jit(solution)/shard_map/ppermute | solution.py:307
  42.7 4.9 %collective-permute-done.9.refs_4_.refs_14_ = f32[1032,128]{1,0:T(8,128)S(1)} collective-permute-done((f32[1032,128]{1,0:T(8,128)}, f32[1032,128]{1,0:T(8,128)S(1)}, u32[]{:S(2)}, u32[]{:S(2)}) %collective-permute-start.9) | collective-permute-done | bytes 528416 | tf_op jit(solution)/shard_map/ppermute | solution.py:310
  47.6 4.3 %collective-permute-start.10 = (f32[1032,128]{1,0:T(8,128)}, f32[1032,128]{1,0:T(8,128)S(1)}, u32[]{:S(2)}, u32[]{:S(2)}) collective-permute-start(f32[1032,128]{1,0:T(8,128)} %get-tuple-element.65), channel_id=1, source_target_pairs={{0,4},{1,5},{2,6},{3,7},{4,8},{5,9},{6,10},{7,11},{8,12},{9,13},{1... | collective-permute-start | bytes 1585160 | tf_op jit(solution)/shard_map/ppermute | solution.py:310
  53.0 1.6 %collective-permute-start.13 = (f32[1032,128]{1,0:T(8,128)S(1)}, f32[1032,128]{1,0:T(8,128)}, u32[]{:S(2)}, u32[]{:S(2)}) collective-permute-start(f32[1032,128]{1,0:T(8,128)S(1)} %get-tuple-element.71), channel_id=1, source_target_pairs={{0,2},{2,0},{1,3},{3,1},{4,6},{6,4},{5,7},{7,5},{8,10},{10,8},{9,1... | collective-permute-start | bytes 1585160 | tf_op jit(solution)/shard_map/ppermute | solution.py:307
  57.0 3.8 %collective-permute-done.10.refs_5_.refs_15_ = f32[1032,128]{1,0:T(8,128)S(1)} collective-permute-done((f32[1032,128]{1,0:T(8,128)}, f32[1032,128]{1,0:T(8,128)S(1)}, u32[]{:S(2)}, u32[]{:S(2)}) %collective-permute-start.10) | collective-permute-done | bytes 528416 | tf_op jit(solution)/shard_map/ppermute | solution.py:310
  62.2 2.9 %collective-permute-done.13.refs_13_.refs_6_.refs_24_ = f32[1032,128]{1,0:T(8,128)} collective-permute-done((f32[1032,128]{1,0:T(8,128)S(1)}, f32[1032,128]{1,0:T(8,128)}, u32[]{:S(2)}, u32[]{:S(2)}) %collective-permute-start.13) | collective-permute-done | bytes 528416 | tf_op jit(solution)/shard_map/ppermute | solution.py:307
  65.1 1.5 %collective-permute-start.16 = (f32[1032,128]{1,0:T(8,128)}, f32[1032,128]{1,0:T(8,128)S(1)}, u32[]{:S(2)}, u32[]{:S(2)}) collective-permute-start(f32[1032,128]{1,0:T(8,128)} %get-tuple-element.76), channel_id=1, source_target_pairs={{0,2},{2,0},{1,3},{3,1},{4,6},{6,4},{5,7},{7,5},{8,10},{10,8},{9,1... | collective-permute-start | bytes 1585160 | tf_op jit(solution)/shard_map/ppermute | solution.py:307
  66.6 1.6 %collective-permute-start.15 = (f32[1032,128]{1,0:T(8,128)}, f32[1032,128]{1,0:T(8,128)S(1)}, u32[]{:S(2)}, u32[]{:S(2)}) collective-permute-start(f32[1032,128]{1,0:T(8,128)} %get-tuple-element.75), channel_id=1, source_target_pairs={{0,1},{1,0},{2,3},{3,2},{4,5},{5,4},{6,7},{7,6},{8,9},{9,8},{10,11... | collective-permute-start | bytes 1585160 | tf_op jit(solution)/shard_map/ppermute | solution.py:307
  68.1 8.2 %shard_map.47 = (f32[512,512]{1,0:T(8,128)}, f32[512,512]{1,0:T(8,128)}, f32[512,512]{1,0:T(8,128)}) custom-call(s32[4]{0:T(128)} %pad_add_fusion.flag_ref.refs_1_, bf16[4,512,256]{2,1,0:T(8,128)(2,1)} %get-tuple-element.79.refs_0_, bf16[4,512,256]{2,1,0:T(8,128)(2,1)} %get-tuple-element.80.refs_1_, f32[1032,128]{1,0:T(8,128)} %copy-done.20, ...), custom_call_target="tpu_custom_call" | custom-call | tf_op jit(solution)/shard_map/pallas_call | solution.py:83
  78.4 4.5 %shard_map.48 = (f32[512,512]{1,0:T(8,128)}, f32[512,512]{1,0:T(8,128)}) custom-call(s32[4]{0:T(128)} %pad_add_fusion.flag_ref.refs_1_, bf16[4,512,256]{2,1,0:T(8,128)(2,1)} %get-tuple-element.79.refs_0_, bf16[4,512,256]{2,1,0:T(8,128)(2,1)} %get-tuple-element.80.refs_1_, f32[512,512]{1,0:T(8,128)} %get-tuple-element.73.refs_2_, ...), custom_call_target="tpu_custom_call" | custom-call | tf_op jit(solution)/shard_map/pallas_call | solution.py:83
  84.8 7.2 %collective-permute-done.12.refs_5_.refs_3_.refs_9_ = f32[1032,128]{1,0:T(8,128)S(1)} collective-permute-done((f32[1032,128]{1,0:T(8,128)}, f32[1032,128]{1,0:T(8,128)S(1)}, u32[]{:S(2)}, u32[]{:S(2)}) %collective-permute-start.12) | collective-permute-done | bytes 528416 | tf_op jit(solution)/shard_map/ppermute | solution.py:307
  92.0 4.1 %collective-permute-start.21 = (f32[1032,128]{1,0:T(8,128)}, f32[1032,128]{1,0:T(8,128)}, u32[]{:S(2)}, u32[]{:S(2)}) collective-permute-start(f32[1032,128]{1,0:T(8,128)} %copy-done.2), channel_id=1, source_target_pairs={{0,1},{1,0},{4,5},{5,4},{8,9},{9,8},{12,13},{13,12},{16,17},{17,16... | collective-permute-start | bytes 1585160 | tf_op jit(solution)/shard_map/ppermute | solution.py:307
  97.0 13.9 %shard_map.49.refs_5_ = f32[4096,128]{1,0:T(8,128)} custom-call(f32[5]{0:T(128)} %stack.34.refs_0_, s32[4]{0:T(128)} %pad_add_fusion.flag_ref.refs_1_, f32[1,512]{1,0:T(1,128)} %bitcast.15, f32[512,512]{1,0:T(8,128)} %get-tuple-element.69.refs_3_, f32[512,512]{1,0:T(8,128)} %copy-done.28, f32[512,512]{1,0:T(8,128)} %get-tuple-element.72.refs_5_, ...), custom_call_target="tpu_custom_call" | custom-call | tf_op jit(solution)/shard_map/pallas_call | solution.py:83
  111.8 4.0 %shard_map.50.refs_2_ = f32[512,512]{1,0:T(8,128)} custom-call(s32[4]{0:T(128)} %pad_add_fusion.flag_ref.refs_1_, bf16[4,512,256]{2,1,0:T(8,128)(2,1)} %get-tuple-element.79.refs_0_, bf16[4,512,256]{2,1,0:T(8,128)(2,1)} %get-tuple-element.80.refs_1_, f32[1032,128]{1,0:T(8,128)} %copy-done.2, f32[1032,128]{1,0:T(8,128)} %copy-done.12, f32[1032,128]{1,0:T(8,128)} %copy-done.4, ...), custom_call_target="tpu_custom_call" | custom-call | tf_op jit(solution)/shard_map/pallas_call | solution.py:83
  117.3 2.8 %shard_map.51.refs_3_ = f32[512,512]{1,0:T(8,128)S(1)} custom-call(s32[4]{0:T(128)S(1)} %copy-done.14, bf16[4,512,256]{2,1,0:T(8,128)(2,1)S(1)} %copy-done, bf16[4,512,256]{2,1,0:T(8,128)(2,1)S(1)} %copy-done.1, f32[512,512]{1,0:T(8,128)S(1)} %copy-done.11, f32[1032,128]{1,0:T(8,128)S(1)} %copy-done.8, f32[1032,128]{1,0:T(8,128)} %collective-permute-done.20.refs_4_.refs_10_, ...), custom_call_target="tpu_custom_call" | custom-call | tf_op jit(solution)/shard_map/pallas_call | solution.py:83
  120.2 2.6 %collective-permute-done.22.refs_4_ = f32[512,512]{1,0:T(8,128)S(1)} collective-permute-done((f32[512,512]{1,0:T(8,128)S(1)}, f32[512,512]{1,0:T(8,128)S(1)}, u32[]{:S(2)}, u32[]{:S(2)}) %collective-permute-start.22) | collective-permute-done | bytes 1048608 | tf_op jit(solution)/shard_map/ppermute | solution.py:314
  122.9 4.9 %shard_map.52 = f32[4096,128]{1,0:T(8,128)} custom-call(f32[5]{0:T(128)S(1)} %copy-done.16, s32[4]{0:T(128)S(1)} %copy-done.14, f32[1,512]{1,0:T(1,128)S(1)} %bitcast.16, f32[512,512]{1,0:T(8,128)S(1)} %shard_map.51.refs_3_, f32[512,512]{1,0:T(8,128)S(1)} %collective-permute-done.22.refs_4_, f32[4096,128]{1,0:T(8,128)S(1)} %copy-done.6, ...), custom_call_target="tpu_custom_call" | custom-call | tf_op jit(solution)/shard_map/pallas_call | solution.py:83
  (104 shorter events, 22.8 us)
Async XLA Ops:
  2.1 16.9 %collective-permute-start = (f32[1032,128]{1,0:T(8,128)S(1)}, f32[1032,128]{1,0:T(8,128)S(1)}, u32[]{:S(2)}, u32[]{:S(2)}) collective-permute-start(f32[1032,128]{1,0:T(8,128)S(1)} %pad_maximum_fusion.refs_26_.refs_12_), channel_id=1, source_target_pairs={{0,4},{1,5},{2,6},{3,7},{4,8},{5,9},{6,10},{7,11},{8,12},{9,13},{1... | collective-permute-start | bytes 1585160 | tf_op jit(solution)/shard_map/ppermute | solution.py:310
  7.1 17.8 %collective-permute-start.2 = (f32[1032,128]{1,0:T(8,128)S(1)}, f32[1032,128]{1,0:T(8,128)S(1)}, u32[]{:S(2)}, u32[]{:S(2)}) collective-permute-start(f32[1032,128]{1,0:T(8,128)S(1)} %pad_maximum_fusion.refs_26_.refs_12_), channel_id=1, source_target_pairs={{0,2},{1,3},{4,6},{5,7},{8,10},{9,11},{12,14},{13,15},{16,18},{17,... | collective-permute-start | bytes 1585160 | tf_op jit(solution)/shard_map/ppermute | solution.py:307
  10.6 15.1 %collective-permute-start.1 = (f32[1032,128]{1,0:T(8,128)S(1)}, f32[1032,128]{1,0:T(8,128)S(1)}, u32[]{:S(2)}, u32[]{:S(2)}) collective-permute-start(f32[1032,128]{1,0:T(8,128)S(1)} %pad_maximum_fusion.refs_26_.refs_12_), channel_id=1, source_target_pairs={{0,1},{2,3},{1,0},{4,5},{6,7},{5,4},{8,9},{10,11},{9,8},{12,13},{1... | collective-permute-start | bytes 1585160 | tf_op jit(solution)/shard_map/ppermute | solution.py:307
  19.1 14.3 %collective-permute-start.4 = (f32[1032,128]{1,0:T(8,128)}, f32[1032,128]{1,0:T(8,128)S(1)}, u32[]{:S(2)}, u32[]{:S(2)}) collective-permute-start(f32[1032,128]{1,0:T(8,128)} %get-tuple-element.52), channel_id=1, source_target_pairs={{0,4},{1,5},{2,6},{3,7},{4,8},{5,9},{6,10},{7,11},{8,12},{9,13},{1... | collective-permute-start | bytes 1585160 | tf_op jit(solution)/shard_map/ppermute | solution.py:310
  25.7 35.1 %copy-start.23 = (f32[1032,128]{1,0:T(8,128)}, f32[1032,128]{1,0:T(8,128)S(1)}, u32[]{:S(2)}) copy-start(f32[1032,128]{1,0:T(8,128)S(1)} %collective-permute-done.1.refs_6_.refs_16_) | copy-start | bytes 1585156
  25.7 13.2 %collective-permute-start.7 = (f32[1032,128]{1,0:T(8,128)}, f32[1032,128]{1,0:T(8,128)S(1)}, u32[]{:S(2)}, u32[]{:S(2)}) collective-permute-start(f32[1032,128]{1,0:T(8,128)} %get-tuple-element.54), channel_id=1, source_target_pairs={{0,2},{2,0},{1,3},{3,1},{4,6},{6,4},{5,7},{7,5},{8,10},{10,8},{9,1... | collective-permute-start | bytes 1585160 | tf_op jit(solution)/shard_map/ppermute | solution.py:307
  26.5 14.6 %collective-permute-start.5 = (f32[1032,128]{1,0:T(8,128)}, f32[1032,128]{1,0:T(8,128)}, u32[]{:S(2)}, u32[]{:S(2)}) collective-permute-start(f32[1032,128]{1,0:T(8,128)} %get-tuple-element.53), channel_id=1, source_target_pairs={{0,1},{1,0},{2,3},{3,2},{4,5},{5,4},{6,7},{7,6},{8,9},{9,8},{10,11... | collective-permute-start | bytes 1585160 | tf_op jit(solution)/shard_map/ppermute | solution.py:307
  33.4 14.2 %collective-permute-start.9 = (f32[1032,128]{1,0:T(8,128)}, f32[1032,128]{1,0:T(8,128)S(1)}, u32[]{:S(2)}, u32[]{:S(2)}) collective-permute-start(f32[1032,128]{1,0:T(8,128)} %get-tuple-element.60), channel_id=1, source_target_pairs={{0,4},{1,5},{2,6},{3,7},{4,8},{5,9},{6,10},{7,11},{8,12},{9,13},{1... | collective-permute-start | bytes 1585160 | tf_op jit(solution)/shard_map/ppermute | solution.py:310
  39.7 13.3 %collective-permute-start.8 = (f32[1032,128]{1,0:T(8,128)S(1)}, f32[1032,128]{1,0:T(8,128)S(1)}, u32[]{:S(2)}, u32[]{:S(2)}) collective-permute-start(f32[1032,128]{1,0:T(8,128)S(1)} %get-tuple-element.62), channel_id=1, source_target_pairs={{0,2},{2,0},{1,3},{3,1},{4,6},{6,4},{5,7},{7,5},{8,10},{10,8},{9,1... | collective-permute-start | bytes 1585160 | tf_op jit(solution)/shard_map/ppermute | solution.py:307
  41.2 13.4 %collective-permute-start.6 = (f32[1032,128]{1,0:T(8,128)S(1)}, f32[1032,128]{1,0:T(8,128)S(1)}, u32[]{:S(2)}, u32[]{:S(2)}) collective-permute-start(f32[1032,128]{1,0:T(8,128)S(1)} %get-tuple-element.61), channel_id=1, source_target_pairs={{0,1},{1,0},{2,3},{3,2},{4,5},{5,4},{6,7},{7,6},{8,9},{9,8},{10,11... | collective-permute-start | bytes 1585160 | tf_op jit(solution)/shard_map/ppermute | solution.py:307
  47.6 13.2 %collective-permute-start.10 = (f32[1032,128]{1,0:T(8,128)}, f32[1032,128]{1,0:T(8,128)S(1)}, u32[]{:S(2)}, u32[]{:S(2)}) collective-permute-start(f32[1032,128]{1,0:T(8,128)} %get-tuple-element.65), channel_id=1, source_target_pairs={{0,4},{1,5},{2,6},{3,7},{4,8},{5,9},{6,10},{7,11},{8,12},{9,13},{1... | collective-permute-start | bytes 1585160 | tf_op jit(solution)/shard_map/ppermute | solution.py:310
  53.0 12.0 %collective-permute-start.13 = (f32[1032,128]{1,0:T(8,128)S(1)}, f32[1032,128]{1,0:T(8,128)}, u32[]{:S(2)}, u32[]{:S(2)}) collective-permute-start(f32[1032,128]{1,0:T(8,128)S(1)} %get-tuple-element.71), channel_id=1, source_target_pairs={{0,2},{2,0},{1,3},{3,1},{4,6},{6,4},{5,7},{7,5},{8,10},{10,8},{9,1... | collective-permute-start | bytes 1585160 | tf_op jit(solution)/shard_map/ppermute | solution.py:307
  54.6 12.0 %collective-permute-start.11 = (f32[1032,128]{1,0:T(8,128)S(1)}, f32[1032,128]{1,0:T(8,128)S(1)}, u32[]{:S(2)}, u32[]{:S(2)}) collective-permute-start(f32[1032,128]{1,0:T(8,128)S(1)} %get-tuple-element.67), channel_id=1, source_target_pairs={{0,1},{1,0},{2,3},{3,2},{4,5},{5,4},{6,7},{7,6},{8,9},{9,8},{10,11... | collective-permute-start | bytes 1585160 | tf_op jit(solution)/shard_map/ppermute | solution.py:307
  65.1 12.4 %collective-permute-start.16 = (f32[1032,128]{1,0:T(8,128)}, f32[1032,128]{1,0:T(8,128)S(1)}, u32[]{:S(2)}, u32[]{:S(2)}) collective-permute-start(f32[1032,128]{1,0:T(8,128)} %get-tuple-element.76), channel_id=1, source_target_pairs={{0,2},{2,0},{1,3},{3,1},{4,6},{6,4},{5,7},{7,5},{8,10},{10,8},{9,1... | collective-permute-start | bytes 1585160 | tf_op jit(solution)/shard_map/ppermute | solution.py:307
  66.6 10.8 %collective-permute-start.15 = (f32[1032,128]{1,0:T(8,128)}, f32[1032,128]{1,0:T(8,128)S(1)}, u32[]{:S(2)}, u32[]{:S(2)}) collective-permute-start(f32[1032,128]{1,0:T(8,128)} %get-tuple-element.75), channel_id=1, source_target_pairs={{0,1},{1,0},{2,3},{3,2},{4,5},{5,4},{6,7},{7,6},{8,9},{9,8},{10,11... | collective-permute-start | bytes 1585160 | tf_op jit(solution)/shard_map/ppermute | solution.py:307
  68.1 15.3 %collective-permute-start.3 = (f32[512,512]{1,0:T(8,128)}, f32[512,512]{1,0:T(8,128)S(1)}, u32[]{:S(2)}, u32[]{:S(2)}) collective-permute-start(f32[512,512]{1,0:T(8,128)} %get-tuple-element.69.refs_3_), channel_id=1, source_target_pairs={{0,16},{16,0},{1,17},{17,1},{2,18},{18,2},{3,19},{19,3},{4,20},{20... | collective-permute-start | bytes 3145736 | tf_op jit(solution)/shard_map/ppermute | solution.py:314
  76.3 15.7 %collective-permute-start.14 = (f32[512,512]{1,0:T(8,128)}, f32[512,512]{1,0:T(8,128)}, u32[]{:S(2)}, u32[]{:S(2)}) collective-permute-start(f32[512,512]{1,0:T(8,128)} %get-tuple-element.72.refs_5_), channel_id=1, source_target_pairs={{0,16},{16,0},{1,17},{17,1},{2,18},{18,2},{3,19},{19,3},{4,20},{20... | collective-permute-start | bytes 3145736 | tf_op jit(solution)/shard_map/ppermute | solution.py:314
  76.9 15.1 %collective-permute-start.12 = (f32[1032,128]{1,0:T(8,128)}, f32[1032,128]{1,0:T(8,128)S(1)}, u32[]{:S(2)}, u32[]{:S(2)}) collective-permute-start(f32[1032,128]{1,0:T(8,128)} %broadcast_select_fusion.1), channel_id=1, source_target_pairs={{0,1},{1,3},{3,2},{2,0},{4,5},{5,7},{7,6},{6,4},{8,9},{9,11},{11,1... | collective-permute-start | bytes 1585160 | tf_op jit(solution)/shard_map/ppermute | solution.py:307
  82.9 13.2 %collective-permute-start.17 = (f32[512,512]{1,0:T(8,128)}, f32[512,512]{1,0:T(8,128)S(1)}, u32[]{:S(2)}, u32[]{:S(2)}) collective-permute-start(f32[512,512]{1,0:T(8,128)} %get-tuple-element.77.refs_7_), channel_id=1, source_target_pairs={{0,16},{16,0},{1,17},{17,1},{2,18},{18,2},{3,19},{19,3},{4,20},{20... | collective-permute-start | bytes 3145736 | tf_op jit(solution)/shard_map/ppermute | solution.py:314
  83.0 13.1 %collective-permute-start.18 = (f32[512,512]{1,0:T(8,128)}, f32[512,512]{1,0:T(8,128)}, u32[]{:S(2)}, u32[]{:S(2)}) collective-permute-start(f32[512,512]{1,0:T(8,128)} %get-tuple-element.78.refs_9_), channel_id=1, source_target_pairs={{0,16},{16,0},{1,17},{17,1},{2,18},{18,2},{3,19},{19,3},{4,20},{20... | collective-permute-start | bytes 3145736 | tf_op jit(solution)/shard_map/ppermute | solution.py:314
  83.5 27.5 %collective-permute-start.19 = (f32[1032,128]{1,0:T(8,128)}, f32[1032,128]{1,0:T(8,128)S(1)}, u32[]{:S(2)}, u32[]{:S(2)}) collective-permute-start(f32[1032,128]{1,0:T(8,128)} %get-tuple-element.91), channel_id=1, source_target_pairs={{2,0},{3,2},{6,4},{7,6},{10,8},{11,10},{14,12},{15,14},{18,16},{19... | collective-permute-start | bytes 1585160 | tf_op jit(solution)/shard_map/ppermute | solution.py:307
  92.0 23.9 %collective-permute-start.20 = (f32[1032,128]{1,0:T(8,128)}, f32[1032,128]{1,0:T(8,128)}, u32[]{:S(2)}, u32[]{:S(2)}) collective-permute-start(f32[1032,128]{1,0:T(8,128)} %collective-permute-done.13.refs_13_.refs_6_.refs_24_), channel_id=1, source_target_pairs={{0,1},{1,0},{2,3},{3,2},{4,5},{5,4},{6,7},{7,6},{8,9},{9,8},{10,11... | collective-permute-start | bytes 1585160 | tf_op jit(solution)/shard_map/ppermute | solution.py:307
  92.0 23.9 %collective-permute-start.21 = (f32[1032,128]{1,0:T(8,128)}, f32[1032,128]{1,0:T(8,128)}, u32[]{:S(2)}, u32[]{:S(2)}) collective-permute-start(f32[1032,128]{1,0:T(8,128)} %copy-done.2), channel_id=1, source_target_pairs={{0,1},{1,0},{4,5},{5,4},{8,9},{9,8},{12,13},{13,12},{16,17},{17,16... | collective-permute-start | bytes 1585160 | tf_op jit(solution)/shard_map/ppermute | solution.py:307
  120.2 2.7 %collective-permute-start.22 = (f32[512,512]{1,0:T(8,128)S(1)}, f32[512,512]{1,0:T(8,128)S(1)}, u32[]{:S(2)}, u32[]{:S(2)}) collective-permute-start(f32[512,512]{1,0:T(8,128)S(1)} %shard_map.51.refs_3_), channel_id=1, source_target_pairs={{0,16},{16,0},{1,17},{17,1},{2,18},{18,2},{3,19},{19,3},{4,20},{20... | collective-permute-start | bytes 3145736 | tf_op jit(solution)/shard_map/ppermute | solution.py:314
  (31 other events, 258.4 us)

commit v5 on v4

--- a/solution.py
+++ b/solution.py
@@ -14,6 +14,7 @@
 CHUNKS = 4
 VMEM_LIMIT = 60 * 1024 * 1024
 LAST_LIMIT = 24 * 1024 * 1024
+HALVES = 2
 
 
 def split(value):
@@ -94,8 +95,10 @@
 def prepare(own, energies, rows, width):
     size = rows // CHUNKS
     cut = size * width // LANES
-
-    def kernel(energy_ref, own_ref, high_out, low_out, integrals_out, *refs):
+    share = width // HALVES
+
+    def kernel(energy_ref, own_ref, high_out, low_out, *refs):
+        integral_outs, refs = refs[:HALVES], refs[HALVES:]
         sent_refs = refs[: CHUNKS - 1]
         block_ref, turned_ref, integrals_ref, semaphores = refs[CHUNKS - 1 :]
         copies = Copies(semaphores)
@@ -113,20 +116,21 @@
             leaving.append(copies.start(turned_ref.at[1, at], low_out.at[at]))
             value = dot(jnp.concatenate([high, low, high], axis=1), deep_right(block))
             integrals_ref[...] = integrals_ref[...] + value if at else value
-        leaving.append(copies.start(integrals_ref, integrals_out))
+        for at, out_ref in enumerate(integral_outs):
+            leaving.append(copies.start(integrals_ref.at[pl.ds(at * share, share)], out_ref))
         for copy in leaving:
             copy.wait()
 
     turned = jax.ShapeDtypeStruct((CHUNKS, width, size), jnp.bfloat16)
-    square = jax.ShapeDtypeStruct((width, width), jnp.float32)
+    square = jax.ShapeDtypeStruct((share, width), jnp.float32)
     sent = jax.ShapeDtypeStruct((cut + SUBLANES, LANES), jnp.float32)
     scratch = [
         pltpu.VMEM((CHUNKS, cut, LANES), jnp.float32),
         pltpu.VMEM((2, CHUNKS, width, size), jnp.bfloat16),
         pltpu.VMEM((width, width), jnp.float32),
-        pltpu.SemaphoreType.DMA((5 * CHUNKS,)),
+        pltpu.SemaphoreType.DMA((5 * CHUNKS + HALVES,)),
     ]
-    outs = [turned, turned, square] + [sent] * (CHUNKS - 1)
+    outs = [turned, turned] + [square] * HALVES + [sent] * (CHUNKS - 1)
     return call(kernel, [], [energies], [own], outs, pl.ANY, scratch)
 
 
@@ -141,14 +145,15 @@
     arrays = arrays_of(pieces)
     numbers = [list(range(start, start + len(slot))) for slot, start in zip(slots, first)]
     needed = sorted({number for some in numbers for number in some})
-    before = list(before)
+    before = [part for parts in before for part in parts]
+    share = width // HALVES
 
     def kernel(flag_ref, *refs):
         given = iter(refs)
         high_ref, low_ref = next(given), next(given)
         before_refs = [next(given) for _ in before]
         ref_of = {id(array): next(given) for array in arrays}
-        outs = [next(given) for _ in range(count)]
+        outs = [[next(given) for _ in range(HALVES)] for _ in range(count)]
         turned_ref, block_ref, before_ref, semaphores = given
         copies = Copies(semaphores)
         coming, turning = [], {}
@@ -167,9 +172,13 @@
                 turn(number)
                 coming.append(copies.start_piece(piece, ref_of, flag_ref, cut, block_ref.at[at]))
                 at += 1
-        adding = [copies.start(ref, before_ref.at[slot]) for slot, ref in enumerate(before_refs)]
+        adding = [
+            copies.start(ref, before_ref.at[at // HALVES, pl.ds(at % HALVES * share, share)])
+            for at, ref in enumerate(before_refs)
+        ]
         at = 0
         for slot in range(count):
+            total = None
             for place, number in enumerate(numbers[slot]):
                 for copy in turning.pop(number, []):
                     copy.wait()
@@ -178,31 +187,36 @@
                 high, low = turned_ref[there, 0], turned_ref[there, 1]
                 left = jnp.concatenate([high, low, high], axis=1)
                 value = dot(left, deep_right(rows_of(block_ref.at[at], 0, size, width)))
-                outs[slot][...] = outs[slot][...] + value if place else value
+                total = total + value if place else value
                 at += 1
             if before:
-                adding[slot].wait()
-                outs[slot][...] += before_ref[slot]
-
-    out = [jax.ShapeDtypeStruct((width, width), jnp.float32)] * count
+                for number in range(HALVES):
+                    adding[slot * HALVES + number].wait()
+                total = total + before_ref[slot]
+            for number, out_ref in enumerate(outs[slot]):
+                out_ref[...] = total[number * share : (number + 1) * share]
+
+    out = [jax.ShapeDtypeStruct((share, width), jnp.float32)] * (HALVES * count)
     scratch = [
         pltpu.VMEM((len(needed), 2, width, size), jnp.bfloat16),
         pltpu.VMEM((len(pieces), cut, LANES), jnp.float32),
-        pltpu.VMEM((max(len(before), 1), width, width), jnp.float32),
+        pltpu.VMEM((max(len(before) // HALVES, 1), width, width), jnp.float32),
         pltpu.SemaphoreType.DMA((2 * len(needed) + len(pieces) + len(before),)),
     ]
-    return call(kernel, [flags], [], [*turned, *before, *arrays], out, pltpu.VMEM, scratch, limit)
+    made = call(kernel, [flags], [], [*turned, *before, *arrays], out, pltpu.VMEM, scratch, limit)
+    return [made[slot * HALVES : (slot + 1) * HALVES] for slot in range(count)]
 
 
 def contract(partials, slots, signs, first_sign, energies, flags, eps_virt, size, before=None, limit=VMEM_LIMIT):
     count = len(slots)
     chunks = len(slots[0])
     virt = eps_virt.shape[1]
-    width = partials[0][0].shape[0]
+    width = partials[0][0][0].shape[1]
+    share = width // HALVES
     occ_rows = width // virt
     lines = width // LANES
     cut = size * lines
-    sums = [array for slot in partials for array in slot]
+    sums = [part for slot in partials for term in slot for part in term]
     pieces = [piece for slot in slots for piece in slot]
     arrays = arrays_of([*pieces, *energies])
     last = [before] if before is not None else []
@@ -219,7 +233,10 @@
             copies.start_piece(piece, ref_of, flag_ref, SUBLANES, energy_ref.at[at])
             for at, piece in enumerate(energies)
         ]
-        arriving += [copies.start(ref, sum_ref.at[at]) for at, ref in enumerate(sum_refs)]
+        arriving += [
+            copies.start(ref, sum_ref.at[at // HALVES, pl.ds(at % HALVES * share, share)])
+            for at, ref in enumerate(sum_refs)
+        ]
         coming = [
             [
                 copies.start_piece(slots[slot][at], ref_of, flag_ref, cut, block_ref.at[slot, at])
@@ -268,7 +285,7 @@
     out = jax.ShapeDtypeStruct((rows * lines, LANES), jnp.float32)
     scratch = [
         pltpu.VMEM((len(energies), SUBLANES, LANES), jnp.float32),
-        pltpu.VMEM((len(sums), width, width), jnp.float32),
+        pltpu.VMEM((len(sums) // HALVES, width, width), jnp.float32),
         pltpu.VMEM((count, chunks, cut, LANES), jnp.float32),
         pltpu.VMEM((chunks, cut, LANES), jnp.float32),
         pltpu.VMEM((width, count * 3 * width), jnp.bfloat16),
@@ -309,10 +326,10 @@
     def up(block):
         return lax.ppermute(block, "occ", [(g, g + PLANE) for g in range(groups - PLANE)])
 
-    def totals(partial):
+    def totals(parts):
         if shares == 2:
-            return [partial, lax.ppermute(partial, "aux", [(0, 1), (1, 0)])]
-        return [lax.psum(partial, "aux")]
+            return [parts, [lax.ppermute(part, "aux", [(0, 1), (1, 0)]) for part in parts]]
+        return [[lax.psum(part, "aux") for part in parts]]
 
     first_sent = jnp.concatenate([part(own, 0), energies])
     def choices(sent):
@@ -343,12 +360,13 @@
     from_z = [up(first_sent)]
     up_x = within(first_sent, [(0, 1), (2, 3), (1, 0)])
     up_y = within(first_sent, [(0, 2), (1, 3)])
-    high, low, partial_own, *own_sent = prepare(own, energies, rows, width)
-    from_own += own_sent
+    high, low, *made = prepare(own, energies, rows, width)
+    partial_own = made[:HALVES]
+    from_own += made[HALVES:]
     turned = (high, low)
     sums_own = totals(partial_own)
     swap_x, swap_y = [], []
-    passed = [partial_own]
+    passed = [partial_own[0]]
     for at in range(CHUNKS):
         came = after(from_z[at], *passed)
         if at < last:

time: 129 us -> 127 us (0.984)
  waiting for transfers between devices: 23 us -> 20.7 us
  starting transfers between devices: 42.7 us -> 44.5 us
    ppermute x14, waiting for transfers between devices: 10.9 us -> 5.95 us  [within(): lax.ppermute(block, 'occ', [(g + a, g + b) for g in planes for a, b in mo...]
    ppermute x5 -> x10, waiting for transfers between devices: 2.66 us -> 4.65 us  [totals(): lax.ppermute(part, 'aux', [(0, 1), (1, 0)])]
    unnamed x64 -> x74, local copies, waits for them, and re-layouts: 4.95 us -> 4.05 us
  transfers between devices with their start and end apart: 23 -> 28, of which waited for: 7 -> 11; matrix products, arithmetic and copies ran while one was open for 7% -> 6% of each run, Pallas kernels for 28% -> 29%
where the time goes in v5:
time: 127 us; the launch traced here: 126 us
  starting transfers between devices  44.5 us (35%)
  Pallas kernels  44.5 us (35%)
  waiting for transfers between devices  20.7 us (16%)
  other arithmetic  6.76 us (5%)
  local copies, waits for them, and re-layouts  6.05 us (5%)
  between operations  3.92 us (3%)
    pallas_call x7, Pallas kernels, call(): pl.pallas_call(kernel, out_shape=outputs, in_specs=[pl.BlockSpec(memory_s...  44.5 us
    ppermute x14, starting transfers between devices, within(): lax.ppermute(block, 'occ', [(g + a, g + b) for g in planes for a, b in mo...  25.1 us
    ppermute x4, starting transfers between devices, up(): lax.ppermute(block, 'occ', [(g, g + PLANE) for g in range(groups - PLANE)])  17.3 us
    ppermute x4, waiting for transfers between devices, up(): lax.ppermute(block, 'occ', [(g, g + PLANE) for g in range(groups - PLANE)])  10.1 us
    ppermute x14, waiting for transfers between devices, within(): lax.ppermute(block, 'occ', [(g + a, g + b) for g in planes for a, b in mo...  5.95 us
    ppermute x10, waiting for transfers between devices, totals(): lax.ppermute(part, 'aux', [(0, 1), (1, 0)])  4.65 us
    unnamed x74, local copies, waits for them, and re-layouts  4.05 us
    select_n x3, other arithmetic, on_device(): jnp.where(odd_y, came, up_part)  3.4 us
  transfers between devices with their start and end apart: 28, of which 11 were waited for; matrix products, arithmetic and copies ran while one was open for 6% of the time, Pallas kernels for 29%

profile of v5, /device:TPU:0, one launch (start us, length us, event | category | flops | bytes accessed | tf_op | source)
XLA Modules:
  0.0 126.5 jit_solution(13304796675708726252)
XLA Ops:
  2.1 5.0 %collective-permute-start = (f32[1032,128]{1,0:T(8,128)S(1)}, f32[1032,128]{1,0:T(8,128)S(1)}, u32[]{:S(2)}, u32[]{:S(2)}) collective-permute-start(f32[1032,128]{1,0:T(8,128)S(1)} %pad_maximum_fusion.refs_34_.refs_14_), channel_id=1, source_target_pairs={{0,4},{1,5},{2,6},{3,7},{4,8},{5,9},{6,10},{7,11},{8,12},{9,13},{1... | collective-permute-start | bytes 1585160 | tf_op jit(solution)/shard_map/ppermute | solution.py:327
  7.1 3.5 %collective-permute-start.2 = (f32[1032,128]{1,0:T(8,128)S(1)}, f32[1032,128]{1,0:T(8,128)S(1)}, u32[]{:S(2)}, u32[]{:S(2)}) collective-permute-start(f32[1032,128]{1,0:T(8,128)S(1)} %pad_maximum_fusion.refs_34_.refs_14_), channel_id=1, source_target_pairs={{0,2},{1,3},{4,6},{5,7},{8,10},{9,11},{12,14},{13,15},{16,18},{17,... | collective-permute-start | bytes 1585160 | tf_op jit(solution)/shard_map/ppermute | solution.py:324
  10.6 3.4 %collective-permute-start.1 = (f32[1032,128]{1,0:T(8,128)S(1)}, f32[1032,128]{1,0:T(8,128)S(1)}, u32[]{:S(2)}, u32[]{:S(2)}) collective-permute-start(f32[1032,128]{1,0:T(8,128)S(1)} %pad_maximum_fusion.refs_34_.refs_14_), channel_id=1, source_target_pairs={{0,1},{2,3},{1,0},{4,5},{6,7},{5,4},{8,9},{10,11},{9,8},{12,13},{1... | collective-permute-start | bytes 1585160 | tf_op jit(solution)/shard_map/ppermute | solution.py:324
  14.0 5.1 %shard_map.46 = (bf16[4,512,256]{2,1,0:T(8,128)(2,1)}, bf16[4,512,256]{2,1,0:T(8,128)(2,1)}, f32[256,512]{1,0:T(8,128)}, f32[256,512]{1,0:T(8,128)}, f32[1032,12...) custom-call(f32[8,128]{1,0:T(8,128)} %copy-done.35, f32[4096,128]{1,0:T(8,128)} %bitcast.17), custom_call_target="tpu_custom_call" | custom-call | tf_op jit(solution)/shard_map/pallas_call | solution.py:84
  19.2 3.7 %collective-permute-start.5 = (f32[1032,128]{1,0:T(8,128)}, f32[1032,128]{1,0:T(8,128)S(1)}, u32[]{:S(2)}, u32[]{:S(2)}) collective-permute-start(f32[1032,128]{1,0:T(8,128)} %get-tuple-element.64), channel_id=1, source_target_pairs={{0,4},{1,5},{2,6},{3,7},{4,8},{5,9},{6,10},{7,11},{8,12},{9,13},{1... | collective-permute-start | bytes 1585160 | tf_op jit(solution)/shard_map/ppermute | solution.py:327
  22.9 2.2 %broadcast_select_fusion.5 = (f32[1032,128]{1,0:T(8,128)}, f32[1032,128]{1,0:T(8,128)}) fusion(f32[1032,128]{1,0:T(8,128)S(1)} %collective-permute-done.refs_2_.refs_20_, f32[1032,128]{1,0:T(8,128)} %get-tuple-element.64, pred[]{:T(512)S(6)} %eq.44, pred[]{:T(512)S(6)} %eq.43), kind=kLoop, calls=%fused_computation.6 | loop fusion | flops 264192 | bytes 2113538 | tf_op jit(solution)/shard_map/jit(_where)/select_n | solution.py:375
  33.5 4.3 %collective-permute-start.10 = (f32[1032,128]{1,0:T(8,128)}, f32[1032,128]{1,0:T(8,128)S(1)}, u32[]{:S(2)}, u32[]{:S(2)}) collective-permute-start(f32[1032,128]{1,0:T(8,128)} %get-tuple-element.73), channel_id=1, source_target_pairs={{0,4},{1,5},{2,6},{3,7},{4,8},{5,9},{6,10},{7,11},{8,12},{9,13},{1... | collective-permute-start | bytes 1585160 | tf_op jit(solution)/shard_map/ppermute | solution.py:327
  39.0 1.6 %collective-permute-start.9 = (f32[1032,128]{1,0:T(8,128)S(1)}, f32[1032,128]{1,0:T(8,128)S(1)}, u32[]{:S(2)}, u32[]{:S(2)}) collective-permute-start(f32[1032,128]{1,0:T(8,128)S(1)} %get-tuple-element.75), channel_id=1, source_target_pairs={{0,2},{2,0},{1,3},{3,1},{4,6},{6,4},{5,7},{7,5},{8,10},{10,8},{9,1... | collective-permute-start | bytes 1585160 | tf_op jit(solution)/shard_map/ppermute | solution.py:324
  42.1 5.5 %collective-permute-done.10.refs_4_.refs_22_ = f32[1032,128]{1,0:T(8,128)S(1)} collective-permute-done((f32[1032,128]{1,0:T(8,128)}, f32[1032,128]{1,0:T(8,128)S(1)}, u32[]{:S(2)}, u32[]{:S(2)}) %collective-permute-start.10) | collective-permute-done | bytes 528416 | tf_op jit(solution)/shard_map/ppermute | solution.py:327
  47.6 4.3 %collective-permute-start.11 = (f32[1032,128]{1,0:T(8,128)S(1)}, f32[1032,128]{1,0:T(8,128)S(1)}, u32[]{:S(2)}, u32[]{:S(2)}) collective-permute-start(f32[1032,128]{1,0:T(8,128)S(1)} %copy-done.29), channel_id=1, source_target_pairs={{0,4},{1,5},{2,6},{3,7},{4,8},{5,9},{6,10},{7,11},{8,12},{9,13},{1... | collective-permute-start | bytes 1585160 | tf_op jit(solution)/shard_map/ppermute | solution.py:327
  52.0 1.6 %collective-permute-start.14 = (f32[1032,128]{1,0:T(8,128)S(1)}, f32[1032,128]{1,0:T(8,128)}, u32[]{:S(2)}, u32[]{:S(2)}) collective-permute-start(f32[1032,128]{1,0:T(8,128)S(1)} %get-tuple-element.86), channel_id=1, source_target_pairs={{0,2},{2,0},{1,3},{3,1},{4,6},{6,4},{5,7},{7,5},{8,10},{10,8},{9,1... | collective-permute-start | bytes 1585160 | tf_op jit(solution)/shard_map/ppermute | solution.py:324
  53.6 1.6 %collective-permute-start.12 = (f32[1032,128]{1,0:T(8,128)S(1)}, f32[1032,128]{1,0:T(8,128)S(1)}, u32[]{:S(2)}, u32[]{:S(2)}) collective-permute-start(f32[1032,128]{1,0:T(8,128)S(1)} %get-tuple-element.80), channel_id=1, source_target_pairs={{0,1},{1,0},{2,3},{3,2},{4,5},{5,4},{6,7},{7,6},{8,9},{9,8},{10,11... | collective-permute-start | bytes 1585160 | tf_op jit(solution)/shard_map/ppermute | solution.py:324
  56.1 4.3 %collective-permute-done.11.refs_5_.refs_23_ = f32[1032,128]{1,0:T(8,128)S(1)} collective-permute-done((f32[1032,128]{1,0:T(8,128)S(1)}, f32[1032,128]{1,0:T(8,128)S(1)}, u32[]{:S(2)}, u32[]{:S(2)}) %collective-permute-start.11) | collective-permute-done | bytes 528416 | tf_op jit(solution)/shard_map/ppermute | solution.py:327
  61.6 2.5 %collective-permute-done.14.refs_13_.refs_8_.refs_32_ = f32[1032,128]{1,0:T(8,128)} collective-permute-done((f32[1032,128]{1,0:T(8,128)S(1)}, f32[1032,128]{1,0:T(8,128)}, u32[]{:S(2)}, u32[]{:S(2)}) %collective-permute-start.14) | collective-permute-done | bytes 528416 | tf_op jit(solution)/shard_map/ppermute | solution.py:324
  68.1 8.5 %shard_map.47 = (f32[256,512]{1,0:T(8,128)}, f32[256,512]{1,0:T(8,128)}, f32[256,512]{1,0:T(8,128)}, f32[256,512]{1,0:T(8,128)}, f32[256,512]{1,0:T(8,128)}, /*index=5*/f32[256,512]{1,0:T(8,128)}) custom-call(s32[4]{0:T(128)} %pad_add_fusion.flag_ref.refs_1_, bf16[4,512,256]{2,1,0:T(8,128)(2,1)} %get-tuple-element.99.refs_0_, ...), custom_call_target="tpu_custom_call" | custom-call | tf_op jit(solution)/shard_map/pallas_call | solution.py:84
  77.9 1.7 %collective-permute-done.17.refs_7_.refs_28_.refs_4_.refs_10_ = f32[1032,128]{1,0:T(8,128)S(1)} collective-permute-done((f32[1032,128]{1,0:T(8,128)S(1)}, f32[1032,128]{1,0:T(8,128)S(1)}, u32[]{:S(2)}, u32[]{:S(2)}) %collective-permute-start.17) | collective-permute-done | bytes 528416 | tf_op jit(solution)/shard_map/ppermute | solution.py:324
  80.3 4.6 %shard_map.48 = (f32[256,512]{1,0:T(8,128)}, f32[256,512]{1,0:T(8,128)}, f32[256,512]{1,0:T(8,128)}, f32[256,512]{1,0:T(8,128)}) custom-call(s32[4]{0:T(128)} %pad_add_fusion.flag_ref.refs_1_, bf16[4,512,256]{2,1,0:T(8,128)(2,1)} %get-tuple-element.99.refs_0_, bf16[4,512,256]{2,1,0:T(8,128)(2,1)} %get-tuple-element.100.refs_1_, ...), custom_call_target="tpu_custom_call" | custom-call | tf_op jit(solution)/shard_map/pallas_call | solution.py:84
  86.8 1.9 %collective-permute-start.24 = (f32[1032,128]{1,0:T(8,128)}, f32[1032,128]{1,0:T(8,128)}, u32[]{:S(2)}, u32[]{:S(2)}) collective-permute-start(f32[1032,128]{1,0:T(8,128)} %collective-permute-done.14.refs_13_.refs_8_.refs_32_), channel_id=1, source_target_pairs={{0,1},{1,0},{2,3},{3,2},{4,5},{5,4},{6,7},{7,6},{8,9},{9,8},{10,11... | collective-permute-start | bytes 1585160 | tf_op jit(solution)/shard_map/ppermute | solution.py:324
  88.8 2.2 %collective-permute-start.25 = (f32[1032,128]{1,0:T(8,128)}, f32[1032,128]{1,0:T(8,128)}, u32[]{:S(2)}, u32[]{:S(2)}) collective-permute-start(f32[1032,128]{1,0:T(8,128)} %copy-done.2), channel_id=1, source_target_pairs={{0,1},{1,0},{4,5},{5,4},{8,9},{9,8},{12,13},{13,12},{16,17},{17,16... | collective-permute-start | bytes 1585160 | tf_op jit(solution)/shard_map/ppermute | solution.py:324
  91.6 1.7 %collective-permute-done.21.refs_17_ = f32[256,512]{1,0:T(8,128)} collective-permute-done((f32[256,512]{1,0:T(8,128)}, f32[256,512]{1,0:T(8,128)}, u32[]{:S(2)}, u32[]{:S(2)}) %collective-permute-start.21) | collective-permute-done | bytes 524320 | tf_op jit(solution)/shard_map/ppermute | solution.py:331
  94.2 13.9 %shard_map.49.refs_7_ = f32[4096,128]{1,0:T(8,128)} custom-call(f32[5]{0:T(128)} %stack.34.refs_0_, s32[4]{0:T(128)} %pad_add_fusion.flag_ref.refs_1_, f32[1,512]{1,0:T(1,128)} %bitcast.15, f32[256,512]{1,0:T(8,128)} %get-tuple-element.82.refs_3_, f32[256,512]{1,0:T(8,128)} %get-tuple-element.83.refs_4_, f32[256,512]{1,0:T(8,128)} %copy-done.30, ...), custom_call_target="tpu_custom_call" | custom-call | tf_op jit(solution)/shard_map/pallas_call | solution.py:84
  109.0 4.2 %shard_map.50 = (f32[256,512]{1,0:T(8,128)}, f32[256,512]{1,0:T(8,128)}) custom-call(s32[4]{0:T(128)} %pad_add_fusion.flag_ref.refs_1_, bf16[4,512,256]{2,1,0:T(8,128)(2,1)} %get-tuple-element.99.refs_0_, bf16[4,512,256]{2,1,0:T(8,128)(2,1)} %get-tuple-element.100.refs_1_, f32[1032,128]{1,0:T(8,128)} %copy-done.2, f32[1032,128]{1,0:T(8,128)} %copy-done.11, ...), custom_call_target="tpu_custom_call" | custom-call | tf_op jit(solution)/shard_map/pallas_call | solution.py:84
  115.4 3.2 %shard_map.51 = (f32[256,512]{1,0:T(8,128)S(1)}, f32[256,512]{1,0:T(8,128)S(1)}) custom-call(s32[4]{0:T(128)S(1)} %copy-done.15, bf16[4,512,256]{2,1,0:T(8,128)(2,1)S(1)} %copy-done, bf16[4,512,256]{2,1,0:T(8,128)(2,1)S(1)} %copy-done.1, f32[256,512]{1,0:T(8,128)S(1)} %copy-done.13, f32[256,512]{1,0:T(8,128)S(1)} %copy-done.14, f32[1032,128]{1,0:T(8,128)S(1)} %copy-done.8, ...), custom_call_target="tpu_custom_call" | custom-call | tf_op jit(solution)/shard_map/pallas_call | solution.py:84
  121.4 4.9 %shard_map.52 = f32[4096,128]{1,0:T(8,128)} custom-call(f32[5]{0:T(128)S(1)} %copy-done.17, s32[4]{0:T(128)S(1)} %copy-done.15, f32[1,512]{1,0:T(1,128)S(1)} %bitcast.16, f32[256,512]{1,0:T(8,128)S(1)} %get-tuple-element.103.refs_3_, f32[256,512]{1,0:T(8,128)S(1)} %get-tuple-element.104.refs_4_, f32[256,512]{1,0:T(8,128)S(1)} %collective-permute-done.26.refs_5_, ...), custom_call_target="tpu_custom_call" | custom-call | tf_op jit(solution)/shard_map/pallas_call | solution.py:84
  (124 shorter events, 27.2 us)
Async XLA Ops:
  2.1 17.0 %collective-permute-start = (f32[1032,128]{1,0:T(8,128)S(1)}, f32[1032,128]{1,0:T(8,128)S(1)}, u32[]{:S(2)}, u32[]{:S(2)}) collective-permute-start(f32[1032,128]{1,0:T(8,128)S(1)} %pad_maximum_fusion.refs_34_.refs_14_), channel_id=1, source_target_pairs={{0,4},{1,5},{2,6},{3,7},{4,8},{5,9},{6,10},{7,11},{8,12},{9,13},{1... | collective-permute-start | bytes 1585160 | tf_op jit(solution)/shard_map/ppermute | solution.py:327
  7.1 18.0 %collective-permute-start.2 = (f32[1032,128]{1,0:T(8,128)S(1)}, f32[1032,128]{1,0:T(8,128)S(1)}, u32[]{:S(2)}, u32[]{:S(2)}) collective-permute-start(f32[1032,128]{1,0:T(8,128)S(1)} %pad_maximum_fusion.refs_34_.refs_14_), channel_id=1, source_target_pairs={{0,2},{1,3},{4,6},{5,7},{8,10},{9,11},{12,14},{13,15},{16,18},{17,... | collective-permute-start | bytes 1585160 | tf_op jit(solution)/shard_map/ppermute | solution.py:324
  10.6 15.1 %collective-permute-start.1 = (f32[1032,128]{1,0:T(8,128)S(1)}, f32[1032,128]{1,0:T(8,128)S(1)}, u32[]{:S(2)}, u32[]{:S(2)}) collective-permute-start(f32[1032,128]{1,0:T(8,128)S(1)} %pad_maximum_fusion.refs_34_.refs_14_), channel_id=1, source_target_pairs={{0,1},{2,3},{1,0},{4,5},{6,7},{5,4},{8,9},{10,11},{9,8},{12,13},{1... | collective-permute-start | bytes 1585160 | tf_op jit(solution)/shard_map/ppermute | solution.py:324
  19.2 14.4 %collective-permute-start.5 = (f32[1032,128]{1,0:T(8,128)}, f32[1032,128]{1,0:T(8,128)S(1)}, u32[]{:S(2)}, u32[]{:S(2)}) collective-permute-start(f32[1032,128]{1,0:T(8,128)} %get-tuple-element.64), channel_id=1, source_target_pairs={{0,4},{1,5},{2,6},{3,7},{4,8},{5,9},{6,10},{7,11},{8,12},{9,13},{1... | collective-permute-start | bytes 1585160 | tf_op jit(solution)/shard_map/ppermute | solution.py:327
  25.9 13.1 %collective-permute-start.8 = (f32[1032,128]{1,0:T(8,128)}, f32[1032,128]{1,0:T(8,128)S(1)}, u32[]{:S(2)}, u32[]{:S(2)}) collective-permute-start(f32[1032,128]{1,0:T(8,128)} %get-tuple-element.66), channel_id=1, source_target_pairs={{0,2},{2,0},{1,3},{3,1},{4,6},{6,4},{5,7},{7,5},{8,10},{10,8},{9,1... | collective-permute-start | bytes 1585160 | tf_op jit(solution)/shard_map/ppermute | solution.py:324
  27.4 13.2 %collective-permute-start.6 = (f32[1032,128]{1,0:T(8,128)}, f32[1032,128]{1,0:T(8,128)S(1)}, u32[]{:S(2)}, u32[]{:S(2)}) collective-permute-start(f32[1032,128]{1,0:T(8,128)} %get-tuple-element.65), channel_id=1, source_target_pairs={{0,1},{1,0},{2,3},{3,2},{4,5},{5,4},{6,7},{7,6},{8,9},{9,8},{10,11... | collective-permute-start | bytes 1585160 | tf_op jit(solution)/shard_map/ppermute | solution.py:324
  33.5 14.1 %collective-permute-start.10 = (f32[1032,128]{1,0:T(8,128)}, f32[1032,128]{1,0:T(8,128)S(1)}, u32[]{:S(2)}, u32[]{:S(2)}) collective-permute-start(f32[1032,128]{1,0:T(8,128)} %get-tuple-element.73), channel_id=1, source_target_pairs={{0,4},{1,5},{2,6},{3,7},{4,8},{5,9},{6,10},{7,11},{8,12},{9,13},{1... | collective-permute-start | bytes 1585160 | tf_op jit(solution)/shard_map/ppermute | solution.py:327
  39.0 13.0 %collective-permute-start.9 = (f32[1032,128]{1,0:T(8,128)S(1)}, f32[1032,128]{1,0:T(8,128)S(1)}, u32[]{:S(2)}, u32[]{:S(2)}) collective-permute-start(f32[1032,128]{1,0:T(8,128)S(1)} %get-tuple-element.75), channel_id=1, source_target_pairs={{0,2},{2,0},{1,3},{3,1},{4,6},{6,4},{5,7},{7,5},{8,10},{10,8},{9,1... | collective-permute-start | bytes 1585160 | tf_op jit(solution)/shard_map/ppermute | solution.py:324
  40.6 13.0 %collective-permute-start.7 = (f32[1032,128]{1,0:T(8,128)S(1)}, f32[1032,128]{1,0:T(8,128)S(1)}, u32[]{:S(2)}, u32[]{:S(2)}) collective-permute-start(f32[1032,128]{1,0:T(8,128)S(1)} %get-tuple-element.74), channel_id=1, source_target_pairs={{0,1},{1,0},{2,3},{3,2},{4,5},{5,4},{6,7},{7,6},{8,9},{9,8},{10,11... | collective-permute-start | bytes 1585160 | tf_op jit(solution)/shard_map/ppermute | solution.py:324
  47.6 12.8 %collective-permute-start.11 = (f32[1032,128]{1,0:T(8,128)S(1)}, f32[1032,128]{1,0:T(8,128)S(1)}, u32[]{:S(2)}, u32[]{:S(2)}) collective-permute-start(f32[1032,128]{1,0:T(8,128)S(1)} %copy-done.29), channel_id=1, source_target_pairs={{0,4},{1,5},{2,6},{3,7},{4,8},{5,9},{6,10},{7,11},{8,12},{9,13},{1... | collective-permute-start | bytes 1585160 | tf_op jit(solution)/shard_map/ppermute | solution.py:327
  52.0 12.0 %collective-permute-start.14 = (f32[1032,128]{1,0:T(8,128)S(1)}, f32[1032,128]{1,0:T(8,128)}, u32[]{:S(2)}, u32[]{:S(2)}) collective-permute-start(f32[1032,128]{1,0:T(8,128)S(1)} %get-tuple-element.86), channel_id=1, source_target_pairs={{0,2},{2,0},{1,3},{3,1},{4,6},{6,4},{5,7},{7,5},{8,10},{10,8},{9,1... | collective-permute-start | bytes 1585160 | tf_op jit(solution)/shard_map/ppermute | solution.py:324
  53.6 12.0 %collective-permute-start.12 = (f32[1032,128]{1,0:T(8,128)S(1)}, f32[1032,128]{1,0:T(8,128)S(1)}, u32[]{:S(2)}, u32[]{:S(2)}) collective-permute-start(f32[1032,128]{1,0:T(8,128)S(1)} %get-tuple-element.80), channel_id=1, source_target_pairs={{0,1},{1,0},{2,3},{3,2},{4,5},{5,4},{6,7},{7,6},{8,9},{9,8},{10,11... | collective-permute-start | bytes 1585160 | tf_op jit(solution)/shard_map/ppermute | solution.py:324
  64.0 13.8 %collective-permute-start.18 = (f32[1032,128]{1,0:T(8,128)}, f32[1032,128]{1,0:T(8,128)S(1)}, u32[]{:S(2)}, u32[]{:S(2)}) collective-permute-start(f32[1032,128]{1,0:T(8,128)} %get-tuple-element.94), channel_id=1, source_target_pairs={{0,2},{2,0},{1,3},{3,1},{4,6},{6,4},{5,7},{7,5},{8,10},{10,8},{9,1... | collective-permute-start | bytes 1585160 | tf_op jit(solution)/shard_map/ppermute | solution.py:324
  65.6 14.0 %collective-permute-start.17 = (f32[1032,128]{1,0:T(8,128)S(1)}, f32[1032,128]{1,0:T(8,128)S(1)}, u32[]{:S(2)}, u32[]{:S(2)}) collective-permute-start(f32[1032,128]{1,0:T(8,128)S(1)} %get-tuple-element.93), channel_id=1, source_target_pairs={{0,1},{1,0},{2,3},{3,2},{4,5},{5,4},{6,7},{7,6},{8,9},{9,8},{10,11... | collective-permute-start | bytes 1585160 | tf_op jit(solution)/shard_map/ppermute | solution.py:324
  67.1 17.9 %collective-permute-start.3 = (f32[256,512]{1,0:T(8,128)}, f32[256,512]{1,0:T(8,128)S(1)}, u32[]{:S(2)}, u32[]{:S(2)}) collective-permute-start(f32[256,512]{1,0:T(8,128)} %get-tuple-element.82.refs_3_), channel_id=1, source_target_pairs={{0,16},{16,0},{1,17},{17,1},{2,18},{18,2},{3,19},{19,3},{4,20},{20... | collective-permute-start | bytes 1572872 | tf_op jit(solution)/shard_map/ppermute | solution.py:331
  67.1 18.0 %collective-permute-start.4 = (f32[256,512]{1,0:T(8,128)}, f32[256,512]{1,0:T(8,128)S(1)}, u32[]{:S(2)}, u32[]{:S(2)}) collective-permute-start(f32[256,512]{1,0:T(8,128)} %get-tuple-element.83.refs_4_), channel_id=1, source_target_pairs={{0,16},{16,0},{1,17},{17,1},{2,18},{18,2},{3,19},{19,3},{4,20},{20... | collective-permute-start | bytes 1572872 | tf_op jit(solution)/shard_map/ppermute | solution.py:331
  67.6 21.2 %collective-permute-start.13 = (f32[1032,128]{1,0:T(8,128)}, f32[1032,128]{1,0:T(8,128)S(1)}, u32[]{:S(2)}, u32[]{:S(2)}) collective-permute-start(f32[1032,128]{1,0:T(8,128)} %broadcast_select_fusion.1), channel_id=1, source_target_pairs={{0,1},{1,3},{3,2},{2,0},{4,5},{5,7},{7,6},{6,4},{8,9},{9,11},{11,1... | collective-permute-start | bytes 1585160 | tf_op jit(solution)/shard_map/ppermute | solution.py:324
  77.9 7.7 %collective-permute-start.15 = (f32[256,512]{1,0:T(8,128)}, f32[256,512]{1,0:T(8,128)S(1)}, u32[]{:S(2)}, u32[]{:S(2)}) collective-permute-start(f32[256,512]{1,0:T(8,128)} %get-tuple-element.87.refs_7_), channel_id=1, source_target_pairs={{0,16},{16,0},{1,17},{17,1},{2,18},{18,2},{3,19},{19,3},{4,20},{20... | collective-permute-start | bytes 1572872 | tf_op jit(solution)/shard_map/ppermute | solution.py:331
  79.5 7.3 %collective-permute-start.16 = (f32[256,512]{1,0:T(8,128)}, f32[256,512]{1,0:T(8,128)S(1)}, u32[]{:S(2)}, u32[]{:S(2)}) collective-permute-start(f32[256,512]{1,0:T(8,128)} %get-tuple-element.88.refs_8_), channel_id=1, source_target_pairs={{0,16},{16,0},{1,17},{17,1},{2,18},{18,2},{3,19},{19,3},{4,20},{20... | collective-permute-start | bytes 1572872 | tf_op jit(solution)/shard_map/ppermute | solution.py:331
  85.0 6.1 %collective-permute-start.19 = (f32[256,512]{1,0:T(8,128)}, f32[256,512]{1,0:T(8,128)S(1)}, u32[]{:S(2)}, u32[]{:S(2)}) collective-permute-start(f32[256,512]{1,0:T(8,128)} %get-tuple-element.95.refs_11_), channel_id=1, source_target_pairs={{0,16},{16,0},{1,17},{17,1},{2,18},{18,2},{3,19},{19,3},{4,20},{20... | collective-permute-start | bytes 1572872 | tf_op jit(solution)/shard_map/ppermute | solution.py:331
  85.0 6.1 %collective-permute-start.20 = (f32[256,512]{1,0:T(8,128)}, f32[256,512]{1,0:T(8,128)}, u32[]{:S(2)}, u32[]{:S(2)}) collective-permute-start(f32[256,512]{1,0:T(8,128)} %get-tuple-element.96.refs_12_), channel_id=1, source_target_pairs={{0,16},{16,0},{1,17},{17,1},{2,18},{18,2},{3,19},{19,3},{4,20},{20... | collective-permute-start | bytes 1572872 | tf_op jit(solution)/shard_map/ppermute | solution.py:331
  85.5 22.6 %collective-permute-start.23 = (f32[1032,128]{1,0:T(8,128)}, f32[1032,128]{1,0:T(8,128)S(1)}, u32[]{:S(2)}, u32[]{:S(2)}) collective-permute-start(f32[1032,128]{1,0:T(8,128)} %get-tuple-element.115), channel_id=1, source_target_pairs={{2,0},{3,2},{6,4},{7,6},{10,8},{11,10},{14,12},{15,14},{18,16},{19... | collective-permute-start | bytes 1585160 | tf_op jit(solution)/shard_map/ppermute | solution.py:324
  86.8 26.4 %collective-permute-start.24 = (f32[1032,128]{1,0:T(8,128)}, f32[1032,128]{1,0:T(8,128)}, u32[]{:S(2)}, u32[]{:S(2)}) collective-permute-start(f32[1032,128]{1,0:T(8,128)} %collective-permute-done.14.refs_13_.refs_8_.refs_32_), channel_id=1, source_target_pairs={{0,1},{1,0},{2,3},{3,2},{4,5},{5,4},{6,7},{7,6},{8,9},{9,8},{10,11... | collective-permute-start | bytes 1585160 | tf_op jit(solution)/shard_map/ppermute | solution.py:324
  88.8 24.4 %collective-permute-start.25 = (f32[1032,128]{1,0:T(8,128)}, f32[1032,128]{1,0:T(8,128)}, u32[]{:S(2)}, u32[]{:S(2)}) collective-permute-start(f32[1032,128]{1,0:T(8,128)} %copy-done.2), channel_id=1, source_target_pairs={{0,1},{1,0},{4,5},{5,4},{8,9},{9,8},{12,13},{13,12},{16,17},{17,16... | collective-permute-start | bytes 1585160 | tf_op jit(solution)/shard_map/ppermute | solution.py:324
  (41 other events, 363.4 us)

commit v6 on v5

--- a/solution.py
+++ b/solution.py
@@ -386,8 +386,12 @@
             swap_x.append(within(send_x, [(0, 1), (1, 0), (2, 3), (3, 2)]))
             swap_y.append(within(send_y, [(0, 2), (2, 0), (1, 3), (3, 1)]))
         passed = []
+        if at == 0:
+            own_eps = Piece(((first_sent, cut),))
+            slot_own = [Piece(((own, number * cut),)) for number in range(CHUNKS)]
+            gradient = add(0, [after(sums_own, swap_x[0])], [slot_own], [own_eps, own_eps])
         if at == 1:
-            passed = [signs, flags]
+            passed = [signs, flags, gradient]
             middle = (place == 1) | (place == 2)
             turning = jnp.where(middle, swap_x[1], swap_y[1])
         if at == 2:
@@ -404,7 +408,6 @@
     def whole(array, base):
         return Piece(((array, base),))
 
-    slot_own = [whole(own, at * cut) for at in range(CHUNKS)]
     slot_z = [whole(block, 0) for block in from_z]
     slot_x = pieces_of(up_x, swap_x, 0, 0)
     slot_y = pieces_of(up_y, swap_y, 1, 0)
@@ -421,15 +424,15 @@
     partial_z, *early = integrate(
         turned, [slot_z, slot_x[:last], slot_y[:last]], [0, 0, 0], flags, size, width
     )
-    own_eps = whole(first_sent, cut)
     partial_x, partial_y = integrate(
         turned, [slot_x[last:], slot_y[last:]], [last, last], flags, size, width, early
     )
     gradient = add(
-        0,
-        [after(sums_own, cycle), totals(partial_z), totals(partial_x), totals(partial_y)],
-        [slot_own, slot_z, slot_x, slot_y],
-        [own_eps, own_eps, whole(from_z[0], cut), eps_x, eps_y],
+        1,
+        [after(totals(partial_z), cycle), totals(partial_x), totals(partial_y)],
+        [slot_z, slot_x, slot_y],
+        [own_eps, whole(from_z[0], cut), eps_x, eps_y],
+        gradient,
     )
     turned = after(turned, gradient)
     half = CHUNKS // 2

time: 127 us -> 129 us (1.016)
  starting transfers between devices: 44.5 us -> 39.8 us
  Pallas kernels: 44.5 us -> 49.1 us
    ppermute x14, starting transfers between devices: 25.1 us -> 20 us  [within(): lax.ppermute(block, 'occ', [(g + a, g + b) for g in planes for a, b in mo...]
    pallas_call x7 -> x8, Pallas kernels: 44.5 us -> 49.1 us  [call(): pl.pallas_call(kernel, out_shape=outputs, in_specs=[pl.BlockSpec(memory_s...]
  transfers between devices with their start and end apart: 28 -> 28, of which waited for: 11 -> 10; matrix products, arithmetic and copies ran while one was open for 6% -> 7% of each run, Pallas kernels for 29% -> 32%
where the time goes in v6:
time: 129 us; the launch traced here: 128 us
  Pallas kernels  49.1 us (38%)
  starting transfers between devices  39.8 us (31%)
  waiting for transfers between devices  20.7 us (16%)
  other arithmetic  7.92 us (6%)
  local copies, waits for them, and re-layouts  6.81 us (5%)
  between operations  3.93 us (3%)
    pallas_call x8, Pallas kernels, call(): pl.pallas_call(kernel, out_shape=outputs, in_specs=[pl.BlockSpec(memory_s...  49.1 us
    ppermute x14, starting transfers between devices, within(): lax.ppermute(block, 'occ', [(g + a, g + b) for g in planes for a, b in mo...  20 us
    ppermute x4, starting transfers between devices, up(): lax.ppermute(block, 'occ', [(g, g + PLANE) for g in range(groups - PLANE)])  17 us
    ppermute x4, waiting for transfers between devices, up(): lax.ppermute(block, 'occ', [(g, g + PLANE) for g in range(groups - PLANE)])  10.4 us
    ppermute x14, waiting for transfers between devices, within(): lax.ppermute(block, 'occ', [(g + a, g + b) for g in planes for a, b in mo...  5.61 us
    unnamed x74, local copies, waits for them, and re-layouts  4.81 us
    ppermute x10, waiting for transfers between devices, totals(): lax.ppermute(part, 'aux', [(0, 1), (1, 0)])  4.65 us
    select_n x3, other arithmetic, on_device(): jnp.where(odd_y, came, up_part)  4.34 us
  transfers between devices with their start and end apart: 28, of which 10 were waited for; matrix products, arithmetic and copies ran while one was open for 7% of the time, Pallas kernels for 32%

profile of v6, /device:TPU:0, one launch (start us, length us, event | category | flops | bytes accessed | tf_op | source)
XLA Modules:
  0.0 128.3 jit_solution(11401891524055337746)
XLA Ops:
  2.1 5.0 %collective-permute-start = (f32[1032,128]{1,0:T(8,128)S(1)}, f32[1032,128]{1,0:T(8,128)S(1)}, u32[]{:S(2)}, u32[]{:S(2)}) collective-permute-start(f32[1032,128]{1,0:T(8,128)S(1)} %pad_maximum_fusion.refs_8_.refs_30_.refs_14_), channel_id=1, source_target_pairs={{0,4},{1,5},{2,6},{3,7},{4,8},{5,9},{6,10},{7,11},{8,12},{9,13},{1... | collective-permute-start | bytes 1585160 | tf_op jit(solution)/shard_map/ppermute | solution.py:327
  7.1 3.5 %collective-permute-start.2 = (f32[1032,128]{1,0:T(8,128)S(1)}, f32[1032,128]{1,0:T(8,128)S(1)}, u32[]{:S(2)}, u32[]{:S(2)}) collective-permute-start(f32[1032,128]{1,0:T(8,128)S(1)} %pad_maximum_fusion.refs_8_.refs_30_.refs_14_), channel_id=1, source_target_pairs={{0,2},{1,3},{4,6},{5,7},{8,10},{9,11},{12,14},{13,15},{16,18},{17,... | collective-permute-start | bytes 1585160 | tf_op jit(solution)/shard_map/ppermute | solution.py:324
  10.6 3.4 %collective-permute-start.1 = (f32[1032,128]{1,0:T(8,128)S(1)}, f32[1032,128]{1,0:T(8,128)S(1)}, u32[]{:S(2)}, u32[]{:S(2)}) collective-permute-start(f32[1032,128]{1,0:T(8,128)S(1)} %pad_maximum_fusion.refs_8_.refs_30_.refs_14_), channel_id=1, source_target_pairs={{0,1},{2,3},{1,0},{4,5},{6,7},{5,4},{8,9},{10,11},{9,8},{12,13},{1... | collective-permute-start | bytes 1585160 | tf_op jit(solution)/shard_map/ppermute | solution.py:324
  14.0 5.1 %shard_map.46 = (bf16[4,512,256]{2,1,0:T(8,128)(2,1)}, bf16[4,512,256]{2,1,0:T(8,128)(2,1)}, f32[256,512]{1,0:T(8,128)}, f32[256,512]{1,0:T(8,128)}, f32[1032,12...) custom-call(f32[8,128]{1,0:T(8,128)} %copy-done.35, f32[4096,128]{1,0:T(8,128)} %bitcast.18), custom_call_target="tpu_custom_call" | custom-call | tf_op jit(solution)/shard_map/pallas_call | solution.py:84
  19.7 3.5 %collective-permute-start.3 = (f32[1032,128]{1,0:T(8,128)}, f32[1032,128]{1,0:T(8,128)S(1)}, u32[]{:S(2)}, u32[]{:S(2)}) collective-permute-start(f32[1032,128]{1,0:T(8,128)} %get-tuple-element.68), channel_id=1, source_target_pairs={{0,4},{1,5},{2,6},{3,7},{4,8},{5,9},{6,10},{7,11},{8,12},{9,13},{1... | collective-permute-start | bytes 1585160 | tf_op jit(solution)/shard_map/ppermute | solution.py:327
  23.1 2.1 %broadcast_select_fusion.5 = (f32[1032,128]{1,0:T(8,128)}, f32[1032,128]{1,0:T(8,128)}) fusion(f32[1032,128]{1,0:T(8,128)S(1)} %collective-permute-done.refs_2_.refs_16_, f32[1032,128]{1,0:T(8,128)} %get-tuple-element.68, pred[]{:T(512)S(6)} %eq.44, pred[]{:T(512)S(6)} %eq.43), kind=kLoop, calls=%fused_computation.6 | loop fusion | flops 264192 | bytes 2113538 | tf_op jit(solution)/shard_map/jit(_where)/select_n | solution.py:375
  27.2 1.5 %collective-permute-start.7 = (f32[1032,128]{1,0:T(8,128)}, f32[1032,128]{1,0:T(8,128)S(1)}, u32[]{:S(2)}, u32[]{:S(2)}) collective-permute-start(f32[1032,128]{1,0:T(8,128)} %get-tuple-element.69), channel_id=1, source_target_pairs={{0,1},{1,0},{2,3},{3,2},{4,5},{5,4},{6,7},{7,6},{8,9},{9,8},{10,11... | collective-permute-start | bytes 1585160 | tf_op jit(solution)/shard_map/ppermute | solution.py:324
  33.2 1.7 %collective-permute-done.3.refs_3_.refs_17_ = f32[1032,128]{1,0:T(8,128)S(1)} collective-permute-done((f32[1032,128]{1,0:T(8,128)}, f32[1032,128]{1,0:T(8,128)S(1)}, u32[]{:S(2)}, u32[]{:S(2)}) %collective-permute-start.3) | collective-permute-done | bytes 528416 | tf_op jit(solution)/shard_map/ppermute | solution.py:327
  34.9 4.3 %collective-permute-start.4 = (f32[1032,128]{1,0:T(8,128)}, f32[1032,128]{1,0:T(8,128)S(1)}, u32[]{:S(2)}, u32[]{:S(2)}) collective-permute-start(f32[1032,128]{1,0:T(8,128)} %get-tuple-element.76), channel_id=1, source_target_pairs={{0,4},{1,5},{2,6},{3,7},{4,8},{5,9},{6,10},{7,11},{8,12},{9,13},{1... | collective-permute-start | bytes 1585160 | tf_op jit(solution)/shard_map/ppermute | solution.py:327
  39.2 2.1 %broadcast_select_fusion.4 = (f32[1032,128]{1,0:T(8,128)}, f32[1032,128]{1,0:T(8,128)}) fusion(f32[1032,128]{1,0:T(8,128)S(1)} %collective-permute-done.3.refs_3_.refs_17_, f32[1032,128]{1,0:T(8,128)} %get-tuple-element.76, pred[]{:T(512)S(6)} %eq.44, pred[]{:T(512)S(6)} %eq.43), kind=kLoop, calls=%fused_computation.5 | loop fusion | flops 264192 | bytes 2113538 | tf_op jit(solution)/shard_map/jit(_where)/select_n | solution.py:375
  41.5 1.5 %collective-permute-start.9 = (f32[1032,128]{1,0:T(8,128)}, f32[1032,128]{1,0:T(8,128)S(1)}, u32[]{:S(2)}, u32[]{:S(2)}) collective-permute-start(f32[1032,128]{1,0:T(8,128)} %get-tuple-element.85), channel_id=1, source_target_pairs={{0,1},{1,0},{2,3},{3,2},{4,5},{5,4},{6,7},{7,6},{8,9},{9,8},{10,11... | collective-permute-start | bytes 1585160 | tf_op jit(solution)/shard_map/ppermute | solution.py:324
  43.0 6.2 %shard_map.47.refs_15_ = f32[4096,128]{1,0:T(8,128)} custom-call(f32[5]{0:T(128)} %stack.34.refs_0_, s32[4]{0:T(128)} %pad_add_fusion.refs_1_.flag_ref, f32[1,512]{1,0:T(1,128)} %bitcast.15, f32[256,512]{1,0:T(8,128)} %get-tuple-element.79.refs_3_, f32[256,512]{1,0:T(8,128)} %get-tuple-element.80.refs_4_, f32[256,512]{1,0:T(8,128)} %collective-permute-done.5.refs_5_, ...), custom_call_target="tpu_custom_call" | custom-call | tf_op jit(solution)/shard_map/pallas_call | solution.py:84
  50.2 4.3 %collective-permute-start.8 = (f32[1032,128]{1,0:T(8,128)S(1)}, f32[1032,128]{1,0:T(8,128)S(1)}, u32[]{:S(2)}, u32[]{:S(2)}) collective-permute-start(f32[1032,128]{1,0:T(8,128)S(1)} %copy-done.29), channel_id=1, source_target_pairs={{0,4},{1,5},{2,6},{3,7},{4,8},{5,9},{6,10},{7,11},{8,12},{9,13},{1... | collective-permute-start | bytes 1585160 | tf_op jit(solution)/shard_map/ppermute | solution.py:327
  56.4 7.8 %collective-permute-done.8.refs_5_.refs_19_ = f32[1032,128]{1,0:T(8,128)S(1)} collective-permute-done((f32[1032,128]{1,0:T(8,128)S(1)}, f32[1032,128]{1,0:T(8,128)S(1)}, u32[]{:S(2)}, u32[]{:S(2)}) %collective-permute-start.8) | collective-permute-done | bytes 528416 | tf_op jit(solution)/shard_map/ppermute | solution.py:327
  67.6 1.6 %collective-permute-start.16 = (f32[1032,128]{1,0:T(8,128)}, f32[1032,128]{1,0:T(8,128)S(1)}, u32[]{:S(2)}, u32[]{:S(2)}) collective-permute-start(f32[1032,128]{1,0:T(8,128)} %broadcast_select_fusion.1), channel_id=1, source_target_pairs={{0,1},{1,3},{3,2},{2,0},{4,5},{5,7},{7,6},{6,4},{8,9},{9,11},{11,1... | collective-permute-start | bytes 1585160 | tf_op jit(solution)/shard_map/ppermute | solution.py:324
  69.2 8.5 %shard_map.48 = (f32[256,512]{1,0:T(8,128)}, f32[256,512]{1,0:T(8,128)}, f32[256,512]{1,0:T(8,128)}, f32[256,512]{1,0:T(8,128)}, f32[256,512]{1,0:T(8,128)}, /*index=5*/f32[256,512]{1,0:T(8,128)}) custom-call(s32[4]{0:T(128)} %pad_add_fusion.refs_1_.flag_ref, bf16[4,512,256]{2,1,0:T(8,128)(2,1)} %get-tuple-element.107.refs_0_, ...), custom_call_target="tpu_custom_call" | custom-call | tf_op jit(solution)/shard_map/pallas_call | solution.py:84
  78.3 3.5 %collective-permute-done.18.refs_9_.refs_29_.refs_2_.refs_8_ = f32[1032,128]{1,0:T(8,128)S(1)} collective-permute-done((f32[1032,128]{1,0:T(8,128)}, f32[1032,128]{1,0:T(8,128)S(1)}, u32[]{:S(2)}, u32[]{:S(2)}) %collective-permute-start.18) | collective-permute-done | bytes 528416 | tf_op jit(solution)/shard_map/ppermute | solution.py:324
  82.9 4.6 %shard_map.49 = (f32[256,512]{1,0:T(8,128)}, f32[256,512]{1,0:T(8,128)}, f32[256,512]{1,0:T(8,128)}, f32[256,512]{1,0:T(8,128)}) custom-call(s32[4]{0:T(128)} %pad_add_fusion.refs_1_.flag_ref, bf16[4,512,256]{2,1,0:T(8,128)(2,1)} %get-tuple-element.107.refs_0_, bf16[4,512,256]{2,1,0:T(8,128)(2,1)} %get-tuple-element.108.refs_1_, ...), custom_call_target="tpu_custom_call" | custom-call | tf_op jit(solution)/shard_map/pallas_call | solution.py:84
  89.6 4.0 %collective-permute-start.25 = (f32[1032,128]{1,0:T(8,128)}, f32[1032,128]{1,0:T(8,128)}, u32[]{:S(2)}, u32[]{:S(2)}) collective-permute-start(f32[1032,128]{1,0:T(8,128)} %copy-done.2), channel_id=1, source_target_pairs={{0,1},{1,0},{4,5},{5,4},{8,9},{9,8},{12,13},{13,12},{16,17},{17,16... | collective-permute-start | bytes 1585160 | tf_op jit(solution)/shard_map/ppermute | solution.py:324
  94.2 1.6 %collective-permute-done.21.refs_13_ = f32[256,512]{1,0:T(8,128)S(1)} collective-permute-done((f32[256,512]{1,0:T(8,128)}, f32[256,512]{1,0:T(8,128)S(1)}, u32[]{:S(2)}, u32[]{:S(2)}) %collective-permute-start.21) | collective-permute-done | bytes 524320 | tf_op jit(solution)/shard_map/ppermute | solution.py:331
  96.7 12.3 %shard_map.50.refs_7_ = f32[4096,128]{1,0:T(8,128)} custom-call(f32[5]{0:T(128)} %stack.34.refs_0_, s32[4]{0:T(128)} %pad_add_fusion.refs_1_.flag_ref, f32[1,512]{1,0:T(1,128)} %bitcast.16, f32[256,512]{1,0:T(8,128)} %get-tuple-element.93.refs_3_, f32[256,512]{1,0:T(8,128)} %get-tuple-element.94.refs_4_, f32[256,512]{1,0:T(8,128)} %copy-done.30, ...), custom_call_target="tpu_custom_call" | custom-call | tf_op jit(solution)/shard_map/pallas_call | solution.py:84
  109.9 4.3 %shard_map.51 = (f32[256,512]{1,0:T(8,128)}, f32[256,512]{1,0:T(8,128)}) custom-call(s32[4]{0:T(128)} %pad_add_fusion.refs_1_.flag_ref, bf16[4,512,256]{2,1,0:T(8,128)(2,1)} %get-tuple-element.107.refs_0_, bf16[4,512,256]{2,1,0:T(8,128)(2,1)} %get-tuple-element.108.refs_1_, f32[1032,128]{1,0:T(8,128)} %copy-done.2, f32[1032,128]{1,0:T(8,128)} %copy-done.11, ...), custom_call_target="tpu_custom_call" | custom-call | tf_op jit(solution)/shard_map/pallas_call | solution.py:84
  117.2 3.2 %shard_map.52 = (f32[256,512]{1,0:T(8,128)S(1)}, f32[256,512]{1,0:T(8,128)S(1)}) custom-call(s32[4]{0:T(128)S(1)} %copy-done.15, bf16[4,512,256]{2,1,0:T(8,128)(2,1)S(1)} %copy-done, bf16[4,512,256]{2,1,0:T(8,128)(2,1)S(1)} %copy-done.1, f32[256,512]{1,0:T(8,128)S(1)} %copy-done.13, f32[256,512]{1,0:T(8,128)S(1)} %copy-done.14, f32[1032,128]{1,0:T(8,128)S(1)} %copy-done.10, ...), custom_call_target="tpu_custom_call" | custom-call | tf_op jit(solution)/shard_map/pallas_call | solution.py:84
  123.3 4.9 %shard_map.53 = f32[4096,128]{1,0:T(8,128)} custom-call(f32[5]{0:T(128)S(1)} %copy-done.17, s32[4]{0:T(128)S(1)} %copy-done.15, f32[1,512]{1,0:T(1,128)S(1)} %bitcast.17, f32[256,512]{1,0:T(8,128)S(1)} %get-tuple-element.111.refs_3_, f32[256,512]{1,0:T(8,128)S(1)} %get-tuple-element.112.refs_4_, f32[256,512]{1,0:T(8,128)S(1)} %collective-permute-done.26.refs_5_, ...), custom_call_target="tpu_custom_call" | custom-call | tf_op jit(solution)/shard_map/pallas_call | solution.py:84
  (125 shorter events, 23.9 us)
Async XLA Ops:
  2.1 17.5 %collective-permute-start = (f32[1032,128]{1,0:T(8,128)S(1)}, f32[1032,128]{1,0:T(8,128)S(1)}, u32[]{:S(2)}, u32[]{:S(2)}) collective-permute-start(f32[1032,128]{1,0:T(8,128)S(1)} %pad_maximum_fusion.refs_8_.refs_30_.refs_14_), channel_id=1, source_target_pairs={{0,4},{1,5},{2,6},{3,7},{4,8},{5,9},{6,10},{7,11},{8,12},{9,13},{1... | collective-permute-start | bytes 1585160 | tf_op jit(solution)/shard_map/ppermute | solution.py:327
  7.1 18.2 %collective-permute-start.2 = (f32[1032,128]{1,0:T(8,128)S(1)}, f32[1032,128]{1,0:T(8,128)S(1)}, u32[]{:S(2)}, u32[]{:S(2)}) collective-permute-start(f32[1032,128]{1,0:T(8,128)S(1)} %pad_maximum_fusion.refs_8_.refs_30_.refs_14_), channel_id=1, source_target_pairs={{0,2},{1,3},{4,6},{5,7},{8,10},{9,11},{12,14},{13,15},{16,18},{17,... | collective-permute-start | bytes 1585160 | tf_op jit(solution)/shard_map/ppermute | solution.py:324
  10.6 16.7 %collective-permute-start.1 = (f32[1032,128]{1,0:T(8,128)S(1)}, f32[1032,128]{1,0:T(8,128)S(1)}, u32[]{:S(2)}, u32[]{:S(2)}) collective-permute-start(f32[1032,128]{1,0:T(8,128)S(1)} %pad_maximum_fusion.refs_8_.refs_30_.refs_14_), channel_id=1, source_target_pairs={{0,1},{2,3},{1,0},{4,5},{6,7},{5,4},{8,9},{10,11},{9,8},{12,13},{1... | collective-permute-start | bytes 1585160 | tf_op jit(solution)/shard_map/ppermute | solution.py:324
  19.1 23.9 %collective-permute-start.5 = (f32[256,512]{1,0:T(8,128)}, f32[256,512]{1,0:T(8,128)}, u32[]{:S(2)}, u32[]{:S(2)}) collective-permute-start(f32[256,512]{1,0:T(8,128)} %get-tuple-element.79.refs_3_), channel_id=1, source_target_pairs={{0,16},{16,0},{1,17},{17,1},{2,18},{18,2},{3,19},{19,3},{4,20},{20... | collective-permute-start | bytes 1572872 | tf_op jit(solution)/shard_map/ppermute | solution.py:331
  19.2 23.8 %collective-permute-start.6 = (f32[256,512]{1,0:T(8,128)}, f32[256,512]{1,0:T(8,128)}, u32[]{:S(2)}, u32[]{:S(2)}) collective-permute-start(f32[256,512]{1,0:T(8,128)} %get-tuple-element.80.refs_4_), channel_id=1, source_target_pairs={{0,16},{16,0},{1,17},{17,1},{2,18},{18,2},{3,19},{19,3},{4,20},{20... | collective-permute-start | bytes 1572872 | tf_op jit(solution)/shard_map/ppermute | solution.py:331
  19.7 15.3 %collective-permute-start.3 = (f32[1032,128]{1,0:T(8,128)}, f32[1032,128]{1,0:T(8,128)S(1)}, u32[]{:S(2)}, u32[]{:S(2)}) collective-permute-start(f32[1032,128]{1,0:T(8,128)} %get-tuple-element.68), channel_id=1, source_target_pairs={{0,4},{1,5},{2,6},{3,7},{4,8},{5,9},{6,10},{7,11},{8,12},{9,13},{1... | collective-permute-start | bytes 1585160 | tf_op jit(solution)/shard_map/ppermute | solution.py:327
  26.1 15.2 %collective-permute-start.11 = (f32[1032,128]{1,0:T(8,128)}, f32[1032,128]{1,0:T(8,128)S(1)}, u32[]{:S(2)}, u32[]{:S(2)}) collective-permute-start(f32[1032,128]{1,0:T(8,128)} %get-tuple-element.70), channel_id=1, source_target_pairs={{0,2},{2,0},{1,3},{3,1},{4,6},{6,4},{5,7},{7,5},{8,10},{10,8},{9,1... | collective-permute-start | bytes 1585160 | tf_op jit(solution)/shard_map/ppermute | solution.py:324
  27.2 14.2 %collective-permute-start.7 = (f32[1032,128]{1,0:T(8,128)}, f32[1032,128]{1,0:T(8,128)S(1)}, u32[]{:S(2)}, u32[]{:S(2)}) collective-permute-start(f32[1032,128]{1,0:T(8,128)} %get-tuple-element.69), channel_id=1, source_target_pairs={{0,1},{1,0},{2,3},{3,2},{4,5},{5,4},{6,7},{7,6},{8,9},{9,8},{10,11... | collective-permute-start | bytes 1585160 | tf_op jit(solution)/shard_map/ppermute | solution.py:324
  34.9 15.2 %collective-permute-start.4 = (f32[1032,128]{1,0:T(8,128)}, f32[1032,128]{1,0:T(8,128)S(1)}, u32[]{:S(2)}, u32[]{:S(2)}) collective-permute-start(f32[1032,128]{1,0:T(8,128)} %get-tuple-element.76), channel_id=1, source_target_pairs={{0,4},{1,5},{2,6},{3,7},{4,8},{5,9},{6,10},{7,11},{8,12},{9,13},{1... | collective-permute-start | bytes 1585160 | tf_op jit(solution)/shard_map/ppermute | solution.py:327
  41.3 13.2 %collective-permute-start.12 = (f32[1032,128]{1,0:T(8,128)}, f32[1032,128]{1,0:T(8,128)S(1)}, u32[]{:S(2)}, u32[]{:S(2)}) collective-permute-start(f32[1032,128]{1,0:T(8,128)} %get-tuple-element.87), channel_id=1, source_target_pairs={{0,2},{2,0},{1,3},{3,1},{4,6},{6,4},{5,7},{7,5},{8,10},{10,8},{9,1... | collective-permute-start | bytes 1585160 | tf_op jit(solution)/shard_map/ppermute | solution.py:324
  41.5 13.3 %collective-permute-start.9 = (f32[1032,128]{1,0:T(8,128)}, f32[1032,128]{1,0:T(8,128)S(1)}, u32[]{:S(2)}, u32[]{:S(2)}) collective-permute-start(f32[1032,128]{1,0:T(8,128)} %get-tuple-element.85), channel_id=1, source_target_pairs={{0,1},{1,0},{2,3},{3,2},{4,5},{5,4},{6,7},{7,6},{8,9},{9,8},{10,11... | collective-permute-start | bytes 1585160 | tf_op jit(solution)/shard_map/ppermute | solution.py:324
  50.2 14.0 %collective-permute-start.8 = (f32[1032,128]{1,0:T(8,128)S(1)}, f32[1032,128]{1,0:T(8,128)S(1)}, u32[]{:S(2)}, u32[]{:S(2)}) collective-permute-start(f32[1032,128]{1,0:T(8,128)S(1)} %copy-done.29), channel_id=1, source_target_pairs={{0,4},{1,5},{2,6},{3,7},{4,8},{5,9},{6,10},{7,11},{8,12},{9,13},{1... | collective-permute-start | bytes 1585160 | tf_op jit(solution)/shard_map/ppermute | solution.py:327
  54.6 12.1 %collective-permute-start.13 = (f32[1032,128]{1,0:T(8,128)S(1)}, f32[1032,128]{1,0:T(8,128)}, u32[]{:S(2)}, u32[]{:S(2)}) collective-permute-start(f32[1032,128]{1,0:T(8,128)S(1)} %get-tuple-element.88), channel_id=1, source_target_pairs={{0,2},{2,0},{1,3},{3,1},{4,6},{6,4},{5,7},{7,5},{8,10},{10,8},{9,1... | collective-permute-start | bytes 1585160 | tf_op jit(solution)/shard_map/ppermute | solution.py:324
  54.8 12.3 %collective-permute-start.10 = (f32[1032,128]{1,0:T(8,128)S(1)}, f32[1032,128]{1,0:T(8,128)S(1)}, u32[]{:S(2)}, u32[]{:S(2)}) collective-permute-start(f32[1032,128]{1,0:T(8,128)S(1)} %get-tuple-element.86), channel_id=1, source_target_pairs={{0,1},{1,0},{2,3},{3,2},{4,5},{5,4},{6,7},{7,6},{8,9},{9,8},{10,11... | collective-permute-start | bytes 1585160 | tf_op jit(solution)/shard_map/ppermute | solution.py:324
  66.7 15.2 %collective-permute-start.18 = (f32[1032,128]{1,0:T(8,128)}, f32[1032,128]{1,0:T(8,128)S(1)}, u32[]{:S(2)}, u32[]{:S(2)}) collective-permute-start(f32[1032,128]{1,0:T(8,128)} %get-tuple-element.102), channel_id=1, source_target_pairs={{0,2},{2,0},{1,3},{3,1},{4,6},{6,4},{5,7},{7,5},{8,10},{10,8},{9,1... | collective-permute-start | bytes 1585160 | tf_op jit(solution)/shard_map/ppermute | solution.py:324
  67.1 14.7 %collective-permute-start.17 = (f32[1032,128]{1,0:T(8,128)}, f32[1032,128]{1,0:T(8,128)S(1)}, u32[]{:S(2)}, u32[]{:S(2)}) collective-permute-start(f32[1032,128]{1,0:T(8,128)} %get-tuple-element.101), channel_id=1, source_target_pairs={{0,1},{1,0},{2,3},{3,2},{4,5},{5,4},{6,7},{7,6},{8,9},{9,8},{10,11... | collective-permute-start | bytes 1585160 | tf_op jit(solution)/shard_map/ppermute | solution.py:324
  67.6 21.9 %collective-permute-start.16 = (f32[1032,128]{1,0:T(8,128)}, f32[1032,128]{1,0:T(8,128)S(1)}, u32[]{:S(2)}, u32[]{:S(2)}) collective-permute-start(f32[1032,128]{1,0:T(8,128)} %broadcast_select_fusion.1), channel_id=1, source_target_pairs={{0,1},{1,3},{3,2},{2,0},{4,5},{5,7},{7,6},{6,4},{8,9},{9,11},{11,1... | collective-permute-start | bytes 1585160 | tf_op jit(solution)/shard_map/ppermute | solution.py:324
  77.7 10.3 %collective-permute-start.14 = (f32[256,512]{1,0:T(8,128)}, f32[256,512]{1,0:T(8,128)S(1)}, u32[]{:S(2)}, u32[]{:S(2)}) collective-permute-start(f32[256,512]{1,0:T(8,128)} %get-tuple-element.93.refs_3_), channel_id=1, source_target_pairs={{0,16},{16,0},{1,17},{17,1},{2,18},{18,2},{3,19},{19,3},{4,20},{20... | collective-permute-start | bytes 1572872 | tf_op jit(solution)/shard_map/ppermute | solution.py:331
  77.8 11.5 %collective-permute-start.15 = (f32[256,512]{1,0:T(8,128)}, f32[256,512]{1,0:T(8,128)S(1)}, u32[]{:S(2)}, u32[]{:S(2)}) collective-permute-start(f32[256,512]{1,0:T(8,128)} %get-tuple-element.94.refs_4_), channel_id=1, source_target_pairs={{0,16},{16,0},{1,17},{17,1},{2,18},{18,2},{3,19},{19,3},{4,20},{20... | collective-permute-start | bytes 1572872 | tf_op jit(solution)/shard_map/ppermute | solution.py:331
  87.5 6.1 %collective-permute-start.19 = (f32[256,512]{1,0:T(8,128)}, f32[256,512]{1,0:T(8,128)S(1)}, u32[]{:S(2)}, u32[]{:S(2)}) collective-permute-start(f32[256,512]{1,0:T(8,128)} %get-tuple-element.103.refs_7_), channel_id=1, source_target_pairs={{0,16},{16,0},{1,17},{17,1},{2,18},{18,2},{3,19},{19,3},{4,20},{20... | collective-permute-start | bytes 1572872 | tf_op jit(solution)/shard_map/ppermute | solution.py:331
  87.6 6.1 %collective-permute-start.20 = (f32[256,512]{1,0:T(8,128)}, f32[256,512]{1,0:T(8,128)S(1)}, u32[]{:S(2)}, u32[]{:S(2)}) collective-permute-start(f32[256,512]{1,0:T(8,128)} %get-tuple-element.104.refs_8_), channel_id=1, source_target_pairs={{0,16},{16,0},{1,17},{17,1},{2,18},{18,2},{3,19},{19,3},{4,20},{20... | collective-permute-start | bytes 1572872 | tf_op jit(solution)/shard_map/ppermute | solution.py:331
  88.1 21.0 %collective-permute-start.23 = (f32[1032,128]{1,0:T(8,128)}, f32[1032,128]{1,0:T(8,128)S(1)}, u32[]{:S(2)}, u32[]{:S(2)}) collective-permute-start(f32[1032,128]{1,0:T(8,128)} %get-tuple-element.123), channel_id=1, source_target_pairs={{2,0},{3,2},{6,4},{7,6},{10,8},{11,10},{14,12},{15,14},{18,16},{19... | collective-permute-start | bytes 1585160 | tf_op jit(solution)/shard_map/ppermute | solution.py:324
  89.4 24.8 %collective-permute-start.24 = (f32[1032,128]{1,0:T(8,128)}, f32[1032,128]{1,0:T(8,128)}, u32[]{:S(2)}, u32[]{:S(2)}) collective-permute-start(f32[1032,128]{1,0:T(8,128)} %collective-permute-done.13.refs_13_.refs_8_.refs_28_), channel_id=1, source_target_pairs={{0,1},{1,0},{2,3},{3,2},{4,5},{5,4},{6,7},{7,6},{8,9},{9,8},{10,11... | collective-permute-start | bytes 1585160 | tf_op jit(solution)/shard_map/ppermute | solution.py:324
  89.6 25.5 %collective-permute-start.25 = (f32[1032,128]{1,0:T(8,128)}, f32[1032,128]{1,0:T(8,128)}, u32[]{:S(2)}, u32[]{:S(2)}) collective-permute-start(f32[1032,128]{1,0:T(8,128)} %copy-done.2), channel_id=1, source_target_pairs={{0,1},{1,0},{4,5},{5,4},{8,9},{9,8},{12,13},{13,12},{16,17},{17,16... | collective-permute-start | bytes 1585160 | tf_op jit(solution)/shard_map/ppermute | solution.py:324
  (41 other events, 323.8 us)

commit v7 on v5

--- a/solution.py
+++ b/solution.py
@@ -12,7 +12,7 @@
 SUBLANES = 8
 PLANE = 4
 CHUNKS = 4
-VMEM_LIMIT = 60 * 1024 * 1024
+VMEM_LIMIT = 32 * 1024 * 1024
 LAST_LIMIT = 24 * 1024 * 1024
 HALVES = 2
 

time: 127 us -> 124 us (0.976)
  waiting for transfers between devices: 20.7 us -> 38.4 us
  Pallas kernels: 44.5 us -> 32.7 us
  starting transfers between devices: 44.5 us -> 36.2 us
    pallas_call x7, Pallas kernels: 44.5 us -> 32.7 us  [call(): pl.pallas_call(kernel, out_shape=outputs, in_specs=[pl.BlockSpec(memory_s...]
    ppermute x14, starting transfers between devices: 25.1 us -> 15.5 us  [within(): lax.ppermute(block, 'occ', [(g + a, g + b) for g in planes for a, b in mo...]
    ppermute x4, waiting for transfers between devices: 10.1 us -> 19.2 us  [up(): lax.ppermute(block, 'occ', [(g, g + PLANE) for g in range(groups - PLANE)])]
    ppermute x14, waiting for transfers between devices: 5.95 us -> 14.9 us  [within(): lax.ppermute(block, 'occ', [(g + a, g + b) for g in planes for a, b in mo...]
    unnamed x74 -> x24, local copies, waits for them, and re-layouts: 4.05 us -> 5.63 us
  transfers between devices with their start and end apart: 28 -> 28, of which waited for: 11 -> 11; matrix products, arithmetic and copies ran while one was open for 6% -> 5% of each run, Pallas kernels for 29% -> 21%
where the time goes in v7:
time: 124 us
  waiting for transfers between devices  38.4 us (31%)
  starting transfers between devices  36.2 us (29%)
  Pallas kernels  32.7 us (26%)
  local copies, waits for them, and re-layouts  7.13 us (6%)
  other arithmetic  5.77 us (5%)
  between operations  3.71 us (3%)
    pallas_call x7, Pallas kernels, call(): pl.pallas_call(kernel, out_shape=outputs, in_specs=[pl.BlockSpec(memory_s...  32.7 us
    ppermute x4, waiting for transfers between devices, up(): lax.ppermute(block, 'occ', [(g, g + PLANE) for g in range(groups - PLANE)])  19.2 us
    ppermute x4, starting transfers between devices, up(): lax.ppermute(block, 'occ', [(g, g + PLANE) for g in range(groups - PLANE)])  17.9 us
    ppermute x14, starting transfers between devices, within(): lax.ppermute(block, 'occ', [(g + a, g + b) for g in planes for a, b in mo...  15.5 us
    ppermute x14, waiting for transfers between devices, within(): lax.ppermute(block, 'occ', [(g + a, g + b) for g in planes for a, b in mo...  14.9 us
    unnamed x24, local copies, waits for them, and re-layouts  5.63 us
    ppermute x10, waiting for transfers between devices, totals(): lax.ppermute(part, 'aux', [(0, 1), (1, 0)])  4.31 us
    select_n x3, other arithmetic, on_device(): jnp.where(odd_y, came, up_part)  3.51 us
  transfers between devices with their start and end apart: 28, of which 11 were waited for; matrix products, arithmetic and copies ran while one was open for 5% of the time, Pallas kernels for 21%

profile of v7, /device:TPU:0, one launch (start us, length us, event | category | flops | bytes accessed | tf_op | source)
XLA Modules:
  0.0 123.9 jit_solution(1563062773222250762)
XLA Ops:
  2.1 5.0 %collective-permute-start = (f32[1032,128]{1,0:T(8,128)S(1)}, f32[1032,128]{1,0:T(8,128)S(1)}, u32[]{:S(2)}, u32[]{:S(2)}) collective-permute-start(f32[1032,128]{1,0:T(8,128)S(1)} %pad_maximum_fusion.refs_34_.refs_14_), channel_id=1, source_target_pairs={{0,4},{1,5},{2,6},{3,7},{4,8},{5,9},{6,10},{7,11},{8,12},{9,13},{1... | collective-permute-start | bytes 1585160 | tf_op jit(solution)/shard_map/ppermute | solution.py:327
  7.1 4.2 %collective-permute-start.2 = (f32[1032,128]{1,0:T(8,128)S(1)}, f32[1032,128]{1,0:T(8,128)}, u32[]{:S(2)}, u32[]{:S(2)}) collective-permute-start(f32[1032,128]{1,0:T(8,128)S(1)} %pad_maximum_fusion.refs_34_.refs_14_), channel_id=1, source_target_pairs={{0,2},{1,3},{4,6},{5,7},{8,10},{9,11},{12,14},{13,15},{16,18},{17,... | collective-permute-start | bytes 1585160 | tf_op jit(solution)/shard_map/ppermute | solution.py:324
  11.3 3.4 %collective-permute-start.1 = (f32[1032,128]{1,0:T(8,128)S(1)}, f32[1032,128]{1,0:T(8,128)}, u32[]{:S(2)}, u32[]{:S(2)}) collective-permute-start(f32[1032,128]{1,0:T(8,128)S(1)} %pad_maximum_fusion.refs_34_.refs_14_), channel_id=1, source_target_pairs={{0,1},{2,3},{1,0},{4,5},{6,7},{5,4},{8,9},{10,11},{9,8},{12,13},{1... | collective-permute-start | bytes 1585160 | tf_op jit(solution)/shard_map/ppermute | solution.py:324
  14.8 1.6 %copy-done = f32[1024,1,512]{2,1,0:T(1,128)S(1)} copy-done((f32[1024,1,512]{2,1,0:T(1,128)S(1)}, f32[1024,1,512]{2,1,0:T(1,128)}, u32[]{:S(2)}) %copy-start) | copy-done | bytes 2097176
  16.4 3.5 %shard_map.46 = (bf16[4,512,256]{2,1,0:T(8,128)(2,1)S(1)}, bf16[4,512,256]{2,1,0:T(8,128)(2,1)S(1)}, f32[256,512]{1,0:T(8,128)S(1)}, f32[256,512]{1,0:T(8,128)S(...) custom-call(f32[8,128]{1,0:T(8,128)S(1)} %pad_bitcast_fusion.energy_ref, ...), custom_call_target="tpu_custom_call" | custom-call | tf_op jit(solution)/shard_map/pallas_call | solution.py:84
  23.9 4.2 %collective-permute-start.5 = (f32[1032,128]{1,0:T(8,128)}, f32[1032,128]{1,0:T(8,128)}, u32[]{:S(2)}, u32[]{:S(2)}) collective-permute-start(f32[1032,128]{1,0:T(8,128)} %copy-done.5), channel_id=1, source_target_pairs={{0,4},{1,5},{2,6},{3,7},{4,8},{5,9},{6,10},{7,11},{8,12},{9,13},{1... | collective-permute-start | bytes 1585160 | tf_op jit(solution)/shard_map/ppermute | solution.py:327
  28.2 2.2 %broadcast_select_fusion.5 = (f32[1032,128]{1,0:T(8,128)}, f32[1032,128]{1,0:T(8,128)}) fusion(f32[1032,128]{1,0:T(8,128)S(1)} %collective-permute-done.refs_2_.refs_20_, f32[1032,128]{1,0:T(8,128)} %copy-done.5, pred[]{:T(512)S(6)} %eq.44, pred[]{:T(512)S(6)} %eq.43), kind=kLoop, calls=%fused_computation.6 | loop fusion | flops 264192 | bytes 2113538 | tf_op jit(solution)/shard_map/jit(_where)/select_n | solution.py:375
  34.4 3.7 %collective-permute-done.5.refs_3_.refs_21_ = f32[1032,128]{1,0:T(8,128)} collective-permute-done((f32[1032,128]{1,0:T(8,128)}, f32[1032,128]{1,0:T(8,128)}, u32[]{:S(2)}, u32[]{:S(2)}) %collective-permute-start.5) | collective-permute-done | bytes 528416 | tf_op jit(solution)/shard_map/ppermute | solution.py:327
  38.1 4.4 %collective-permute-start.10 = (f32[1032,128]{1,0:T(8,128)}, f32[1032,128]{1,0:T(8,128)S(1)}, u32[]{:S(2)}, u32[]{:S(2)}) collective-permute-start(f32[1032,128]{1,0:T(8,128)} %copy-done.4), channel_id=1, source_target_pairs={{0,4},{1,5},{2,6},{3,7},{4,8},{5,9},{6,10},{7,11},{8,12},{9,13},{1... | collective-permute-start | bytes 1585160 | tf_op jit(solution)/shard_map/ppermute | solution.py:327
  44.5 7.8 %collective-permute-done.10.refs_4_.refs_22_ = f32[1032,128]{1,0:T(8,128)S(1)} collective-permute-done((f32[1032,128]{1,0:T(8,128)}, f32[1032,128]{1,0:T(8,128)S(1)}, u32[]{:S(2)}, u32[]{:S(2)}) %collective-permute-start.10) | collective-permute-done | bytes 528416 | tf_op jit(solution)/shard_map/ppermute | solution.py:327
  52.3 4.3 %collective-permute-start.11 = (f32[1032,128]{1,0:T(8,128)S(1)}, f32[1032,128]{1,0:T(8,128)S(1)}, u32[]{:S(2)}, u32[]{:S(2)}) collective-permute-start(f32[1032,128]{1,0:T(8,128)S(1)} %copy-done.3), channel_id=1, source_target_pairs={{0,4},{1,5},{2,6},{3,7},{4,8},{5,9},{6,10},{7,11},{8,12},{9,13},{1... | collective-permute-start | bytes 1585160 | tf_op jit(solution)/shard_map/ppermute | solution.py:327
  57.4 7.7 %collective-permute-done.11.refs_5_.refs_23_ = f32[1032,128]{1,0:T(8,128)S(1)} collective-permute-done((f32[1032,128]{1,0:T(8,128)S(1)}, f32[1032,128]{1,0:T(8,128)S(1)}, u32[]{:S(2)}, u32[]{:S(2)}) %collective-permute-start.11) | collective-permute-done | bytes 528416 | tf_op jit(solution)/shard_map/ppermute | solution.py:327
  66.5 2.4 %collective-permute-done.14.refs_13_.refs_8_.refs_32_ = f32[1032,128]{1,0:T(8,128)S(1)} collective-permute-done((f32[1032,128]{1,0:T(8,128)S(1)}, f32[1032,128]{1,0:T(8,128)S(1)}, u32[]{:S(2)}, u32[]{:S(2)}) %collective-permute-start.14) | collective-permute-done | bytes 528416 | tf_op jit(solution)/shard_map/ppermute | solution.py:324
  70.0 1.5 %collective-permute-start.13 = (f32[1032,128]{1,0:T(8,128)S(1)}, f32[1032,128]{1,0:T(8,128)S(1)}, u32[]{:S(2)}, u32[]{:S(2)}) collective-permute-start(f32[1032,128]{1,0:T(8,128)S(1)} %broadcast_select_fusion.1), channel_id=1, source_target_pairs={{0,1},{1,3},{3,2},{2,0},{4,5},{5,7},{7,6},{6,4},{8,9},{9,11},{11,1... | collective-permute-start | bytes 1585160 | tf_op jit(solution)/shard_map/ppermute | solution.py:324
  71.5 6.9 %shard_map.47 = (f32[256,512]{1,0:T(8,128)S(1)}, f32[256,512]{1,0:T(8,128)S(1)}, f32[256,512]{1,0:T(8,128)S(1)}, f32[256,512]{1,0:T(8,128)S(1)}, f32[256,512]{1,0:T(8,128)S(1)}, /*index=5*/f32[256,512]{1,0:T(8,128)S(1)}) custom-call(s32[4]{0:T(128)S(1)} %pad_add_fusion.flag_ref.refs_1_, bf16[4,512,256]{2,1,0:T(8,128)(2,1)S(1)} %get-tuple-element.99.refs_0_, ...), custom_call_target="tpu_custom_call" | custom-call | tf_op jit(solution)/shard_map/pallas_call | solution.py:84
  78.4 5.5 %collective-permute-done.18.refs_9_.refs_33_.refs_2_.refs_8_ = f32[1032,128]{1,0:T(8,128)S(1)} collective-permute-done((f32[1032,128]{1,0:T(8,128)S(1)}, f32[1032,128]{1,0:T(8,128)S(1)}, u32[]{:S(2)}, u32[]{:S(2)}) %collective-permute-start.18) | collective-permute-done | bytes 528416 | tf_op jit(solution)/shard_map/ppermute | solution.py:324
  84.4 2.3 %shard_map.48 = (f32[256,512]{1,0:T(8,128)S(1)}, f32[256,512]{1,0:T(8,128)S(1)}, f32[256,512]{1,0:T(8,128)S(1)}, f32[256,512]{1,0:T(8,128)S(1)}) custom-call(s32[4]{0:T(128)S(1)} %pad_add_fusion.flag_ref.refs_1_, bf16[4,512,256]{2,1,0:T(8,128)(2,1)S(1)} %get-tuple-element.99.refs_0_, bf16[4,512,256]{2,1,0:T(8,128)(2,1)S(1)} %get-tuple-element.100.refs_1_, ...), custom_call_target="tpu_custom_call" | custom-call | tf_op jit(solution)/shard_map/pallas_call | solution.py:84
  88.6 1.5 %collective-permute-done.13.refs_5_.refs_4_.refs_11_ = f32[1032,128]{1,0:T(8,128)S(1)} collective-permute-done((f32[1032,128]{1,0:T(8,128)S(1)}, f32[1032,128]{1,0:T(8,128)S(1)}, u32[]{:S(2)}, u32[]{:S(2)}) %collective-permute-start.13) | collective-permute-done | bytes 528416 | tf_op jit(solution)/shard_map/ppermute | solution.py:324
  90.2 2.5 %collective-permute-start.25 = (f32[1032,128]{1,0:T(8,128)S(1)}, f32[1032,128]{1,0:T(8,128)S(1)}, u32[]{:S(2)}, u32[]{:S(2)}) collective-permute-start(f32[1032,128]{1,0:T(8,128)S(1)} %collective-permute-done.18.refs_9_.refs_33_.refs_2_.refs_8_), channel_id=1, source_target_pairs={{0,1},{1,0},{4,5},{5,4},{8,9},{9,8},{12,13},{13,12},{16,17},{17,16... | collective-permute-start | bytes 1585160 | tf_op jit(solution)/shard_map/ppermute | solution.py:324
  95.4 11.2 %shard_map.49.refs_7_ = f32[4096,128]{1,0:T(8,128)S(1)} custom-call(f32[5]{0:T(128)S(1)} %stack.34.refs_0_, s32[4]{0:T(128)S(1)} %pad_add_fusion.flag_ref.refs_1_, f32[1,512]{1,0:T(1,128)S(1)} %bitcast.17, f32[256,512]{1,0:T(8,128)S(1)} %copy-done.7, f32[256,512]{1,0:T(8,128)S(1)} %copy-done.9, f32[256,512]{1,0:T(8,128)S(1)} %collective-permute-done.3.refs_5_, ...), custom_call_target="tpu_custom_call" | custom-call | tf_op jit(solution)/shard_map/pallas_call | solution.py:84
  106.6 1.9 %shard_map.50 = (f32[256,512]{1,0:T(8,128)S(1)}, f32[256,512]{1,0:T(8,128)S(1)}) custom-call(s32[4]{0:T(128)S(1)} %pad_add_fusion.flag_ref.refs_1_, bf16[4,512,256]{2,1,0:T(8,128)(2,1)S(1)} %get-tuple-element.99.refs_0_, bf16[4,512,256]{2,1,0:T(8,128)(2,1)S(1)} %get-tuple-element.100.refs_1_, ...), custom_call_target="tpu_custom_call" | custom-call | tf_op jit(solution)/shard_map/pallas_call | solution.py:84
  108.5 5.4 %collective-permute-done.25.refs_6_.refs_13_ = f32[1032,128]{1,0:T(8,128)S(1)} collective-permute-done((f32[1032,128]{1,0:T(8,128)S(1)}, f32[1032,128]{1,0:T(8,128)S(1)}, u32[]{:S(2)}, u32[]{:S(2)}) %collective-permute-start.25) | collective-permute-done | bytes 528416 | tf_op jit(solution)/shard_map/ppermute | solution.py:324
  114.0 2.1 %shard_map.51 = (f32[256,512]{1,0:T(8,128)S(1)}, f32[256,512]{1,0:T(8,128)S(1)}) custom-call(s32[4]{0:T(128)S(1)} %pad_add_fusion.flag_ref.refs_1_, bf16[4,512,256]{2,1,0:T(8,128)(2,1)S(1)} %get-tuple-element.99.refs_0_, bf16[4,512,256]{2,1,0:T(8,128)(2,1)S(1)} %get-tuple-element.100.refs_1_, f32[256,512]{1,0:T(8,128)S(1)} %get-tuple-element.101.refs_2_, ...), custom_call_target="tpu_custom_call" | custom-call | tf_op jit(solution)/shard_map/pallas_call | solution.py:84
  118.7 5.0 %shard_map.52 = f32[4096,128]{1,0:T(8,128)} custom-call(f32[5]{0:T(128)S(1)} %stack.34.refs_0_, s32[4]{0:T(128)S(1)} %pad_add_fusion.flag_ref.refs_1_, f32[1,512]{1,0:T(1,128)S(1)} %bitcast.18, f32[256,512]{1,0:T(8,128)S(1)} %get-tuple-element.103.refs_3_, f32[256,512]{1,0:T(8,128)S(1)} %get-tuple-element.104.refs_4_, ...), custom_call_target="tpu_custom_call" | custom-call | tf_op jit(solution)/shard_map/pallas_call | solution.py:84
  (74 shorter events, 20.1 us)
Async XLA Ops:
  2.1 21.8 %collective-permute-start = (f32[1032,128]{1,0:T(8,128)S(1)}, f32[1032,128]{1,0:T(8,128)S(1)}, u32[]{:S(2)}, u32[]{:S(2)}) collective-permute-start(f32[1032,128]{1,0:T(8,128)S(1)} %pad_maximum_fusion.refs_34_.refs_14_), channel_id=1, source_target_pairs={{0,4},{1,5},{2,6},{3,7},{4,8},{5,9},{6,10},{7,11},{8,12},{9,13},{1... | collective-permute-start | bytes 1585160 | tf_op jit(solution)/shard_map/ppermute | solution.py:327
  7.1 23.2 %collective-permute-start.2 = (f32[1032,128]{1,0:T(8,128)S(1)}, f32[1032,128]{1,0:T(8,128)}, u32[]{:S(2)}, u32[]{:S(2)}) collective-permute-start(f32[1032,128]{1,0:T(8,128)S(1)} %pad_maximum_fusion.refs_34_.refs_14_), channel_id=1, source_target_pairs={{0,2},{1,3},{4,6},{5,7},{8,10},{9,11},{12,14},{13,15},{16,18},{17,... | collective-permute-start | bytes 1585160 | tf_op jit(solution)/shard_map/ppermute | solution.py:324
  11.3 19.0 %collective-permute-start.1 = (f32[1032,128]{1,0:T(8,128)S(1)}, f32[1032,128]{1,0:T(8,128)}, u32[]{:S(2)}, u32[]{:S(2)}) collective-permute-start(f32[1032,128]{1,0:T(8,128)S(1)} %pad_maximum_fusion.refs_34_.refs_14_), channel_id=1, source_target_pairs={{0,1},{2,3},{1,0},{4,5},{6,7},{5,4},{8,9},{10,11},{9,8},{12,13},{1... | collective-permute-start | bytes 1585160 | tf_op jit(solution)/shard_map/ppermute | solution.py:324
  23.9 14.2 %collective-permute-start.5 = (f32[1032,128]{1,0:T(8,128)}, f32[1032,128]{1,0:T(8,128)}, u32[]{:S(2)}, u32[]{:S(2)}) collective-permute-start(f32[1032,128]{1,0:T(8,128)} %copy-done.5), channel_id=1, source_target_pairs={{0,4},{1,5},{2,6},{3,7},{4,8},{5,9},{6,10},{7,11},{8,12},{9,13},{1... | collective-permute-start | bytes 1585160 | tf_op jit(solution)/shard_map/ppermute | solution.py:327
  30.3 13.5 %collective-permute-start.8 = (f32[1032,128]{1,0:T(8,128)}, f32[1032,128]{1,0:T(8,128)}, u32[]{:S(2)}, u32[]{:S(2)}) collective-permute-start(f32[1032,128]{1,0:T(8,128)} %get-tuple-element.66), channel_id=1, source_target_pairs={{0,2},{2,0},{1,3},{3,1},{4,6},{6,4},{5,7},{7,5},{8,10},{10,8},{9,1... | collective-permute-start | bytes 1585160 | tf_op jit(solution)/shard_map/ppermute | solution.py:324
  30.4 13.5 %collective-permute-start.6 = (f32[1032,128]{1,0:T(8,128)}, f32[1032,128]{1,0:T(8,128)}, u32[]{:S(2)}, u32[]{:S(2)}) collective-permute-start(f32[1032,128]{1,0:T(8,128)} %get-tuple-element.65), channel_id=1, source_target_pairs={{0,1},{1,0},{2,3},{3,2},{4,5},{5,4},{6,7},{7,6},{8,9},{9,8},{10,11... | collective-permute-start | bytes 1585160 | tf_op jit(solution)/shard_map/ppermute | solution.py:324
  38.1 14.2 %collective-permute-start.10 = (f32[1032,128]{1,0:T(8,128)}, f32[1032,128]{1,0:T(8,128)S(1)}, u32[]{:S(2)}, u32[]{:S(2)}) collective-permute-start(f32[1032,128]{1,0:T(8,128)} %copy-done.4), channel_id=1, source_target_pairs={{0,4},{1,5},{2,6},{3,7},{4,8},{5,9},{6,10},{7,11},{8,12},{9,13},{1... | collective-permute-start | bytes 1585160 | tf_op jit(solution)/shard_map/ppermute | solution.py:327
  43.8 12.9 %collective-permute-start.9 = (f32[1032,128]{1,0:T(8,128)S(1)}, f32[1032,128]{1,0:T(8,128)S(1)}, u32[]{:S(2)}, u32[]{:S(2)}) collective-permute-start(f32[1032,128]{1,0:T(8,128)S(1)} %get-tuple-element.75), channel_id=1, source_target_pairs={{0,2},{2,0},{1,3},{3,1},{4,6},{6,4},{5,7},{7,5},{8,10},{10,8},{9,1... | collective-permute-start | bytes 1585160 | tf_op jit(solution)/shard_map/ppermute | solution.py:324
  43.9 12.9 %collective-permute-start.7 = (f32[1032,128]{1,0:T(8,128)S(1)}, f32[1032,128]{1,0:T(8,128)S(1)}, u32[]{:S(2)}, u32[]{:S(2)}) collective-permute-start(f32[1032,128]{1,0:T(8,128)S(1)} %get-tuple-element.74), channel_id=1, source_target_pairs={{0,1},{1,0},{2,3},{3,2},{4,5},{5,4},{6,7},{7,6},{8,9},{9,8},{10,11... | collective-permute-start | bytes 1585160 | tf_op jit(solution)/shard_map/ppermute | solution.py:324
  52.3 12.8 %collective-permute-start.11 = (f32[1032,128]{1,0:T(8,128)S(1)}, f32[1032,128]{1,0:T(8,128)S(1)}, u32[]{:S(2)}, u32[]{:S(2)}) collective-permute-start(f32[1032,128]{1,0:T(8,128)S(1)} %copy-done.3), channel_id=1, source_target_pairs={{0,4},{1,5},{2,6},{3,7},{4,8},{5,9},{6,10},{7,11},{8,12},{9,13},{1... | collective-permute-start | bytes 1585160 | tf_op jit(solution)/shard_map/ppermute | solution.py:327
  56.7 12.2 %collective-permute-start.14 = (f32[1032,128]{1,0:T(8,128)S(1)}, f32[1032,128]{1,0:T(8,128)S(1)}, u32[]{:S(2)}, u32[]{:S(2)}) collective-permute-start(f32[1032,128]{1,0:T(8,128)S(1)} %get-tuple-element.86), channel_id=1, source_target_pairs={{0,2},{2,0},{1,3},{3,1},{4,6},{6,4},{5,7},{7,5},{8,10},{10,8},{9,1... | collective-permute-start | bytes 1585160 | tf_op jit(solution)/shard_map/ppermute | solution.py:324
  56.8 12.2 %collective-permute-start.12 = (f32[1032,128]{1,0:T(8,128)S(1)}, f32[1032,128]{1,0:T(8,128)S(1)}, u32[]{:S(2)}, u32[]{:S(2)}) collective-permute-start(f32[1032,128]{1,0:T(8,128)S(1)} %get-tuple-element.80), channel_id=1, source_target_pairs={{0,1},{1,0},{2,3},{3,2},{4,5},{5,4},{6,7},{7,6},{8,9},{9,8},{10,11... | collective-permute-start | bytes 1585160 | tf_op jit(solution)/shard_map/ppermute | solution.py:324
  68.9 14.9 %collective-permute-start.18 = (f32[1032,128]{1,0:T(8,128)S(1)}, f32[1032,128]{1,0:T(8,128)S(1)}, u32[]{:S(2)}, u32[]{:S(2)}) collective-permute-start(f32[1032,128]{1,0:T(8,128)S(1)} %get-tuple-element.94), channel_id=1, source_target_pairs={{0,2},{2,0},{1,3},{3,1},{4,6},{6,4},{5,7},{7,5},{8,10},{10,8},{9,1... | collective-permute-start | bytes 1585160 | tf_op jit(solution)/shard_map/ppermute | solution.py:324
  68.9 14.9 %collective-permute-start.17 = (f32[1032,128]{1,0:T(8,128)S(1)}, f32[1032,128]{1,0:T(8,128)S(1)}, u32[]{:S(2)}, u32[]{:S(2)}) collective-permute-start(f32[1032,128]{1,0:T(8,128)S(1)} %get-tuple-element.93), channel_id=1, source_target_pairs={{0,1},{1,0},{2,3},{3,2},{4,5},{5,4},{6,7},{7,6},{8,9},{9,8},{10,11... | collective-permute-start | bytes 1585160 | tf_op jit(solution)/shard_map/ppermute | solution.py:324
  69.5 17.2 %collective-permute-start.3 = (f32[256,512]{1,0:T(8,128)S(1)}, f32[256,512]{1,0:T(8,128)S(1)}, u32[]{:S(2)}, u32[]{:S(2)}) collective-permute-start(f32[256,512]{1,0:T(8,128)S(1)} %copy-done.7), channel_id=1, source_target_pairs={{0,16},{16,0},{1,17},{17,1},{2,18},{18,2},{3,19},{19,3},{4,20},{20... | collective-permute-start | bytes 1572872 | tf_op jit(solution)/shard_map/ppermute | solution.py:331
  69.5 17.3 %collective-permute-start.4 = (f32[256,512]{1,0:T(8,128)S(1)}, f32[256,512]{1,0:T(8,128)S(1)}, u32[]{:S(2)}, u32[]{:S(2)}) collective-permute-start(f32[256,512]{1,0:T(8,128)S(1)} %copy-done.9), channel_id=1, source_target_pairs={{0,16},{16,0},{1,17},{17,1},{2,18},{18,2},{3,19},{19,3},{4,20},{20... | collective-permute-start | bytes 1572872 | tf_op jit(solution)/shard_map/ppermute | solution.py:331
  70.0 20.2 %collective-permute-start.13 = (f32[1032,128]{1,0:T(8,128)S(1)}, f32[1032,128]{1,0:T(8,128)S(1)}, u32[]{:S(2)}, u32[]{:S(2)}) collective-permute-start(f32[1032,128]{1,0:T(8,128)S(1)} %broadcast_select_fusion.1), channel_id=1, source_target_pairs={{0,1},{1,3},{3,2},{2,0},{4,5},{5,7},{7,6},{6,4},{8,9},{9,11},{11,1... | collective-permute-start | bytes 1585160 | tf_op jit(solution)/shard_map/ppermute | solution.py:324
  83.9 3.4 %collective-permute-start.15 = (f32[256,512]{1,0:T(8,128)S(1)}, f32[256,512]{1,0:T(8,128)S(1)}, u32[]{:S(2)}, u32[]{:S(2)}) collective-permute-start(f32[256,512]{1,0:T(8,128)S(1)} %get-tuple-element.87.refs_7_), channel_id=1, source_target_pairs={{0,16},{16,0},{1,17},{17,1},{2,18},{18,2},{3,19},{19,3},{4,20},{20... | collective-permute-start | bytes 1572872 | tf_op jit(solution)/shard_map/ppermute | solution.py:331
  83.9 4.7 %collective-permute-start.16 = (f32[256,512]{1,0:T(8,128)S(1)}, f32[256,512]{1,0:T(8,128)S(1)}, u32[]{:S(2)}, u32[]{:S(2)}) collective-permute-start(f32[256,512]{1,0:T(8,128)S(1)} %get-tuple-element.88.refs_8_), channel_id=1, source_target_pairs={{0,16},{16,0},{1,17},{17,1},{2,18},{18,2},{3,19},{19,3},{4,20},{20... | collective-permute-start | bytes 1572872 | tf_op jit(solution)/shard_map/ppermute | solution.py:331
  86.7 6.0 %collective-permute-start.19 = (f32[256,512]{1,0:T(8,128)S(1)}, f32[256,512]{1,0:T(8,128)S(1)}, u32[]{:S(2)}, u32[]{:S(2)}) collective-permute-start(f32[256,512]{1,0:T(8,128)S(1)} %get-tuple-element.95.refs_11_), channel_id=1, source_target_pairs={{0,16},{16,0},{1,17},{17,1},{2,18},{18,2},{3,19},{19,3},{4,20},{20... | collective-permute-start | bytes 1572872 | tf_op jit(solution)/shard_map/ppermute | solution.py:331
  86.8 6.0 %collective-permute-start.20 = (f32[256,512]{1,0:T(8,128)S(1)}, f32[256,512]{1,0:T(8,128)S(1)}, u32[]{:S(2)}, u32[]{:S(2)}) collective-permute-start(f32[256,512]{1,0:T(8,128)S(1)} %get-tuple-element.96.refs_12_), channel_id=1, source_target_pairs={{0,16},{16,0},{1,17},{17,1},{2,18},{18,2},{3,19},{19,3},{4,20},{20... | collective-permute-start | bytes 1572872 | tf_op jit(solution)/shard_map/ppermute | solution.py:331
  87.3 19.3 %collective-permute-start.23 = (f32[1032,128]{1,0:T(8,128)S(1)}, f32[1032,128]{1,0:T(8,128)S(1)}, u32[]{:S(2)}, u32[]{:S(2)}) collective-permute-start(f32[1032,128]{1,0:T(8,128)S(1)} %get-tuple-element.115), channel_id=1, source_target_pairs={{2,0},{3,2},{6,4},{7,6},{10,8},{11,10},{14,12},{15,14},{18,16},{19... | collective-permute-start | bytes 1585160 | tf_op jit(solution)/shard_map/ppermute | solution.py:324
  88.6 20.0 %collective-permute-start.24 = (f32[1032,128]{1,0:T(8,128)S(1)}, f32[1032,128]{1,0:T(8,128)S(1)}, u32[]{:S(2)}, u32[]{:S(2)}) collective-permute-start(f32[1032,128]{1,0:T(8,128)S(1)} %collective-permute-done.14.refs_13_.refs_8_.refs_32_), channel_id=1, source_target_pairs={{0,1},{1,0},{2,3},{3,2},{4,5},{5,4},{6,7},{7,6},{8,9},{9,8},{10,11... | collective-permute-start | bytes 1585160 | tf_op jit(solution)/shard_map/ppermute | solution.py:324
  90.2 23.8 %collective-permute-start.25 = (f32[1032,128]{1,0:T(8,128)S(1)}, f32[1032,128]{1,0:T(8,128)S(1)}, u32[]{:S(2)}, u32[]{:S(2)}) collective-permute-start(f32[1032,128]{1,0:T(8,128)S(1)} %collective-permute-done.18.refs_9_.refs_33_.refs_2_.refs_8_), channel_id=1, source_target_pairs={{0,1},{1,0},{4,5},{5,4},{8,9},{9,8},{12,13},{13,12},{16,17},{17,16... | collective-permute-start | bytes 1585160 | tf_op jit(solution)/shard_map/ppermute | solution.py:324
  (16 other events, 93.6 us)

commit v8 on v7

--- a/solution.py
+++ b/solution.py
@@ -13,6 +13,7 @@
 PLANE = 4
 CHUNKS = 4
 VMEM_LIMIT = 32 * 1024 * 1024
+FIRST_LIMIT = 60 * 1024 * 1024
 LAST_LIMIT = 24 * 1024 * 1024
 HALVES = 2
 
@@ -131,7 +132,7 @@
         pltpu.SemaphoreType.DMA((5 * CHUNKS + HALVES,)),
     ]
     outs = [turned, turned] + [square] * HALVES + [sent] * (CHUNKS - 1)
-    return call(kernel, [], [energies], [own], outs, pl.ANY, scratch)
+    return call(kernel, [], [energies], [own], outs, pl.ANY, scratch, FIRST_LIMIT)
 
 
 def arrays_of(pieces):

time: 124 us -> 120 us (0.968)
  starting transfers between devices: 36.2 us -> 46.4 us
  waiting for transfers between devices: 38.4 us -> 28.7 us
  local copies, waits for them, and re-layouts: 7.13 us -> 2.34 us
  Pallas kernels: 32.7 us -> 34.1 us
  other arithmetic: 5.77 us -> 4.39 us
    ppermute x14, starting transfers between devices: 15.5 us -> 27 us  [within(): lax.ppermute(block, 'occ', [(g + a, g + b) for g in planes for a, b in mo...]
    ppermute x4, waiting for transfers between devices: 19.2 us -> 12 us  [up(): lax.ppermute(block, 'occ', [(g, g + PLANE) for g in range(groups - PLANE)])]
    unnamed x24 -> x22, local copies, waits for them, and re-layouts: 5.63 us -> 0.84 us
    ppermute x14, waiting for transfers between devices: 14.9 us -> 12.4 us  [within(): lax.ppermute(block, 'occ', [(g + a, g + b) for g in planes for a, b in mo...]
    pallas_call x7, Pallas kernels: 32.7 us -> 34.1 us  [call(): pl.pallas_call(kernel, out_shape=outputs, in_specs=[pl.BlockSpec(memory_s...]
  transfers between devices with their start and end apart: 28 -> 28, of which waited for: 11 -> 11; matrix products, arithmetic and copies ran while one was open for 5% -> 4% of each run, Pallas kernels for 21% -> 23%
where the time goes in v8:
time: 120 us
  starting transfers between devices  46.4 us (39%)
  Pallas kernels  34.1 us (28%)
  waiting for transfers between devices  28.7 us (24%)
  other arithmetic  4.39 us (4%)
  between operations  3.74 us (3%)
  local copies, waits for them, and re-layouts  2.34 us (2%)
    pallas_call x7, Pallas kernels, call(): pl.pallas_call(kernel, out_shape=outputs, in_specs=[pl.BlockSpec(memory_s...  34.1 us
    ppermute x14, starting transfers between devices, within(): lax.ppermute(block, 'occ', [(g + a, g + b) for g in planes for a, b in mo...  27 us
    ppermute x4, starting transfers between devices, up(): lax.ppermute(block, 'occ', [(g, g + PLANE) for g in range(groups - PLANE)])  17.1 us
    ppermute x14, waiting for transfers between devices, within(): lax.ppermute(block, 'occ', [(g + a, g + b) for g in planes for a, b in mo...  12.4 us
    ppermute x4, waiting for transfers between devices, up(): lax.ppermute(block, 'occ', [(g, g + PLANE) for g in range(groups - PLANE)])  12 us
    ppermute x10, waiting for transfers between devices, totals(): lax.ppermute(part, 'aux', [(0, 1), (1, 0)])  4.31 us
    select_n x3, other arithmetic, on_device(): jnp.where(odd_y, came, up_part)  3.34 us
  transfers between devices with their start and end apart: 28, of which 11 were waited for; matrix products, arithmetic and copies ran while one was open for 4% of the time, Pallas kernels for 23%

profile of v8, /device:TPU:0, one launch (start us, length us, event | category | flops | bytes accessed | tf_op | source)
XLA Modules:
  0.0 119.6 jit_solution(10515879292695664334)
XLA Ops:
  2.1 5.0 %collective-permute-start = (f32[1032,128]{1,0:T(8,128)S(1)}, f32[1032,128]{1,0:T(8,128)S(1)}, u32[]{:S(2)}, u32[]{:S(2)}) collective-permute-start(f32[1032,128]{1,0:T(8,128)S(1)} %pad_maximum_fusion.refs_34_.refs_14_), channel_id=1, source_target_pairs={{0,4},{1,5},{2,6},{3,7},{4,8},{5,9},{6,10},{7,11},{8,12},{9,13},{1... | collective-permute-start | bytes 1585160 | tf_op jit(solution)/shard_map/ppermute | solution.py:328
  7.1 3.5 %collective-permute-start.2 = (f32[1032,128]{1,0:T(8,128)S(1)}, f32[1032,128]{1,0:T(8,128)S(1)}, u32[]{:S(2)}, u32[]{:S(2)}) collective-permute-start(f32[1032,128]{1,0:T(8,128)S(1)} %pad_maximum_fusion.refs_34_.refs_14_), channel_id=1, source_target_pairs={{0,2},{1,3},{4,6},{5,7},{8,10},{9,11},{12,14},{13,15},{16,18},{17,... | collective-permute-start | bytes 1585160 | tf_op jit(solution)/shard_map/ppermute | solution.py:325
  10.6 3.4 %collective-permute-start.1 = (f32[1032,128]{1,0:T(8,128)S(1)}, f32[1032,128]{1,0:T(8,128)S(1)}, u32[]{:S(2)}, u32[]{:S(2)}) collective-permute-start(f32[1032,128]{1,0:T(8,128)S(1)} %pad_maximum_fusion.refs_34_.refs_14_), channel_id=1, source_target_pairs={{0,1},{2,3},{1,0},{4,5},{6,7},{5,4},{8,9},{10,11},{9,8},{12,13},{1... | collective-permute-start | bytes 1585160 | tf_op jit(solution)/shard_map/ppermute | solution.py:325
  14.0 5.1 %shard_map.46 = (bf16[4,512,256]{2,1,0:T(8,128)(2,1)}, bf16[4,512,256]{2,1,0:T(8,128)(2,1)}, f32[256,512]{1,0:T(8,128)}, f32[256,512]{1,0:T(8,128)}, f32[1032,12...) custom-call(f32[8,128]{1,0:T(8,128)} %copy-done.9, f32[4096,128]{1,0:T(8,128)} %bitcast.15), custom_call_target="tpu_custom_call" | custom-call | tf_op jit(solution)/shard_map/pallas_call | solution.py:85
  19.1 3.6 %collective-permute-start.5 = (f32[1032,128]{1,0:T(8,128)}, f32[1032,128]{1,0:T(8,128)S(1)}, u32[]{:S(2)}, u32[]{:S(2)}) collective-permute-start(f32[1032,128]{1,0:T(8,128)} %get-tuple-element.64), channel_id=1, source_target_pairs={{0,4},{1,5},{2,6},{3,7},{4,8},{5,9},{6,10},{7,11},{8,12},{9,13},{1... | collective-permute-start | bytes 1585160 | tf_op jit(solution)/shard_map/ppermute | solution.py:328
  22.7 2.1 %broadcast_select_fusion.5 = (f32[1032,128]{1,0:T(8,128)}, f32[1032,128]{1,0:T(8,128)}) fusion(f32[1032,128]{1,0:T(8,128)S(1)} %collective-permute-done.refs_2_.refs_20_, f32[1032,128]{1,0:T(8,128)} %get-tuple-element.64, pred[]{:T(512)S(6)} %eq.44, pred[]{:T(512)S(6)} %eq.43), kind=kLoop, calls=%fused_computation.6 | loop fusion | flops 264192 | bytes 2113538 | tf_op jit(solution)/shard_map/jit(_where)/select_n | solution.py:376
  33.4 4.3 %collective-permute-start.10 = (f32[1032,128]{1,0:T(8,128)}, f32[1032,128]{1,0:T(8,128)S(1)}, u32[]{:S(2)}, u32[]{:S(2)}) collective-permute-start(f32[1032,128]{1,0:T(8,128)} %get-tuple-element.73), channel_id=1, source_target_pairs={{0,4},{1,5},{2,6},{3,7},{4,8},{5,9},{6,10},{7,11},{8,12},{9,13},{1... | collective-permute-start | bytes 1585160 | tf_op jit(solution)/shard_map/ppermute | solution.py:328
  38.8 1.6 %collective-permute-start.9 = (f32[1032,128]{1,0:T(8,128)S(1)}, f32[1032,128]{1,0:T(8,128)S(1)}, u32[]{:S(2)}, u32[]{:S(2)}) collective-permute-start(f32[1032,128]{1,0:T(8,128)S(1)} %get-tuple-element.75), channel_id=1, source_target_pairs={{0,2},{2,0},{1,3},{3,1},{4,6},{6,4},{5,7},{7,5},{8,10},{10,8},{9,1... | collective-permute-start | bytes 1585160 | tf_op jit(solution)/shard_map/ppermute | solution.py:325
  41.9 5.5 %collective-permute-done.10.refs_4_.refs_22_ = f32[1032,128]{1,0:T(8,128)S(1)} collective-permute-done((f32[1032,128]{1,0:T(8,128)}, f32[1032,128]{1,0:T(8,128)S(1)}, u32[]{:S(2)}, u32[]{:S(2)}) %collective-permute-start.10) | collective-permute-done | bytes 528416 | tf_op jit(solution)/shard_map/ppermute | solution.py:328
  47.4 4.3 %collective-permute-start.11 = (f32[1032,128]{1,0:T(8,128)S(1)}, f32[1032,128]{1,0:T(8,128)S(1)}, u32[]{:S(2)}, u32[]{:S(2)}) collective-permute-start(f32[1032,128]{1,0:T(8,128)S(1)} %copy-done.8), channel_id=1, source_target_pairs={{0,4},{1,5},{2,6},{3,7},{4,8},{5,9},{6,10},{7,11},{8,12},{9,13},{1... | collective-permute-start | bytes 1585160 | tf_op jit(solution)/shard_map/ppermute | solution.py:328
  51.8 1.6 %collective-permute-start.14 = (f32[1032,128]{1,0:T(8,128)S(1)}, f32[1032,128]{1,0:T(8,128)S(1)}, u32[]{:S(2)}, u32[]{:S(2)}) collective-permute-start(f32[1032,128]{1,0:T(8,128)S(1)} %get-tuple-element.86), channel_id=1, source_target_pairs={{0,2},{2,0},{1,3},{3,1},{4,6},{6,4},{5,7},{7,5},{8,10},{10,8},{9,1... | collective-permute-start | bytes 1585160 | tf_op jit(solution)/shard_map/ppermute | solution.py:325
  55.0 5.2 %collective-permute-done.11.refs_5_.refs_23_ = f32[1032,128]{1,0:T(8,128)S(1)} collective-permute-done((f32[1032,128]{1,0:T(8,128)S(1)}, f32[1032,128]{1,0:T(8,128)S(1)}, u32[]{:S(2)}, u32[]{:S(2)}) %collective-permute-start.11) | collective-permute-done | bytes 528416 | tf_op jit(solution)/shard_map/ppermute | solution.py:328
  60.4 3.7 %collective-permute-done.14.refs_13_.refs_8_.refs_32_ = f32[1032,128]{1,0:T(8,128)S(1)} collective-permute-done((f32[1032,128]{1,0:T(8,128)S(1)}, f32[1032,128]{1,0:T(8,128)S(1)}, u32[]{:S(2)}, u32[]{:S(2)}) %collective-permute-start.14) | collective-permute-done | bytes 528416 | tf_op jit(solution)/shard_map/ppermute | solution.py:325
  68.2 6.5 %shard_map.47 = (f32[256,512]{1,0:T(8,128)S(1)}, f32[256,512]{1,0:T(8,128)S(1)}, f32[256,512]{1,0:T(8,128)S(1)}, f32[256,512]{1,0:T(8,128)S(1)}, f32[256,512]{1,0:T(8,128)S(1)}, /*index=5*/f32[256,512]{1,0:T(8,128)S(1)}) custom-call(s32[4]{0:T(128)S(1)} %pad_add_fusion.flag_ref.refs_1_, bf16[4,512,256]{2,1,0:T(8,128)(2,1)S(1)} %copy-done, ...), custom_call_target="tpu_custom_call" | custom-call | tf_op jit(solution)/shard_map/pallas_call | solution.py:85
  74.6 3.0 %collective-permute-done.18.refs_9_.refs_33_.refs_2_.refs_8_ = f32[1032,128]{1,0:T(8,128)S(1)} collective-permute-done((f32[1032,128]{1,0:T(8,128)S(1)}, f32[1032,128]{1,0:T(8,128)S(1)}, u32[]{:S(2)}, u32[]{:S(2)}) %collective-permute-start.18) | collective-permute-done | bytes 528416 | tf_op jit(solution)/shard_map/ppermute | solution.py:325
  77.6 1.9 %collective-permute-done.17.refs_7_.refs_28_.refs_4_.refs_10_ = f32[1032,128]{1,0:T(8,128)S(1)} collective-permute-done((f32[1032,128]{1,0:T(8,128)S(1)}, f32[1032,128]{1,0:T(8,128)S(1)}, u32[]{:S(2)}, u32[]{:S(2)}) %collective-permute-start.17) | collective-permute-done | bytes 528416 | tf_op jit(solution)/shard_map/ppermute | solution.py:325
  79.6 2.3 %shard_map.48 = (f32[256,512]{1,0:T(8,128)S(1)}, f32[256,512]{1,0:T(8,128)S(1)}, f32[256,512]{1,0:T(8,128)S(1)}, f32[256,512]{1,0:T(8,128)S(1)}) custom-call(s32[4]{0:T(128)S(1)} %pad_add_fusion.flag_ref.refs_1_, bf16[4,512,256]{2,1,0:T(8,128)(2,1)S(1)} %copy-done, bf16[4,512,256]{2,1,0:T(8,128)(2,1)S(1)} %copy-done.1, ...), custom_call_target="tpu_custom_call" | custom-call | tf_op jit(solution)/shard_map/pallas_call | solution.py:85
  83.8 1.9 %collective-permute-start.24 = (f32[1032,128]{1,0:T(8,128)S(1)}, f32[1032,128]{1,0:T(8,128)S(1)}, u32[]{:S(2)}, u32[]{:S(2)}) collective-permute-start(f32[1032,128]{1,0:T(8,128)S(1)} %collective-permute-done.14.refs_13_.refs_8_.refs_32_), channel_id=1, source_target_pairs={{0,1},{1,0},{2,3},{3,2},{4,5},{5,4},{6,7},{7,6},{8,9},{9,8},{10,11... | collective-permute-start | bytes 1585160 | tf_op jit(solution)/shard_map/ppermute | solution.py:325
  85.8 4.2 %collective-permute-start.25 = (f32[1032,128]{1,0:T(8,128)S(1)}, f32[1032,128]{1,0:T(8,128)S(1)}, u32[]{:S(2)}, u32[]{:S(2)}) collective-permute-start(f32[1032,128]{1,0:T(8,128)S(1)} %collective-permute-done.18.refs_9_.refs_33_.refs_2_.refs_8_), channel_id=1, source_target_pairs={{0,1},{1,0},{4,5},{5,4},{8,9},{9,8},{12,13},{13,12},{16,17},{17,16... | collective-permute-start | bytes 1585160 | tf_op jit(solution)/shard_map/ppermute | solution.py:325
  92.7 11.3 %shard_map.49.refs_7_ = f32[4096,128]{1,0:T(8,128)S(1)} custom-call(f32[5]{0:T(128)S(1)} %stack.34.refs_0_, s32[4]{0:T(128)S(1)} %pad_add_fusion.flag_ref.refs_1_, f32[1,512]{1,0:T(1,128)S(1)} %bitcast.17, f32[256,512]{1,0:T(8,128)S(1)} %copy-done.5, f32[256,512]{1,0:T(8,128)S(1)} %copy-done.6, f32[256,512]{1,0:T(8,128)S(1)} %collective-permute-done.3.refs_5_, ...), custom_call_target="tpu_custom_call" | custom-call | tf_op jit(solution)/shard_map/pallas_call | solution.py:85
  104.1 1.9 %shard_map.50 = (f32[256,512]{1,0:T(8,128)S(1)}, f32[256,512]{1,0:T(8,128)S(1)}) custom-call(s32[4]{0:T(128)S(1)} %pad_add_fusion.flag_ref.refs_1_, bf16[4,512,256]{2,1,0:T(8,128)(2,1)S(1)} %copy-done, bf16[4,512,256]{2,1,0:T(8,128)(2,1)S(1)} %copy-done.1, f32[1032,128]{1,0:T(8,128)S(1)} %collective-permute-done.18.refs_9_.refs_33_.refs_2_.refs_8_, ...), custom_call_target="tpu_custom_call" | custom-call | tf_op jit(solution)/shard_map/pallas_call | solution.py:85
  106.0 3.7 %collective-permute-done.25.refs_6_.refs_13_ = f32[1032,128]{1,0:T(8,128)S(1)} collective-permute-done((f32[1032,128]{1,0:T(8,128)S(1)}, f32[1032,128]{1,0:T(8,128)S(1)}, u32[]{:S(2)}, u32[]{:S(2)}) %collective-permute-start.25) | collective-permute-done | bytes 528416 | tf_op jit(solution)/shard_map/ppermute | solution.py:325
  109.7 2.1 %shard_map.51 = (f32[256,512]{1,0:T(8,128)S(1)}, f32[256,512]{1,0:T(8,128)S(1)}) custom-call(s32[4]{0:T(128)S(1)} %pad_add_fusion.flag_ref.refs_1_, bf16[4,512,256]{2,1,0:T(8,128)(2,1)S(1)} %copy-done, bf16[4,512,256]{2,1,0:T(8,128)(2,1)S(1)} %copy-done.1, f32[256,512]{1,0:T(8,128)S(1)} %get-tuple-element.101.refs_2_, ...), custom_call_target="tpu_custom_call" | custom-call | tf_op jit(solution)/shard_map/pallas_call | solution.py:85
  114.5 5.0 %shard_map.52 = f32[4096,128]{1,0:T(8,128)} custom-call(f32[5]{0:T(128)S(1)} %stack.34.refs_0_, s32[4]{0:T(128)S(1)} %pad_add_fusion.flag_ref.refs_1_, f32[1,512]{1,0:T(1,128)S(1)} %bitcast.18, f32[256,512]{1,0:T(8,128)S(1)} %get-tuple-element.103.refs_3_, f32[256,512]{1,0:T(8,128)S(1)} %get-tuple-element.104.refs_4_, ...), custom_call_target="tpu_custom_call" | custom-call | tf_op jit(solution)/shard_map/pallas_call | solution.py:85
  (72 shorter events, 23.3 us)
Async XLA Ops:
  2.1 17.0 %collective-permute-start = (f32[1032,128]{1,0:T(8,128)S(1)}, f32[1032,128]{1,0:T(8,128)S(1)}, u32[]{:S(2)}, u32[]{:S(2)}) collective-permute-start(f32[1032,128]{1,0:T(8,128)S(1)} %pad_maximum_fusion.refs_34_.refs_14_), channel_id=1, source_target_pairs={{0,4},{1,5},{2,6},{3,7},{4,8},{5,9},{6,10},{7,11},{8,12},{9,13},{1... | collective-permute-start | bytes 1585160 | tf_op jit(solution)/shard_map/ppermute | solution.py:328
  7.1 17.8 %collective-permute-start.2 = (f32[1032,128]{1,0:T(8,128)S(1)}, f32[1032,128]{1,0:T(8,128)S(1)}, u32[]{:S(2)}, u32[]{:S(2)}) collective-permute-start(f32[1032,128]{1,0:T(8,128)S(1)} %pad_maximum_fusion.refs_34_.refs_14_), channel_id=1, source_target_pairs={{0,2},{1,3},{4,6},{5,7},{8,10},{9,11},{12,14},{13,15},{16,18},{17,... | collective-permute-start | bytes 1585160 | tf_op jit(solution)/shard_map/ppermute | solution.py:325
  10.6 15.1 %collective-permute-start.1 = (f32[1032,128]{1,0:T(8,128)S(1)}, f32[1032,128]{1,0:T(8,128)S(1)}, u32[]{:S(2)}, u32[]{:S(2)}) collective-permute-start(f32[1032,128]{1,0:T(8,128)S(1)} %pad_maximum_fusion.refs_34_.refs_14_), channel_id=1, source_target_pairs={{0,1},{2,3},{1,0},{4,5},{6,7},{5,4},{8,9},{10,11},{9,8},{12,13},{1... | collective-permute-start | bytes 1585160 | tf_op jit(solution)/shard_map/ppermute | solution.py:325
  19.1 14.3 %collective-permute-start.5 = (f32[1032,128]{1,0:T(8,128)}, f32[1032,128]{1,0:T(8,128)S(1)}, u32[]{:S(2)}, u32[]{:S(2)}) collective-permute-start(f32[1032,128]{1,0:T(8,128)} %get-tuple-element.64), channel_id=1, source_target_pairs={{0,4},{1,5},{2,6},{3,7},{4,8},{5,9},{6,10},{7,11},{8,12},{9,13},{1... | collective-permute-start | bytes 1585160 | tf_op jit(solution)/shard_map/ppermute | solution.py:328
  25.7 13.2 %collective-permute-start.8 = (f32[1032,128]{1,0:T(8,128)}, f32[1032,128]{1,0:T(8,128)S(1)}, u32[]{:S(2)}, u32[]{:S(2)}) collective-permute-start(f32[1032,128]{1,0:T(8,128)} %get-tuple-element.66), channel_id=1, source_target_pairs={{0,2},{2,0},{1,3},{3,1},{4,6},{6,4},{5,7},{7,5},{8,10},{10,8},{9,1... | collective-permute-start | bytes 1585160 | tf_op jit(solution)/shard_map/ppermute | solution.py:325
  27.2 13.2 %collective-permute-start.6 = (f32[1032,128]{1,0:T(8,128)}, f32[1032,128]{1,0:T(8,128)S(1)}, u32[]{:S(2)}, u32[]{:S(2)}) collective-permute-start(f32[1032,128]{1,0:T(8,128)} %get-tuple-element.65), channel_id=1, source_target_pairs={{0,1},{1,0},{2,3},{3,2},{4,5},{5,4},{6,7},{7,6},{8,9},{9,8},{10,11... | collective-permute-start | bytes 1585160 | tf_op jit(solution)/shard_map/ppermute | solution.py:325
  33.4 14.1 %collective-permute-start.10 = (f32[1032,128]{1,0:T(8,128)}, f32[1032,128]{1,0:T(8,128)S(1)}, u32[]{:S(2)}, u32[]{:S(2)}) collective-permute-start(f32[1032,128]{1,0:T(8,128)} %get-tuple-element.73), channel_id=1, source_target_pairs={{0,4},{1,5},{2,6},{3,7},{4,8},{5,9},{6,10},{7,11},{8,12},{9,13},{1... | collective-permute-start | bytes 1585160 | tf_op jit(solution)/shard_map/ppermute | solution.py:328
  38.8 13.0 %collective-permute-start.9 = (f32[1032,128]{1,0:T(8,128)S(1)}, f32[1032,128]{1,0:T(8,128)S(1)}, u32[]{:S(2)}, u32[]{:S(2)}) collective-permute-start(f32[1032,128]{1,0:T(8,128)S(1)} %get-tuple-element.75), channel_id=1, source_target_pairs={{0,2},{2,0},{1,3},{3,1},{4,6},{6,4},{5,7},{7,5},{8,10},{10,8},{9,1... | collective-permute-start | bytes 1585160 | tf_op jit(solution)/shard_map/ppermute | solution.py:325
  40.4 13.0 %collective-permute-start.7 = (f32[1032,128]{1,0:T(8,128)S(1)}, f32[1032,128]{1,0:T(8,128)S(1)}, u32[]{:S(2)}, u32[]{:S(2)}) collective-permute-start(f32[1032,128]{1,0:T(8,128)S(1)} %get-tuple-element.74), channel_id=1, source_target_pairs={{0,1},{1,0},{2,3},{3,2},{4,5},{5,4},{6,7},{7,6},{8,9},{9,8},{10,11... | collective-permute-start | bytes 1585160 | tf_op jit(solution)/shard_map/ppermute | solution.py:325
  47.4 12.8 %collective-permute-start.11 = (f32[1032,128]{1,0:T(8,128)S(1)}, f32[1032,128]{1,0:T(8,128)S(1)}, u32[]{:S(2)}, u32[]{:S(2)}) collective-permute-start(f32[1032,128]{1,0:T(8,128)S(1)} %copy-done.8), channel_id=1, source_target_pairs={{0,4},{1,5},{2,6},{3,7},{4,8},{5,9},{6,10},{7,11},{8,12},{9,13},{1... | collective-permute-start | bytes 1585160 | tf_op jit(solution)/shard_map/ppermute | solution.py:328
  51.8 12.2 %collective-permute-start.14 = (f32[1032,128]{1,0:T(8,128)S(1)}, f32[1032,128]{1,0:T(8,128)S(1)}, u32[]{:S(2)}, u32[]{:S(2)}) collective-permute-start(f32[1032,128]{1,0:T(8,128)S(1)} %get-tuple-element.86), channel_id=1, source_target_pairs={{0,2},{2,0},{1,3},{3,1},{4,6},{6,4},{5,7},{7,5},{8,10},{10,8},{9,1... | collective-permute-start | bytes 1585160 | tf_op jit(solution)/shard_map/ppermute | solution.py:325
  53.4 12.2 %collective-permute-start.12 = (f32[1032,128]{1,0:T(8,128)S(1)}, f32[1032,128]{1,0:T(8,128)S(1)}, u32[]{:S(2)}, u32[]{:S(2)}) collective-permute-start(f32[1032,128]{1,0:T(8,128)S(1)} %get-tuple-element.80), channel_id=1, source_target_pairs={{0,1},{1,0},{2,3},{3,2},{4,5},{5,4},{6,7},{7,6},{8,9},{9,8},{10,11... | collective-permute-start | bytes 1585160 | tf_op jit(solution)/shard_map/ppermute | solution.py:325
  64.1 13.5 %collective-permute-start.18 = (f32[1032,128]{1,0:T(8,128)S(1)}, f32[1032,128]{1,0:T(8,128)S(1)}, u32[]{:S(2)}, u32[]{:S(2)}) collective-permute-start(f32[1032,128]{1,0:T(8,128)S(1)} %get-tuple-element.94), channel_id=1, source_target_pairs={{0,2},{2,0},{1,3},{3,1},{4,6},{6,4},{5,7},{7,5},{8,10},{10,8},{9,1... | collective-permute-start | bytes 1585160 | tf_op jit(solution)/shard_map/ppermute | solution.py:325
  65.6 14.0 %collective-permute-start.17 = (f32[1032,128]{1,0:T(8,128)S(1)}, f32[1032,128]{1,0:T(8,128)S(1)}, u32[]{:S(2)}, u32[]{:S(2)}) collective-permute-start(f32[1032,128]{1,0:T(8,128)S(1)} %get-tuple-element.93), channel_id=1, source_target_pairs={{0,1},{1,0},{2,3},{3,2},{4,5},{5,4},{6,7},{7,6},{8,9},{9,8},{10,11... | collective-permute-start | bytes 1585160 | tf_op jit(solution)/shard_map/ppermute | solution.py:325
  67.1 14.8 %collective-permute-start.3 = (f32[256,512]{1,0:T(8,128)S(1)}, f32[256,512]{1,0:T(8,128)S(1)}, u32[]{:S(2)}, u32[]{:S(2)}) collective-permute-start(f32[256,512]{1,0:T(8,128)S(1)} %copy-done.5), channel_id=1, source_target_pairs={{0,16},{16,0},{1,17},{17,1},{2,18},{18,2},{3,19},{19,3},{4,20},{20... | collective-permute-start | bytes 1572872 | tf_op jit(solution)/shard_map/ppermute | solution.py:332
  67.1 15.3 %collective-permute-start.4 = (f32[256,512]{1,0:T(8,128)S(1)}, f32[256,512]{1,0:T(8,128)S(1)}, u32[]{:S(2)}, u32[]{:S(2)}) collective-permute-start(f32[256,512]{1,0:T(8,128)S(1)} %copy-done.6), channel_id=1, source_target_pairs={{0,16},{16,0},{1,17},{17,1},{2,18},{18,2},{3,19},{19,3},{4,20},{20... | collective-permute-start | bytes 1572872 | tf_op jit(solution)/shard_map/ppermute | solution.py:332
  67.6 18.2 %collective-permute-start.13 = (f32[1032,128]{1,0:T(8,128)S(1)}, f32[1032,128]{1,0:T(8,128)S(1)}, u32[]{:S(2)}, u32[]{:S(2)}) collective-permute-start(f32[1032,128]{1,0:T(8,128)S(1)} %broadcast_select_fusion.1), channel_id=1, source_target_pairs={{0,1},{1,3},{3,2},{2,0},{4,5},{5,7},{7,6},{6,4},{8,9},{9,11},{11,1... | collective-permute-start | bytes 1585160 | tf_op jit(solution)/shard_map/ppermute | solution.py:325
  77.6 4.9 %collective-permute-start.15 = (f32[256,512]{1,0:T(8,128)S(1)}, f32[256,512]{1,0:T(8,128)S(1)}, u32[]{:S(2)}, u32[]{:S(2)}) collective-permute-start(f32[256,512]{1,0:T(8,128)S(1)} %get-tuple-element.87.refs_7_), channel_id=1, source_target_pairs={{0,16},{16,0},{1,17},{17,1},{2,18},{18,2},{3,19},{19,3},{4,20},{20... | collective-permute-start | bytes 1572872 | tf_op jit(solution)/shard_map/ppermute | solution.py:332
  79.6 4.3 %collective-permute-start.16 = (f32[256,512]{1,0:T(8,128)S(1)}, f32[256,512]{1,0:T(8,128)S(1)}, u32[]{:S(2)}, u32[]{:S(2)}) collective-permute-start(f32[256,512]{1,0:T(8,128)S(1)} %get-tuple-element.88.refs_8_), channel_id=1, source_target_pairs={{0,16},{16,0},{1,17},{17,1},{2,18},{18,2},{3,19},{19,3},{4,20},{20... | collective-permute-start | bytes 1572872 | tf_op jit(solution)/shard_map/ppermute | solution.py:332
  81.9 8.1 %collective-permute-start.19 = (f32[256,512]{1,0:T(8,128)S(1)}, f32[256,512]{1,0:T(8,128)S(1)}, u32[]{:S(2)}, u32[]{:S(2)}) collective-permute-start(f32[256,512]{1,0:T(8,128)S(1)} %get-tuple-element.95.refs_11_), channel_id=1, source_target_pairs={{0,16},{16,0},{1,17},{17,1},{2,18},{18,2},{3,19},{19,3},{4,20},{20... | collective-permute-start | bytes 1572872 | tf_op jit(solution)/shard_map/ppermute | solution.py:332
  82.4 7.6 %collective-permute-start.20 = (f32[256,512]{1,0:T(8,128)S(1)}, f32[256,512]{1,0:T(8,128)S(1)}, u32[]{:S(2)}, u32[]{:S(2)}) collective-permute-start(f32[256,512]{1,0:T(8,128)S(1)} %get-tuple-element.96.refs_12_), channel_id=1, source_target_pairs={{0,16},{16,0},{1,17},{17,1},{2,18},{18,2},{3,19},{19,3},{4,20},{20... | collective-permute-start | bytes 1572872 | tf_op jit(solution)/shard_map/ppermute | solution.py:332
  82.5 21.5 %collective-permute-start.23 = (f32[1032,128]{1,0:T(8,128)S(1)}, f32[1032,128]{1,0:T(8,128)S(1)}, u32[]{:S(2)}, u32[]{:S(2)}) collective-permute-start(f32[1032,128]{1,0:T(8,128)S(1)} %get-tuple-element.115), channel_id=1, source_target_pairs={{2,0},{3,2},{6,4},{7,6},{10,8},{11,10},{14,12},{15,14},{18,16},{19... | collective-permute-start | bytes 1585160 | tf_op jit(solution)/shard_map/ppermute | solution.py:325
  83.8 22.1 %collective-permute-start.24 = (f32[1032,128]{1,0:T(8,128)S(1)}, f32[1032,128]{1,0:T(8,128)S(1)}, u32[]{:S(2)}, u32[]{:S(2)}) collective-permute-start(f32[1032,128]{1,0:T(8,128)S(1)} %collective-permute-done.14.refs_13_.refs_8_.refs_32_), channel_id=1, source_target_pairs={{0,1},{1,0},{2,3},{3,2},{4,5},{5,4},{6,7},{7,6},{8,9},{9,8},{10,11... | collective-permute-start | bytes 1585160 | tf_op jit(solution)/shard_map/ppermute | solution.py:325
  85.8 23.9 %collective-permute-start.25 = (f32[1032,128]{1,0:T(8,128)S(1)}, f32[1032,128]{1,0:T(8,128)S(1)}, u32[]{:S(2)}, u32[]{:S(2)}) collective-permute-start(f32[1032,128]{1,0:T(8,128)S(1)} %collective-permute-done.18.refs_9_.refs_33_.refs_2_.refs_8_), channel_id=1, source_target_pairs={{0,1},{1,0},{4,5},{5,4},{8,9},{9,8},{12,13},{13,12},{16,17},{17,16... | collective-permute-start | bytes 1585160 | tf_op jit(solution)/shard_map/ppermute | solution.py:325
  (15 other events, 143.4 us)

commit v9 on v8

--- a/solution.py
+++ b/solution.py
@@ -373,9 +373,9 @@
         if at < last:
             from_z.append(up(after(from_own[at + 1], came)))
             up_part = after(from_own[at + 1], came)
-            send_x, send_y = jnp.where(odd_x, came, up_part), jnp.where(odd_y, came, up_part)
-            send_x = after(send_x, swap_x[at - 1] if at else up_x)
-            send_y = after(send_y, swap_y[at - 1] if at else up_y)
+            send_x = after(jnp.where(odd_x, came, up_part), swap_x[at - 1] if at else up_x)
+            came, up_part, _ = lax.optimization_barrier((came, up_part, send_x))
+            send_y = after(jnp.where(odd_y, came, up_part), swap_y[at - 1] if at else up_y)
             if at == 0:
                 signs, flags = choices((send_x, send_y))
             swap_x.append(within(send_x, [(0, 1), (1, 0), (2, 3), (3, 2)]))
@@ -383,7 +383,7 @@
         else:
             cycle = within(after(turning, came, swap_x[last - 1]), [(0, 1), (1, 3), (3, 2), (2, 0)])
             send_x = after(jnp.where(odd_x, came, swap_y[0]), swap_x[last - 1])
-            send_y = after(jnp.where(odd_y, came, up_x), swap_y[last - 1])
+            send_y = after(jnp.where(odd_y, after(came, send_x), up_x), swap_y[last - 1])
             swap_x.append(within(send_x, [(0, 1), (1, 0), (2, 3), (3, 2)]))
             swap_y.append(within(send_y, [(0, 2), (2, 0), (1, 3), (3, 1)]))
         passed = []

time: 120 us -> 121 us (level)
  starting transfers between devices: 46.4 us -> 38.4 us
  waiting for transfers between devices: 28.7 us -> 34.7 us
  other arithmetic: 4.39 us -> 7.26 us
    ppermute x14, starting transfers between devices: 27 us -> 18.6 us  [within(): lax.ppermute(block, 'occ', [(g + a, g + b) for g in planes for a, b in mo...]
    ppermute x14, waiting for transfers between devices: 12.4 us -> 17.9 us  [within(): lax.ppermute(block, 'occ', [(g + a, g + b) for g in planes for a, b in mo...]
    select_n x0 -> x4, other arithmetic: none -> 3.17 us  [the longest x3 3.1 us: on_device(): jnp.where(odd_x, came, up_part)]
  transfers between devices with their start and end apart: 28 -> 28, of which waited for: 11 -> 15; matrix products, arithmetic and copies ran while one was open for 4% -> 6% of each run, Pallas kernels for 23% -> 22%
where the time goes in v9:
time: 121 us; the launch traced here: 120 us
  starting transfers between devices  38.4 us (32%)
  waiting for transfers between devices  34.7 us (29%)
  Pallas kernels  34.1 us (28%)
  other arithmetic  7.26 us (6%)
  between operations  3.67 us (3%)
  local copies, waits for them, and re-layouts  2.33 us (2%)
    pallas_call x7, Pallas kernels, call(): pl.pallas_call(kernel, out_shape=outputs, in_specs=[pl.BlockSpec(memory_s...  34.1 us
    ppermute x14, starting transfers between devices, within(): lax.ppermute(block, 'occ', [(g + a, g + b) for g in planes for a, b in mo...  18.6 us
    ppermute x14, waiting for transfers between devices, within(): lax.ppermute(block, 'occ', [(g + a, g + b) for g in planes for a, b in mo...  17.9 us
    ppermute x4, starting transfers between devices, up(): lax.ppermute(block, 'occ', [(g, g + PLANE) for g in range(groups - PLANE)])  17.1 us
    ppermute x4, waiting for transfers between devices, up(): lax.ppermute(block, 'occ', [(g, g + PLANE) for g in range(groups - PLANE)])  12.5 us
    ppermute x10, waiting for transfers between devices, totals(): lax.ppermute(part, 'aux', [(0, 1), (1, 0)])  4.31 us
    select_n x3, other arithmetic, on_device(): jnp.where(odd_x, came, up_part)  3.1 us
    select_n x3, other arithmetic, on_device(): jnp.where(odd_y, came, up_part)  3.09 us
  transfers between devices with their start and end apart: 28, of which 15 were waited for; matrix products, arithmetic and copies ran while one was open for 6% of the time, Pallas kernels for 22%

profile of v9, /device:TPU:0, one launch (start us, length us, event | category | flops | bytes accessed | tf_op | source)
XLA Modules:
  0.0 120.4 jit_solution(9280353519676856855)
XLA Ops:
  2.1 5.0 %collective-permute-start = (f32[1032,128]{1,0:T(8,128)S(1)}, f32[1032,128]{1,0:T(8,128)S(1)}, u32[]{:S(2)}, u32[]{:S(2)}) collective-permute-start(f32[1032,128]{1,0:T(8,128)S(1)} %pad_maximum_fusion.refs_34_.refs_14_), channel_id=1, source_target_pairs={{0,4},{1,5},{2,6},{3,7},{4,8},{5,9},{6,10},{7,11},{8,12},{9,13},{1... | collective-permute-start | bytes 1585160 | tf_op jit(solution)/shard_map/ppermute | solution.py:328
  7.1 3.4 %collective-permute-start.1 = (f32[1032,128]{1,0:T(8,128)S(1)}, f32[1032,128]{1,0:T(8,128)S(1)}, u32[]{:S(2)}, u32[]{:S(2)}) collective-permute-start(f32[1032,128]{1,0:T(8,128)S(1)} %pad_maximum_fusion.refs_34_.refs_14_), channel_id=1, source_target_pairs={{0,1},{2,3},{1,0},{4,5},{6,7},{5,4},{8,9},{10,11},{9,8},{12,13},{1... | collective-permute-start | bytes 1585160 | tf_op jit(solution)/shard_map/ppermute | solution.py:325
  10.5 3.5 %collective-permute-start.2 = (f32[1032,128]{1,0:T(8,128)S(1)}, f32[1032,128]{1,0:T(8,128)S(1)}, u32[]{:S(2)}, u32[]{:S(2)}) collective-permute-start(f32[1032,128]{1,0:T(8,128)S(1)} %pad_maximum_fusion.refs_34_.refs_14_), channel_id=1, source_target_pairs={{0,2},{1,3},{4,6},{5,7},{8,10},{9,11},{12,14},{13,15},{16,18},{17,... | collective-permute-start | bytes 1585160 | tf_op jit(solution)/shard_map/ppermute | solution.py:325
  14.0 5.1 %shard_map.46 = (bf16[4,512,256]{2,1,0:T(8,128)(2,1)}, bf16[4,512,256]{2,1,0:T(8,128)(2,1)}, f32[256,512]{1,0:T(8,128)}, f32[256,512]{1,0:T(8,128)}, f32[1032,12...) custom-call(f32[8,128]{1,0:T(8,128)} %copy-done.9, f32[4096,128]{1,0:T(8,128)} %bitcast.15), custom_call_target="tpu_custom_call" | custom-call | tf_op jit(solution)/shard_map/pallas_call | solution.py:85
  19.2 3.5 %collective-permute-start.5 = (f32[1032,128]{1,0:T(8,128)}, f32[1032,128]{1,0:T(8,128)S(1)}, u32[]{:S(2)}, u32[]{:S(2)}) collective-permute-start(f32[1032,128]{1,0:T(8,128)} %get-tuple-element.74), channel_id=1, source_target_pairs={{0,4},{1,5},{2,6},{3,7},{4,8},{5,9},{6,10},{7,11},{8,12},{9,13},{1... | collective-permute-start | bytes 1585160 | tf_op jit(solution)/shard_map/ppermute | solution.py:328
  22.7 1.9 %broadcast_select_fusion.9 = f32[1032,128]{1,0:T(8,128)} fusion(f32[1032,128]{1,0:T(8,128)S(1)} %collective-permute-done.refs_2_.refs_20_, f32[1032,128]{1,0:T(8,128)} %get-tuple-element.74, pred[]{:T(512)S(6)} %eq.43), kind=kLoop, calls=%fused_computation.10 | loop fusion | flops 132096 | bytes 1585153 | tf_op jit(solution)/shard_map/jit(_where)/select_n | solution.py:376
  24.6 1.9 %broadcast_select_fusion.5 = f32[1032,128]{1,0:T(8,128)} fusion(f32[1032,128]{1,0:T(8,128)S(1)} %collective-permute-done.refs_2_.refs_20_, f32[1032,128]{1,0:T(8,128)} %get-tuple-element.74, pred[]{:T(512)S(6)} %eq.44), kind=kLoop, calls=%fused_computation.6 | loop fusion | flops 132096 | bytes 1585153 | tf_op jit(solution)/shard_map/jit(_where)/select_n | solution.py:378
  31.6 1.8 %collective-permute-done.5.refs_3_.refs_21_ = f32[1032,128]{1,0:T(8,128)S(1)} collective-permute-done((f32[1032,128]{1,0:T(8,128)}, f32[1032,128]{1,0:T(8,128)S(1)}, u32[]{:S(2)}, u32[]{:S(2)}) %collective-permute-start.5) | collective-permute-done | bytes 528416 | tf_op jit(solution)/shard_map/ppermute | solution.py:328
  33.4 4.3 %collective-permute-start.10 = (f32[1032,128]{1,0:T(8,128)}, f32[1032,128]{1,0:T(8,128)S(1)}, u32[]{:S(2)}, u32[]{:S(2)}) collective-permute-start(f32[1032,128]{1,0:T(8,128)} %get-tuple-element.85), channel_id=1, source_target_pairs={{0,4},{1,5},{2,6},{3,7},{4,8},{5,9},{6,10},{7,11},{8,12},{9,13},{1... | collective-permute-start | bytes 1585160 | tf_op jit(solution)/shard_map/ppermute | solution.py:328
  41.8 5.6 %collective-permute-done.10.refs_4_.refs_22_ = f32[1032,128]{1,0:T(8,128)S(1)} collective-permute-done((f32[1032,128]{1,0:T(8,128)}, f32[1032,128]{1,0:T(8,128)S(1)}, u32[]{:S(2)}, u32[]{:S(2)}) %collective-permute-start.10) | collective-permute-done | bytes 528416 | tf_op jit(solution)/shard_map/ppermute | solution.py:328
  47.4 4.3 %collective-permute-start.11 = (f32[1032,128]{1,0:T(8,128)S(1)}, f32[1032,128]{1,0:T(8,128)S(1)}, u32[]{:S(2)}, u32[]{:S(2)}) collective-permute-start(f32[1032,128]{1,0:T(8,128)S(1)} %copy-done.8), channel_id=1, source_target_pairs={{0,4},{1,5},{2,6},{3,7},{4,8},{5,9},{6,10},{7,11},{8,12},{9,13},{1... | collective-permute-start | bytes 1585160 | tf_op jit(solution)/shard_map/ppermute | solution.py:328
  55.2 5.1 %collective-permute-done.11.refs_5_.refs_23_ = f32[1032,128]{1,0:T(8,128)S(1)} collective-permute-done((f32[1032,128]{1,0:T(8,128)S(1)}, f32[1032,128]{1,0:T(8,128)S(1)}, u32[]{:S(2)}, u32[]{:S(2)}) %collective-permute-start.11) | collective-permute-done | bytes 528416 | tf_op jit(solution)/shard_map/ppermute | solution.py:328
  60.4 2.8 %collective-permute-done.12.refs_9_.refs_6_.refs_27_ = f32[1032,128]{1,0:T(8,128)S(1)} collective-permute-done((f32[1032,128]{1,0:T(8,128)S(1)}, f32[1032,128]{1,0:T(8,128)S(1)}, u32[]{:S(2)}, u32[]{:S(2)}) %collective-permute-start.12) | collective-permute-done | bytes 528416 | tf_op jit(solution)/shard_map/ppermute | solution.py:325
  63.2 2.6 %collective-permute-done.14.refs_13_.refs_8_.refs_32_ = f32[1032,128]{1,0:T(8,128)S(1)} collective-permute-done((f32[1032,128]{1,0:T(8,128)S(1)}, f32[1032,128]{1,0:T(8,128)S(1)}, u32[]{:S(2)}, u32[]{:S(2)}) %collective-permute-start.14) | collective-permute-done | bytes 528416 | tf_op jit(solution)/shard_map/ppermute | solution.py:325
  69.8 6.5 %shard_map.47 = (f32[256,512]{1,0:T(8,128)S(1)}, f32[256,512]{1,0:T(8,128)S(1)}, f32[256,512]{1,0:T(8,128)S(1)}, f32[256,512]{1,0:T(8,128)S(1)}, f32[256,512]{1,0:T(8,128)S(1)}, /*index=5*/f32[256,512]{1,0:T(8,128)S(1)}) custom-call(s32[4]{0:T(128)S(1)} %pad_add_fusion.flag_ref.refs_1_, bf16[4,512,256]{2,1,0:T(8,128)(2,1)S(1)} %copy-done, ...), custom_call_target="tpu_custom_call" | custom-call | tf_op jit(solution)/shard_map/pallas_call | solution.py:85
  76.2 4.2 %collective-permute-done.18.refs_9_.refs_33_.refs_2_.refs_8_ = f32[1032,128]{1,0:T(8,128)S(1)} collective-permute-done((f32[1032,128]{1,0:T(8,128)S(1)}, f32[1032,128]{1,0:T(8,128)S(1)}, u32[]{:S(2)}, u32[]{:S(2)}) %collective-permute-start.18) | collective-permute-done | bytes 528416 | tf_op jit(solution)/shard_map/ppermute | solution.py:325
  80.9 2.3 %shard_map.48 = (f32[256,512]{1,0:T(8,128)S(1)}, f32[256,512]{1,0:T(8,128)S(1)}, f32[256,512]{1,0:T(8,128)S(1)}, f32[256,512]{1,0:T(8,128)S(1)}) custom-call(s32[4]{0:T(128)S(1)} %pad_add_fusion.flag_ref.refs_1_, bf16[4,512,256]{2,1,0:T(8,128)(2,1)S(1)} %copy-done, bf16[4,512,256]{2,1,0:T(8,128)(2,1)S(1)} %copy-done.1, ...), custom_call_target="tpu_custom_call" | custom-call | tf_op jit(solution)/shard_map/pallas_call | solution.py:85
  85.2 1.9 %collective-permute-done.13.refs_5_.refs_4_.refs_11_ = f32[1032,128]{1,0:T(8,128)S(1)} collective-permute-done((f32[1032,128]{1,0:T(8,128)S(1)}, f32[1032,128]{1,0:T(8,128)S(1)}, u32[]{:S(2)}, u32[]{:S(2)}) %collective-permute-start.13) | collective-permute-done | bytes 528416 | tf_op jit(solution)/shard_map/ppermute | solution.py:325
  87.2 3.0 %collective-permute-start.25 = (f32[1032,128]{1,0:T(8,128)S(1)}, f32[1032,128]{1,0:T(8,128)S(1)}, u32[]{:S(2)}, u32[]{:S(2)}) collective-permute-start(f32[1032,128]{1,0:T(8,128)S(1)} %collective-permute-done.18.refs_9_.refs_33_.refs_2_.refs_8_), channel_id=1, source_target_pairs={{0,1},{1,0},{4,5},{5,4},{8,9},{9,8},{12,13},{13,12},{16,17},{17,16... | collective-permute-start | bytes 1585160 | tf_op jit(solution)/shard_map/ppermute | solution.py:325
  93.0 11.3 %shard_map.49.refs_7_ = f32[4096,128]{1,0:T(8,128)S(1)} custom-call(f32[5]{0:T(128)S(1)} %stack.34.refs_0_, s32[4]{0:T(128)S(1)} %pad_add_fusion.flag_ref.refs_1_, f32[1,512]{1,0:T(1,128)S(1)} %bitcast.17, f32[256,512]{1,0:T(8,128)S(1)} %copy-done.5, f32[256,512]{1,0:T(8,128)S(1)} %copy-done.6, f32[256,512]{1,0:T(8,128)S(1)} %collective-permute-done.3.refs_5_, ...), custom_call_target="tpu_custom_call" | custom-call | tf_op jit(solution)/shard_map/pallas_call | solution.py:85
  104.3 1.9 %shard_map.50 = (f32[256,512]{1,0:T(8,128)S(1)}, f32[256,512]{1,0:T(8,128)S(1)}) custom-call(s32[4]{0:T(128)S(1)} %pad_add_fusion.flag_ref.refs_1_, bf16[4,512,256]{2,1,0:T(8,128)(2,1)S(1)} %copy-done, bf16[4,512,256]{2,1,0:T(8,128)(2,1)S(1)} %copy-done.1, f32[1032,128]{1,0:T(8,128)S(1)} %collective-permute-done.18.refs_9_.refs_33_.refs_2_.refs_8_, ...), custom_call_target="tpu_custom_call" | custom-call | tf_op jit(solution)/shard_map/pallas_call | solution.py:85
  106.2 4.3 %collective-permute-done.25.refs_6_.refs_13_ = f32[1032,128]{1,0:T(8,128)S(1)} collective-permute-done((f32[1032,128]{1,0:T(8,128)S(1)}, f32[1032,128]{1,0:T(8,128)S(1)}, u32[]{:S(2)}, u32[]{:S(2)}) %collective-permute-start.25) | collective-permute-done | bytes 528416 | tf_op jit(solution)/shard_map/ppermute | solution.py:325
  110.5 2.1 %shard_map.51 = (f32[256,512]{1,0:T(8,128)S(1)}, f32[256,512]{1,0:T(8,128)S(1)}) custom-call(s32[4]{0:T(128)S(1)} %pad_add_fusion.flag_ref.refs_1_, bf16[4,512,256]{2,1,0:T(8,128)(2,1)S(1)} %copy-done, bf16[4,512,256]{2,1,0:T(8,128)(2,1)S(1)} %copy-done.1, f32[256,512]{1,0:T(8,128)S(1)} %get-tuple-element.115.refs_2_, ...), custom_call_target="tpu_custom_call" | custom-call | tf_op jit(solution)/shard_map/pallas_call | solution.py:85
  115.3 5.0 %shard_map.52 = f32[4096,128]{1,0:T(8,128)} custom-call(f32[5]{0:T(128)S(1)} %stack.34.refs_0_, s32[4]{0:T(128)S(1)} %pad_add_fusion.flag_ref.refs_1_, f32[1,512]{1,0:T(1,128)S(1)} %bitcast.18, f32[256,512]{1,0:T(8,128)S(1)} %get-tuple-element.117.refs_3_, f32[256,512]{1,0:T(8,128)S(1)} %get-tuple-element.118.refs_4_, ...), custom_call_target="tpu_custom_call" | custom-call | tf_op jit(solution)/shard_map/pallas_call | solution.py:85
  (76 shorter events, 23.6 us)
Async XLA Ops:
  2.1 17.1 %collective-permute-start = (f32[1032,128]{1,0:T(8,128)S(1)}, f32[1032,128]{1,0:T(8,128)S(1)}, u32[]{:S(2)}, u32[]{:S(2)}) collective-permute-start(f32[1032,128]{1,0:T(8,128)S(1)} %pad_maximum_fusion.refs_34_.refs_14_), channel_id=1, source_target_pairs={{0,4},{1,5},{2,6},{3,7},{4,8},{5,9},{6,10},{7,11},{8,12},{9,13},{1... | collective-permute-start | bytes 1585160 | tf_op jit(solution)/shard_map/ppermute | solution.py:328
  7.1 17.5 %collective-permute-start.1 = (f32[1032,128]{1,0:T(8,128)S(1)}, f32[1032,128]{1,0:T(8,128)S(1)}, u32[]{:S(2)}, u32[]{:S(2)}) collective-permute-start(f32[1032,128]{1,0:T(8,128)S(1)} %pad_maximum_fusion.refs_34_.refs_14_), channel_id=1, source_target_pairs={{0,1},{2,3},{1,0},{4,5},{6,7},{5,4},{8,9},{10,11},{9,8},{12,13},{1... | collective-permute-start | bytes 1585160 | tf_op jit(solution)/shard_map/ppermute | solution.py:325
  10.5 16.1 %collective-permute-start.2 = (f32[1032,128]{1,0:T(8,128)S(1)}, f32[1032,128]{1,0:T(8,128)S(1)}, u32[]{:S(2)}, u32[]{:S(2)}) collective-permute-start(f32[1032,128]{1,0:T(8,128)S(1)} %pad_maximum_fusion.refs_34_.refs_14_), channel_id=1, source_target_pairs={{0,2},{1,3},{4,6},{5,7},{8,10},{9,11},{12,14},{13,15},{16,18},{17,... | collective-permute-start | bytes 1585160 | tf_op jit(solution)/shard_map/ppermute | solution.py:325
  19.2 14.2 %collective-permute-start.5 = (f32[1032,128]{1,0:T(8,128)}, f32[1032,128]{1,0:T(8,128)S(1)}, u32[]{:S(2)}, u32[]{:S(2)}) collective-permute-start(f32[1032,128]{1,0:T(8,128)} %get-tuple-element.74), channel_id=1, source_target_pairs={{0,4},{1,5},{2,6},{3,7},{4,8},{5,9},{6,10},{7,11},{8,12},{9,13},{1... | collective-permute-start | bytes 1585160 | tf_op jit(solution)/shard_map/ppermute | solution.py:328
  27.4 12.8 %collective-permute-start.6 = (f32[1032,128]{1,0:T(8,128)}, f32[1032,128]{1,0:T(8,128)S(1)}, u32[]{:S(2)}, u32[]{:S(2)}) collective-permute-start(f32[1032,128]{1,0:T(8,128)} %broadcast_select_fusion.9), channel_id=1, source_target_pairs={{0,1},{1,0},{2,3},{3,2},{4,5},{5,4},{6,7},{7,6},{8,9},{9,8},{10,11... | collective-permute-start | bytes 1585160 | tf_op jit(solution)/shard_map/ppermute | solution.py:325
  27.8 13.9 %collective-permute-start.8 = (f32[1032,128]{1,0:T(8,128)}, f32[1032,128]{1,0:T(8,128)S(1)}, u32[]{:S(2)}, u32[]{:S(2)}) collective-permute-start(f32[1032,128]{1,0:T(8,128)} %broadcast_select_fusion.5), channel_id=1, source_target_pairs={{0,2},{2,0},{1,3},{3,1},{4,6},{6,4},{5,7},{7,5},{8,10},{10,8},{9,1... | collective-permute-start | bytes 1585160 | tf_op jit(solution)/shard_map/ppermute | solution.py:325
  33.4 14.1 %collective-permute-start.10 = (f32[1032,128]{1,0:T(8,128)}, f32[1032,128]{1,0:T(8,128)S(1)}, u32[]{:S(2)}, u32[]{:S(2)}) collective-permute-start(f32[1032,128]{1,0:T(8,128)} %get-tuple-element.85), channel_id=1, source_target_pairs={{0,4},{1,5},{2,6},{3,7},{4,8},{5,9},{6,10},{7,11},{8,12},{9,13},{1... | collective-permute-start | bytes 1585160 | tf_op jit(solution)/shard_map/ppermute | solution.py:328
  40.2 12.1 %collective-permute-start.7 = (f32[1032,128]{1,0:T(8,128)S(1)}, f32[1032,128]{1,0:T(8,128)S(1)}, u32[]{:S(2)}, u32[]{:S(2)}) collective-permute-start(f32[1032,128]{1,0:T(8,128)S(1)} %broadcast_select_fusion.8), channel_id=1, source_target_pairs={{0,1},{1,0},{2,3},{3,2},{4,5},{5,4},{6,7},{7,6},{8,9},{9,8},{10,11... | collective-permute-start | bytes 1585160 | tf_op jit(solution)/shard_map/ppermute | solution.py:325
  41.7 11.9 %collective-permute-start.9 = (f32[1032,128]{1,0:T(8,128)S(1)}, f32[1032,128]{1,0:T(8,128)S(1)}, u32[]{:S(2)}, u32[]{:S(2)}) collective-permute-start(f32[1032,128]{1,0:T(8,128)S(1)} %broadcast_select_fusion.4), channel_id=1, source_target_pairs={{0,2},{2,0},{1,3},{3,1},{4,6},{6,4},{5,7},{7,5},{8,10},{10,8},{9,1... | collective-permute-start | bytes 1585160 | tf_op jit(solution)/shard_map/ppermute | solution.py:325
  47.4 12.8 %collective-permute-start.11 = (f32[1032,128]{1,0:T(8,128)S(1)}, f32[1032,128]{1,0:T(8,128)S(1)}, u32[]{:S(2)}, u32[]{:S(2)}) collective-permute-start(f32[1032,128]{1,0:T(8,128)S(1)} %copy-done.8), channel_id=1, source_target_pairs={{0,4},{1,5},{2,6},{3,7},{4,8},{5,9},{6,10},{7,11},{8,12},{9,13},{1... | collective-permute-start | bytes 1585160 | tf_op jit(solution)/shard_map/ppermute | solution.py:328
  52.3 10.9 %collective-permute-start.12 = (f32[1032,128]{1,0:T(8,128)S(1)}, f32[1032,128]{1,0:T(8,128)S(1)}, u32[]{:S(2)}, u32[]{:S(2)}) collective-permute-start(f32[1032,128]{1,0:T(8,128)S(1)} %broadcast_select_fusion.7), channel_id=1, source_target_pairs={{0,1},{1,0},{2,3},{3,2},{4,5},{5,4},{6,7},{7,6},{8,9},{9,8},{10,11... | collective-permute-start | bytes 1585160 | tf_op jit(solution)/shard_map/ppermute | solution.py:325
  53.7 12.2 %collective-permute-start.14 = (f32[1032,128]{1,0:T(8,128)S(1)}, f32[1032,128]{1,0:T(8,128)S(1)}, u32[]{:S(2)}, u32[]{:S(2)}) collective-permute-start(f32[1032,128]{1,0:T(8,128)S(1)} %broadcast_select_fusion.3), channel_id=1, source_target_pairs={{0,2},{2,0},{1,3},{3,1},{4,6},{6,4},{5,7},{7,5},{8,10},{10,8},{9,1... | collective-permute-start | bytes 1585160 | tf_op jit(solution)/shard_map/ppermute | solution.py:325
  65.8 14.6 %collective-permute-start.18 = (f32[1032,128]{1,0:T(8,128)S(1)}, f32[1032,128]{1,0:T(8,128)S(1)}, u32[]{:S(2)}, u32[]{:S(2)}) collective-permute-start(f32[1032,128]{1,0:T(8,128)S(1)} %broadcast_select_fusion.2), channel_id=1, source_target_pairs={{0,2},{2,0},{1,3},{3,1},{4,6},{6,4},{5,7},{7,5},{8,10},{10,8},{9,1... | collective-permute-start | bytes 1585160 | tf_op jit(solution)/shard_map/ppermute | solution.py:325
  67.2 13.2 %collective-permute-start.17 = (f32[1032,128]{1,0:T(8,128)S(1)}, f32[1032,128]{1,0:T(8,128)S(1)}, u32[]{:S(2)}, u32[]{:S(2)}) collective-permute-start(f32[1032,128]{1,0:T(8,128)S(1)} %get-tuple-element.106), channel_id=1, source_target_pairs={{0,1},{1,0},{2,3},{3,2},{4,5},{5,4},{6,7},{7,6},{8,9},{9,8},{10,11... | collective-permute-start | bytes 1585160 | tf_op jit(solution)/shard_map/ppermute | solution.py:325
  67.8 15.5 %collective-permute-start.3 = (f32[256,512]{1,0:T(8,128)S(1)}, f32[256,512]{1,0:T(8,128)S(1)}, u32[]{:S(2)}, u32[]{:S(2)}) collective-permute-start(f32[256,512]{1,0:T(8,128)S(1)} %copy-done.5), channel_id=1, source_target_pairs={{0,16},{16,0},{1,17},{17,1},{2,18},{18,2},{3,19},{19,3},{4,20},{20... | collective-permute-start | bytes 1572872 | tf_op jit(solution)/shard_map/ppermute | solution.py:332
  67.8 15.6 %collective-permute-start.4 = (f32[256,512]{1,0:T(8,128)S(1)}, f32[256,512]{1,0:T(8,128)S(1)}, u32[]{:S(2)}, u32[]{:S(2)}) collective-permute-start(f32[256,512]{1,0:T(8,128)S(1)} %copy-done.6), channel_id=1, source_target_pairs={{0,16},{16,0},{1,17},{17,1},{2,18},{18,2},{3,19},{19,3},{4,20},{20... | collective-permute-start | bytes 1572872 | tf_op jit(solution)/shard_map/ppermute | solution.py:332
  68.3 18.9 %collective-permute-start.13 = (f32[1032,128]{1,0:T(8,128)S(1)}, f32[1032,128]{1,0:T(8,128)S(1)}, u32[]{:S(2)}, u32[]{:S(2)}) collective-permute-start(f32[1032,128]{1,0:T(8,128)S(1)} %broadcast_select_fusion.1), channel_id=1, source_target_pairs={{0,1},{1,3},{3,2},{2,0},{4,5},{5,7},{7,6},{6,4},{8,9},{9,11},{11,1... | collective-permute-start | bytes 1585160 | tf_op jit(solution)/shard_map/ppermute | solution.py:325
  80.4 3.4 %collective-permute-start.15 = (f32[256,512]{1,0:T(8,128)S(1)}, f32[256,512]{1,0:T(8,128)S(1)}, u32[]{:S(2)}, u32[]{:S(2)}) collective-permute-start(f32[256,512]{1,0:T(8,128)S(1)} %get-tuple-element.100.refs_7_), channel_id=1, source_target_pairs={{0,16},{16,0},{1,17},{17,1},{2,18},{18,2},{3,19},{19,3},{4,20},{20... | collective-permute-start | bytes 1572872 | tf_op jit(solution)/shard_map/ppermute | solution.py:332
  80.4 4.7 %collective-permute-start.16 = (f32[256,512]{1,0:T(8,128)S(1)}, f32[256,512]{1,0:T(8,128)S(1)}, u32[]{:S(2)}, u32[]{:S(2)}) collective-permute-start(f32[256,512]{1,0:T(8,128)S(1)} %get-tuple-element.101.refs_8_), channel_id=1, source_target_pairs={{0,16},{16,0},{1,17},{17,1},{2,18},{18,2},{3,19},{19,3},{4,20},{20... | collective-permute-start | bytes 1572872 | tf_op jit(solution)/shard_map/ppermute | solution.py:332
  83.2 7.0 %collective-permute-start.19 = (f32[256,512]{1,0:T(8,128)S(1)}, f32[256,512]{1,0:T(8,128)S(1)}, u32[]{:S(2)}, u32[]{:S(2)}) collective-permute-start(f32[256,512]{1,0:T(8,128)S(1)} %get-tuple-element.109.refs_11_), channel_id=1, source_target_pairs={{0,16},{16,0},{1,17},{17,1},{2,18},{18,2},{3,19},{19,3},{4,20},{20... | collective-permute-start | bytes 1572872 | tf_op jit(solution)/shard_map/ppermute | solution.py:332
  83.3 7.0 %collective-permute-start.20 = (f32[256,512]{1,0:T(8,128)S(1)}, f32[256,512]{1,0:T(8,128)S(1)}, u32[]{:S(2)}, u32[]{:S(2)}) collective-permute-start(f32[256,512]{1,0:T(8,128)S(1)} %get-tuple-element.110.refs_12_), channel_id=1, source_target_pairs={{0,16},{16,0},{1,17},{17,1},{2,18},{18,2},{3,19},{19,3},{4,20},{20... | collective-permute-start | bytes 1572872 | tf_op jit(solution)/shard_map/ppermute | solution.py:332
  83.8 20.5 %collective-permute-start.23 = (f32[1032,128]{1,0:T(8,128)S(1)}, f32[1032,128]{1,0:T(8,128)S(1)}, u32[]{:S(2)}, u32[]{:S(2)}) collective-permute-start(f32[1032,128]{1,0:T(8,128)S(1)} %get-tuple-element.123), channel_id=1, source_target_pairs={{2,0},{3,2},{6,4},{7,6},{10,8},{11,10},{14,12},{15,14},{18,16},{19... | collective-permute-start | bytes 1585160 | tf_op jit(solution)/shard_map/ppermute | solution.py:325
  85.1 21.1 %collective-permute-start.24 = (f32[1032,128]{1,0:T(8,128)S(1)}, f32[1032,128]{1,0:T(8,128)S(1)}, u32[]{:S(2)}, u32[]{:S(2)}) collective-permute-start(f32[1032,128]{1,0:T(8,128)S(1)} %collective-permute-done.14.refs_13_.refs_8_.refs_32_), channel_id=1, source_target_pairs={{0,1},{1,0},{2,3},{3,2},{4,5},{5,4},{6,7},{7,6},{8,9},{9,8},{10,11... | collective-permute-start | bytes 1585160 | tf_op jit(solution)/shard_map/ppermute | solution.py:325
  87.2 23.3 %collective-permute-start.25 = (f32[1032,128]{1,0:T(8,128)S(1)}, f32[1032,128]{1,0:T(8,128)S(1)}, u32[]{:S(2)}, u32[]{:S(2)}) collective-permute-start(f32[1032,128]{1,0:T(8,128)S(1)} %collective-permute-done.18.refs_9_.refs_33_.refs_2_.refs_8_), channel_id=1, source_target_pairs={{0,1},{1,0},{4,5},{5,4},{8,9},{9,8},{12,13},{13,12},{16,17},{17,16... | collective-permute-start | bytes 1585160 | tf_op jit(solution)/shard_map/ppermute | solution.py:325
  (15 other events, 141.5 us)

commit v10 on v8

--- a/solution.py
+++ b/solution.py
@@ -208,7 +208,7 @@
     return [made[slot * HALVES : (slot + 1) * HALVES] for slot in range(count)]
 
 
-def contract(partials, slots, signs, first_sign, energies, flags, eps_virt, size, before=None, limit=VMEM_LIMIT):
+def contract(partials, slots, signs, first_sign, energies, flags, eps_virt, size, before=None, limit=VMEM_LIMIT, space=pltpu.VMEM):
     count = len(slots)
     chunks = len(slots[0])
     virt = eps_virt.shape[1]
@@ -292,7 +292,7 @@
         pltpu.VMEM((width, count * 3 * width), jnp.bfloat16),
         pltpu.SemaphoreType.DMA((len(energies) + len(sums) + len(pieces) + 2 * chunks,)),
     ]
-    return call(kernel, [signs, flags], [eps_virt], [*sums, *last, *arrays], [out], pl.ANY, scratch, limit)[0]
+    return call(kernel, [signs, flags], [eps_virt], [*sums, *last, *arrays], [out], space, scratch, limit)[0]
 
 
 def after(block, *others):
@@ -352,9 +352,9 @@
         ]
         return jnp.stack(signs), jnp.stack(flags).astype(jnp.int32)
 
-    def add(first_sign, partials, slots, carriers, before=None, limit=VMEM_LIMIT):
+    def add(first_sign, partials, slots, carriers, before=None, limit=VMEM_LIMIT, space=pltpu.VMEM):
         return contract(
-            partials, slots, signs, first_sign, carriers, flags, eps_virt[None, :], size, before, limit
+            partials, slots, signs, first_sign, carriers, flags, eps_virt[None, :], size, before, limit, space
         )
 
     from_own = [first_sent]
@@ -436,7 +436,7 @@
     half = CHUNKS // 2
     partial_d = integrate(turned, [slot_d[:half]], [0], flags, size, width)
     (partial_d,) = integrate(turned, [slot_d[half:]], [half], flags, size, width, partial_d, LAST_LIMIT)
-    gradient = add(4, [totals(partial_d)], [slot_d], [own_eps, eps_d], gradient, LAST_LIMIT)
+    gradient = add(4, [totals(partial_d)], [slot_d], [own_eps, eps_d], gradient, LAST_LIMIT, pl.ANY)
     return gradient.reshape(rows, occ_rows, virt)
 
 

time: 120 us -> 120 us (level)
  no operation moved by 1% of the time
where the time goes in v10:
time: 120 us
  starting transfers between devices  46.4 us (39%)
  Pallas kernels  34.1 us (28%)
  waiting for transfers between devices  28.7 us (24%)
  other arithmetic  4.39 us (4%)
  between operations  3.74 us (3%)
  local copies, waits for them, and re-layouts  2.34 us (2%)
    pallas_call x7, Pallas kernels, call(): pl.pallas_call(kernel, out_shape=outputs, in_specs=[pl.BlockSpec(memory_s...  34.1 us
    ppermute x14, starting transfers between devices, within(): lax.ppermute(block, 'occ', [(g + a, g + b) for g in planes for a, b in mo...  27 us
    ppermute x4, starting transfers between devices, up(): lax.ppermute(block, 'occ', [(g, g + PLANE) for g in range(groups - PLANE)])  17.1 us
    ppermute x14, waiting for transfers between devices, within(): lax.ppermute(block, 'occ', [(g + a, g + b) for g in planes for a, b in mo...  12.4 us
    ppermute x4, waiting for transfers between devices, up(): lax.ppermute(block, 'occ', [(g, g + PLANE) for g in range(groups - PLANE)])  12 us
    ppermute x10, waiting for transfers between devices, totals(): lax.ppermute(part, 'aux', [(0, 1), (1, 0)])  4.31 us
    select_n x3, other arithmetic, on_device(): jnp.where(odd_y, came, up_part)  3.34 us
  transfers between devices with their start and end apart: 28, of which 11 were waited for; matrix products, arithmetic and copies ran while one was open for 4% of the time, Pallas kernels for 23%

profile of v10, /device:TPU:0, one launch (start us, length us, event | category | flops | bytes accessed | tf_op | source)
XLA Modules:
  0.0 119.6 jit_solution(10515879292695664334)
XLA Ops:
  2.1 5.0 %collective-permute-start = (f32[1032,128]{1,0:T(8,128)S(1)}, f32[1032,128]{1,0:T(8,128)S(1)}, u32[]{:S(2)}, u32[]{:S(2)}) collective-permute-start(f32[1032,128]{1,0:T(8,128)S(1)} %pad_maximum_fusion.refs_34_.refs_14_), channel_id=1, source_target_pairs={{0,4},{1,5},{2,6},{3,7},{4,8},{5,9},{6,10},{7,11},{8,12},{9,13},{1... | collective-permute-start | bytes 1585160 | tf_op jit(solution)/shard_map/ppermute | solution.py:328
  7.1 3.5 %collective-permute-start.2 = (f32[1032,128]{1,0:T(8,128)S(1)}, f32[1032,128]{1,0:T(8,128)S(1)}, u32[]{:S(2)}, u32[]{:S(2)}) collective-permute-start(f32[1032,128]{1,0:T(8,128)S(1)} %pad_maximum_fusion.refs_34_.refs_14_), channel_id=1, source_target_pairs={{0,2},{1,3},{4,6},{5,7},{8,10},{9,11},{12,14},{13,15},{16,18},{17,... | collective-permute-start | bytes 1585160 | tf_op jit(solution)/shard_map/ppermute | solution.py:325
  10.6 3.4 %collective-permute-start.1 = (f32[1032,128]{1,0:T(8,128)S(1)}, f32[1032,128]{1,0:T(8,128)S(1)}, u32[]{:S(2)}, u32[]{:S(2)}) collective-permute-start(f32[1032,128]{1,0:T(8,128)S(1)} %pad_maximum_fusion.refs_34_.refs_14_), channel_id=1, source_target_pairs={{0,1},{2,3},{1,0},{4,5},{6,7},{5,4},{8,9},{10,11},{9,8},{12,13},{1... | collective-permute-start | bytes 1585160 | tf_op jit(solution)/shard_map/ppermute | solution.py:325
  14.0 5.1 %shard_map.46 = (bf16[4,512,256]{2,1,0:T(8,128)(2,1)}, bf16[4,512,256]{2,1,0:T(8,128)(2,1)}, f32[256,512]{1,0:T(8,128)}, f32[256,512]{1,0:T(8,128)}, f32[1032,12...) custom-call(f32[8,128]{1,0:T(8,128)} %copy-done.9, f32[4096,128]{1,0:T(8,128)} %bitcast.15), custom_call_target="tpu_custom_call" | custom-call | tf_op jit(solution)/shard_map/pallas_call | solution.py:85
  19.1 3.6 %collective-permute-start.5 = (f32[1032,128]{1,0:T(8,128)}, f32[1032,128]{1,0:T(8,128)S(1)}, u32[]{:S(2)}, u32[]{:S(2)}) collective-permute-start(f32[1032,128]{1,0:T(8,128)} %get-tuple-element.64), channel_id=1, source_target_pairs={{0,4},{1,5},{2,6},{3,7},{4,8},{5,9},{6,10},{7,11},{8,12},{9,13},{1... | collective-permute-start | bytes 1585160 | tf_op jit(solution)/shard_map/ppermute | solution.py:328
  22.7 2.1 %broadcast_select_fusion.5 = (f32[1032,128]{1,0:T(8,128)}, f32[1032,128]{1,0:T(8,128)}) fusion(f32[1032,128]{1,0:T(8,128)S(1)} %collective-permute-done.refs_2_.refs_20_, f32[1032,128]{1,0:T(8,128)} %get-tuple-element.64, pred[]{:T(512)S(6)} %eq.44, pred[]{:T(512)S(6)} %eq.43), kind=kLoop, calls=%fused_computation.6 | loop fusion | flops 264192 | bytes 2113538 | tf_op jit(solution)/shard_map/jit(_where)/select_n | solution.py:376
  33.4 4.3 %collective-permute-start.10 = (f32[1032,128]{1,0:T(8,128)}, f32[1032,128]{1,0:T(8,128)S(1)}, u32[]{:S(2)}, u32[]{:S(2)}) collective-permute-start(f32[1032,128]{1,0:T(8,128)} %get-tuple-element.73), channel_id=1, source_target_pairs={{0,4},{1,5},{2,6},{3,7},{4,8},{5,9},{6,10},{7,11},{8,12},{9,13},{1... | collective-permute-start | bytes 1585160 | tf_op jit(solution)/shard_map/ppermute | solution.py:328
  38.8 1.6 %collective-permute-start.9 = (f32[1032,128]{1,0:T(8,128)S(1)}, f32[1032,128]{1,0:T(8,128)S(1)}, u32[]{:S(2)}, u32[]{:S(2)}) collective-permute-start(f32[1032,128]{1,0:T(8,128)S(1)} %get-tuple-element.75), channel_id=1, source_target_pairs={{0,2},{2,0},{1,3},{3,1},{4,6},{6,4},{5,7},{7,5},{8,10},{10,8},{9,1... | collective-permute-start | bytes 1585160 | tf_op jit(solution)/shard_map/ppermute | solution.py:325
  41.9 5.5 %collective-permute-done.10.refs_4_.refs_22_ = f32[1032,128]{1,0:T(8,128)S(1)} collective-permute-done((f32[1032,128]{1,0:T(8,128)}, f32[1032,128]{1,0:T(8,128)S(1)}, u32[]{:S(2)}, u32[]{:S(2)}) %collective-permute-start.10) | collective-permute-done | bytes 528416 | tf_op jit(solution)/shard_map/ppermute | solution.py:328
  47.4 4.3 %collective-permute-start.11 = (f32[1032,128]{1,0:T(8,128)S(1)}, f32[1032,128]{1,0:T(8,128)S(1)}, u32[]{:S(2)}, u32[]{:S(2)}) collective-permute-start(f32[1032,128]{1,0:T(8,128)S(1)} %copy-done.8), channel_id=1, source_target_pairs={{0,4},{1,5},{2,6},{3,7},{4,8},{5,9},{6,10},{7,11},{8,12},{9,13},{1... | collective-permute-start | bytes 1585160 | tf_op jit(solution)/shard_map/ppermute | solution.py:328
  51.8 1.6 %collective-permute-start.14 = (f32[1032,128]{1,0:T(8,128)S(1)}, f32[1032,128]{1,0:T(8,128)S(1)}, u32[]{:S(2)}, u32[]{:S(2)}) collective-permute-start(f32[1032,128]{1,0:T(8,128)S(1)} %get-tuple-element.86), channel_id=1, source_target_pairs={{0,2},{2,0},{1,3},{3,1},{4,6},{6,4},{5,7},{7,5},{8,10},{10,8},{9,1... | collective-permute-start | bytes 1585160 | tf_op jit(solution)/shard_map/ppermute | solution.py:325
  55.0 5.2 %collective-permute-done.11.refs_5_.refs_23_ = f32[1032,128]{1,0:T(8,128)S(1)} collective-permute-done((f32[1032,128]{1,0:T(8,128)S(1)}, f32[1032,128]{1,0:T(8,128)S(1)}, u32[]{:S(2)}, u32[]{:S(2)}) %collective-permute-start.11) | collective-permute-done | bytes 528416 | tf_op jit(solution)/shard_map/ppermute | solution.py:328
  60.4 3.7 %collective-permute-done.14.refs_13_.refs_8_.refs_32_ = f32[1032,128]{1,0:T(8,128)S(1)} collective-permute-done((f32[1032,128]{1,0:T(8,128)S(1)}, f32[1032,128]{1,0:T(8,128)S(1)}, u32[]{:S(2)}, u32[]{:S(2)}) %collective-permute-start.14) | collective-permute-done | bytes 528416 | tf_op jit(solution)/shard_map/ppermute | solution.py:325
  68.2 6.5 %shard_map.47 = (f32[256,512]{1,0:T(8,128)S(1)}, f32[256,512]{1,0:T(8,128)S(1)}, f32[256,512]{1,0:T(8,128)S(1)}, f32[256,512]{1,0:T(8,128)S(1)}, f32[256,512]{1,0:T(8,128)S(1)}, /*index=5*/f32[256,512]{1,0:T(8,128)S(1)}) custom-call(s32[4]{0:T(128)S(1)} %pad_add_fusion.flag_ref.refs_1_, bf16[4,512,256]{2,1,0:T(8,128)(2,1)S(1)} %copy-done, ...), custom_call_target="tpu_custom_call" | custom-call | tf_op jit(solution)/shard_map/pallas_call | solution.py:85
  74.6 3.0 %collective-permute-done.18.refs_9_.refs_33_.refs_2_.refs_8_ = f32[1032,128]{1,0:T(8,128)S(1)} collective-permute-done((f32[1032,128]{1,0:T(8,128)S(1)}, f32[1032,128]{1,0:T(8,128)S(1)}, u32[]{:S(2)}, u32[]{:S(2)}) %collective-permute-start.18) | collective-permute-done | bytes 528416 | tf_op jit(solution)/shard_map/ppermute | solution.py:325
  77.6 1.9 %collective-permute-done.17.refs_7_.refs_28_.refs_4_.refs_10_ = f32[1032,128]{1,0:T(8,128)S(1)} collective-permute-done((f32[1032,128]{1,0:T(8,128)S(1)}, f32[1032,128]{1,0:T(8,128)S(1)}, u32[]{:S(2)}, u32[]{:S(2)}) %collective-permute-start.17) | collective-permute-done | bytes 528416 | tf_op jit(solution)/shard_map/ppermute | solution.py:325
  79.6 2.3 %shard_map.48 = (f32[256,512]{1,0:T(8,128)S(1)}, f32[256,512]{1,0:T(8,128)S(1)}, f32[256,512]{1,0:T(8,128)S(1)}, f32[256,512]{1,0:T(8,128)S(1)}) custom-call(s32[4]{0:T(128)S(1)} %pad_add_fusion.flag_ref.refs_1_, bf16[4,512,256]{2,1,0:T(8,128)(2,1)S(1)} %copy-done, bf16[4,512,256]{2,1,0:T(8,128)(2,1)S(1)} %copy-done.1, ...), custom_call_target="tpu_custom_call" | custom-call | tf_op jit(solution)/shard_map/pallas_call | solution.py:85
  83.8 1.9 %collective-permute-start.24 = (f32[1032,128]{1,0:T(8,128)S(1)}, f32[1032,128]{1,0:T(8,128)S(1)}, u32[]{:S(2)}, u32[]{:S(2)}) collective-permute-start(f32[1032,128]{1,0:T(8,128)S(1)} %collective-permute-done.14.refs_13_.refs_8_.refs_32_), channel_id=1, source_target_pairs={{0,1},{1,0},{2,3},{3,2},{4,5},{5,4},{6,7},{7,6},{8,9},{9,8},{10,11... | collective-permute-start | bytes 1585160 | tf_op jit(solution)/shard_map/ppermute | solution.py:325
  85.8 4.2 %collective-permute-start.25 = (f32[1032,128]{1,0:T(8,128)S(1)}, f32[1032,128]{1,0:T(8,128)S(1)}, u32[]{:S(2)}, u32[]{:S(2)}) collective-permute-start(f32[1032,128]{1,0:T(8,128)S(1)} %collective-permute-done.18.refs_9_.refs_33_.refs_2_.refs_8_), channel_id=1, source_target_pairs={{0,1},{1,0},{4,5},{5,4},{8,9},{9,8},{12,13},{13,12},{16,17},{17,16... | collective-permute-start | bytes 1585160 | tf_op jit(solution)/shard_map/ppermute | solution.py:325
  92.7 11.3 %shard_map.49.refs_7_ = f32[4096,128]{1,0:T(8,128)S(1)} custom-call(f32[5]{0:T(128)S(1)} %stack.34.refs_0_, s32[4]{0:T(128)S(1)} %pad_add_fusion.flag_ref.refs_1_, f32[1,512]{1,0:T(1,128)S(1)} %bitcast.17, f32[256,512]{1,0:T(8,128)S(1)} %copy-done.5, f32[256,512]{1,0:T(8,128)S(1)} %copy-done.6, f32[256,512]{1,0:T(8,128)S(1)} %collective-permute-done.3.refs_5_, ...), custom_call_target="tpu_custom_call" | custom-call | tf_op jit(solution)/shard_map/pallas_call | solution.py:85
  104.1 1.9 %shard_map.50 = (f32[256,512]{1,0:T(8,128)S(1)}, f32[256,512]{1,0:T(8,128)S(1)}) custom-call(s32[4]{0:T(128)S(1)} %pad_add_fusion.flag_ref.refs_1_, bf16[4,512,256]{2,1,0:T(8,128)(2,1)S(1)} %copy-done, bf16[4,512,256]{2,1,0:T(8,128)(2,1)S(1)} %copy-done.1, f32[1032,128]{1,0:T(8,128)S(1)} %collective-permute-done.18.refs_9_.refs_33_.refs_2_.refs_8_, ...), custom_call_target="tpu_custom_call" | custom-call | tf_op jit(solution)/shard_map/pallas_call | solution.py:85
  106.0 3.7 %collective-permute-done.25.refs_6_.refs_13_ = f32[1032,128]{1,0:T(8,128)S(1)} collective-permute-done((f32[1032,128]{1,0:T(8,128)S(1)}, f32[1032,128]{1,0:T(8,128)S(1)}, u32[]{:S(2)}, u32[]{:S(2)}) %collective-permute-start.25) | collective-permute-done | bytes 528416 | tf_op jit(solution)/shard_map/ppermute | solution.py:325
  109.7 2.1 %shard_map.51 = (f32[256,512]{1,0:T(8,128)S(1)}, f32[256,512]{1,0:T(8,128)S(1)}) custom-call(s32[4]{0:T(128)S(1)} %pad_add_fusion.flag_ref.refs_1_, bf16[4,512,256]{2,1,0:T(8,128)(2,1)S(1)} %copy-done, bf16[4,512,256]{2,1,0:T(8,128)(2,1)S(1)} %copy-done.1, f32[256,512]{1,0:T(8,128)S(1)} %get-tuple-element.101.refs_2_, ...), custom_call_target="tpu_custom_call" | custom-call | tf_op jit(solution)/shard_map/pallas_call | solution.py:85
  114.5 5.0 %shard_map.52 = f32[4096,128]{1,0:T(8,128)} custom-call(f32[5]{0:T(128)S(1)} %stack.34.refs_0_, s32[4]{0:T(128)S(1)} %pad_add_fusion.flag_ref.refs_1_, f32[1,512]{1,0:T(1,128)S(1)} %bitcast.18, f32[256,512]{1,0:T(8,128)S(1)} %get-tuple-element.103.refs_3_, f32[256,512]{1,0:T(8,128)S(1)} %get-tuple-element.104.refs_4_, ...), custom_call_target="tpu_custom_call" | custom-call | tf_op jit(solution)/shard_map/pallas_call | solution.py:85
  (72 shorter events, 23.3 us)
Async XLA Ops:
  2.1 17.0 %collective-permute-start = (f32[1032,128]{1,0:T(8,128)S(1)}, f32[1032,128]{1,0:T(8,128)S(1)}, u32[]{:S(2)}, u32[]{:S(2)}) collective-permute-start(f32[1032,128]{1,0:T(8,128)S(1)} %pad_maximum_fusion.refs_34_.refs_14_), channel_id=1, source_target_pairs={{0,4},{1,5},{2,6},{3,7},{4,8},{5,9},{6,10},{7,11},{8,12},{9,13},{1... | collective-permute-start | bytes 1585160 | tf_op jit(solution)/shard_map/ppermute | solution.py:328
  7.1 17.8 %collective-permute-start.2 = (f32[1032,128]{1,0:T(8,128)S(1)}, f32[1032,128]{1,0:T(8,128)S(1)}, u32[]{:S(2)}, u32[]{:S(2)}) collective-permute-start(f32[1032,128]{1,0:T(8,128)S(1)} %pad_maximum_fusion.refs_34_.refs_14_), channel_id=1, source_target_pairs={{0,2},{1,3},{4,6},{5,7},{8,10},{9,11},{12,14},{13,15},{16,18},{17,... | collective-permute-start | bytes 1585160 | tf_op jit(solution)/shard_map/ppermute | solution.py:325
  10.6 15.1 %collective-permute-start.1 = (f32[1032,128]{1,0:T(8,128)S(1)}, f32[1032,128]{1,0:T(8,128)S(1)}, u32[]{:S(2)}, u32[]{:S(2)}) collective-permute-start(f32[1032,128]{1,0:T(8,128)S(1)} %pad_maximum_fusion.refs_34_.refs_14_), channel_id=1, source_target_pairs={{0,1},{2,3},{1,0},{4,5},{6,7},{5,4},{8,9},{10,11},{9,8},{12,13},{1... | collective-permute-start | bytes 1585160 | tf_op jit(solution)/shard_map/ppermute | solution.py:325
  19.1 14.3 %collective-permute-start.5 = (f32[1032,128]{1,0:T(8,128)}, f32[1032,128]{1,0:T(8,128)S(1)}, u32[]{:S(2)}, u32[]{:S(2)}) collective-permute-start(f32[1032,128]{1,0:T(8,128)} %get-tuple-element.64), channel_id=1, source_target_pairs={{0,4},{1,5},{2,6},{3,7},{4,8},{5,9},{6,10},{7,11},{8,12},{9,13},{1... | collective-permute-start | bytes 1585160 | tf_op jit(solution)/shard_map/ppermute | solution.py:328
  25.7 13.2 %collective-permute-start.8 = (f32[1032,128]{1,0:T(8,128)}, f32[1032,128]{1,0:T(8,128)S(1)}, u32[]{:S(2)}, u32[]{:S(2)}) collective-permute-start(f32[1032,128]{1,0:T(8,128)} %get-tuple-element.66), channel_id=1, source_target_pairs={{0,2},{2,0},{1,3},{3,1},{4,6},{6,4},{5,7},{7,5},{8,10},{10,8},{9,1... | collective-permute-start | bytes 1585160 | tf_op jit(solution)/shard_map/ppermute | solution.py:325
  27.2 13.2 %collective-permute-start.6 = (f32[1032,128]{1,0:T(8,128)}, f32[1032,128]{1,0:T(8,128)S(1)}, u32[]{:S(2)}, u32[]{:S(2)}) collective-permute-start(f32[1032,128]{1,0:T(8,128)} %get-tuple-element.65), channel_id=1, source_target_pairs={{0,1},{1,0},{2,3},{3,2},{4,5},{5,4},{6,7},{7,6},{8,9},{9,8},{10,11... | collective-permute-start | bytes 1585160 | tf_op jit(solution)/shard_map/ppermute | solution.py:325
  33.4 14.1 %collective-permute-start.10 = (f32[1032,128]{1,0:T(8,128)}, f32[1032,128]{1,0:T(8,128)S(1)}, u32[]{:S(2)}, u32[]{:S(2)}) collective-permute-start(f32[1032,128]{1,0:T(8,128)} %get-tuple-element.73), channel_id=1, source_target_pairs={{0,4},{1,5},{2,6},{3,7},{4,8},{5,9},{6,10},{7,11},{8,12},{9,13},{1... | collective-permute-start | bytes 1585160 | tf_op jit(solution)/shard_map/ppermute | solution.py:328
  38.8 13.0 %collective-permute-start.9 = (f32[1032,128]{1,0:T(8,128)S(1)}, f32[1032,128]{1,0:T(8,128)S(1)}, u32[]{:S(2)}, u32[]{:S(2)}) collective-permute-start(f32[1032,128]{1,0:T(8,128)S(1)} %get-tuple-element.75), channel_id=1, source_target_pairs={{0,2},{2,0},{1,3},{3,1},{4,6},{6,4},{5,7},{7,5},{8,10},{10,8},{9,1... | collective-permute-start | bytes 1585160 | tf_op jit(solution)/shard_map/ppermute | solution.py:325
  40.4 13.0 %collective-permute-start.7 = (f32[1032,128]{1,0:T(8,128)S(1)}, f32[1032,128]{1,0:T(8,128)S(1)}, u32[]{:S(2)}, u32[]{:S(2)}) collective-permute-start(f32[1032,128]{1,0:T(8,128)S(1)} %get-tuple-element.74), channel_id=1, source_target_pairs={{0,1},{1,0},{2,3},{3,2},{4,5},{5,4},{6,7},{7,6},{8,9},{9,8},{10,11... | collective-permute-start | bytes 1585160 | tf_op jit(solution)/shard_map/ppermute | solution.py:325
  47.4 12.8 %collective-permute-start.11 = (f32[1032,128]{1,0:T(8,128)S(1)}, f32[1032,128]{1,0:T(8,128)S(1)}, u32[]{:S(2)}, u32[]{:S(2)}) collective-permute-start(f32[1032,128]{1,0:T(8,128)S(1)} %copy-done.8), channel_id=1, source_target_pairs={{0,4},{1,5},{2,6},{3,7},{4,8},{5,9},{6,10},{7,11},{8,12},{9,13},{1... | collective-permute-start | bytes 1585160 | tf_op jit(solution)/shard_map/ppermute | solution.py:328
  51.8 12.2 %collective-permute-start.14 = (f32[1032,128]{1,0:T(8,128)S(1)}, f32[1032,128]{1,0:T(8,128)S(1)}, u32[]{:S(2)}, u32[]{:S(2)}) collective-permute-start(f32[1032,128]{1,0:T(8,128)S(1)} %get-tuple-element.86), channel_id=1, source_target_pairs={{0,2},{2,0},{1,3},{3,1},{4,6},{6,4},{5,7},{7,5},{8,10},{10,8},{9,1... | collective-permute-start | bytes 1585160 | tf_op jit(solution)/shard_map/ppermute | solution.py:325
  53.4 12.2 %collective-permute-start.12 = (f32[1032,128]{1,0:T(8,128)S(1)}, f32[1032,128]{1,0:T(8,128)S(1)}, u32[]{:S(2)}, u32[]{:S(2)}) collective-permute-start(f32[1032,128]{1,0:T(8,128)S(1)} %get-tuple-element.80), channel_id=1, source_target_pairs={{0,1},{1,0},{2,3},{3,2},{4,5},{5,4},{6,7},{7,6},{8,9},{9,8},{10,11... | collective-permute-start | bytes 1585160 | tf_op jit(solution)/shard_map/ppermute | solution.py:325
  64.1 13.5 %collective-permute-start.18 = (f32[1032,128]{1,0:T(8,128)S(1)}, f32[1032,128]{1,0:T(8,128)S(1)}, u32[]{:S(2)}, u32[]{:S(2)}) collective-permute-start(f32[1032,128]{1,0:T(8,128)S(1)} %get-tuple-element.94), channel_id=1, source_target_pairs={{0,2},{2,0},{1,3},{3,1},{4,6},{6,4},{5,7},{7,5},{8,10},{10,8},{9,1... | collective-permute-start | bytes 1585160 | tf_op jit(solution)/shard_map/ppermute | solution.py:325
  65.6 14.0 %collective-permute-start.17 = (f32[1032,128]{1,0:T(8,128)S(1)}, f32[1032,128]{1,0:T(8,128)S(1)}, u32[]{:S(2)}, u32[]{:S(2)}) collective-permute-start(f32[1032,128]{1,0:T(8,128)S(1)} %get-tuple-element.93), channel_id=1, source_target_pairs={{0,1},{1,0},{2,3},{3,2},{4,5},{5,4},{6,7},{7,6},{8,9},{9,8},{10,11... | collective-permute-start | bytes 1585160 | tf_op jit(solution)/shard_map/ppermute | solution.py:325
  67.1 14.8 %collective-permute-start.3 = (f32[256,512]{1,0:T(8,128)S(1)}, f32[256,512]{1,0:T(8,128)S(1)}, u32[]{:S(2)}, u32[]{:S(2)}) collective-permute-start(f32[256,512]{1,0:T(8,128)S(1)} %copy-done.5), channel_id=1, source_target_pairs={{0,16},{16,0},{1,17},{17,1},{2,18},{18,2},{3,19},{19,3},{4,20},{20... | collective-permute-start | bytes 1572872 | tf_op jit(solution)/shard_map/ppermute | solution.py:332
  67.1 15.3 %collective-permute-start.4 = (f32[256,512]{1,0:T(8,128)S(1)}, f32[256,512]{1,0:T(8,128)S(1)}, u32[]{:S(2)}, u32[]{:S(2)}) collective-permute-start(f32[256,512]{1,0:T(8,128)S(1)} %copy-done.6), channel_id=1, source_target_pairs={{0,16},{16,0},{1,17},{17,1},{2,18},{18,2},{3,19},{19,3},{4,20},{20... | collective-permute-start | bytes 1572872 | tf_op jit(solution)/shard_map/ppermute | solution.py:332
  67.6 18.2 %collective-permute-start.13 = (f32[1032,128]{1,0:T(8,128)S(1)}, f32[1032,128]{1,0:T(8,128)S(1)}, u32[]{:S(2)}, u32[]{:S(2)}) collective-permute-start(f32[1032,128]{1,0:T(8,128)S(1)} %broadcast_select_fusion.1), channel_id=1, source_target_pairs={{0,1},{1,3},{3,2},{2,0},{4,5},{5,7},{7,6},{6,4},{8,9},{9,11},{11,1... | collective-permute-start | bytes 1585160 | tf_op jit(solution)/shard_map/ppermute | solution.py:325
  77.6 4.9 %collective-permute-start.15 = (f32[256,512]{1,0:T(8,128)S(1)}, f32[256,512]{1,0:T(8,128)S(1)}, u32[]{:S(2)}, u32[]{:S(2)}) collective-permute-start(f32[256,512]{1,0:T(8,128)S(1)} %get-tuple-element.87.refs_7_), channel_id=1, source_target_pairs={{0,16},{16,0},{1,17},{17,1},{2,18},{18,2},{3,19},{19,3},{4,20},{20... | collective-permute-start | bytes 1572872 | tf_op jit(solution)/shard_map/ppermute | solution.py:332
  79.6 4.3 %collective-permute-start.16 = (f32[256,512]{1,0:T(8,128)S(1)}, f32[256,512]{1,0:T(8,128)S(1)}, u32[]{:S(2)}, u32[]{:S(2)}) collective-permute-start(f32[256,512]{1,0:T(8,128)S(1)} %get-tuple-element.88.refs_8_), channel_id=1, source_target_pairs={{0,16},{16,0},{1,17},{17,1},{2,18},{18,2},{3,19},{19,3},{4,20},{20... | collective-permute-start | bytes 1572872 | tf_op jit(solution)/shard_map/ppermute | solution.py:332
  81.9 8.1 %collective-permute-start.19 = (f32[256,512]{1,0:T(8,128)S(1)}, f32[256,512]{1,0:T(8,128)S(1)}, u32[]{:S(2)}, u32[]{:S(2)}) collective-permute-start(f32[256,512]{1,0:T(8,128)S(1)} %get-tuple-element.95.refs_11_), channel_id=1, source_target_pairs={{0,16},{16,0},{1,17},{17,1},{2,18},{18,2},{3,19},{19,3},{4,20},{20... | collective-permute-start | bytes 1572872 | tf_op jit(solution)/shard_map/ppermute | solution.py:332
  82.4 7.6 %collective-permute-start.20 = (f32[256,512]{1,0:T(8,128)S(1)}, f32[256,512]{1,0:T(8,128)S(1)}, u32[]{:S(2)}, u32[]{:S(2)}) collective-permute-start(f32[256,512]{1,0:T(8,128)S(1)} %get-tuple-element.96.refs_12_), channel_id=1, source_target_pairs={{0,16},{16,0},{1,17},{17,1},{2,18},{18,2},{3,19},{19,3},{4,20},{20... | collective-permute-start | bytes 1572872 | tf_op jit(solution)/shard_map/ppermute | solution.py:332
  82.5 21.5 %collective-permute-start.23 = (f32[1032,128]{1,0:T(8,128)S(1)}, f32[1032,128]{1,0:T(8,128)S(1)}, u32[]{:S(2)}, u32[]{:S(2)}) collective-permute-start(f32[1032,128]{1,0:T(8,128)S(1)} %get-tuple-element.115), channel_id=1, source_target_pairs={{2,0},{3,2},{6,4},{7,6},{10,8},{11,10},{14,12},{15,14},{18,16},{19... | collective-permute-start | bytes 1585160 | tf_op jit(solution)/shard_map/ppermute | solution.py:325
  83.8 22.1 %collective-permute-start.24 = (f32[1032,128]{1,0:T(8,128)S(1)}, f32[1032,128]{1,0:T(8,128)S(1)}, u32[]{:S(2)}, u32[]{:S(2)}) collective-permute-start(f32[1032,128]{1,0:T(8,128)S(1)} %collective-permute-done.14.refs_13_.refs_8_.refs_32_), channel_id=1, source_target_pairs={{0,1},{1,0},{2,3},{3,2},{4,5},{5,4},{6,7},{7,6},{8,9},{9,8},{10,11... | collective-permute-start | bytes 1585160 | tf_op jit(solution)/shard_map/ppermute | solution.py:325
  85.8 23.9 %collective-permute-start.25 = (f32[1032,128]{1,0:T(8,128)S(1)}, f32[1032,128]{1,0:T(8,128)S(1)}, u32[]{:S(2)}, u32[]{:S(2)}) collective-permute-start(f32[1032,128]{1,0:T(8,128)S(1)} %collective-permute-done.18.refs_9_.refs_33_.refs_2_.refs_8_), channel_id=1, source_target_pairs={{0,1},{1,0},{4,5},{5,4},{8,9},{9,8},{12,13},{13,12},{16,17},{17,16... | collective-permute-start | bytes 1585160 | tf_op jit(solution)/shard_map/ppermute | solution.py:325
  (15 other events, 143.4 us)

commit v11 on v8

--- a/solution.py
+++ b/solution.py
@@ -221,6 +221,7 @@
     pieces = [piece for slot in slots for piece in slot]
     arrays = arrays_of([*pieces, *energies])
     last = [before] if before is not None else []
+    ahead = count == 1
 
     def kernel(*refs):
         given = iter(refs)
@@ -228,7 +229,7 @@
         sum_refs = [next(given) for _ in sums]
         before_refs = [next(given) for _ in last]
         ref_of = {id(array): next(given) for array in arrays}
-        out_ref, energy_ref, sum_ref, block_ref, result_ref, right_ref, semaphores = given
+        out_ref, energy_ref, sum_ref, block_ref, result_ref, right_ref, left_ref, semaphores = given
         copies = Copies(semaphores)
         arriving = [
             copies.start_piece(piece, ref_of, flag_ref, SUBLANES, energy_ref.at[at])
@@ -249,6 +250,10 @@
             [copies.start(ref.at[pl.ds(at * cut, cut)], result_ref.at[at]) for ref in before_refs]
             for at in range(chunks)
         ]
+        if ahead:
+            for at in range(chunks):
+                coming[at][0].wait()
+                left_ref[at] = deep_left(rows_of(block_ref.at[0, at], 0, size, width))
         for copy in arriving:
             copy.wait()
 
@@ -268,10 +273,14 @@
             right_ref[:, pl.ds(slot * 3 * width, 3 * width)] = deep_right(amplitude, 1)
         leaving = []
         for at in range(chunks):
-            for copy in coming[at] + adding[at]:
+            for copy in adding[at] if ahead else coming[at] + adding[at]:
                 copy.wait()
-            left = [deep_left(rows_of(block_ref.at[slot, at], 0, size, width)) for slot in range(count)]
-            value = dot(jnp.concatenate(left, axis=1), right_ref[...], 1)
+            if ahead:
+                left = left_ref[at]
+            else:
+                left = [deep_left(rows_of(block_ref.at[slot, at], 0, size, width)) for slot in range(count)]
+                left = jnp.concatenate(left, axis=1)
+            value = dot(left, right_ref[...], 1)
             for column in range(lines):
                 lanes = value[:, column * LANES : (column + 1) * LANES]
                 where = pl.ds(column, size, stride=lines)
@@ -290,6 +299,7 @@
         pltpu.VMEM((count, chunks, cut, LANES), jnp.float32),
         pltpu.VMEM((chunks, cut, LANES), jnp.float32),
         pltpu.VMEM((width, count * 3 * width), jnp.bfloat16),
+        pltpu.VMEM((chunks, size, 3 * width) if ahead else (2 * SUBLANES, LANES), jnp.bfloat16),
         pltpu.SemaphoreType.DMA((len(energies) + len(sums) + len(pieces) + 2 * chunks,)),
     ]
     return call(kernel, [signs, flags], [eps_virt], [*sums, *last, *arrays], [out], pl.ANY, scratch, limit)[0]

time: 120 us -> 120 us (level)
  no operation moved by 1% of the time
where the time goes in v11:
time: 120 us
  starting transfers between devices  46.4 us (39%)
  Pallas kernels  34.4 us (29%)
  waiting for transfers between devices  28.7 us (24%)
  other arithmetic  4.39 us (4%)
  between operations  3.74 us (3%)
  local copies, waits for them, and re-layouts  2.34 us (2%)
    pallas_call x7, Pallas kernels, call(): pl.pallas_call(kernel, out_shape=outputs, in_specs=[pl.BlockSpec(memory_s...  34.4 us
    ppermute x14, starting transfers between devices, within(): lax.ppermute(block, 'occ', [(g + a, g + b) for g in planes for a, b in mo...  27 us
    ppermute x4, starting transfers between devices, up(): lax.ppermute(block, 'occ', [(g, g + PLANE) for g in range(groups - PLANE)])  17.1 us
    ppermute x14, waiting for transfers between devices, within(): lax.ppermute(block, 'occ', [(g + a, g + b) for g in planes for a, b in mo...  12.4 us
    ppermute x4, waiting for transfers between devices, up(): lax.ppermute(block, 'occ', [(g, g + PLANE) for g in range(groups - PLANE)])  12 us
    ppermute x10, waiting for transfers between devices, totals(): lax.ppermute(part, 'aux', [(0, 1), (1, 0)])  4.31 us
    select_n x3, other arithmetic, on_device(): jnp.where(odd_y, came, up_part)  3.34 us
  transfers between devices with their start and end apart: 28, of which 11 were waited for; matrix products, arithmetic and copies ran while one was open for 4% of the time, Pallas kernels for 23%

profile of v11, /device:TPU:0, one launch (start us, length us, event | category | flops | bytes accessed | tf_op | source)
XLA Modules:
  0.0 119.9 jit_solution(17278992673903438213)
XLA Ops:
  2.1 5.0 %collective-permute-start = (f32[1032,128]{1,0:T(8,128)S(1)}, f32[1032,128]{1,0:T(8,128)S(1)}, u32[]{:S(2)}, u32[]{:S(2)}) collective-permute-start(f32[1032,128]{1,0:T(8,128)S(1)} %pad_maximum_fusion.refs_34_.refs_14_), channel_id=1, source_target_pairs={{0,4},{1,5},{2,6},{3,7},{4,8},{5,9},{6,10},{7,11},{8,12},{9,13},{1... | collective-permute-start | bytes 1585160 | tf_op jit(solution)/shard_map/ppermute | solution.py:338
  7.1 3.5 %collective-permute-start.2 = (f32[1032,128]{1,0:T(8,128)S(1)}, f32[1032,128]{1,0:T(8,128)S(1)}, u32[]{:S(2)}, u32[]{:S(2)}) collective-permute-start(f32[1032,128]{1,0:T(8,128)S(1)} %pad_maximum_fusion.refs_34_.refs_14_), channel_id=1, source_target_pairs={{0,2},{1,3},{4,6},{5,7},{8,10},{9,11},{12,14},{13,15},{16,18},{17,... | collective-permute-start | bytes 1585160 | tf_op jit(solution)/shard_map/ppermute | solution.py:335
  10.6 3.4 %collective-permute-start.1 = (f32[1032,128]{1,0:T(8,128)S(1)}, f32[1032,128]{1,0:T(8,128)S(1)}, u32[]{:S(2)}, u32[]{:S(2)}) collective-permute-start(f32[1032,128]{1,0:T(8,128)S(1)} %pad_maximum_fusion.refs_34_.refs_14_), channel_id=1, source_target_pairs={{0,1},{2,3},{1,0},{4,5},{6,7},{5,4},{8,9},{10,11},{9,8},{12,13},{1... | collective-permute-start | bytes 1585160 | tf_op jit(solution)/shard_map/ppermute | solution.py:335
  14.0 5.1 %shard_map.46 = (bf16[4,512,256]{2,1,0:T(8,128)(2,1)}, bf16[4,512,256]{2,1,0:T(8,128)(2,1)}, f32[256,512]{1,0:T(8,128)}, f32[256,512]{1,0:T(8,128)}, f32[1032,12...) custom-call(f32[8,128]{1,0:T(8,128)} %copy-done.9, f32[4096,128]{1,0:T(8,128)} %bitcast.15), custom_call_target="tpu_custom_call" | custom-call | tf_op jit(solution)/shard_map/pallas_call | solution.py:85
  19.1 3.6 %collective-permute-start.5 = (f32[1032,128]{1,0:T(8,128)}, f32[1032,128]{1,0:T(8,128)S(1)}, u32[]{:S(2)}, u32[]{:S(2)}) collective-permute-start(f32[1032,128]{1,0:T(8,128)} %get-tuple-element.64), channel_id=1, source_target_pairs={{0,4},{1,5},{2,6},{3,7},{4,8},{5,9},{6,10},{7,11},{8,12},{9,13},{1... | collective-permute-start | bytes 1585160 | tf_op jit(solution)/shard_map/ppermute | solution.py:338
  22.7 2.1 %broadcast_select_fusion.5 = (f32[1032,128]{1,0:T(8,128)}, f32[1032,128]{1,0:T(8,128)}) fusion(f32[1032,128]{1,0:T(8,128)S(1)} %collective-permute-done.refs_2_.refs_20_, f32[1032,128]{1,0:T(8,128)} %get-tuple-element.64, pred[]{:T(512)S(6)} %eq.44, pred[]{:T(512)S(6)} %eq.43), kind=kLoop, calls=%fused_computation.6 | loop fusion | flops 264192 | bytes 2113538 | tf_op jit(solution)/shard_map/jit(_where)/select_n | solution.py:386
  33.4 4.3 %collective-permute-start.10 = (f32[1032,128]{1,0:T(8,128)}, f32[1032,128]{1,0:T(8,128)S(1)}, u32[]{:S(2)}, u32[]{:S(2)}) collective-permute-start(f32[1032,128]{1,0:T(8,128)} %get-tuple-element.73), channel_id=1, source_target_pairs={{0,4},{1,5},{2,6},{3,7},{4,8},{5,9},{6,10},{7,11},{8,12},{9,13},{1... | collective-permute-start | bytes 1585160 | tf_op jit(solution)/shard_map/ppermute | solution.py:338
  38.8 1.6 %collective-permute-start.9 = (f32[1032,128]{1,0:T(8,128)S(1)}, f32[1032,128]{1,0:T(8,128)S(1)}, u32[]{:S(2)}, u32[]{:S(2)}) collective-permute-start(f32[1032,128]{1,0:T(8,128)S(1)} %get-tuple-element.75), channel_id=1, source_target_pairs={{0,2},{2,0},{1,3},{3,1},{4,6},{6,4},{5,7},{7,5},{8,10},{10,8},{9,1... | collective-permute-start | bytes 1585160 | tf_op jit(solution)/shard_map/ppermute | solution.py:335
  41.9 5.5 %collective-permute-done.10.refs_4_.refs_22_ = f32[1032,128]{1,0:T(8,128)S(1)} collective-permute-done((f32[1032,128]{1,0:T(8,128)}, f32[1032,128]{1,0:T(8,128)S(1)}, u32[]{:S(2)}, u32[]{:S(2)}) %collective-permute-start.10) | collective-permute-done | bytes 528416 | tf_op jit(solution)/shard_map/ppermute | solution.py:338
  47.4 4.3 %collective-permute-start.11 = (f32[1032,128]{1,0:T(8,128)S(1)}, f32[1032,128]{1,0:T(8,128)S(1)}, u32[]{:S(2)}, u32[]{:S(2)}) collective-permute-start(f32[1032,128]{1,0:T(8,128)S(1)} %copy-done.8), channel_id=1, source_target_pairs={{0,4},{1,5},{2,6},{3,7},{4,8},{5,9},{6,10},{7,11},{8,12},{9,13},{1... | collective-permute-start | bytes 1585160 | tf_op jit(solution)/shard_map/ppermute | solution.py:338
  51.8 1.6 %collective-permute-start.14 = (f32[1032,128]{1,0:T(8,128)S(1)}, f32[1032,128]{1,0:T(8,128)S(1)}, u32[]{:S(2)}, u32[]{:S(2)}) collective-permute-start(f32[1032,128]{1,0:T(8,128)S(1)} %get-tuple-element.86), channel_id=1, source_target_pairs={{0,2},{2,0},{1,3},{3,1},{4,6},{6,4},{5,7},{7,5},{8,10},{10,8},{9,1... | collective-permute-start | bytes 1585160 | tf_op jit(solution)/shard_map/ppermute | solution.py:335
  55.0 5.2 %collective-permute-done.11.refs_5_.refs_23_ = f32[1032,128]{1,0:T(8,128)S(1)} collective-permute-done((f32[1032,128]{1,0:T(8,128)S(1)}, f32[1032,128]{1,0:T(8,128)S(1)}, u32[]{:S(2)}, u32[]{:S(2)}) %collective-permute-start.11) | collective-permute-done | bytes 528416 | tf_op jit(solution)/shard_map/ppermute | solution.py:338
  60.4 3.7 %collective-permute-done.14.refs_13_.refs_8_.refs_32_ = f32[1032,128]{1,0:T(8,128)S(1)} collective-permute-done((f32[1032,128]{1,0:T(8,128)S(1)}, f32[1032,128]{1,0:T(8,128)S(1)}, u32[]{:S(2)}, u32[]{:S(2)}) %collective-permute-start.14) | collective-permute-done | bytes 528416 | tf_op jit(solution)/shard_map/ppermute | solution.py:335
  68.2 6.5 %shard_map.47 = (f32[256,512]{1,0:T(8,128)S(1)}, f32[256,512]{1,0:T(8,128)S(1)}, f32[256,512]{1,0:T(8,128)S(1)}, f32[256,512]{1,0:T(8,128)S(1)}, f32[256,512]{1,0:T(8,128)S(1)}, /*index=5*/f32[256,512]{1,0:T(8,128)S(1)}) custom-call(s32[4]{0:T(128)S(1)} %pad_add_fusion.flag_ref.refs_1_, bf16[4,512,256]{2,1,0:T(8,128)(2,1)S(1)} %copy-done, ...), custom_call_target="tpu_custom_call" | custom-call | tf_op jit(solution)/shard_map/pallas_call | solution.py:85
  74.6 3.0 %collective-permute-done.18.refs_9_.refs_33_.refs_2_.refs_8_ = f32[1032,128]{1,0:T(8,128)S(1)} collective-permute-done((f32[1032,128]{1,0:T(8,128)S(1)}, f32[1032,128]{1,0:T(8,128)S(1)}, u32[]{:S(2)}, u32[]{:S(2)}) %collective-permute-start.18) | collective-permute-done | bytes 528416 | tf_op jit(solution)/shard_map/ppermute | solution.py:335
  77.6 1.9 %collective-permute-done.17.refs_7_.refs_28_.refs_4_.refs_10_ = f32[1032,128]{1,0:T(8,128)S(1)} collective-permute-done((f32[1032,128]{1,0:T(8,128)S(1)}, f32[1032,128]{1,0:T(8,128)S(1)}, u32[]{:S(2)}, u32[]{:S(2)}) %collective-permute-start.17) | collective-permute-done | bytes 528416 | tf_op jit(solution)/shard_map/ppermute | solution.py:335
  79.6 2.3 %shard_map.48 = (f32[256,512]{1,0:T(8,128)S(1)}, f32[256,512]{1,0:T(8,128)S(1)}, f32[256,512]{1,0:T(8,128)S(1)}, f32[256,512]{1,0:T(8,128)S(1)}) custom-call(s32[4]{0:T(128)S(1)} %pad_add_fusion.flag_ref.refs_1_, bf16[4,512,256]{2,1,0:T(8,128)(2,1)S(1)} %copy-done, bf16[4,512,256]{2,1,0:T(8,128)(2,1)S(1)} %copy-done.1, ...), custom_call_target="tpu_custom_call" | custom-call | tf_op jit(solution)/shard_map/pallas_call | solution.py:85
  83.8 1.9 %collective-permute-start.24 = (f32[1032,128]{1,0:T(8,128)S(1)}, f32[1032,128]{1,0:T(8,128)S(1)}, u32[]{:S(2)}, u32[]{:S(2)}) collective-permute-start(f32[1032,128]{1,0:T(8,128)S(1)} %collective-permute-done.14.refs_13_.refs_8_.refs_32_), channel_id=1, source_target_pairs={{0,1},{1,0},{2,3},{3,2},{4,5},{5,4},{6,7},{7,6},{8,9},{9,8},{10,11... | collective-permute-start | bytes 1585160 | tf_op jit(solution)/shard_map/ppermute | solution.py:335
  85.8 4.2 %collective-permute-start.25 = (f32[1032,128]{1,0:T(8,128)S(1)}, f32[1032,128]{1,0:T(8,128)S(1)}, u32[]{:S(2)}, u32[]{:S(2)}) collective-permute-start(f32[1032,128]{1,0:T(8,128)S(1)} %collective-permute-done.18.refs_9_.refs_33_.refs_2_.refs_8_), channel_id=1, source_target_pairs={{0,1},{1,0},{4,5},{5,4},{8,9},{9,8},{12,13},{13,12},{16,17},{17,16... | collective-permute-start | bytes 1585160 | tf_op jit(solution)/shard_map/ppermute | solution.py:335
  92.7 11.3 %shard_map.49.refs_7_ = f32[4096,128]{1,0:T(8,128)S(1)} custom-call(f32[5]{0:T(128)S(1)} %stack.34.refs_0_, s32[4]{0:T(128)S(1)} %pad_add_fusion.flag_ref.refs_1_, f32[1,512]{1,0:T(1,128)S(1)} %bitcast.17, f32[256,512]{1,0:T(8,128)S(1)} %copy-done.5, f32[256,512]{1,0:T(8,128)S(1)} %copy-done.6, f32[256,512]{1,0:T(8,128)S(1)} %collective-permute-done.3.refs_5_, ...), custom_call_target="tpu_custom_call" | custom-call | tf_op jit(solution)/shard_map/pallas_call | solution.py:85
  104.1 1.9 %shard_map.50 = (f32[256,512]{1,0:T(8,128)S(1)}, f32[256,512]{1,0:T(8,128)S(1)}) custom-call(s32[4]{0:T(128)S(1)} %pad_add_fusion.flag_ref.refs_1_, bf16[4,512,256]{2,1,0:T(8,128)(2,1)S(1)} %copy-done, bf16[4,512,256]{2,1,0:T(8,128)(2,1)S(1)} %copy-done.1, f32[1032,128]{1,0:T(8,128)S(1)} %collective-permute-done.18.refs_9_.refs_33_.refs_2_.refs_8_, ...), custom_call_target="tpu_custom_call" | custom-call | tf_op jit(solution)/shard_map/pallas_call | solution.py:85
  106.0 3.7 %collective-permute-done.25.refs_6_.refs_13_ = f32[1032,128]{1,0:T(8,128)S(1)} collective-permute-done((f32[1032,128]{1,0:T(8,128)S(1)}, f32[1032,128]{1,0:T(8,128)S(1)}, u32[]{:S(2)}, u32[]{:S(2)}) %collective-permute-start.25) | collective-permute-done | bytes 528416 | tf_op jit(solution)/shard_map/ppermute | solution.py:335
  109.7 2.1 %shard_map.51 = (f32[256,512]{1,0:T(8,128)S(1)}, f32[256,512]{1,0:T(8,128)S(1)}) custom-call(s32[4]{0:T(128)S(1)} %pad_add_fusion.flag_ref.refs_1_, bf16[4,512,256]{2,1,0:T(8,128)(2,1)S(1)} %copy-done, bf16[4,512,256]{2,1,0:T(8,128)(2,1)S(1)} %copy-done.1, f32[256,512]{1,0:T(8,128)S(1)} %get-tuple-element.101.refs_2_, ...), custom_call_target="tpu_custom_call" | custom-call | tf_op jit(solution)/shard_map/pallas_call | solution.py:85
  114.5 5.3 %shard_map.52 = f32[4096,128]{1,0:T(8,128)} custom-call(f32[5]{0:T(128)S(1)} %stack.34.refs_0_, s32[4]{0:T(128)S(1)} %pad_add_fusion.flag_ref.refs_1_, f32[1,512]{1,0:T(1,128)S(1)} %bitcast.18, f32[256,512]{1,0:T(8,128)S(1)} %get-tuple-element.103.refs_3_, f32[256,512]{1,0:T(8,128)S(1)} %get-tuple-element.104.refs_4_, ...), custom_call_target="tpu_custom_call" | custom-call | tf_op jit(solution)/shard_map/pallas_call | solution.py:85
  (72 shorter events, 23.3 us)
Async XLA Ops:
  2.1 17.0 %collective-permute-start = (f32[1032,128]{1,0:T(8,128)S(1)}, f32[1032,128]{1,0:T(8,128)S(1)}, u32[]{:S(2)}, u32[]{:S(2)}) collective-permute-start(f32[1032,128]{1,0:T(8,128)S(1)} %pad_maximum_fusion.refs_34_.refs_14_), channel_id=1, source_target_pairs={{0,4},{1,5},{2,6},{3,7},{4,8},{5,9},{6,10},{7,11},{8,12},{9,13},{1... | collective-permute-start | bytes 1585160 | tf_op jit(solution)/shard_map/ppermute | solution.py:338
  7.1 17.8 %collective-permute-start.2 = (f32[1032,128]{1,0:T(8,128)S(1)}, f32[1032,128]{1,0:T(8,128)S(1)}, u32[]{:S(2)}, u32[]{:S(2)}) collective-permute-start(f32[1032,128]{1,0:T(8,128)S(1)} %pad_maximum_fusion.refs_34_.refs_14_), channel_id=1, source_target_pairs={{0,2},{1,3},{4,6},{5,7},{8,10},{9,11},{12,14},{13,15},{16,18},{17,... | collective-permute-start | bytes 1585160 | tf_op jit(solution)/shard_map/ppermute | solution.py:335
  10.6 15.1 %collective-permute-start.1 = (f32[1032,128]{1,0:T(8,128)S(1)}, f32[1032,128]{1,0:T(8,128)S(1)}, u32[]{:S(2)}, u32[]{:S(2)}) collective-permute-start(f32[1032,128]{1,0:T(8,128)S(1)} %pad_maximum_fusion.refs_34_.refs_14_), channel_id=1, source_target_pairs={{0,1},{2,3},{1,0},{4,5},{6,7},{5,4},{8,9},{10,11},{9,8},{12,13},{1... | collective-permute-start | bytes 1585160 | tf_op jit(solution)/shard_map/ppermute | solution.py:335
  19.1 14.3 %collective-permute-start.5 = (f32[1032,128]{1,0:T(8,128)}, f32[1032,128]{1,0:T(8,128)S(1)}, u32[]{:S(2)}, u32[]{:S(2)}) collective-permute-start(f32[1032,128]{1,0:T(8,128)} %get-tuple-element.64), channel_id=1, source_target_pairs={{0,4},{1,5},{2,6},{3,7},{4,8},{5,9},{6,10},{7,11},{8,12},{9,13},{1... | collective-permute-start | bytes 1585160 | tf_op jit(solution)/shard_map/ppermute | solution.py:338
  25.7 13.2 %collective-permute-start.8 = (f32[1032,128]{1,0:T(8,128)}, f32[1032,128]{1,0:T(8,128)S(1)}, u32[]{:S(2)}, u32[]{:S(2)}) collective-permute-start(f32[1032,128]{1,0:T(8,128)} %get-tuple-element.66), channel_id=1, source_target_pairs={{0,2},{2,0},{1,3},{3,1},{4,6},{6,4},{5,7},{7,5},{8,10},{10,8},{9,1... | collective-permute-start | bytes 1585160 | tf_op jit(solution)/shard_map/ppermute | solution.py:335
  27.2 13.2 %collective-permute-start.6 = (f32[1032,128]{1,0:T(8,128)}, f32[1032,128]{1,0:T(8,128)S(1)}, u32[]{:S(2)}, u32[]{:S(2)}) collective-permute-start(f32[1032,128]{1,0:T(8,128)} %get-tuple-element.65), channel_id=1, source_target_pairs={{0,1},{1,0},{2,3},{3,2},{4,5},{5,4},{6,7},{7,6},{8,9},{9,8},{10,11... | collective-permute-start | bytes 1585160 | tf_op jit(solution)/shard_map/ppermute | solution.py:335
  33.4 14.1 %collective-permute-start.10 = (f32[1032,128]{1,0:T(8,128)}, f32[1032,128]{1,0:T(8,128)S(1)}, u32[]{:S(2)}, u32[]{:S(2)}) collective-permute-start(f32[1032,128]{1,0:T(8,128)} %get-tuple-element.73), channel_id=1, source_target_pairs={{0,4},{1,5},{2,6},{3,7},{4,8},{5,9},{6,10},{7,11},{8,12},{9,13},{1... | collective-permute-start | bytes 1585160 | tf_op jit(solution)/shard_map/ppermute | solution.py:338
  38.8 13.0 %collective-permute-start.9 = (f32[1032,128]{1,0:T(8,128)S(1)}, f32[1032,128]{1,0:T(8,128)S(1)}, u32[]{:S(2)}, u32[]{:S(2)}) collective-permute-start(f32[1032,128]{1,0:T(8,128)S(1)} %get-tuple-element.75), channel_id=1, source_target_pairs={{0,2},{2,0},{1,3},{3,1},{4,6},{6,4},{5,7},{7,5},{8,10},{10,8},{9,1... | collective-permute-start | bytes 1585160 | tf_op jit(solution)/shard_map/ppermute | solution.py:335
  40.4 13.0 %collective-permute-start.7 = (f32[1032,128]{1,0:T(8,128)S(1)}, f32[1032,128]{1,0:T(8,128)S(1)}, u32[]{:S(2)}, u32[]{:S(2)}) collective-permute-start(f32[1032,128]{1,0:T(8,128)S(1)} %get-tuple-element.74), channel_id=1, source_target_pairs={{0,1},{1,0},{2,3},{3,2},{4,5},{5,4},{6,7},{7,6},{8,9},{9,8},{10,11... | collective-permute-start | bytes 1585160 | tf_op jit(solution)/shard_map/ppermute | solution.py:335
  47.4 12.8 %collective-permute-start.11 = (f32[1032,128]{1,0:T(8,128)S(1)}, f32[1032,128]{1,0:T(8,128)S(1)}, u32[]{:S(2)}, u32[]{:S(2)}) collective-permute-start(f32[1032,128]{1,0:T(8,128)S(1)} %copy-done.8), channel_id=1, source_target_pairs={{0,4},{1,5},{2,6},{3,7},{4,8},{5,9},{6,10},{7,11},{8,12},{9,13},{1... | collective-permute-start | bytes 1585160 | tf_op jit(solution)/shard_map/ppermute | solution.py:338
  51.8 12.2 %collective-permute-start.14 = (f32[1032,128]{1,0:T(8,128)S(1)}, f32[1032,128]{1,0:T(8,128)S(1)}, u32[]{:S(2)}, u32[]{:S(2)}) collective-permute-start(f32[1032,128]{1,0:T(8,128)S(1)} %get-tuple-element.86), channel_id=1, source_target_pairs={{0,2},{2,0},{1,3},{3,1},{4,6},{6,4},{5,7},{7,5},{8,10},{10,8},{9,1... | collective-permute-start | bytes 1585160 | tf_op jit(solution)/shard_map/ppermute | solution.py:335
  53.4 12.2 %collective-permute-start.12 = (f32[1032,128]{1,0:T(8,128)S(1)}, f32[1032,128]{1,0:T(8,128)S(1)}, u32[]{:S(2)}, u32[]{:S(2)}) collective-permute-start(f32[1032,128]{1,0:T(8,128)S(1)} %get-tuple-element.80), channel_id=1, source_target_pairs={{0,1},{1,0},{2,3},{3,2},{4,5},{5,4},{6,7},{7,6},{8,9},{9,8},{10,11... | collective-permute-start | bytes 1585160 | tf_op jit(solution)/shard_map/ppermute | solution.py:335
  64.1 13.5 %collective-permute-start.18 = (f32[1032,128]{1,0:T(8,128)S(1)}, f32[1032,128]{1,0:T(8,128)S(1)}, u32[]{:S(2)}, u32[]{:S(2)}) collective-permute-start(f32[1032,128]{1,0:T(8,128)S(1)} %get-tuple-element.94), channel_id=1, source_target_pairs={{0,2},{2,0},{1,3},{3,1},{4,6},{6,4},{5,7},{7,5},{8,10},{10,8},{9,1... | collective-permute-start | bytes 1585160 | tf_op jit(solution)/shard_map/ppermute | solution.py:335
  65.6 14.0 %collective-permute-start.17 = (f32[1032,128]{1,0:T(8,128)S(1)}, f32[1032,128]{1,0:T(8,128)S(1)}, u32[]{:S(2)}, u32[]{:S(2)}) collective-permute-start(f32[1032,128]{1,0:T(8,128)S(1)} %get-tuple-element.93), channel_id=1, source_target_pairs={{0,1},{1,0},{2,3},{3,2},{4,5},{5,4},{6,7},{7,6},{8,9},{9,8},{10,11... | collective-permute-start | bytes 1585160 | tf_op jit(solution)/shard_map/ppermute | solution.py:335
  67.1 14.8 %collective-permute-start.3 = (f32[256,512]{1,0:T(8,128)S(1)}, f32[256,512]{1,0:T(8,128)S(1)}, u32[]{:S(2)}, u32[]{:S(2)}) collective-permute-start(f32[256,512]{1,0:T(8,128)S(1)} %copy-done.5), channel_id=1, source_target_pairs={{0,16},{16,0},{1,17},{17,1},{2,18},{18,2},{3,19},{19,3},{4,20},{20... | collective-permute-start | bytes 1572872 | tf_op jit(solution)/shard_map/ppermute | solution.py:342
  67.1 15.3 %collective-permute-start.4 = (f32[256,512]{1,0:T(8,128)S(1)}, f32[256,512]{1,0:T(8,128)S(1)}, u32[]{:S(2)}, u32[]{:S(2)}) collective-permute-start(f32[256,512]{1,0:T(8,128)S(1)} %copy-done.6), channel_id=1, source_target_pairs={{0,16},{16,0},{1,17},{17,1},{2,18},{18,2},{3,19},{19,3},{4,20},{20... | collective-permute-start | bytes 1572872 | tf_op jit(solution)/shard_map/ppermute | solution.py:342
  67.6 18.2 %collective-permute-start.13 = (f32[1032,128]{1,0:T(8,128)S(1)}, f32[1032,128]{1,0:T(8,128)S(1)}, u32[]{:S(2)}, u32[]{:S(2)}) collective-permute-start(f32[1032,128]{1,0:T(8,128)S(1)} %broadcast_select_fusion.1), channel_id=1, source_target_pairs={{0,1},{1,3},{3,2},{2,0},{4,5},{5,7},{7,6},{6,4},{8,9},{9,11},{11,1... | collective-permute-start | bytes 1585160 | tf_op jit(solution)/shard_map/ppermute | solution.py:335
  77.6 4.9 %collective-permute-start.15 = (f32[256,512]{1,0:T(8,128)S(1)}, f32[256,512]{1,0:T(8,128)S(1)}, u32[]{:S(2)}, u32[]{:S(2)}) collective-permute-start(f32[256,512]{1,0:T(8,128)S(1)} %get-tuple-element.87.refs_7_), channel_id=1, source_target_pairs={{0,16},{16,0},{1,17},{17,1},{2,18},{18,2},{3,19},{19,3},{4,20},{20... | collective-permute-start | bytes 1572872 | tf_op jit(solution)/shard_map/ppermute | solution.py:342
  79.6 4.3 %collective-permute-start.16 = (f32[256,512]{1,0:T(8,128)S(1)}, f32[256,512]{1,0:T(8,128)S(1)}, u32[]{:S(2)}, u32[]{:S(2)}) collective-permute-start(f32[256,512]{1,0:T(8,128)S(1)} %get-tuple-element.88.refs_8_), channel_id=1, source_target_pairs={{0,16},{16,0},{1,17},{17,1},{2,18},{18,2},{3,19},{19,3},{4,20},{20... | collective-permute-start | bytes 1572872 | tf_op jit(solution)/shard_map/ppermute | solution.py:342
  81.9 8.1 %collective-permute-start.19 = (f32[256,512]{1,0:T(8,128)S(1)}, f32[256,512]{1,0:T(8,128)S(1)}, u32[]{:S(2)}, u32[]{:S(2)}) collective-permute-start(f32[256,512]{1,0:T(8,128)S(1)} %get-tuple-element.95.refs_11_), channel_id=1, source_target_pairs={{0,16},{16,0},{1,17},{17,1},{2,18},{18,2},{3,19},{19,3},{4,20},{20... | collective-permute-start | bytes 1572872 | tf_op jit(solution)/shard_map/ppermute | solution.py:342
  82.4 7.6 %collective-permute-start.20 = (f32[256,512]{1,0:T(8,128)S(1)}, f32[256,512]{1,0:T(8,128)S(1)}, u32[]{:S(2)}, u32[]{:S(2)}) collective-permute-start(f32[256,512]{1,0:T(8,128)S(1)} %get-tuple-element.96.refs_12_), channel_id=1, source_target_pairs={{0,16},{16,0},{1,17},{17,1},{2,18},{18,2},{3,19},{19,3},{4,20},{20... | collective-permute-start | bytes 1572872 | tf_op jit(solution)/shard_map/ppermute | solution.py:342
  82.5 21.5 %collective-permute-start.23 = (f32[1032,128]{1,0:T(8,128)S(1)}, f32[1032,128]{1,0:T(8,128)S(1)}, u32[]{:S(2)}, u32[]{:S(2)}) collective-permute-start(f32[1032,128]{1,0:T(8,128)S(1)} %get-tuple-element.115), channel_id=1, source_target_pairs={{2,0},{3,2},{6,4},{7,6},{10,8},{11,10},{14,12},{15,14},{18,16},{19... | collective-permute-start | bytes 1585160 | tf_op jit(solution)/shard_map/ppermute | solution.py:335
  83.8 22.1 %collective-permute-start.24 = (f32[1032,128]{1,0:T(8,128)S(1)}, f32[1032,128]{1,0:T(8,128)S(1)}, u32[]{:S(2)}, u32[]{:S(2)}) collective-permute-start(f32[1032,128]{1,0:T(8,128)S(1)} %collective-permute-done.14.refs_13_.refs_8_.refs_32_), channel_id=1, source_target_pairs={{0,1},{1,0},{2,3},{3,2},{4,5},{5,4},{6,7},{7,6},{8,9},{9,8},{10,11... | collective-permute-start | bytes 1585160 | tf_op jit(solution)/shard_map/ppermute | solution.py:335
  85.8 23.9 %collective-permute-start.25 = (f32[1032,128]{1,0:T(8,128)S(1)}, f32[1032,128]{1,0:T(8,128)S(1)}, u32[]{:S(2)}, u32[]{:S(2)}) collective-permute-start(f32[1032,128]{1,0:T(8,128)S(1)} %collective-permute-done.18.refs_9_.refs_33_.refs_2_.refs_8_), channel_id=1, source_target_pairs={{0,1},{1,0},{4,5},{5,4},{8,9},{9,8},{12,13},{13,12},{16,17},{17,16... | collective-permute-start | bytes 1585160 | tf_op jit(solution)/shard_map/ppermute | solution.py:335
  (15 other events, 143.4 us)

commit v12 on v11

--- a/solution.py
+++ b/solution.py
@@ -14,7 +14,7 @@
 CHUNKS = 4
 VMEM_LIMIT = 32 * 1024 * 1024
 FIRST_LIMIT = 60 * 1024 * 1024
-LAST_LIMIT = 24 * 1024 * 1024
+LAST_LIMIT = 16 * 1024 * 1024
 HALVES = 2
 
 

time: 120 us -> 120 us (level)
  no operation moved by 1% of the time
where the time goes in v12:
time: 120 us
  starting transfers between devices  46.4 us (39%)
  Pallas kernels  34.4 us (29%)
  waiting for transfers between devices  28.7 us (24%)
  other arithmetic  4.39 us (4%)
  between operations  3.74 us (3%)
  local copies, waits for them, and re-layouts  2.34 us (2%)
    pallas_call x7, Pallas kernels, call(): pl.pallas_call(kernel, out_shape=outputs, in_specs=[pl.BlockSpec(memory_s...  34.4 us
    ppermute x14, starting transfers between devices, within(): lax.ppermute(block, 'occ', [(g + a, g + b) for g in planes for a, b in mo...  27 us
    ppermute x4, starting transfers between devices, up(): lax.ppermute(block, 'occ', [(g, g + PLANE) for g in range(groups - PLANE)])  17.1 us
    ppermute x14, waiting for transfers between devices, within(): lax.ppermute(block, 'occ', [(g + a, g + b) for g in planes for a, b in mo...  12.4 us
    ppermute x4, waiting for transfers between devices, up(): lax.ppermute(block, 'occ', [(g, g + PLANE) for g in range(groups - PLANE)])  12 us
    ppermute x10, waiting for transfers between devices, totals(): lax.ppermute(part, 'aux', [(0, 1), (1, 0)])  4.31 us
    select_n x3, other arithmetic, on_device(): jnp.where(odd_y, came, up_part)  3.34 us
  transfers between devices with their start and end apart: 28, of which 11 were waited for; matrix products, arithmetic and copies ran while one was open for 4% of the time, Pallas kernels for 23%

profile of v12, /device:TPU:0, one launch (start us, length us, event | category | flops | bytes accessed | tf_op | source)
XLA Modules:
  0.0 119.9 jit_solution(17278992673903438213)
XLA Ops:
  2.1 5.0 %collective-permute-start = (f32[1032,128]{1,0:T(8,128)S(1)}, f32[1032,128]{1,0:T(8,128)S(1)}, u32[]{:S(2)}, u32[]{:S(2)}) collective-permute-start(f32[1032,128]{1,0:T(8,128)S(1)} %pad_maximum_fusion.refs_34_.refs_14_), channel_id=1, source_target_pairs={{0,4},{1,5},{2,6},{3,7},{4,8},{5,9},{6,10},{7,11},{8,12},{9,13},{1... | collective-permute-start | bytes 1585160 | tf_op jit(solution)/shard_map/ppermute | solution.py:338
  7.1 3.5 %collective-permute-start.2 = (f32[1032,128]{1,0:T(8,128)S(1)}, f32[1032,128]{1,0:T(8,128)S(1)}, u32[]{:S(2)}, u32[]{:S(2)}) collective-permute-start(f32[1032,128]{1,0:T(8,128)S(1)} %pad_maximum_fusion.refs_34_.refs_14_), channel_id=1, source_target_pairs={{0,2},{1,3},{4,6},{5,7},{8,10},{9,11},{12,14},{13,15},{16,18},{17,... | collective-permute-start | bytes 1585160 | tf_op jit(solution)/shard_map/ppermute | solution.py:335
  10.6 3.4 %collective-permute-start.1 = (f32[1032,128]{1,0:T(8,128)S(1)}, f32[1032,128]{1,0:T(8,128)S(1)}, u32[]{:S(2)}, u32[]{:S(2)}) collective-permute-start(f32[1032,128]{1,0:T(8,128)S(1)} %pad_maximum_fusion.refs_34_.refs_14_), channel_id=1, source_target_pairs={{0,1},{2,3},{1,0},{4,5},{6,7},{5,4},{8,9},{10,11},{9,8},{12,13},{1... | collective-permute-start | bytes 1585160 | tf_op jit(solution)/shard_map/ppermute | solution.py:335
  14.0 5.1 %shard_map.46 = (bf16[4,512,256]{2,1,0:T(8,128)(2,1)}, bf16[4,512,256]{2,1,0:T(8,128)(2,1)}, f32[256,512]{1,0:T(8,128)}, f32[256,512]{1,0:T(8,128)}, f32[1032,12...) custom-call(f32[8,128]{1,0:T(8,128)} %copy-done.9, f32[4096,128]{1,0:T(8,128)} %bitcast.15), custom_call_target="tpu_custom_call" | custom-call | tf_op jit(solution)/shard_map/pallas_call | solution.py:85
  19.1 3.6 %collective-permute-start.5 = (f32[1032,128]{1,0:T(8,128)}, f32[1032,128]{1,0:T(8,128)S(1)}, u32[]{:S(2)}, u32[]{:S(2)}) collective-permute-start(f32[1032,128]{1,0:T(8,128)} %get-tuple-element.64), channel_id=1, source_target_pairs={{0,4},{1,5},{2,6},{3,7},{4,8},{5,9},{6,10},{7,11},{8,12},{9,13},{1... | collective-permute-start | bytes 1585160 | tf_op jit(solution)/shard_map/ppermute | solution.py:338
  22.7 2.1 %broadcast_select_fusion.5 = (f32[1032,128]{1,0:T(8,128)}, f32[1032,128]{1,0:T(8,128)}) fusion(f32[1032,128]{1,0:T(8,128)S(1)} %collective-permute-done.refs_2_.refs_20_, f32[1032,128]{1,0:T(8,128)} %get-tuple-element.64, pred[]{:T(512)S(6)} %eq.44, pred[]{:T(512)S(6)} %eq.43), kind=kLoop, calls=%fused_computation.6 | loop fusion | flops 264192 | bytes 2113538 | tf_op jit(solution)/shard_map/jit(_where)/select_n | solution.py:386
  33.4 4.3 %collective-permute-start.10 = (f32[1032,128]{1,0:T(8,128)}, f32[1032,128]{1,0:T(8,128)S(1)}, u32[]{:S(2)}, u32[]{:S(2)}) collective-permute-start(f32[1032,128]{1,0:T(8,128)} %get-tuple-element.73), channel_id=1, source_target_pairs={{0,4},{1,5},{2,6},{3,7},{4,8},{5,9},{6,10},{7,11},{8,12},{9,13},{1... | collective-permute-start | bytes 1585160 | tf_op jit(solution)/shard_map/ppermute | solution.py:338
  38.8 1.6 %collective-permute-start.9 = (f32[1032,128]{1,0:T(8,128)S(1)}, f32[1032,128]{1,0:T(8,128)S(1)}, u32[]{:S(2)}, u32[]{:S(2)}) collective-permute-start(f32[1032,128]{1,0:T(8,128)S(1)} %get-tuple-element.75), channel_id=1, source_target_pairs={{0,2},{2,0},{1,3},{3,1},{4,6},{6,4},{5,7},{7,5},{8,10},{10,8},{9,1... | collective-permute-start | bytes 1585160 | tf_op jit(solution)/shard_map/ppermute | solution.py:335
  41.9 5.5 %collective-permute-done.10.refs_4_.refs_22_ = f32[1032,128]{1,0:T(8,128)S(1)} collective-permute-done((f32[1032,128]{1,0:T(8,128)}, f32[1032,128]{1,0:T(8,128)S(1)}, u32[]{:S(2)}, u32[]{:S(2)}) %collective-permute-start.10) | collective-permute-done | bytes 528416 | tf_op jit(solution)/shard_map/ppermute | solution.py:338
  47.4 4.3 %collective-permute-start.11 = (f32[1032,128]{1,0:T(8,128)S(1)}, f32[1032,128]{1,0:T(8,128)S(1)}, u32[]{:S(2)}, u32[]{:S(2)}) collective-permute-start(f32[1032,128]{1,0:T(8,128)S(1)} %copy-done.8), channel_id=1, source_target_pairs={{0,4},{1,5},{2,6},{3,7},{4,8},{5,9},{6,10},{7,11},{8,12},{9,13},{1... | collective-permute-start | bytes 1585160 | tf_op jit(solution)/shard_map/ppermute | solution.py:338
  51.8 1.6 %collective-permute-start.14 = (f32[1032,128]{1,0:T(8,128)S(1)}, f32[1032,128]{1,0:T(8,128)S(1)}, u32[]{:S(2)}, u32[]{:S(2)}) collective-permute-start(f32[1032,128]{1,0:T(8,128)S(1)} %get-tuple-element.86), channel_id=1, source_target_pairs={{0,2},{2,0},{1,3},{3,1},{4,6},{6,4},{5,7},{7,5},{8,10},{10,8},{9,1... | collective-permute-start | bytes 1585160 | tf_op jit(solution)/shard_map/ppermute | solution.py:335
  55.0 5.2 %collective-permute-done.11.refs_5_.refs_23_ = f32[1032,128]{1,0:T(8,128)S(1)} collective-permute-done((f32[1032,128]{1,0:T(8,128)S(1)}, f32[1032,128]{1,0:T(8,128)S(1)}, u32[]{:S(2)}, u32[]{:S(2)}) %collective-permute-start.11) | collective-permute-done | bytes 528416 | tf_op jit(solution)/shard_map/ppermute | solution.py:338
  60.4 3.7 %collective-permute-done.14.refs_13_.refs_8_.refs_32_ = f32[1032,128]{1,0:T(8,128)S(1)} collective-permute-done((f32[1032,128]{1,0:T(8,128)S(1)}, f32[1032,128]{1,0:T(8,128)S(1)}, u32[]{:S(2)}, u32[]{:S(2)}) %collective-permute-start.14) | collective-permute-done | bytes 528416 | tf_op jit(solution)/shard_map/ppermute | solution.py:335
  68.2 6.5 %shard_map.47 = (f32[256,512]{1,0:T(8,128)S(1)}, f32[256,512]{1,0:T(8,128)S(1)}, f32[256,512]{1,0:T(8,128)S(1)}, f32[256,512]{1,0:T(8,128)S(1)}, f32[256,512]{1,0:T(8,128)S(1)}, /*index=5*/f32[256,512]{1,0:T(8,128)S(1)}) custom-call(s32[4]{0:T(128)S(1)} %pad_add_fusion.flag_ref.refs_1_, bf16[4,512,256]{2,1,0:T(8,128)(2,1)S(1)} %copy-done, ...), custom_call_target="tpu_custom_call" | custom-call | tf_op jit(solution)/shard_map/pallas_call | solution.py:85
  74.6 3.0 %collective-permute-done.18.refs_9_.refs_33_.refs_2_.refs_8_ = f32[1032,128]{1,0:T(8,128)S(1)} collective-permute-done((f32[1032,128]{1,0:T(8,128)S(1)}, f32[1032,128]{1,0:T(8,128)S(1)}, u32[]{:S(2)}, u32[]{:S(2)}) %collective-permute-start.18) | collective-permute-done | bytes 528416 | tf_op jit(solution)/shard_map/ppermute | solution.py:335
  77.6 1.9 %collective-permute-done.17.refs_7_.refs_28_.refs_4_.refs_10_ = f32[1032,128]{1,0:T(8,128)S(1)} collective-permute-done((f32[1032,128]{1,0:T(8,128)S(1)}, f32[1032,128]{1,0:T(8,128)S(1)}, u32[]{:S(2)}, u32[]{:S(2)}) %collective-permute-start.17) | collective-permute-done | bytes 528416 | tf_op jit(solution)/shard_map/ppermute | solution.py:335
  79.6 2.3 %shard_map.48 = (f32[256,512]{1,0:T(8,128)S(1)}, f32[256,512]{1,0:T(8,128)S(1)}, f32[256,512]{1,0:T(8,128)S(1)}, f32[256,512]{1,0:T(8,128)S(1)}) custom-call(s32[4]{0:T(128)S(1)} %pad_add_fusion.flag_ref.refs_1_, bf16[4,512,256]{2,1,0:T(8,128)(2,1)S(1)} %copy-done, bf16[4,512,256]{2,1,0:T(8,128)(2,1)S(1)} %copy-done.1, ...), custom_call_target="tpu_custom_call" | custom-call | tf_op jit(solution)/shard_map/pallas_call | solution.py:85
  83.8 1.9 %collective-permute-start.24 = (f32[1032,128]{1,0:T(8,128)S(1)}, f32[1032,128]{1,0:T(8,128)S(1)}, u32[]{:S(2)}, u32[]{:S(2)}) collective-permute-start(f32[1032,128]{1,0:T(8,128)S(1)} %collective-permute-done.14.refs_13_.refs_8_.refs_32_), channel_id=1, source_target_pairs={{0,1},{1,0},{2,3},{3,2},{4,5},{5,4},{6,7},{7,6},{8,9},{9,8},{10,11... | collective-permute-start | bytes 1585160 | tf_op jit(solution)/shard_map/ppermute | solution.py:335
  85.8 4.2 %collective-permute-start.25 = (f32[1032,128]{1,0:T(8,128)S(1)}, f32[1032,128]{1,0:T(8,128)S(1)}, u32[]{:S(2)}, u32[]{:S(2)}) collective-permute-start(f32[1032,128]{1,0:T(8,128)S(1)} %collective-permute-done.18.refs_9_.refs_33_.refs_2_.refs_8_), channel_id=1, source_target_pairs={{0,1},{1,0},{4,5},{5,4},{8,9},{9,8},{12,13},{13,12},{16,17},{17,16... | collective-permute-start | bytes 1585160 | tf_op jit(solution)/shard_map/ppermute | solution.py:335
  92.7 11.3 %shard_map.49.refs_7_ = f32[4096,128]{1,0:T(8,128)S(1)} custom-call(f32[5]{0:T(128)S(1)} %stack.34.refs_0_, s32[4]{0:T(128)S(1)} %pad_add_fusion.flag_ref.refs_1_, f32[1,512]{1,0:T(1,128)S(1)} %bitcast.17, f32[256,512]{1,0:T(8,128)S(1)} %copy-done.5, f32[256,512]{1,0:T(8,128)S(1)} %copy-done.6, f32[256,512]{1,0:T(8,128)S(1)} %collective-permute-done.3.refs_5_, ...), custom_call_target="tpu_custom_call" | custom-call | tf_op jit(solution)/shard_map/pallas_call | solution.py:85
  104.1 1.9 %shard_map.50 = (f32[256,512]{1,0:T(8,128)S(1)}, f32[256,512]{1,0:T(8,128)S(1)}) custom-call(s32[4]{0:T(128)S(1)} %pad_add_fusion.flag_ref.refs_1_, bf16[4,512,256]{2,1,0:T(8,128)(2,1)S(1)} %copy-done, bf16[4,512,256]{2,1,0:T(8,128)(2,1)S(1)} %copy-done.1, f32[1032,128]{1,0:T(8,128)S(1)} %collective-permute-done.18.refs_9_.refs_33_.refs_2_.refs_8_, ...), custom_call_target="tpu_custom_call" | custom-call | tf_op jit(solution)/shard_map/pallas_call | solution.py:85
  106.0 3.7 %collective-permute-done.25.refs_6_.refs_13_ = f32[1032,128]{1,0:T(8,128)S(1)} collective-permute-done((f32[1032,128]{1,0:T(8,128)S(1)}, f32[1032,128]{1,0:T(8,128)S(1)}, u32[]{:S(2)}, u32[]{:S(2)}) %collective-permute-start.25) | collective-permute-done | bytes 528416 | tf_op jit(solution)/shard_map/ppermute | solution.py:335
  109.7 2.1 %shard_map.51 = (f32[256,512]{1,0:T(8,128)S(1)}, f32[256,512]{1,0:T(8,128)S(1)}) custom-call(s32[4]{0:T(128)S(1)} %pad_add_fusion.flag_ref.refs_1_, bf16[4,512,256]{2,1,0:T(8,128)(2,1)S(1)} %copy-done, bf16[4,512,256]{2,1,0:T(8,128)(2,1)S(1)} %copy-done.1, f32[256,512]{1,0:T(8,128)S(1)} %get-tuple-element.101.refs_2_, ...), custom_call_target="tpu_custom_call" | custom-call | tf_op jit(solution)/shard_map/pallas_call | solution.py:85
  114.5 5.3 %shard_map.52 = f32[4096,128]{1,0:T(8,128)} custom-call(f32[5]{0:T(128)S(1)} %stack.34.refs_0_, s32[4]{0:T(128)S(1)} %pad_add_fusion.flag_ref.refs_1_, f32[1,512]{1,0:T(1,128)S(1)} %bitcast.18, f32[256,512]{1,0:T(8,128)S(1)} %get-tuple-element.103.refs_3_, f32[256,512]{1,0:T(8,128)S(1)} %get-tuple-element.104.refs_4_, ...), custom_call_target="tpu_custom_call" | custom-call | tf_op jit(solution)/shard_map/pallas_call | solution.py:85
  (72 shorter events, 23.3 us)
Async XLA Ops:
  2.1 17.0 %collective-permute-start = (f32[1032,128]{1,0:T(8,128)S(1)}, f32[1032,128]{1,0:T(8,128)S(1)}, u32[]{:S(2)}, u32[]{:S(2)}) collective-permute-start(f32[1032,128]{1,0:T(8,128)S(1)} %pad_maximum_fusion.refs_34_.refs_14_), channel_id=1, source_target_pairs={{0,4},{1,5},{2,6},{3,7},{4,8},{5,9},{6,10},{7,11},{8,12},{9,13},{1... | collective-permute-start | bytes 1585160 | tf_op jit(solution)/shard_map/ppermute | solution.py:338
  7.1 17.8 %collective-permute-start.2 = (f32[1032,128]{1,0:T(8,128)S(1)}, f32[1032,128]{1,0:T(8,128)S(1)}, u32[]{:S(2)}, u32[]{:S(2)}) collective-permute-start(f32[1032,128]{1,0:T(8,128)S(1)} %pad_maximum_fusion.refs_34_.refs_14_), channel_id=1, source_target_pairs={{0,2},{1,3},{4,6},{5,7},{8,10},{9,11},{12,14},{13,15},{16,18},{17,... | collective-permute-start | bytes 1585160 | tf_op jit(solution)/shard_map/ppermute | solution.py:335
  10.6 15.1 %collective-permute-start.1 = (f32[1032,128]{1,0:T(8,128)S(1)}, f32[1032,128]{1,0:T(8,128)S(1)}, u32[]{:S(2)}, u32[]{:S(2)}) collective-permute-start(f32[1032,128]{1,0:T(8,128)S(1)} %pad_maximum_fusion.refs_34_.refs_14_), channel_id=1, source_target_pairs={{0,1},{2,3},{1,0},{4,5},{6,7},{5,4},{8,9},{10,11},{9,8},{12,13},{1... | collective-permute-start | bytes 1585160 | tf_op jit(solution)/shard_map/ppermute | solution.py:335
  19.1 14.3 %collective-permute-start.5 = (f32[1032,128]{1,0:T(8,128)}, f32[1032,128]{1,0:T(8,128)S(1)}, u32[]{:S(2)}, u32[]{:S(2)}) collective-permute-start(f32[1032,128]{1,0:T(8,128)} %get-tuple-element.64), channel_id=1, source_target_pairs={{0,4},{1,5},{2,6},{3,7},{4,8},{5,9},{6,10},{7,11},{8,12},{9,13},{1... | collective-permute-start | bytes 1585160 | tf_op jit(solution)/shard_map/ppermute | solution.py:338
  25.7 13.2 %collective-permute-start.8 = (f32[1032,128]{1,0:T(8,128)}, f32[1032,128]{1,0:T(8,128)S(1)}, u32[]{:S(2)}, u32[]{:S(2)}) collective-permute-start(f32[1032,128]{1,0:T(8,128)} %get-tuple-element.66), channel_id=1, source_target_pairs={{0,2},{2,0},{1,3},{3,1},{4,6},{6,4},{5,7},{7,5},{8,10},{10,8},{9,1... | collective-permute-start | bytes 1585160 | tf_op jit(solution)/shard_map/ppermute | solution.py:335
  27.2 13.2 %collective-permute-start.6 = (f32[1032,128]{1,0:T(8,128)}, f32[1032,128]{1,0:T(8,128)S(1)}, u32[]{:S(2)}, u32[]{:S(2)}) collective-permute-start(f32[1032,128]{1,0:T(8,128)} %get-tuple-element.65), channel_id=1, source_target_pairs={{0,1},{1,0},{2,3},{3,2},{4,5},{5,4},{6,7},{7,6},{8,9},{9,8},{10,11... | collective-permute-start | bytes 1585160 | tf_op jit(solution)/shard_map/ppermute | solution.py:335
  33.4 14.1 %collective-permute-start.10 = (f32[1032,128]{1,0:T(8,128)}, f32[1032,128]{1,0:T(8,128)S(1)}, u32[]{:S(2)}, u32[]{:S(2)}) collective-permute-start(f32[1032,128]{1,0:T(8,128)} %get-tuple-element.73), channel_id=1, source_target_pairs={{0,4},{1,5},{2,6},{3,7},{4,8},{5,9},{6,10},{7,11},{8,12},{9,13},{1... | collective-permute-start | bytes 1585160 | tf_op jit(solution)/shard_map/ppermute | solution.py:338
  38.8 13.0 %collective-permute-start.9 = (f32[1032,128]{1,0:T(8,128)S(1)}, f32[1032,128]{1,0:T(8,128)S(1)}, u32[]{:S(2)}, u32[]{:S(2)}) collective-permute-start(f32[1032,128]{1,0:T(8,128)S(1)} %get-tuple-element.75), channel_id=1, source_target_pairs={{0,2},{2,0},{1,3},{3,1},{4,6},{6,4},{5,7},{7,5},{8,10},{10,8},{9,1... | collective-permute-start | bytes 1585160 | tf_op jit(solution)/shard_map/ppermute | solution.py:335
  40.4 13.0 %collective-permute-start.7 = (f32[1032,128]{1,0:T(8,128)S(1)}, f32[1032,128]{1,0:T(8,128)S(1)}, u32[]{:S(2)}, u32[]{:S(2)}) collective-permute-start(f32[1032,128]{1,0:T(8,128)S(1)} %get-tuple-element.74), channel_id=1, source_target_pairs={{0,1},{1,0},{2,3},{3,2},{4,5},{5,4},{6,7},{7,6},{8,9},{9,8},{10,11... | collective-permute-start | bytes 1585160 | tf_op jit(solution)/shard_map/ppermute | solution.py:335
  47.4 12.8 %collective-permute-start.11 = (f32[1032,128]{1,0:T(8,128)S(1)}, f32[1032,128]{1,0:T(8,128)S(1)}, u32[]{:S(2)}, u32[]{:S(2)}) collective-permute-start(f32[1032,128]{1,0:T(8,128)S(1)} %copy-done.8), channel_id=1, source_target_pairs={{0,4},{1,5},{2,6},{3,7},{4,8},{5,9},{6,10},{7,11},{8,12},{9,13},{1... | collective-permute-start | bytes 1585160 | tf_op jit(solution)/shard_map/ppermute | solution.py:338
  51.8 12.2 %collective-permute-start.14 = (f32[1032,128]{1,0:T(8,128)S(1)}, f32[1032,128]{1,0:T(8,128)S(1)}, u32[]{:S(2)}, u32[]{:S(2)}) collective-permute-start(f32[1032,128]{1,0:T(8,128)S(1)} %get-tuple-element.86), channel_id=1, source_target_pairs={{0,2},{2,0},{1,3},{3,1},{4,6},{6,4},{5,7},{7,5},{8,10},{10,8},{9,1... | collective-permute-start | bytes 1585160 | tf_op jit(solution)/shard_map/ppermute | solution.py:335
  53.4 12.2 %collective-permute-start.12 = (f32[1032,128]{1,0:T(8,128)S(1)}, f32[1032,128]{1,0:T(8,128)S(1)}, u32[]{:S(2)}, u32[]{:S(2)}) collective-permute-start(f32[1032,128]{1,0:T(8,128)S(1)} %get-tuple-element.80), channel_id=1, source_target_pairs={{0,1},{1,0},{2,3},{3,2},{4,5},{5,4},{6,7},{7,6},{8,9},{9,8},{10,11... | collective-permute-start | bytes 1585160 | tf_op jit(solution)/shard_map/ppermute | solution.py:335
  64.1 13.5 %collective-permute-start.18 = (f32[1032,128]{1,0:T(8,128)S(1)}, f32[1032,128]{1,0:T(8,128)S(1)}, u32[]{:S(2)}, u32[]{:S(2)}) collective-permute-start(f32[1032,128]{1,0:T(8,128)S(1)} %get-tuple-element.94), channel_id=1, source_target_pairs={{0,2},{2,0},{1,3},{3,1},{4,6},{6,4},{5,7},{7,5},{8,10},{10,8},{9,1... | collective-permute-start | bytes 1585160 | tf_op jit(solution)/shard_map/ppermute | solution.py:335
  65.6 14.0 %collective-permute-start.17 = (f32[1032,128]{1,0:T(8,128)S(1)}, f32[1032,128]{1,0:T(8,128)S(1)}, u32[]{:S(2)}, u32[]{:S(2)}) collective-permute-start(f32[1032,128]{1,0:T(8,128)S(1)} %get-tuple-element.93), channel_id=1, source_target_pairs={{0,1},{1,0},{2,3},{3,2},{4,5},{5,4},{6,7},{7,6},{8,9},{9,8},{10,11... | collective-permute-start | bytes 1585160 | tf_op jit(solution)/shard_map/ppermute | solution.py:335
  67.1 14.8 %collective-permute-start.3 = (f32[256,512]{1,0:T(8,128)S(1)}, f32[256,512]{1,0:T(8,128)S(1)}, u32[]{:S(2)}, u32[]{:S(2)}) collective-permute-start(f32[256,512]{1,0:T(8,128)S(1)} %copy-done.5), channel_id=1, source_target_pairs={{0,16},{16,0},{1,17},{17,1},{2,18},{18,2},{3,19},{19,3},{4,20},{20... | collective-permute-start | bytes 1572872 | tf_op jit(solution)/shard_map/ppermute | solution.py:342
  67.1 15.3 %collective-permute-start.4 = (f32[256,512]{1,0:T(8,128)S(1)}, f32[256,512]{1,0:T(8,128)S(1)}, u32[]{:S(2)}, u32[]{:S(2)}) collective-permute-start(f32[256,512]{1,0:T(8,128)S(1)} %copy-done.6), channel_id=1, source_target_pairs={{0,16},{16,0},{1,17},{17,1},{2,18},{18,2},{3,19},{19,3},{4,20},{20... | collective-permute-start | bytes 1572872 | tf_op jit(solution)/shard_map/ppermute | solution.py:342
  67.6 18.2 %collective-permute-start.13 = (f32[1032,128]{1,0:T(8,128)S(1)}, f32[1032,128]{1,0:T(8,128)S(1)}, u32[]{:S(2)}, u32[]{:S(2)}) collective-permute-start(f32[1032,128]{1,0:T(8,128)S(1)} %broadcast_select_fusion.1), channel_id=1, source_target_pairs={{0,1},{1,3},{3,2},{2,0},{4,5},{5,7},{7,6},{6,4},{8,9},{9,11},{11,1... | collective-permute-start | bytes 1585160 | tf_op jit(solution)/shard_map/ppermute | solution.py:335
  77.6 4.9 %collective-permute-start.15 = (f32[256,512]{1,0:T(8,128)S(1)}, f32[256,512]{1,0:T(8,128)S(1)}, u32[]{:S(2)}, u32[]{:S(2)}) collective-permute-start(f32[256,512]{1,0:T(8,128)S(1)} %get-tuple-element.87.refs_7_), channel_id=1, source_target_pairs={{0,16},{16,0},{1,17},{17,1},{2,18},{18,2},{3,19},{19,3},{4,20},{20... | collective-permute-start | bytes 1572872 | tf_op jit(solution)/shard_map/ppermute | solution.py:342
  79.6 4.3 %collective-permute-start.16 = (f32[256,512]{1,0:T(8,128)S(1)}, f32[256,512]{1,0:T(8,128)S(1)}, u32[]{:S(2)}, u32[]{:S(2)}) collective-permute-start(f32[256,512]{1,0:T(8,128)S(1)} %get-tuple-element.88.refs_8_), channel_id=1, source_target_pairs={{0,16},{16,0},{1,17},{17,1},{2,18},{18,2},{3,19},{19,3},{4,20},{20... | collective-permute-start | bytes 1572872 | tf_op jit(solution)/shard_map/ppermute | solution.py:342
  81.9 8.1 %collective-permute-start.19 = (f32[256,512]{1,0:T(8,128)S(1)}, f32[256,512]{1,0:T(8,128)S(1)}, u32[]{:S(2)}, u32[]{:S(2)}) collective-permute-start(f32[256,512]{1,0:T(8,128)S(1)} %get-tuple-element.95.refs_11_), channel_id=1, source_target_pairs={{0,16},{16,0},{1,17},{17,1},{2,18},{18,2},{3,19},{19,3},{4,20},{20... | collective-permute-start | bytes 1572872 | tf_op jit(solution)/shard_map/ppermute | solution.py:342
  82.4 7.6 %collective-permute-start.20 = (f32[256,512]{1,0:T(8,128)S(1)}, f32[256,512]{1,0:T(8,128)S(1)}, u32[]{:S(2)}, u32[]{:S(2)}) collective-permute-start(f32[256,512]{1,0:T(8,128)S(1)} %get-tuple-element.96.refs_12_), channel_id=1, source_target_pairs={{0,16},{16,0},{1,17},{17,1},{2,18},{18,2},{3,19},{19,3},{4,20},{20... | collective-permute-start | bytes 1572872 | tf_op jit(solution)/shard_map/ppermute | solution.py:342
  82.5 21.5 %collective-permute-start.23 = (f32[1032,128]{1,0:T(8,128)S(1)}, f32[1032,128]{1,0:T(8,128)S(1)}, u32[]{:S(2)}, u32[]{:S(2)}) collective-permute-start(f32[1032,128]{1,0:T(8,128)S(1)} %get-tuple-element.115), channel_id=1, source_target_pairs={{2,0},{3,2},{6,4},{7,6},{10,8},{11,10},{14,12},{15,14},{18,16},{19... | collective-permute-start | bytes 1585160 | tf_op jit(solution)/shard_map/ppermute | solution.py:335
  83.8 22.1 %collective-permute-start.24 = (f32[1032,128]{1,0:T(8,128)S(1)}, f32[1032,128]{1,0:T(8,128)S(1)}, u32[]{:S(2)}, u32[]{:S(2)}) collective-permute-start(f32[1032,128]{1,0:T(8,128)S(1)} %collective-permute-done.14.refs_13_.refs_8_.refs_32_), channel_id=1, source_target_pairs={{0,1},{1,0},{2,3},{3,2},{4,5},{5,4},{6,7},{7,6},{8,9},{9,8},{10,11... | collective-permute-start | bytes 1585160 | tf_op jit(solution)/shard_map/ppermute | solution.py:335
  85.8 23.9 %collective-permute-start.25 = (f32[1032,128]{1,0:T(8,128)S(1)}, f32[1032,128]{1,0:T(8,128)S(1)}, u32[]{:S(2)}, u32[]{:S(2)}) collective-permute-start(f32[1032,128]{1,0:T(8,128)S(1)} %collective-permute-done.18.refs_9_.refs_33_.refs_2_.refs_8_), channel_id=1, source_target_pairs={{0,1},{1,0},{4,5},{5,4},{8,9},{9,8},{12,13},{13,12},{16,17},{17,16... | collective-permute-start | bytes 1585160 | tf_op jit(solution)/shard_map/ppermute | solution.py:335
  (15 other events, 143.4 us)
